TPU v7x, 32 devices: a whole 2x2x4 slice. The times are simulated.
32 devices in a mesh: section: 4 (over y, x), expert: 8 (over z, core).
Axes of the slice: x: 2, y: 2, z: 4, core: 2. Of those that a mesh axis runs over, the one named last changes fastest.
Arguments:
- tokens: bfloat16 [4, 128, 4096], P('section', 'expert'), may hold values from -6 to 6
- norm_gain: float32 [4, 4096], P('section'), may hold values from 0.1 to 1.9
- first_routes: int32 [4, 128, 1], P('section', 'expert'), may hold values from 0 to 3; in each aligned block of 16 rows (0 to 15, 16 to 31, ..., all dimensions but the last counted through in order) at most 5 rows name the same one
- first_gates: float32 [4, 128, 1], P('section', 'expert'), may hold values from 0.25 to 2
- second_routes: int32 [4, 128, 1], P('section', 'expert'), may hold values from 0 to 3; in each aligned block of 16 rows (0 to 15, 16 to 31, ..., all dimensions but the last counted through in order) at most 5 rows name the same one
- second_gates: float32 [4, 128, 1], P('section', 'expert'), may hold values from 0.25 to 2
- gate_proj: bfloat16 [4, 8, 4096, 512], P('section', 'expert'), may hold values from -0.09375 to 0.09375
- up_proj: bfloat16 [4, 8, 4096, 512], P('section', 'expert'), may hold values from -0.09375 to 0.09375
- down_proj: bfloat16 [4, 8, 512, 4096], P('section', 'expert'), may hold values from -0.1875 to 0.1875
Outputs:
- mixed: bfloat16 [4, 128, 4096], P('section', 'expert')
Inputs may be any that keep to these rules, and one draw needn't show every extreme that they name: `first_routes`: within the 16 rows of one device, no expert id appears more than 5 times, and in some devices one id appears exactly 5 times. `second_routes`: within the 16 rows of one device, no expert id appears more than 5 times, and in some devices one id appears exactly 5 times.
All inputs are finite; a program needn't handle non-finite values.
Results may differ from a plain program's by a relative error of at most 0.0078.
Values may be sent and summed in bfloat16 or wider, within the bound.
No kernel may reach another device: no remote copies, remote signals or barrier semaphores. Data moves between devices by JAX's collectives and lax.ppermute only.
A program may use at most 64 MiB of HBM per device.

v0:
```python
import functools

import jax
import jax.numpy as jnp
from jax import lax
from jax.experimental import pallas as pl
from jax.experimental.pallas import tpu as pltpu
from jax.sharding import PartitionSpec as P

EXPERTS = 4
CAP = 5
ROWS = 16
CHUNKS = 3
EPS = 1e-06
F32 = jnp.float32
BF16 = jnp.bfloat16
VMEM = pl.BlockSpec(memory_space=pltpu.VMEM)
HBM = pl.BlockSpec(memory_space=pltpu.HBM)


def distance(place):
    return EXPERTS - 1 - place


def fifth(value):
    return (value * 205) >> 10


def chunk_width(width):
    return -(-width // (CHUNKS * 128)) * 128


def chunk_span(width, chunk):
    start = chunk * chunk_width(width)
    return start, min(width, start + chunk_width(width)) - start


def upright(row):
    rows = row.shape[1]
    same = lax.broadcasted_iota(jnp.int32, (rows, rows), 0) == lax.broadcasted_iota(
        jnp.int32, (rows, rows), 1
    )
    return jnp.sum(jnp.where(same, row, 0.0), axis=1, keepdims=True)


def slots_of(routes):
    rows = routes.shape[0]
    lanes = lax.broadcasted_iota(jnp.int32, (rows, 128), 1).astype(F32)
    one_hot = (routes == lanes).astype(F32)
    earlier = lax.broadcasted_iota(jnp.int32, (rows, rows), 0) > lax.broadcasted_iota(
        jnp.int32, (rows, rows), 1
    )
    before = jnp.dot(earlier.astype(BF16), one_hot.astype(BF16), preferred_element_type=F32)
    return routes * CAP + jnp.sum(before * one_hot, axis=1, keepdims=True)


def block_map(slots, expert, chunk):
    spot = lax.broadcasted_iota(jnp.int32, (slots.shape[0], EXPERTS * ROWS), 1)
    inner = (spot & (ROWS - 1)) - CAP * chunk
    target = (distance(spot >> 4) ^ expert) * CAP + inner
    target = jnp.where((inner >= 0) & (inner < CAP), target, -1)
    return (slots == target.astype(F32)).astype(BF16)


def normalize(values, gain):
    inv_scale = lax.rsqrt(jnp.mean(values * values, axis=-1, keepdims=True) + EPS)
    return (values * inv_scale * gain).astype(BF16)


def write_blocks(normed, slots, expert, block_refs):
    width = normed.shape[1]
    pieces = []
    for chunk in range(CHUNKS):
        start, span = chunk_span(width, chunk)
        piece = lax.dot_general(
            block_map(slots, expert, chunk),
            normed[:, start : start + span],
            (((0,), (0,)), ((), ())),
            preferred_element_type=F32,
        )
        if span < chunk_width(width):
            piece = jnp.concatenate(
                [piece, jnp.zeros((piece.shape[0], chunk_width(width) - span), F32)], axis=1
            )
        pieces.append(piece)
    packed = sum(pieces[1:], pieces[0]).astype(BF16)
    hand_out(packed, block_refs)


def hand_out(values, refs):
    start = 0
    for ref in refs:
        ref[...] = values[start : start + ref.shape[0]]
        start += ref.shape[0]


def my_expert(group):
    return lax.axis_index("expert") // group


def split_parts(values):
    parts = []
    for _ in range(3):
        parts.append(values.astype(BF16))
        values = values - parts[-1].astype(F32)
    return parts


def pack_kernel(group, *refs):
    sources, block_refs, ahead_ref = refs[:4], refs[4 : 4 + EXPERTS], refs[4 + EXPERTS]
    held, sems = refs[5 + EXPERTS : -1], refs[-1]
    copies = [
        pltpu.make_async_copy(source, place, sems.at[i])
        for i, (source, place) in enumerate(zip(sources, held))
    ]
    for copy in copies:
        copy.start()
    for copy in copies:
        copy.wait()
    x_ref, gain_ref, routes_ref, gates_ref = held
    rows, width = x_ref.shape
    slots = slots_of(upright(routes_ref[...].astype(F32)))
    lane = lax.broadcasted_iota(jnp.int32, (rows, 128), 1)
    meta = jnp.zeros((rows, 128), F32)
    for i, column in enumerate([slots, *split_parts(upright(gates_ref[...]))]):
        meta = jnp.where(lane == i, column.astype(F32), meta)
    ahead_ref[:, :width] = x_ref[...]
    ahead_ref[:, width:] = meta.astype(BF16)
    normed = normalize(x_ref[...].astype(F32), gain_ref[...])
    write_blocks(normed, slots, my_expert(group), block_refs)


def residual(x, slots, gates, expert, blocks):
    width = x.shape[1]
    found = []
    for chunk in range(CHUNKS):
        _, span = chunk_span(width, chunk)
        found.append(
            jnp.dot(
                block_map(slots, expert, chunk), blocks[:, :span], preferred_element_type=F32
            )
        )
    update = (gates * jnp.concatenate(found, axis=1)).astype(BF16)
    return x.astype(F32) + update.astype(F32)


def middle_kernel(group, b0, b1, b2, carried_ref, gain_ref, routes_ref, first_ref, *block_refs):
    expert = my_expert(group)
    width = first_ref.shape[1]
    blocks = jnp.concatenate([b0[...], b1[...], b2[...], carried_ref[:, width + 128 :]], axis=0)
    meta = carried_ref[:, width : width + 128].astype(F32)
    gates = meta[:, 1:2] + meta[:, 2:3] + meta[:, 3:4]
    first = residual(carried_ref[:, :width], meta[:, 0:1], gates, expert, blocks).astype(BF16)
    first_ref[...] = first
    slots = slots_of(upright(routes_ref[...].astype(F32)))
    normed = normalize(first.astype(F32), gain_ref[...])
    write_blocks(normed, slots, expert, block_refs)


def last_kernel(group, x_ref, b0, b1, b2, b3, routes_ref, gates_ref, out_ref):
    blocks = jnp.concatenate([b0[...], b1[...], b2[...], b3[...]], axis=0)
    slots = slots_of(upright(routes_ref[...].astype(F32)))
    gates = upright(gates_ref[...])
    out_ref[...] = residual(x_ref[...], slots, gates, my_expert(group), blocks).astype(BF16)


def compact_map(shape, compact_dim, chunk):
    compact = lax.broadcasted_iota(jnp.int32, shape, compact_dim)
    spot = lax.broadcasted_iota(jnp.int32, shape, 1 - compact_dim)
    block = fifth(compact)
    wanted = block * ROWS + CAP * chunk + compact - CAP * block
    return (wanted == spot).astype(BF16)


def expert_kernel(given, w_gate, w_up, w_down, *refs):
    ins, outs, (x_ref, part_ref) = refs[:given], refs[given:-2], refs[-2:]
    count = sum(ref.shape[0] for ref in ins) // ROWS
    width, units = w_gate.shape
    rows = x_ref.shape[0]
    blocks = jnp.concatenate([ref[...] for ref in ins], axis=0)
    for chunk in range(CHUNKS):
        start, span = chunk_span(width, chunk)
        x_ref[:, start : start + span] = jnp.dot(
            compact_map((rows, count * ROWS), 0, chunk),
            blocks[:, :span],
            preferred_element_type=F32,
        ).astype(BF16)
    x = x_ref[...]
    gate_val = jnp.dot(x, w_gate[...], preferred_element_type=F32)
    up_val = jnp.dot(x, w_up[...], preferred_element_type=F32)
    hidden = (gate_val / (1.0 + jnp.exp(-gate_val)) * up_val).astype(BF16)
    part_ref[...] = jnp.dot(hidden, w_down[...], preferred_element_type=F32).astype(BF16)
    total = None
    for chunk in range(CHUNKS):
        start, span = chunk_span(width, chunk)
        piece = jnp.dot(
            compact_map((count * ROWS, rows), 1, chunk),
            part_ref[:, start : start + span],
            preferred_element_type=F32,
        )
        if span < chunk_width(width):
            piece = jnp.concatenate(
                [piece, jnp.zeros((piece.shape[0], chunk_width(width) - span), F32)], axis=1
            )
        total = piece if total is None else total + piece
    total = total.astype(BF16)
    hand_out(total, outs)


def summed(refs):
    total = refs[0][...].astype(F32)
    for ref in refs[1:]:
        total = total + ref[...].astype(F32)
    return total.astype(BF16)


def sum_kernel(given, *refs):
    hand_out(summed(refs[:given]), refs[given:])


def carry_kernel(ahead_ref, *refs):
    ins, out_ref = refs[:-1], refs[-1]
    width = ahead_ref.shape[1]
    out_ref[:, :width] = ahead_ref[...]
    out_ref[:, width:] = summed(ins)


def call(body, outs, ins, megabytes, scratch=(), flops=0, space=VMEM):
    moved = sum(a.size * a.dtype.itemsize for a in (*ins, *outs))
    return pl.pallas_call(
        body,
        out_shape=outs,
        in_specs=[space] * len(ins),
        out_specs=[VMEM] * len(outs),
        scratch_shapes=list(scratch),
        compiler_params=pltpu.CompilerParams(vmem_limit_bytes=megabytes << 20),
        cost_estimate=pl.CostEstimate(flops=flops, bytes_accessed=moved, transcendentals=0),
    )(*ins)


def on_device(tokens, gain, routes_1, gates_1, routes_2, gates_2, gate_proj, up_proj, down_proj):
    sections, devices = lax.axis_size("section"), lax.axis_size("expert")
    group = devices // EXPERTS
    rows, width = tokens.shape[1:]
    weights = (gate_proj[0, 0], up_proj[0, 0], down_proj[0, 0])
    wide = chunk_width(width)
    block = jax.ShapeDtypeStruct((ROWS, wide), BF16)
    whole = jax.ShapeDtypeStruct((rows, width), BF16)
    ahead = jax.ShapeDtypeStruct((rows, width + 128), BF16)
    routes_1, gates_1, routes_2, gates_2 = (
        a.reshape(1, rows) for a in (routes_1, gates_1, routes_2, gates_2)
    )

    def to_expert(place):
        far = distance(place)
        return [(i, (i // group ^ far) * group + i % group) for i in range(devices)]

    def within(shift):
        return [(i, i // group * group + (i + shift) % group) for i in range(devices)]

    def onward(place):
        return [
            (s * devices + i, (s + 1) % sections * devices + j)
            for s in range(sections)
            for i, j in to_expert(place)
        ]

    def across(blocks):
        return [lax.ppermute(blocks[i], "expert", to_expert(i)) for i in range(EXPERTS - 1)]

    def shared(arrived):
        return arrived + [
            lax.ppermute(a, "expert", within(m)) for m in range(1, group) for a in arrived
        ]

    def experts(ins):
        count = sum(a.shape[0] for a in ins) // ROWS
        held = -(-count * CAP // ROWS) * ROWS
        sums = call(
            functools.partial(expert_kernel, len(ins)),
            [jax.ShapeDtypeStruct((count // group * ROWS, wide), BF16)] * group,
            [*weights, *ins],
            24,
            [pltpu.VMEM((held, width), BF16), pltpu.VMEM((held, width), BF16)],
            flops=6 * 256 * width * weights[0].shape[1],
        )
        return [sums[0]] + [
            lax.ppermute(sums[m], "expert", within(-m)) for m in range(1, group)
        ]

    def added(terms):
        parts = terms[0].shape[0] // ROWS
        return call(functools.partial(sum_kernel, group), [block] * parts, terms, 8)

    sources = [
        pltpu.with_memory_space_constraint(a, pltpu.HBM)
        for a in (tokens[0], gain, routes_1, gates_1)
    ]
    *blocks, travelling = call(
        functools.partial(pack_kernel, group),
        [block] * EXPERTS + [ahead],
        sources,
        8,
        [pltpu.VMEM(a.shape, a.dtype) for a in sources]
        + [pltpu.SemaphoreType.DMA((len(sources),))],
        flops=10**10,
        space=HBM,
    )
    arrived = across(blocks[:-1])
    (carry,) = call(
        carry_kernel,
        [jax.ShapeDtypeStruct((rows, width + 128 + wide), BF16)],
        [travelling, *experts(shared(blocks[-1:]))],
        8,
    )
    *ins, carry = lax.optimization_barrier((*shared(arrived), carry))
    carried = lax.ppermute(carry, "section", [(i, (i + 1) % sections) for i in range(sections)])
    sums = added(experts(ins))
    home = [lax.ppermute(sums[i], ("section", "expert"), onward(i)) for i in range(EXPERTS - 1)]
    first, *blocks = call(
        functools.partial(middle_kernel, group),
        [whole] + [block] * EXPERTS,
        [*home, carried, gain, routes_2],
        8,
    )
    sums = added(experts(shared(across(blocks[:-1]) + blocks[-1:])))
    home = across(sums[:-1])
    (mixed,) = call(
        functools.partial(last_kernel, group),
        [whole],
        [first, *home, sums[-1], routes_2, gates_2],
        8,
    )
    return mixed[None]


def solution(mesh):
    rows = P("section", "expert", None)
    slabs = P("section", "expert", None, None)
    return jax.shard_map(
        on_device,
        mesh=mesh,
        in_specs=(rows, P("section", None), rows, rows, rows, rows, slabs, slabs, slabs),
        out_specs=rows,
        check_vma=False,
    )
```

profile of v0, /device:TPU:0, one launch (start us, length us, event | category | flops | bytes accessed | tf_op | source)
XLA Modules:
  0.0 50.0 jit_solution(8326057931958993955)
XLA Ops:
  0.0 1.7 %shard_map.91 = (bf16[16,1408]{1,0:T(8,128)(2,1)S(1)}, bf16[16,1408]{1,0:T(8,128)(2,1)S(1)}, bf16[16,1408]{1,0:T(8,128)(2,1)S(1)}, bf16[16,1408]{1,0:T(8,128)(2,1)S(1)}, bf16[16,4224]{1,0:T(8,128)(2,1)S(1)}) custom-call(bf16[16,4096]{1,0:T(8,128)(2,1)} %bitcast.21, f32[1,4096]{1,0:T(1,128)} %gain_ref.1, s32[1,16]{1,0:T(1,128)} %bitcast.22, f32[1,16]{1,0:T(1,128)} %bitcast.23), custom_call_target="tpu_custom_call" | custom-call | flops 10000000000 | bytes 462976 | tf_op jit(solution)/shard_map/pallas_call | solution.py:230
  1.7 0.5 %collective-permute-start.6 = (bf16[16,1408]{1,0:T(8,128)(2,1)S(1)}, bf16[16,1408]{1,0:T(8,128)(2,1)S(1)}, u32[]{:S(2)}, u32[]{:S(2)}) collective-permute-start(bf16[16,1408]{1,0:T(8,128)(2,1)S(1)} %get-tuple-element.39.refs_0_), channel_id=1, source_target_pairs={{0,1},{1,0},{2,3},{3,2},{4,5},{5,4},{6,7},{7,6},{8,9},{9,8},{10,11... | collective-permute-start | bytes 135176 | tf_op jit(solution)/shard_map/ppermute | solution.py:273
  2.2 4.7 %collective-permute-start = (bf16[16,1408]{1,0:T(8,128)(2,1)S(1)}, bf16[16,1408]{1,0:T(8,128)(2,1)S(1)}, u32[]{:S(2)}, u32[]{:S(2)}) collective-permute-start(bf16[16,1408]{1,0:T(8,128)(2,1)S(1)} %get-tuple-element.35), channel_id=1, source_target_pairs={{0,6},{1,7},{2,4},{3,5},{4,2},{5,3},{6,0},{7,1},{8,14},{9,15},{10,... | collective-permute-start | bytes 135176 | tf_op jit(solution)/shard_map/ppermute | solution.py:269
  6.9 0.6 %collective-permute-start.2 = (bf16[16,1408]{1,0:T(8,128)(2,1)S(1)}, bf16[16,1408]{1,0:T(8,128)(2,1)S(1)}, u32[]{:S(2)}, u32[]{:S(2)}) collective-permute-start(bf16[16,1408]{1,0:T(8,128)(2,1)S(1)} %get-tuple-element.37), channel_id=1, source_target_pairs={{0,2},{1,3},{2,0},{3,1},{4,6},{5,7},{6,4},{7,5},{8,10},{9,11},{10,... | collective-permute-start | bytes 135176 | tf_op jit(solution)/shard_map/ppermute | solution.py:269
  7.6 2.1 %shard_map.92 = (bf16[16,1408]{1,0:T(8,128)(2,1)S(1)}, bf16[16,1408]{1,0:T(8,128)(2,1)S(1)}) custom-call(bf16[4096,512]{1,0:T(8,128)(2,1)S(1)} %bitcast.9, bf16[4096,512]{1,0:T(8,128)(2,1)S(1)} %bitcast.12, bf16[512,4096]{1,0:T(8,128)(2,1)S(1)} %bitcast.15, bf16[16,1408]{1,0:T(8,128)(2,1)S(1)} %get-tuple-element.39.refs_0_, ...), custom_call_target="tpu_custom_call" | custom-call | flops 3221225472 | bytes 12763136 | tf_op jit(solution)/shard_map/pallas_call | solution.py:230
  9.7 0.5 collective-permute-start.3
  10.2 1.7 %collective-permute-done.1.refs_1_ = bf16[16,1408]{1,0:T(8,128)(2,1)S(1)} collective-permute-done((bf16[16,1408]{1,0:T(8,128)(2,1)S(1)}, bf16[16,1408]{1,0:T(8,128)(2,1)S(1)}, u32[]{:S(2)}, u32[]{:S(2)}) %collective-permute-start.1) | collective-permute-done | bytes 45088 | tf_op jit(solution)/shard_map/ppermute | solution.py:269
  11.9 0.5 %collective-permute-start.5 = (bf16[16,1408]{1,0:T(8,128)(2,1)S(1)}, bf16[16,1408]{1,0:T(8,128)(2,1)S(1)}, u32[]{:S(2)}, u32[]{:S(2)}) collective-permute-start(bf16[16,1408]{1,0:T(8,128)(2,1)S(1)} %collective-permute-done.2.refs_2_), channel_id=1, source_target_pairs={{0,1},{1,0},{2,3},{3,2},{4,5},{5,4},{6,7},{7,6},{8,9},{9,8},{10,11... | collective-permute-start | bytes 135176 | tf_op jit(solution)/shard_map/ppermute | solution.py:273
  12.5 0.6 %collective-permute-done.4.refs_4_ = bf16[16,1408]{1,0:T(8,128)(2,1)S(1)} collective-permute-done((bf16[16,1408]{1,0:T(8,128)(2,1)S(1)}, bf16[16,1408]{1,0:T(8,128)(2,1)S(1)}, u32[]{:S(2)}, u32[]{:S(2)}) %collective-permute-start.4) | collective-permute-done | bytes 45088 | tf_op jit(solution)/shard_map/ppermute | solution.py:273
  13.3 2.3 %shard_map.94 = (bf16[48,1408]{1,0:T(8,128)(2,1)S(1)}, bf16[48,1408]{1,0:T(8,128)(2,1)S(1)}) custom-call(bf16[4096,512]{1,0:T(8,128)(2,1)S(1)} %bitcast.10, bf16[4096,512]{1,0:T(8,128)(2,1)S(1)} %bitcast.13, bf16[512,4096]{1,0:T(8,128)(2,1)S(1)} %bitcast.16, bf16[16,1408]{1,0:T(8,128)(2,1)S(1)} %collective-permute-done.refs_0_, ...), custom_call_target="tpu_custom_call" | custom-call | flops 3221225472 | bytes 13123584 | tf_op jit(solution)/shard_map/pallas_call | solution.py:230
  16.1 1.5 %collective-permute-start.12 = (bf16[16,5632]{1,0:T(8,128)(2,1)S(1)}, bf16[16,5632]{1,0:T(8,128)(2,1)S(1)}, u32[]{:S(2)}, u32[]{:S(2)}) collective-permute-start(bf16[16,5632]{1,0:T(8,128)(2,1)S(1)} %shard_map.93), channel_id=1, source_target_pairs={{0,8},{8,16},{16,24},{24,0},{1,9},{9,17},{17,25},{25,1},{2,10},{10... | collective-permute-start | bytes 540680 | tf_op jit(solution)/shard_map/ppermute | solution.py:317
  17.6 3.0 %collective-permute-start.9 = (bf16[16,1408]{1,0:T(8,128)(2,1)S(1)}, bf16[16,1408]{1,0:T(8,128)(2,1)S(1)}, u32[]{:S(2)}, u32[]{:S(2)}) collective-permute-start(bf16[16,1408]{1,0:T(8,128)(2,1)S(1)} %get-tuple-element.50), channel_id=1, source_target_pairs={{0,14},{1,15},{2,12},{3,13},{4,10},{5,11},{6,8},{7,9},{8,22},{9,23... | collective-permute-start | bytes 135176 | tf_op jit(solution)/shard_map/ppermute | solution.py:319
  20.6 1.0 %collective-permute-start.10 = (bf16[16,1408]{1,0:T(8,128)(2,1)S(1)}, bf16[16,1408]{1,0:T(8,128)(2,1)S(1)}, u32[]{:S(2)}, u32[]{:S(2)}) collective-permute-start(bf16[16,1408]{1,0:T(8,128)(2,1)S(1)} %get-tuple-element.51), channel_id=1, source_target_pairs={{0,12},{1,13},{2,14},{3,15},{4,8},{5,9},{6,10},{7,11},{8,20},{9,21... | collective-permute-start | bytes 135176 | tf_op jit(solution)/shard_map/ppermute | solution.py:319
  21.6 2.7 %collective-permute-start.11 = (bf16[16,1408]{1,0:T(8,128)(2,1)S(1)}, bf16[16,1408]{1,0:T(8,128)(2,1)S(1)}, u32[]{:S(2)}, u32[]{:S(2)}) collective-permute-start(bf16[16,1408]{1,0:T(8,128)(2,1)S(1)} %get-tuple-element.52), channel_id=1, source_target_pairs={{0,10},{1,11},{2,8},{3,9},{4,14},{5,15},{6,12},{7,13},{8,18},{9,19... | collective-permute-start | bytes 135176 | tf_op jit(solution)/shard_map/ppermute | solution.py:319
  24.3 1.1 %collective-permute-done.9.b0 = bf16[16,1408]{1,0:T(8,128)(2,1)S(1)} collective-permute-done((bf16[16,1408]{1,0:T(8,128)(2,1)S(1)}, bf16[16,1408]{1,0:T(8,128)(2,1)S(1)}, u32[]{:S(2)}, u32[]{:S(2)}) %collective-permute-start.9) | collective-permute-done | bytes 45088 | tf_op jit(solution)/shard_map/ppermute | solution.py:319
  25.4 2.1 %collective-permute-done.10.b1 = bf16[16,1408]{1,0:T(8,128)(2,1)S(1)} collective-permute-done((bf16[16,1408]{1,0:T(8,128)(2,1)S(1)}, bf16[16,1408]{1,0:T(8,128)(2,1)S(1)}, u32[]{:S(2)}, u32[]{:S(2)}) %collective-permute-start.10) | collective-permute-done | bytes 45088 | tf_op jit(solution)/shard_map/ppermute | solution.py:319
  27.9 0.7 %shard_map.96 = (bf16[16,4096]{1,0:T(8,128)(2,1)S(1)}, bf16[16,1408]{1,0:T(8,128)(2,1)S(1)}, bf16[16,1408]{1,0:T(8,128)(2,1)S(1)}, bf16[16,1408]{1,0:T(8,128)(2,1)S(1)}, bf16[16,1408]{1,0:T(8,128)(2,1)S(1)}) custom-call(bf16[16,1408]{1,0:T(8,128)(2,1)S(1)} %collective-permute-done.9.b0, bf16[16,1408]{1,0:T(8,128)(2,1)S(1)} %collective-permute-done.10.b1, ...), custom_call_target="tpu_custom_call" | custom-call | bytes 643136 | tf_op jit(solution)/shard_map/pallas_call | solution.py:230
  28.6 2.1 %collective-permute-start.13 = (bf16[16,1408]{1,0:T(8,128)(2,1)S(1)}, bf16[16,1408]{1,0:T(8,128)(2,1)S(1)}, u32[]{:S(2)}, u32[]{:S(2)}) collective-permute-start(bf16[16,1408]{1,0:T(8,128)(2,1)S(1)} %get-tuple-element.55), channel_id=1, source_target_pairs={{0,6},{1,7},{2,4},{3,5},{4,2},{5,3},{6,0},{7,1},{8,14},{9,15},{10,... | collective-permute-start | bytes 135176 | tf_op jit(solution)/shard_map/ppermute | solution.py:269
  30.7 1.3 %collective-permute-start.14 = (bf16[16,1408]{1,0:T(8,128)(2,1)S(1)}, bf16[16,1408]{1,0:T(8,128)(2,1)S(1)}, u32[]{:S(2)}, u32[]{:S(2)}) collective-permute-start(bf16[16,1408]{1,0:T(8,128)(2,1)S(1)} %get-tuple-element.56), channel_id=1, source_target_pairs={{0,4},{1,5},{2,6},{3,7},{4,0},{5,1},{6,2},{7,3},{8,12},{9,13},{10,... | collective-permute-start | bytes 135176 | tf_op jit(solution)/shard_map/ppermute | solution.py:269
  32.0 1.1 %collective-permute-start.15 = (bf16[16,1408]{1,0:T(8,128)(2,1)S(1)}, bf16[16,1408]{1,0:T(8,128)(2,1)S(1)}, u32[]{:S(2)}, u32[]{:S(2)}) collective-permute-start(bf16[16,1408]{1,0:T(8,128)(2,1)S(1)} %get-tuple-element.57), channel_id=1, source_target_pairs={{0,2},{1,3},{2,0},{3,1},{4,6},{5,7},{6,4},{7,5},{8,10},{9,11},{10,... | collective-permute-start | bytes 135176 | tf_op jit(solution)/shard_map/ppermute | solution.py:269
  33.1 1.6 %collective-permute-done.13.refs_0_ = bf16[16,1408]{1,0:T(8,128)(2,1)S(1)} collective-permute-done((bf16[16,1408]{1,0:T(8,128)(2,1)S(1)}, bf16[16,1408]{1,0:T(8,128)(2,1)S(1)}, u32[]{:S(2)}, u32[]{:S(2)}) %collective-permute-start.13) | collective-permute-done | bytes 45088 | tf_op jit(solution)/shard_map/ppermute | solution.py:269
  34.7 0.9 %collective-permute-done.14.refs_1_ = bf16[16,1408]{1,0:T(8,128)(2,1)S(1)} collective-permute-done((bf16[16,1408]{1,0:T(8,128)(2,1)S(1)}, bf16[16,1408]{1,0:T(8,128)(2,1)S(1)}, u32[]{:S(2)}, u32[]{:S(2)}) %collective-permute-start.14) | collective-permute-done | bytes 45088 | tf_op jit(solution)/shard_map/ppermute | solution.py:269
  36.1 0.7 %collective-permute-done.17.refs_5_ = bf16[16,1408]{1,0:T(8,128)(2,1)S(1)} collective-permute-done((bf16[16,1408]{1,0:T(8,128)(2,1)S(1)}, bf16[16,1408]{1,0:T(8,128)(2,1)S(1)}, u32[]{:S(2)}, u32[]{:S(2)}) %collective-permute-start.17) | collective-permute-done | bytes 45088 | tf_op jit(solution)/shard_map/ppermute | solution.py:273
  36.8 0.5 collective-permute-done.18.refs_6_
  37.3 2.5 %shard_map.97 = (bf16[64,1408]{1,0:T(8,128)(2,1)S(1)}, bf16[64,1408]{1,0:T(8,128)(2,1)S(1)}) custom-call(bf16[4096,512]{1,0:T(8,128)(2,1)S(1)} %bitcast.11, bf16[4096,512]{1,0:T(8,128)(2,1)S(1)} %bitcast.14, bf16[512,4096]{1,0:T(8,128)(2,1)S(1)} %bitcast.17, bf16[16,1408]{1,0:T(8,128)(2,1)S(1)} %collective-permute-done.13.refs_0_, ...), custom_call_target="tpu_custom_call" | custom-call | flops 3221225472 | bytes 13303808 | tf_op jit(solution)/shard_map/pallas_call | solution.py:230
  40.0 1.3 %collective-permute-done.20.refs_1_ = bf16[64,1408]{1,0:T(8,128)(2,1)S(1)} collective-permute-done((bf16[64,1408]{1,0:T(8,128)(2,1)S(1)}, bf16[64,1408]{1,0:T(8,128)(2,1)S(1)}, u32[]{:S(2)}, u32[]{:S(2)}) %collective-permute-start.20) | collective-permute-done | bytes 180256 | tf_op jit(solution)/shard_map/ppermute | solution.py:288
  41.3 2.1 %collective-permute-start.21 = (bf16[16,1408]{1,0:T(8,128)(2,1)S(1)}, bf16[16,1408]{1,0:T(8,128)(2,1)S(1)}, u32[]{:S(2)}, u32[]{:S(2)}) collective-permute-start(bf16[16,1408]{1,0:T(8,128)(2,1)S(1)} %get-tuple-element.61), channel_id=1, source_target_pairs={{0,6},{1,7},{2,4},{3,5},{4,2},{5,3},{6,0},{7,1},{8,14},{9,15},{10,... | collective-permute-start | bytes 135176 | tf_op jit(solution)/shard_map/ppermute | solution.py:269
  43.4 0.5 collective-permute-start.22
  43.9 1.9 %collective-permute-start.23 = (bf16[16,1408]{1,0:T(8,128)(2,1)S(1)}, bf16[16,1408]{1,0:T(8,128)(2,1)S(1)}, u32[]{:S(2)}, u32[]{:S(2)}) collective-permute-start(bf16[16,1408]{1,0:T(8,128)(2,1)S(1)} %get-tuple-element.63), channel_id=1, source_target_pairs={{0,2},{1,3},{2,0},{3,1},{4,6},{5,7},{6,4},{7,5},{8,10},{9,11},{10,... | collective-permute-start | bytes 135176 | tf_op jit(solution)/shard_map/ppermute | solution.py:269
  45.8 1.7 %collective-permute-done.21.b0 = bf16[16,1408]{1,0:T(8,128)(2,1)S(1)} collective-permute-done((bf16[16,1408]{1,0:T(8,128)(2,1)S(1)}, bf16[16,1408]{1,0:T(8,128)(2,1)S(1)}, u32[]{:S(2)}, u32[]{:S(2)}) %collective-permute-start.21) | collective-permute-done | bytes 45088 | tf_op jit(solution)/shard_map/ppermute | solution.py:269
  47.4 1.4 %collective-permute-done.22.b1 = bf16[16,1408]{1,0:T(8,128)(2,1)S(1)} collective-permute-done((bf16[16,1408]{1,0:T(8,128)(2,1)S(1)}, bf16[16,1408]{1,0:T(8,128)(2,1)S(1)}, u32[]{:S(2)}, u32[]{:S(2)}) %collective-permute-start.22) | collective-permute-done | bytes 45088 | tf_op jit(solution)/shard_map/ppermute | solution.py:269
  48.8 1.1 %shard_map.99 = bf16[16,4096]{1,0:T(8,128)(2,1)} custom-call(bf16[16,4096]{1,0:T(8,128)(2,1)S(1)} %get-tuple-element.54.x_ref, bf16[16,1408]{1,0:T(8,128)(2,1)S(1)} %collective-permute-done.21.b0, bf16[16,1408]{1,0:T(8,128)(2,1)S(1)} %collective-permute-done.22.b1, bf16[16,1408]{1,0:T(8,128)(2,1)S(1)} %collective-permute-done.23.b2, ...), custom_call_target="tpu_custom_call" | custom-call | bytes 442496 | tf_op jit(solution)/shard_map/pallas_call | solution.py:230
  (37 shorter events, 2.0 us)
Async XLA Ops:
  0.0 7.6 %copy-start = (bf16[1,1,4096,512]{3,2,1,0:T(8,128)(2,1)S(1)}, bf16[1,1,4096,512]{3,2,1,0:T(8,128)(2,1)}, u32[]{:S(2)}) copy-start(bf16[1,1,4096,512]{3,2,1,0:T(8,128)(2,1)} %param.15) | copy-start | bytes 12582916
  0.0 7.6 %copy-start.1 = (bf16[1,1,4096,512]{3,2,1,0:T(8,128)(2,1)S(1)}, bf16[1,1,4096,512]{3,2,1,0:T(8,128)(2,1)}, u32[]{:S(2)}) copy-start(bf16[1,1,4096,512]{3,2,1,0:T(8,128)(2,1)} %param.16) | copy-start | bytes 12582916
  0.0 7.6 %copy-start.2 = (bf16[1,1,512,4096]{3,2,1,0:T(8,128)(2,1)S(1)}, bf16[1,1,512,4096]{3,2,1,0:T(8,128)(2,1)}, u32[]{:S(2)}) copy-start(bf16[1,1,512,4096]{3,2,1,0:T(8,128)(2,1)} %param.17) | copy-start | bytes 12582916
  1.7 5.8 %collective-permute-start.6 = (bf16[16,1408]{1,0:T(8,128)(2,1)S(1)}, bf16[16,1408]{1,0:T(8,128)(2,1)S(1)}, u32[]{:S(2)}, u32[]{:S(2)}) collective-permute-start(bf16[16,1408]{1,0:T(8,128)(2,1)S(1)} %get-tuple-element.39.refs_0_), channel_id=1, source_target_pairs={{0,1},{1,0},{2,3},{3,2},{4,5},{5,4},{6,7},{7,6},{8,9},{9,8},{10,11... | collective-permute-start | bytes 135176 | tf_op jit(solution)/shard_map/ppermute | solution.py:273
  2.2 7.5 %collective-permute-start = (bf16[16,1408]{1,0:T(8,128)(2,1)S(1)}, bf16[16,1408]{1,0:T(8,128)(2,1)S(1)}, u32[]{:S(2)}, u32[]{:S(2)}) collective-permute-start(bf16[16,1408]{1,0:T(8,128)(2,1)S(1)} %get-tuple-element.35), channel_id=1, source_target_pairs={{0,6},{1,7},{2,4},{3,5},{4,2},{5,3},{6,0},{7,1},{8,14},{9,15},{10,... | collective-permute-start | bytes 135176 | tf_op jit(solution)/shard_map/ppermute | solution.py:269
  6.9 5.0 %collective-permute-start.1 = (bf16[16,1408]{1,0:T(8,128)(2,1)S(1)}, bf16[16,1408]{1,0:T(8,128)(2,1)S(1)}, u32[]{:S(2)}, u32[]{:S(2)}) collective-permute-start(bf16[16,1408]{1,0:T(8,128)(2,1)S(1)} %get-tuple-element.36), channel_id=1, source_target_pairs={{0,4},{1,5},{2,6},{3,7},{4,0},{5,1},{6,2},{7,3},{8,12},{9,13},{10,... | collective-permute-start | bytes 135176 | tf_op jit(solution)/shard_map/ppermute | solution.py:269
  6.9 5.0 %collective-permute-start.2 = (bf16[16,1408]{1,0:T(8,128)(2,1)S(1)}, bf16[16,1408]{1,0:T(8,128)(2,1)S(1)}, u32[]{:S(2)}, u32[]{:S(2)}) collective-permute-start(bf16[16,1408]{1,0:T(8,128)(2,1)S(1)} %get-tuple-element.37), channel_id=1, source_target_pairs={{0,2},{1,3},{2,0},{3,1},{4,6},{5,7},{6,4},{7,5},{8,10},{9,11},{10,... | collective-permute-start | bytes 135176 | tf_op jit(solution)/shard_map/ppermute | solution.py:269
  9.6 2.8 %collective-permute-start.7 = (bf16[16,1408]{1,0:T(8,128)(2,1)S(1)}, bf16[16,1408]{1,0:T(8,128)(2,1)S(1)}, u32[]{:S(2)}, u32[]{:S(2)}) collective-permute-start(bf16[16,1408]{1,0:T(8,128)(2,1)S(1)} %get-tuple-element.41), channel_id=1, source_target_pairs={{0,1},{1,0},{2,3},{3,2},{4,5},{5,4},{6,7},{7,6},{8,9},{9,8},{10,11... | collective-permute-start | bytes 135176 | tf_op jit(solution)/shard_map/ppermute | solution.py:288
  9.7 2.8 %collective-permute-start.3 = (bf16[16,1408]{1,0:T(8,128)(2,1)S(1)}, bf16[16,1408]{1,0:T(8,128)(2,1)S(1)}, u32[]{:S(2)}, u32[]{:S(2)}) collective-permute-start(bf16[16,1408]{1,0:T(8,128)(2,1)S(1)} %collective-permute-done.refs_0_), channel_id=1, source_target_pairs={{0,1},{1,0},{2,3},{3,2},{4,5},{5,4},{6,7},{7,6},{8,9},{9,8},{10,11... | collective-permute-start | bytes 135176 | tf_op jit(solution)/shard_map/ppermute | solution.py:273
  11.9 1.2 %collective-permute-start.4 = (bf16[16,1408]{1,0:T(8,128)(2,1)S(1)}, bf16[16,1408]{1,0:T(8,128)(2,1)S(1)}, u32[]{:S(2)}, u32[]{:S(2)}) collective-permute-start(bf16[16,1408]{1,0:T(8,128)(2,1)S(1)} %collective-permute-done.1.refs_1_), channel_id=1, source_target_pairs={{0,1},{1,0},{2,3},{3,2},{4,5},{5,4},{6,7},{7,6},{8,9},{9,8},{10,11... | collective-permute-start | bytes 135176 | tf_op jit(solution)/shard_map/ppermute | solution.py:273
  11.9 1.4 %collective-permute-start.5 = (bf16[16,1408]{1,0:T(8,128)(2,1)S(1)}, bf16[16,1408]{1,0:T(8,128)(2,1)S(1)}, u32[]{:S(2)}, u32[]{:S(2)}) collective-permute-start(bf16[16,1408]{1,0:T(8,128)(2,1)S(1)} %collective-permute-done.2.refs_2_), channel_id=1, source_target_pairs={{0,1},{1,0},{2,3},{3,2},{4,5},{5,4},{6,7},{7,6},{8,9},{9,8},{10,11... | collective-permute-start | bytes 135176 | tf_op jit(solution)/shard_map/ppermute | solution.py:273
  12.5 15.5 %copy-start.3 = (f32[1,4096]{1,0:T(1,128)S(1)}, f32[1,4096]{1,0:T(1,128)}, u32[]{:S(2)}) copy-start(f32[1,4096]{1,0:T(1,128)} %gain_ref.1) | copy-start | bytes 49156
  12.5 15.4 %copy-start.4 = (s32[1,16,1]{1,2,0:T(1,128)S(1)}, s32[1,16,1]{1,2,0:T(1,128)}, u32[]{:S(2)}) copy-start(s32[1,16,1]{1,2,0:T(1,128)} %param.13) | copy-start | bytes 196
  15.7 1.9 %collective-permute-start.8 = (bf16[48,1408]{1,0:T(8,128)(2,1)S(1)}, bf16[48,1408]{1,0:T(8,128)(2,1)S(1)}, u32[]{:S(2)}, u32[]{:S(2)}) collective-permute-start(bf16[48,1408]{1,0:T(8,128)(2,1)S(1)} %get-tuple-element.49), channel_id=1, source_target_pairs={{0,1},{1,0},{2,3},{3,2},{4,5},{5,4},{6,7},{7,6},{8,9},{9,8},{10,11... | collective-permute-start | bytes 405512 | tf_op jit(solution)/shard_map/ppermute | solution.py:288
  16.1 11.8 %collective-permute-start.12 = (bf16[16,5632]{1,0:T(8,128)(2,1)S(1)}, bf16[16,5632]{1,0:T(8,128)(2,1)S(1)}, u32[]{:S(2)}, u32[]{:S(2)}) collective-permute-start(bf16[16,5632]{1,0:T(8,128)(2,1)S(1)} %shard_map.93), channel_id=1, source_target_pairs={{0,8},{8,16},{16,24},{24,0},{1,9},{9,17},{17,25},{25,1},{2,10},{10... | collective-permute-start | bytes 540680 | tf_op jit(solution)/shard_map/ppermute | solution.py:317
  17.6 7.8 %collective-permute-start.9 = (bf16[16,1408]{1,0:T(8,128)(2,1)S(1)}, bf16[16,1408]{1,0:T(8,128)(2,1)S(1)}, u32[]{:S(2)}, u32[]{:S(2)}) collective-permute-start(bf16[16,1408]{1,0:T(8,128)(2,1)S(1)} %get-tuple-element.50), channel_id=1, source_target_pairs={{0,14},{1,15},{2,12},{3,13},{4,10},{5,11},{6,8},{7,9},{8,22},{9,23... | collective-permute-start | bytes 135176 | tf_op jit(solution)/shard_map/ppermute | solution.py:319
  20.6 6.9 %collective-permute-start.10 = (bf16[16,1408]{1,0:T(8,128)(2,1)S(1)}, bf16[16,1408]{1,0:T(8,128)(2,1)S(1)}, u32[]{:S(2)}, u32[]{:S(2)}) collective-permute-start(bf16[16,1408]{1,0:T(8,128)(2,1)S(1)} %get-tuple-element.51), channel_id=1, source_target_pairs={{0,12},{1,13},{2,14},{3,15},{4,8},{5,9},{6,10},{7,11},{8,20},{9,21... | collective-permute-start | bytes 135176 | tf_op jit(solution)/shard_map/ppermute | solution.py:319
  21.6 6.3 %collective-permute-start.11 = (bf16[16,1408]{1,0:T(8,128)(2,1)S(1)}, bf16[16,1408]{1,0:T(8,128)(2,1)S(1)}, u32[]{:S(2)}, u32[]{:S(2)}) collective-permute-start(bf16[16,1408]{1,0:T(8,128)(2,1)S(1)} %get-tuple-element.52), channel_id=1, source_target_pairs={{0,10},{1,11},{2,8},{3,9},{4,14},{5,15},{6,12},{7,13},{8,18},{9,19... | collective-permute-start | bytes 135176 | tf_op jit(solution)/shard_map/ppermute | solution.py:319
  28.6 6.1 %collective-permute-start.13 = (bf16[16,1408]{1,0:T(8,128)(2,1)S(1)}, bf16[16,1408]{1,0:T(8,128)(2,1)S(1)}, u32[]{:S(2)}, u32[]{:S(2)}) collective-permute-start(bf16[16,1408]{1,0:T(8,128)(2,1)S(1)} %get-tuple-element.55), channel_id=1, source_target_pairs={{0,6},{1,7},{2,4},{3,5},{4,2},{5,3},{6,0},{7,1},{8,14},{9,15},{10,... | collective-permute-start | bytes 135176 | tf_op jit(solution)/shard_map/ppermute | solution.py:269
  30.7 5.0 %collective-permute-start.14 = (bf16[16,1408]{1,0:T(8,128)(2,1)S(1)}, bf16[16,1408]{1,0:T(8,128)(2,1)S(1)}, u32[]{:S(2)}, u32[]{:S(2)}) collective-permute-start(bf16[16,1408]{1,0:T(8,128)(2,1)S(1)} %get-tuple-element.56), channel_id=1, source_target_pairs={{0,4},{1,5},{2,6},{3,7},{4,0},{5,1},{6,2},{7,3},{8,12},{9,13},{10,... | collective-permute-start | bytes 135176 | tf_op jit(solution)/shard_map/ppermute | solution.py:269
  32.0 4.1 %collective-permute-start.15 = (bf16[16,1408]{1,0:T(8,128)(2,1)S(1)}, bf16[16,1408]{1,0:T(8,128)(2,1)S(1)}, u32[]{:S(2)}, u32[]{:S(2)}) collective-permute-start(bf16[16,1408]{1,0:T(8,128)(2,1)S(1)} %get-tuple-element.57), channel_id=1, source_target_pairs={{0,2},{1,3},{2,0},{3,1},{4,6},{5,7},{6,4},{7,5},{8,10},{9,11},{10,... | collective-permute-start | bytes 135176 | tf_op jit(solution)/shard_map/ppermute | solution.py:269
  33.1 15.8 %copy-start.5 = (f32[1,16,1]{1,2,0:T(1,128)S(1)}, f32[1,16,1]{1,2,0:T(1,128)}, u32[]{:S(2)}) copy-start(f32[1,16,1]{1,2,0:T(1,128)} %param.14) | copy-start | bytes 196
  33.1 3.1 %collective-permute-start.19 = (bf16[16,1408]{1,0:T(8,128)(2,1)S(1)}, bf16[16,1408]{1,0:T(8,128)(2,1)S(1)}, u32[]{:S(2)}, u32[]{:S(2)}) collective-permute-start(bf16[16,1408]{1,0:T(8,128)(2,1)S(1)} %get-tuple-element.58.refs_3_), channel_id=1, source_target_pairs={{0,1},{1,0},{2,3},{3,2},{4,5},{5,4},{6,7},{7,6},{8,9},{9,8},{10,11... | collective-permute-start | bytes 135176 | tf_op jit(solution)/shard_map/ppermute | solution.py:273
  34.7 1.4 %collective-permute-start.16 = (bf16[16,1408]{1,0:T(8,128)(2,1)S(1)}, bf16[16,1408]{1,0:T(8,128)(2,1)S(1)}, u32[]{:S(2)}, u32[]{:S(2)}) collective-permute-start(bf16[16,1408]{1,0:T(8,128)(2,1)S(1)} %collective-permute-done.13.refs_0_), channel_id=1, source_target_pairs={{0,1},{1,0},{2,3},{3,2},{4,5},{5,4},{6,7},{7,6},{8,9},{9,8},{10,11... | collective-permute-start | bytes 135176 | tf_op jit(solution)/shard_map/ppermute | solution.py:273
  35.6 1.2 %collective-permute-start.17 = (bf16[16,1408]{1,0:T(8,128)(2,1)S(1)}, bf16[16,1408]{1,0:T(8,128)(2,1)S(1)}, u32[]{:S(2)}, u32[]{:S(2)}) collective-permute-start(bf16[16,1408]{1,0:T(8,128)(2,1)S(1)} %collective-permute-done.14.refs_1_), channel_id=1, source_target_pairs={{0,1},{1,0},{2,3},{3,2},{4,5},{5,4},{6,7},{7,6},{8,9},{9,8},{10,11... | collective-permute-start | bytes 135176 | tf_op jit(solution)/shard_map/ppermute | solution.py:273
  36.1 1.2 %collective-permute-start.18 = (bf16[16,1408]{1,0:T(8,128)(2,1)S(1)}, bf16[16,1408]{1,0:T(8,128)(2,1)S(1)}, u32[]{:S(2)}, u32[]{:S(2)}) collective-permute-start(bf16[16,1408]{1,0:T(8,128)(2,1)S(1)} %collective-permute-done.15.refs_2_), channel_id=1, source_target_pairs={{0,1},{1,0},{2,3},{3,2},{4,5},{5,4},{6,7},{7,6},{8,9},{9,8},{10,11... | collective-permute-start | bytes 135176 | tf_op jit(solution)/shard_map/ppermute | solution.py:273
  39.8 1.5 %collective-permute-start.20 = (bf16[64,1408]{1,0:T(8,128)(2,1)S(1)}, bf16[64,1408]{1,0:T(8,128)(2,1)S(1)}, u32[]{:S(2)}, u32[]{:S(2)}) collective-permute-start(bf16[64,1408]{1,0:T(8,128)(2,1)S(1)} %get-tuple-element.60), channel_id=1, source_target_pairs={{0,1},{1,0},{2,3},{3,2},{4,5},{5,4},{6,7},{7,6},{8,9},{9,8},{10,11... | collective-permute-start | bytes 540680 | tf_op jit(solution)/shard_map/ppermute | solution.py:288
  41.3 6.1 %collective-permute-start.21 = (bf16[16,1408]{1,0:T(8,128)(2,1)S(1)}, bf16[16,1408]{1,0:T(8,128)(2,1)S(1)}, u32[]{:S(2)}, u32[]{:S(2)}) collective-permute-start(bf16[16,1408]{1,0:T(8,128)(2,1)S(1)} %get-tuple-element.61), channel_id=1, source_target_pairs={{0,6},{1,7},{2,4},{3,5},{4,2},{5,3},{6,0},{7,1},{8,14},{9,15},{10,... | collective-permute-start | bytes 135176 | tf_op jit(solution)/shard_map/ppermute | solution.py:269
  43.4 5.4 %collective-permute-start.22 = (bf16[16,1408]{1,0:T(8,128)(2,1)S(1)}, bf16[16,1408]{1,0:T(8,128)(2,1)S(1)}, u32[]{:S(2)}, u32[]{:S(2)}) collective-permute-start(bf16[16,1408]{1,0:T(8,128)(2,1)S(1)} %get-tuple-element.62), channel_id=1, source_target_pairs={{0,4},{1,5},{2,6},{3,7},{4,0},{5,1},{6,2},{7,3},{8,12},{9,13},{10,... | collective-permute-start | bytes 135176 | tf_op jit(solution)/shard_map/ppermute | solution.py:269
  43.9 5.0 %collective-permute-start.23 = (bf16[16,1408]{1,0:T(8,128)(2,1)S(1)}, bf16[16,1408]{1,0:T(8,128)(2,1)S(1)}, u32[]{:S(2)}, u32[]{:S(2)}) collective-permute-start(bf16[16,1408]{1,0:T(8,128)(2,1)S(1)} %get-tuple-element.63), channel_id=1, source_target_pairs={{0,2},{1,3},{2,0},{3,1},{4,6},{5,7},{6,4},{7,5},{8,10},{9,11},{10,... | collective-permute-start | bytes 135176 | tf_op jit(solution)/shard_map/ppermute | solution.py:269
where the time goes:
time: 50.1 us; the launch traced here: 50 us
  starting transfers between devices  24.7 us (49%)
  waiting for transfers between devices  14.6 us (29%)
  Pallas kernels  10.5 us (21%)
    ppermute x9, starting transfers between devices, across(): lax.ppermute(blocks[i], 'expert', to_expert(i))  14.2 us
    pallas_call x9, Pallas kernels, call(): pl.pallas_call(body, out_shape=outs, in_specs=[space] * len(ins), out_spe...  10.5 us
    ppermute x9, waiting for transfers between devices, across(): lax.ppermute(blocks[i], 'expert', to_expert(i))  7.81 us
    ppermute x3, starting transfers between devices, on_device(): lax.ppermute(sums[i], ('section', 'expert'), onward(i))  6.73 us
    ppermute x3, waiting for transfers between devices, on_device(): lax.ppermute(sums[i], ('section', 'expert'), onward(i))  3.57 us
    ppermute x8, waiting for transfers between devices, shared(): lax.ppermute(a, 'expert', within(m))  1.99 us
    ppermute x8, starting transfers between devices, shared(): lax.ppermute(a, 'expert', within(m))  1.58 us
    ppermute x1, starting transfers between devices, on_device(): lax.ppermute(carry, 'section', [(i, (i + 1) % sections) for i in range(se...  1.49 us
  transfers between devices with their start and end apart: 24, of which 14 were waited for; matrix products, arithmetic and copies ran while one was open for 0% of the time, Pallas kernels for 4%

commit v1 on v0

v1 whole, which is shorter than its diff:
```python
import functools

import jax
import jax.numpy as jnp
from jax import lax
from jax.experimental import pallas as pl
from jax.experimental.pallas import tpu as pltpu
from jax.sharding import PartitionSpec as P

EXPERTS = 4
CAP = 5
ROWS = 16
LANES = 256
EPS = 1e-06
F32 = jnp.float32
BF16 = jnp.bfloat16
VMEM = pl.BlockSpec(memory_space=pltpu.VMEM)
HBM = pl.BlockSpec(memory_space=pltpu.HBM)


def distance(place):
    return EXPERTS - 1 - place


def fifth(value):
    return (value * 205) >> 10


def pad_rows(count):
    return -(-count // ROWS) * ROWS


def block_shape(width):
    return CAP * width // LANES, LANES


def spread_scratch(rows, width):
    return pltpu.VMEM((LANES // 128, rows * width // LANES, 128), F32)


def spread(values, spread_ref):
    rows, width = values.shape
    pieces = width // LANES
    for tile in range(width // 128):
        piece, half = divmod(tile, LANES // 128)
        spread_ref[half, pl.ds(piece, rows, stride=pieces), :] = values[
            :, tile * 128 : (tile + 1) * 128
        ]


def gathered(spread_ref, rows, width):
    pieces = width // LANES
    tiles = []
    for tile in range(width // 128):
        piece, half = divmod(tile, LANES // 128)
        tiles.append(spread_ref[half, pl.ds(piece, rows, stride=pieces), :].astype(BF16))
    return jnp.concatenate(tiles, axis=1)


def to_blocks(spread_ref, refs):
    start = 0
    for ref in refs:
        stop = start + ref.shape[0]
        for half in range(LANES // 128):
            ref[:, half * 128 : (half + 1) * 128] = spread_ref[half, start:stop, :].astype(BF16)
        start = stop


def from_blocks(arrays, spread_ref):
    start = 0
    for array in arrays:
        stop = start + array.shape[0]
        for half in range(LANES // 128):
            spread_ref[half, start:stop, :] = array[:, half * 128 : (half + 1) * 128].astype(F32)
        start = stop
    return start


def upright(row):
    rows = row.shape[1]
    same = lax.broadcasted_iota(jnp.int32, (rows, rows), 0) == lax.broadcasted_iota(
        jnp.int32, (rows, rows), 1
    )
    return jnp.sum(jnp.where(same, row, 0.0), axis=1, keepdims=True)


def slots_of(routes):
    rows = routes.shape[0]
    lanes = lax.broadcasted_iota(jnp.int32, (rows, 128), 1).astype(F32)
    one_hot = (routes == lanes).astype(F32)
    earlier = lax.broadcasted_iota(jnp.int32, (rows, rows), 0) > lax.broadcasted_iota(
        jnp.int32, (rows, rows), 1
    )
    before = jnp.dot(earlier.astype(BF16), one_hot.astype(BF16), preferred_element_type=F32)
    return routes * CAP + jnp.sum(before * one_hot, axis=1, keepdims=True)


def block_map(slots, expert):
    place = lax.broadcasted_iota(jnp.int32, (slots.shape[0], pad_rows(EXPERTS * CAP)), 1)
    block = fifth(place)
    target = (distance(block) ^ expert) * CAP + place - CAP * block
    target = jnp.where(block < EXPERTS, target, -1)
    return (slots == target.astype(F32)).astype(BF16)


def normalize(values, gain):
    inv_scale = lax.rsqrt(jnp.mean(values * values, axis=-1, keepdims=True) + EPS)
    return (values * inv_scale * gain).astype(BF16)


def write_blocks(normed, slots, expert, spread_ref, block_refs):
    packed = lax.dot_general(
        block_map(slots, expert),
        normed,
        (((0,), (0,)), ((), ())),
        preferred_element_type=F32,
    )
    spread(packed, spread_ref)
    to_blocks(spread_ref, block_refs)


def hand_out(values, refs):
    start = 0
    for ref in refs:
        ref[...] = values[start : start + ref.shape[0]]
        start += ref.shape[0]


def my_expert(group):
    return lax.axis_index("expert") // group


def split_parts(values):
    parts = []
    for _ in range(3):
        parts.append(values.astype(BF16))
        values = values - parts[-1].astype(F32)
    return parts


def pack_kernel(group, *refs):
    sources, block_refs, ahead_ref = refs[:4], refs[4 : 4 + EXPERTS], refs[4 + EXPERTS]
    held, spread_ref, sems = refs[5 + EXPERTS : -2], refs[-2], refs[-1]
    copies = [
        pltpu.make_async_copy(source, place, sems.at[i])
        for i, (source, place) in enumerate(zip(sources, held))
    ]
    for copy in copies:
        copy.start()
    for copy in copies:
        copy.wait()
    x_ref, gain_ref, routes_ref, gates_ref = held
    rows, width = x_ref.shape
    slots = slots_of(upright(routes_ref[...].astype(F32)))
    lane = lax.broadcasted_iota(jnp.int32, (rows, LANES), 1)
    meta = jnp.zeros((rows, LANES), F32)
    for i, column in enumerate([slots, *split_parts(upright(gates_ref[...]))]):
        meta = jnp.where(lane == i, column.astype(F32), meta)
    for piece in range(width // LANES):
        ahead_ref[piece * rows : (piece + 1) * rows] = x_ref[:, piece * LANES : (piece + 1) * LANES]
    ahead_ref[width // LANES * rows :] = meta.astype(BF16)
    normed = normalize(x_ref[...].astype(F32), gain_ref[...])
    write_blocks(normed, slots, my_expert(group), spread_ref, block_refs)


def residual(x, slots, gates, expert, blocks, spread_ref):
    width = x.shape[1]
    filled = from_blocks(blocks, spread_ref)
    spread_ref[:, filled:, :] = jnp.zeros(
        (spread_ref.shape[0], spread_ref.shape[1] - filled, 128), F32
    )
    found = jnp.dot(
        block_map(slots, expert),
        gathered(spread_ref, pad_rows(EXPERTS * CAP), width),
        preferred_element_type=F32,
    )
    update = (gates * found).astype(BF16)
    return x.astype(F32) + update.astype(F32)


def middle_kernel(group, *refs):
    block_ins, carried_ref, gain_ref, routes_ref = refs[: EXPERTS - 1], *refs[EXPERTS - 1 : EXPERTS + 2]
    first_ref, block_refs, spread_ref = refs[EXPERTS + 2], refs[EXPERTS + 3 : -1], refs[-1]
    expert = my_expert(group)
    rows, width = first_ref.shape
    pieces = width // LANES
    x = jnp.concatenate(
        [carried_ref[piece * rows : (piece + 1) * rows] for piece in range(pieces)], axis=1
    )
    meta = carried_ref[pieces * rows : (pieces + 1) * rows].astype(F32)
    gates = meta[:, 1:2] + meta[:, 2:3] + meta[:, 3:4]
    blocks = [ref[...] for ref in block_ins] + [carried_ref[(pieces + 1) * rows :]]
    first = residual(x, meta[:, 0:1], gates, expert, blocks, spread_ref).astype(BF16)
    first_ref[...] = first
    slots = slots_of(upright(routes_ref[...].astype(F32)))
    normed = normalize(first.astype(F32), gain_ref[...])
    write_blocks(normed, slots, expert, spread_ref, block_refs)


def last_kernel(group, x_ref, b0, b1, b2, b3, routes_ref, gates_ref, out_ref, spread_ref):
    slots = slots_of(upright(routes_ref[...].astype(F32)))
    gates = upright(gates_ref[...])
    blocks = [ref[...] for ref in (b0, b1, b2, b3)]
    mixed = residual(x_ref[...], slots, gates, my_expert(group), blocks, spread_ref)
    out_ref[...] = mixed.astype(BF16)


def expert_kernel(given, w_gate, w_up, w_down, *refs):
    ins, outs, spread_ref = refs[:given], refs[given:-1], refs[-1]
    width = w_gate.shape[0]
    rows = spread_ref.shape[1] * LANES // width
    from_blocks([ref[...] for ref in ins], spread_ref)
    x = gathered(spread_ref, rows, width)
    gate_val = jnp.dot(x, w_gate[...], preferred_element_type=F32)
    up_val = jnp.dot(x, w_up[...], preferred_element_type=F32)
    hidden = (gate_val / (1.0 + jnp.exp(-gate_val)) * up_val).astype(BF16)
    spread(jnp.dot(hidden, w_down[...], preferred_element_type=F32), spread_ref)
    to_blocks(spread_ref, outs)


def summed(refs):
    total = refs[0][...].astype(F32)
    for ref in refs[1:]:
        total = total + ref[...].astype(F32)
    return total.astype(BF16)


def sum_kernel(given, *refs):
    hand_out(summed(refs[:given]), refs[given:])


def carry_kernel(ahead_ref, *refs):
    ins, out_ref = refs[:-1], refs[-1]
    rows = ahead_ref.shape[0]
    out_ref[:rows] = ahead_ref[...]
    out_ref[rows:] = summed(ins)


def call(body, outs, ins, megabytes, scratch=(), flops=0, space=VMEM):
    moved = sum(a.size * a.dtype.itemsize for a in (*ins, *outs))
    return pl.pallas_call(
        body,
        out_shape=outs,
        in_specs=[space] * len(ins),
        out_specs=[VMEM] * len(outs),
        scratch_shapes=list(scratch),
        compiler_params=pltpu.CompilerParams(vmem_limit_bytes=megabytes << 20),
        cost_estimate=pl.CostEstimate(flops=flops, bytes_accessed=moved, transcendentals=0),
    )(*ins)


def on_device(tokens, gain, routes_1, gates_1, routes_2, gates_2, gate_proj, up_proj, down_proj):
    sections, devices = lax.axis_size("section"), lax.axis_size("expert")
    group = devices // EXPERTS
    rows, width = tokens.shape[1:]
    weights = (gate_proj[0, 0], up_proj[0, 0], down_proj[0, 0])
    tall, wide = block_shape(width)
    block = jax.ShapeDtypeStruct((tall, wide), BF16)
    packing = spread_scratch(pad_rows(EXPERTS * CAP), width)
    whole = jax.ShapeDtypeStruct((rows, width), BF16)
    ahead = (width // LANES + 1) * rows
    routes_1, gates_1, routes_2, gates_2 = (
        a.reshape(1, rows) for a in (routes_1, gates_1, routes_2, gates_2)
    )

    def to_expert(place):
        far = distance(place)
        return [(i, (i // group ^ far) * group + i % group) for i in range(devices)]

    def within(shift):
        return [(i, i // group * group + (i + shift) % group) for i in range(devices)]

    def onward(place):
        return [
            (s * devices + i, (s + 1) % sections * devices + j)
            for s in range(sections)
            for i, j in to_expert(place)
        ]

    def across(blocks):
        return [lax.ppermute(blocks[i], "expert", to_expert(i)) for i in range(EXPERTS - 1)]

    def shared(arrived):
        return arrived + [
            lax.ppermute(a, "expert", within(m)) for m in range(1, group) for a in arrived
        ]

    def experts(ins):
        count = sum(a.shape[0] for a in ins) // tall
        sums = call(
            functools.partial(expert_kernel, len(ins)),
            [jax.ShapeDtypeStruct((count // group * tall, wide), BF16)] * group,
            [*weights, *ins],
            24,
            [spread_scratch(pad_rows(count * CAP), width)],
            flops=6 * 256 * width * weights[0].shape[1],
        )
        return [sums[0]] + [
            lax.ppermute(sums[m], "expert", within(-m)) for m in range(1, group)
        ]

    def added(terms):
        parts = terms[0].shape[0] // tall
        return call(functools.partial(sum_kernel, group), [block] * parts, terms, 8)

    sources = [
        pltpu.with_memory_space_constraint(a, pltpu.HBM)
        for a in (tokens[0], gain, routes_1, gates_1)
    ]
    *blocks, travelling = call(
        functools.partial(pack_kernel, group),
        [block] * EXPERTS + [jax.ShapeDtypeStruct((ahead, LANES), BF16)],
        sources,
        8,
        [pltpu.VMEM(a.shape, a.dtype) for a in sources]
        + [packing, pltpu.SemaphoreType.DMA((len(sources),))],
        flops=10**10,
        space=HBM,
    )
    arrived = across(blocks[:-1])
    (carry,) = call(
        carry_kernel,
        [jax.ShapeDtypeStruct((ahead + tall, LANES), BF16)],
        [travelling, *experts(shared(blocks[-1:]))],
        8,
    )
    *ins, carry = lax.optimization_barrier((*shared(arrived), carry))
    carried = lax.ppermute(carry, "section", [(i, (i + 1) % sections) for i in range(sections)])
    sums = added(experts(ins))
    home = [lax.ppermute(sums[i], ("section", "expert"), onward(i)) for i in range(EXPERTS - 1)]
    first, *blocks = call(
        functools.partial(middle_kernel, group),
        [whole] + [block] * EXPERTS,
        [*home, carried, gain, routes_2],
        8,
        [packing],
    )
    sums = added(experts(shared(across(blocks[:-1]) + blocks[-1:])))
    home = across(sums[:-1])
    (mixed,) = call(
        functools.partial(last_kernel, group),
        [whole],
        [first, *home, sums[-1], routes_2, gates_2],
        8,
        [packing],
    )
    return mixed[None]


def solution(mesh):
    rows = P("section", "expert", None)
    slabs = P("section", "expert", None, None)
    return jax.shard_map(
        on_device,
        mesh=mesh,
        in_specs=(rows, P("section", None), rows, rows, rows, rows, slabs, slabs, slabs),
        out_specs=rows,
        check_vma=False,
    )
```

time: 50.1 us -> 51.2 us (1.022)
  waiting for transfers between devices: 14.6 us -> 16 us
    ppermute x3, waiting for transfers between devices: 1.26 us -> 2.32 us  [experts(): lax.ppermute(sums[m], 'expert', within(-m))]
    ppermute x3, starting transfers between devices: 6.73 us -> 6.21 us  [on_device(): lax.ppermute(sums[i], ('section', 'expert'), onward(i))]
  transfers between devices with their start and end apart: 24 -> 24, of which waited for: 14 -> 14; matrix products, arithmetic and copies ran while one was open for 0% -> 0% of each run, Pallas kernels for 4% -> 8%
where the time goes in v1:
time: 51.2 us; the launch traced here: 51.1 us
  starting transfers between devices  24.6 us (48%)
  waiting for transfers between devices  16 us (31%)
  Pallas kernels  10.3 us (20%)
    ppermute x9, starting transfers between devices, across(): lax.ppermute(blocks[i], 'expert', to_expert(i))  14.2 us
    pallas_call x9, Pallas kernels, call(): pl.pallas_call(body, out_shape=outs, in_specs=[space] * len(ins), out_spe...  10.3 us
    ppermute x9, waiting for transfers between devices, across(): lax.ppermute(blocks[i], 'expert', to_expert(i))  8.01 us
    ppermute x3, starting transfers between devices, on_device(): lax.ppermute(sums[i], ('section', 'expert'), onward(i))  6.21 us
    ppermute x3, waiting for transfers between devices, on_device(): lax.ppermute(sums[i], ('section', 'expert'), onward(i))  4.03 us
    ppermute x3, waiting for transfers between devices, experts(): lax.ppermute(sums[m], 'expert', within(-m))  2.32 us
    ppermute x8, starting transfers between devices, shared(): lax.ppermute(a, 'expert', within(m))  2.04 us
    ppermute x8, waiting for transfers between devices, shared(): lax.ppermute(a, 'expert', within(m))  1.68 us
  transfers between devices with their start and end apart: 24, of which 14 were waited for; matrix products, arithmetic and copies ran while one was open for 0% of the time, Pallas kernels for 8%

profile of v1, /device:TPU:0, one launch (start us, length us, event | category | flops | bytes accessed | tf_op | source)
XLA Modules:
  0.0 51.1 jit_solution(10425279624362427976)
XLA Ops:
  0.0 1.7 %shard_map.91 = (bf16[80,256]{1,0:T(8,128)(2,1)S(1)}, bf16[80,256]{1,0:T(8,128)(2,1)S(1)}, bf16[80,256]{1,0:T(8,128)(2,1)S(1)}, bf16[80,256]{1,0:T(8,128)(2,1)S(1)}, bf16[272,256]{1,0:T(8,128)(2,1)S(1)}) custom-call(bf16[16,4096]{1,0:T(8,128)(2,1)} %bitcast.21, f32[1,4096]{1,0:T(1,128)} %refs_4_.1, s32[1,16]{1,0:T(1,128)} %bitcast.22, f32[1,16]{1,0:T(1,128)} %bitcast.23), custom_call_target="tpu_custom_call" | custom-call | flops 10000000000 | bytes 450688 | tf_op jit(solution)/shard_map/pallas_call | solution.py:241
  1.7 0.5 %collective-permute-start.6 = (bf16[80,256]{1,0:T(8,128)(2,1)S(1)}, bf16[80,256]{1,0:T(8,128)(2,1)S(1)}, u32[]{:S(2)}, u32[]{:S(2)}) collective-permute-start(bf16[80,256]{1,0:T(8,128)(2,1)S(1)} %get-tuple-element.39.refs_0_), channel_id=1, source_target_pairs={{0,1},{1,0},{2,3},{3,2},{4,5},{5,4},{6,7},{7,6},{8,9},{9,8},{10,11... | collective-permute-start | bytes 122888 | tf_op jit(solution)/shard_map/ppermute | solution.py:285
  2.2 4.7 %collective-permute-start = (bf16[80,256]{1,0:T(8,128)(2,1)S(1)}, bf16[80,256]{1,0:T(8,128)(2,1)S(1)}, u32[]{:S(2)}, u32[]{:S(2)}) collective-permute-start(bf16[80,256]{1,0:T(8,128)(2,1)S(1)} %get-tuple-element.35), channel_id=1, source_target_pairs={{0,6},{1,7},{2,4},{3,5},{4,2},{5,3},{6,0},{7,1},{8,14},{9,15},{10,... | collective-permute-start | bytes 122888 | tf_op jit(solution)/shard_map/ppermute | solution.py:281
  6.9 0.6 %collective-permute-start.2 = (bf16[80,256]{1,0:T(8,128)(2,1)S(1)}, bf16[80,256]{1,0:T(8,128)(2,1)S(1)}, u32[]{:S(2)}, u32[]{:S(2)}) collective-permute-start(bf16[80,256]{1,0:T(8,128)(2,1)S(1)} %get-tuple-element.37), channel_id=1, source_target_pairs={{0,2},{1,3},{2,0},{3,1},{4,6},{5,7},{6,4},{7,5},{8,10},{9,11},{10,... | collective-permute-start | bytes 122888 | tf_op jit(solution)/shard_map/ppermute | solution.py:281
  7.6 1.8 %shard_map.92 = (bf16[80,256]{1,0:T(8,128)(2,1)S(1)}, bf16[80,256]{1,0:T(8,128)(2,1)S(1)}) custom-call(bf16[4096,512]{1,0:T(8,128)(2,1)S(1)} %bitcast.9, bf16[4096,512]{1,0:T(8,128)(2,1)S(1)} %bitcast.12, bf16[512,4096]{1,0:T(8,128)(2,1)S(1)} %bitcast.15, bf16[80,256]{1,0:T(8,128)(2,1)S(1)} %get-tuple-element.39.refs_0_, ...), custom_call_target="tpu_custom_call" | custom-call | flops 3221225472 | bytes 12746752 | tf_op jit(solution)/shard_map/pallas_call | solution.py:241
  10.0 1.8 %collective-permute-done.1.refs_1_ = bf16[80,256]{1,0:T(8,128)(2,1)S(1)} collective-permute-done((bf16[80,256]{1,0:T(8,128)(2,1)S(1)}, bf16[80,256]{1,0:T(8,128)(2,1)S(1)}, u32[]{:S(2)}, u32[]{:S(2)}) %collective-permute-start.1) | collective-permute-done | bytes 40992 | tf_op jit(solution)/shard_map/ppermute | solution.py:281
  11.8 0.5 collective-permute-start.5
  12.4 0.6 %collective-permute-done.4.refs_4_ = bf16[80,256]{1,0:T(8,128)(2,1)S(1)} collective-permute-done((bf16[80,256]{1,0:T(8,128)(2,1)S(1)}, bf16[80,256]{1,0:T(8,128)(2,1)S(1)}, u32[]{:S(2)}, u32[]{:S(2)}) %collective-permute-start.4) | collective-permute-done | bytes 40992 | tf_op jit(solution)/shard_map/ppermute | solution.py:285
  13.2 1.5 %collective-permute-start.12 = (bf16[352,256]{1,0:T(8,128)(2,1)S(1)}, bf16[352,256]{1,0:T(8,128)(2,1)S(1)}, u32[]{:S(2)}, u32[]{:S(2)}) collective-permute-start(bf16[352,256]{1,0:T(8,128)(2,1)S(1)} %shard_map.93), channel_id=1, source_target_pairs={{0,8},{8,16},{16,24},{24,0},{1,9},{9,17},{17,25},{25,1},{2,10},{10... | collective-permute-start | bytes 540680 | tf_op jit(solution)/shard_map/ppermute | solution.py:328
  14.7 2.4 %shard_map.94 = (bf16[240,256]{1,0:T(8,128)(2,1)S(1)}, bf16[240,256]{1,0:T(8,128)(2,1)S(1)}) custom-call(bf16[4096,512]{1,0:T(8,128)(2,1)S(1)} %bitcast.10, bf16[4096,512]{1,0:T(8,128)(2,1)S(1)} %bitcast.13, bf16[512,4096]{1,0:T(8,128)(2,1)S(1)} %bitcast.16, bf16[80,256]{1,0:T(8,128)(2,1)S(1)} %collective-permute-done.refs_0_, ...), custom_call_target="tpu_custom_call" | custom-call | flops 3221225472 | bytes 13074432 | tf_op jit(solution)/shard_map/pallas_call | solution.py:241
  17.2 1.3 %collective-permute-done.8.refs_1_ = bf16[240,256]{1,0:T(8,128)(2,1)S(1)} collective-permute-done((bf16[240,256]{1,0:T(8,128)(2,1)S(1)}, bf16[240,256]{1,0:T(8,128)(2,1)S(1)}, u32[]{:S(2)}, u32[]{:S(2)}) %collective-permute-start.8) | collective-permute-done | bytes 122912 | tf_op jit(solution)/shard_map/ppermute | solution.py:299
  18.5 2.9 %collective-permute-start.9 = (bf16[80,256]{1,0:T(8,128)(2,1)S(1)}, bf16[80,256]{1,0:T(8,128)(2,1)S(1)}, u32[]{:S(2)}, u32[]{:S(2)}) collective-permute-start(bf16[80,256]{1,0:T(8,128)(2,1)S(1)} %get-tuple-element.50), channel_id=1, source_target_pairs={{0,14},{1,15},{2,12},{3,13},{4,10},{5,11},{6,8},{7,9},{8,22},{9,23... | collective-permute-start | bytes 122888 | tf_op jit(solution)/shard_map/ppermute | solution.py:330
  21.4 1.1 %collective-permute-start.10 = (bf16[80,256]{1,0:T(8,128)(2,1)S(1)}, bf16[80,256]{1,0:T(8,128)(2,1)S(1)}, u32[]{:S(2)}, u32[]{:S(2)}) collective-permute-start(bf16[80,256]{1,0:T(8,128)(2,1)S(1)} %get-tuple-element.51), channel_id=1, source_target_pairs={{0,12},{1,13},{2,14},{3,15},{4,8},{5,9},{6,10},{7,11},{8,20},{9,21... | collective-permute-start | bytes 122888 | tf_op jit(solution)/shard_map/ppermute | solution.py:330
  22.5 2.2 %collective-permute-start.11 = (bf16[80,256]{1,0:T(8,128)(2,1)S(1)}, bf16[80,256]{1,0:T(8,128)(2,1)S(1)}, u32[]{:S(2)}, u32[]{:S(2)}) collective-permute-start(bf16[80,256]{1,0:T(8,128)(2,1)S(1)} %get-tuple-element.52), channel_id=1, source_target_pairs={{0,10},{1,11},{2,8},{3,9},{4,14},{5,15},{6,12},{7,13},{8,18},{9,19... | collective-permute-start | bytes 122888 | tf_op jit(solution)/shard_map/ppermute | solution.py:330
  24.7 1.4 %collective-permute-done.9.refs_0_ = bf16[80,256]{1,0:T(8,128)(2,1)S(1)} collective-permute-done((bf16[80,256]{1,0:T(8,128)(2,1)S(1)}, bf16[80,256]{1,0:T(8,128)(2,1)S(1)}, u32[]{:S(2)}, u32[]{:S(2)}) %collective-permute-start.9) | collective-permute-done | bytes 40992 | tf_op jit(solution)/shard_map/ppermute | solution.py:330
  26.1 2.4 %collective-permute-done.10.refs_1_ = bf16[80,256]{1,0:T(8,128)(2,1)S(1)} collective-permute-done((bf16[80,256]{1,0:T(8,128)(2,1)S(1)}, bf16[80,256]{1,0:T(8,128)(2,1)S(1)}, u32[]{:S(2)}, u32[]{:S(2)}) %collective-permute-start.10) | collective-permute-done | bytes 40992 | tf_op jit(solution)/shard_map/ppermute | solution.py:330
  28.7 0.7 %shard_map.96 = (bf16[16,4096]{1,0:T(8,128)(2,1)S(1)}, bf16[80,256]{1,0:T(8,128)(2,1)S(1)}, bf16[80,256]{1,0:T(8,128)(2,1)S(1)}, bf16[80,256]{1,0:T(8,128)(2,1)S(1)}, bf16[80,256]{1,0:T(8,128)(2,1)S(1)}) custom-call(bf16[80,256]{1,0:T(8,128)(2,1)S(1)} %collective-permute-done.9.refs_0_, bf16[80,256]{1,0:T(8,128)(2,1)S(1)} %collective-permute-done.10.refs_1_, ...), custom_call_target="tpu_custom_call" | custom-call | bytes 614464 | tf_op jit(solution)/shard_map/pallas_call | solution.py:241
  29.5 2.3 %collective-permute-start.13 = (bf16[80,256]{1,0:T(8,128)(2,1)S(1)}, bf16[80,256]{1,0:T(8,128)(2,1)S(1)}, u32[]{:S(2)}, u32[]{:S(2)}) collective-permute-start(bf16[80,256]{1,0:T(8,128)(2,1)S(1)} %get-tuple-element.55), channel_id=1, source_target_pairs={{0,6},{1,7},{2,4},{3,5},{4,2},{5,3},{6,0},{7,1},{8,14},{9,15},{10,... | collective-permute-start | bytes 122888 | tf_op jit(solution)/shard_map/ppermute | solution.py:281
  31.8 1.1 %collective-permute-start.14 = (bf16[80,256]{1,0:T(8,128)(2,1)S(1)}, bf16[80,256]{1,0:T(8,128)(2,1)S(1)}, u32[]{:S(2)}, u32[]{:S(2)}) collective-permute-start(bf16[80,256]{1,0:T(8,128)(2,1)S(1)} %get-tuple-element.56), channel_id=1, source_target_pairs={{0,4},{1,5},{2,6},{3,7},{4,0},{5,1},{6,2},{7,3},{8,12},{9,13},{10,... | collective-permute-start | bytes 122888 | tf_op jit(solution)/shard_map/ppermute | solution.py:281
  32.9 1.1 %collective-permute-start.15 = (bf16[80,256]{1,0:T(8,128)(2,1)S(1)}, bf16[80,256]{1,0:T(8,128)(2,1)S(1)}, u32[]{:S(2)}, u32[]{:S(2)}) collective-permute-start(bf16[80,256]{1,0:T(8,128)(2,1)S(1)} %get-tuple-element.57), channel_id=1, source_target_pairs={{0,2},{1,3},{2,0},{3,1},{4,6},{5,7},{6,4},{7,5},{8,10},{9,11},{10,... | collective-permute-start | bytes 122888 | tf_op jit(solution)/shard_map/ppermute | solution.py:281
  34.0 1.5 %collective-permute-done.13.refs_0_ = bf16[80,256]{1,0:T(8,128)(2,1)S(1)} collective-permute-done((bf16[80,256]{1,0:T(8,128)(2,1)S(1)}, bf16[80,256]{1,0:T(8,128)(2,1)S(1)}, u32[]{:S(2)}, u32[]{:S(2)}) %collective-permute-start.13) | collective-permute-done | bytes 40992 | tf_op jit(solution)/shard_map/ppermute | solution.py:281
  35.5 1.7 %collective-permute-done.14.refs_1_ = bf16[80,256]{1,0:T(8,128)(2,1)S(1)} collective-permute-done((bf16[80,256]{1,0:T(8,128)(2,1)S(1)}, bf16[80,256]{1,0:T(8,128)(2,1)S(1)}, u32[]{:S(2)}, u32[]{:S(2)}) %collective-permute-start.14) | collective-permute-done | bytes 40992 | tf_op jit(solution)/shard_map/ppermute | solution.py:281
  37.2 0.5 collective-permute-start.18
  37.7 0.7 %collective-permute-done.17.refs_5_ = bf16[80,256]{1,0:T(8,128)(2,1)S(1)} collective-permute-done((bf16[80,256]{1,0:T(8,128)(2,1)S(1)}, bf16[80,256]{1,0:T(8,128)(2,1)S(1)}, u32[]{:S(2)}, u32[]{:S(2)}) %collective-permute-start.17) | collective-permute-done | bytes 40992 | tf_op jit(solution)/shard_map/ppermute | solution.py:285
  38.5 2.4 %shard_map.97 = (bf16[320,256]{1,0:T(8,128)(2,1)S(1)}, bf16[320,256]{1,0:T(8,128)(2,1)S(1)}) custom-call(bf16[4096,512]{1,0:T(8,128)(2,1)S(1)} %bitcast.11, bf16[4096,512]{1,0:T(8,128)(2,1)S(1)} %bitcast.14, bf16[512,4096]{1,0:T(8,128)(2,1)S(1)} %bitcast.17, bf16[80,256]{1,0:T(8,128)(2,1)S(1)} %collective-permute-done.13.refs_0_, ...), custom_call_target="tpu_custom_call" | custom-call | flops 3221225472 | bytes 13238272 | tf_op jit(solution)/shard_map/pallas_call | solution.py:241
  41.4 1.0 %collective-permute-done.20.refs_1_ = bf16[320,256]{1,0:T(8,128)(2,1)S(1)} collective-permute-done((bf16[320,256]{1,0:T(8,128)(2,1)S(1)}, bf16[320,256]{1,0:T(8,128)(2,1)S(1)}, u32[]{:S(2)}, u32[]{:S(2)}) %collective-permute-start.20) | collective-permute-done | bytes 163872 | tf_op jit(solution)/shard_map/ppermute | solution.py:299
  42.5 1.5 %collective-permute-start.21 = (bf16[80,256]{1,0:T(8,128)(2,1)S(1)}, bf16[80,256]{1,0:T(8,128)(2,1)S(1)}, u32[]{:S(2)}, u32[]{:S(2)}) collective-permute-start(bf16[80,256]{1,0:T(8,128)(2,1)S(1)} %get-tuple-element.61), channel_id=1, source_target_pairs={{0,6},{1,7},{2,4},{3,5},{4,2},{5,3},{6,0},{7,1},{8,14},{9,15},{10,... | collective-permute-start | bytes 122888 | tf_op jit(solution)/shard_map/ppermute | solution.py:281
  44.0 0.6 %collective-permute-start.22 = (bf16[80,256]{1,0:T(8,128)(2,1)S(1)}, bf16[80,256]{1,0:T(8,128)(2,1)S(1)}, u32[]{:S(2)}, u32[]{:S(2)}) collective-permute-start(bf16[80,256]{1,0:T(8,128)(2,1)S(1)} %get-tuple-element.62), channel_id=1, source_target_pairs={{0,4},{1,5},{2,6},{3,7},{4,0},{5,1},{6,2},{7,3},{8,12},{9,13},{10,... | collective-permute-start | bytes 122888 | tf_op jit(solution)/shard_map/ppermute | solution.py:281
  44.6 2.3 %collective-permute-start.23 = (bf16[80,256]{1,0:T(8,128)(2,1)S(1)}, bf16[80,256]{1,0:T(8,128)(2,1)S(1)}, u32[]{:S(2)}, u32[]{:S(2)}) collective-permute-start(bf16[80,256]{1,0:T(8,128)(2,1)S(1)} %get-tuple-element.63), channel_id=1, source_target_pairs={{0,2},{1,3},{2,0},{3,1},{4,6},{5,7},{6,4},{7,5},{8,10},{9,11},{10,... | collective-permute-start | bytes 122888 | tf_op jit(solution)/shard_map/ppermute | solution.py:281
  46.9 1.8 %collective-permute-done.21.b0 = bf16[80,256]{1,0:T(8,128)(2,1)S(1)} collective-permute-done((bf16[80,256]{1,0:T(8,128)(2,1)S(1)}, bf16[80,256]{1,0:T(8,128)(2,1)S(1)}, u32[]{:S(2)}, u32[]{:S(2)}) %collective-permute-start.21) | collective-permute-done | bytes 40992 | tf_op jit(solution)/shard_map/ppermute | solution.py:281
  48.7 1.2 %collective-permute-done.22.b1 = bf16[80,256]{1,0:T(8,128)(2,1)S(1)} collective-permute-done((bf16[80,256]{1,0:T(8,128)(2,1)S(1)}, bf16[80,256]{1,0:T(8,128)(2,1)S(1)}, u32[]{:S(2)}, u32[]{:S(2)}) %collective-permute-start.22) | collective-permute-done | bytes 40992 | tf_op jit(solution)/shard_map/ppermute | solution.py:281
  49.9 1.2 %shard_map.99 = bf16[16,4096]{1,0:T(8,128)(2,1)} custom-call(bf16[16,4096]{1,0:T(8,128)(2,1)S(1)} %get-tuple-element.54.x_ref, bf16[80,256]{1,0:T(8,128)(2,1)S(1)} %collective-permute-done.21.b0, bf16[80,256]{1,0:T(8,128)(2,1)S(1)} %collective-permute-done.22.b1, bf16[80,256]{1,0:T(8,128)(2,1)S(1)} %collective-permute-done.23.b2, ...), custom_call_target="tpu_custom_call" | custom-call | bytes 426112 | tf_op jit(solution)/shard_map/pallas_call | solution.py:241
  (37 shorter events, 1.8 us)
Async XLA Ops:
  0.0 7.5 %copy-start = (bf16[1,1,4096,512]{3,2,1,0:T(8,128)(2,1)S(1)}, bf16[1,1,4096,512]{3,2,1,0:T(8,128)(2,1)}, u32[]{:S(2)}) copy-start(bf16[1,1,4096,512]{3,2,1,0:T(8,128)(2,1)} %param.15) | copy-start | bytes 12582916
  0.0 7.5 %copy-start.1 = (bf16[1,1,4096,512]{3,2,1,0:T(8,128)(2,1)S(1)}, bf16[1,1,4096,512]{3,2,1,0:T(8,128)(2,1)}, u32[]{:S(2)}) copy-start(bf16[1,1,4096,512]{3,2,1,0:T(8,128)(2,1)} %param.16) | copy-start | bytes 12582916
  0.0 7.5 %copy-start.2 = (bf16[1,1,512,4096]{3,2,1,0:T(8,128)(2,1)S(1)}, bf16[1,1,512,4096]{3,2,1,0:T(8,128)(2,1)}, u32[]{:S(2)}) copy-start(bf16[1,1,512,4096]{3,2,1,0:T(8,128)(2,1)} %param.17) | copy-start | bytes 12582916
  1.7 5.8 %collective-permute-start.6 = (bf16[80,256]{1,0:T(8,128)(2,1)S(1)}, bf16[80,256]{1,0:T(8,128)(2,1)S(1)}, u32[]{:S(2)}, u32[]{:S(2)}) collective-permute-start(bf16[80,256]{1,0:T(8,128)(2,1)S(1)} %get-tuple-element.39.refs_0_), channel_id=1, source_target_pairs={{0,1},{1,0},{2,3},{3,2},{4,5},{5,4},{6,7},{7,6},{8,9},{9,8},{10,11... | collective-permute-start | bytes 122888 | tf_op jit(solution)/shard_map/ppermute | solution.py:285
  2.2 7.3 %collective-permute-start = (bf16[80,256]{1,0:T(8,128)(2,1)S(1)}, bf16[80,256]{1,0:T(8,128)(2,1)S(1)}, u32[]{:S(2)}, u32[]{:S(2)}) collective-permute-start(bf16[80,256]{1,0:T(8,128)(2,1)S(1)} %get-tuple-element.35), channel_id=1, source_target_pairs={{0,6},{1,7},{2,4},{3,5},{4,2},{5,3},{6,0},{7,1},{8,14},{9,15},{10,... | collective-permute-start | bytes 122888 | tf_op jit(solution)/shard_map/ppermute | solution.py:281
  6.9 4.9 %collective-permute-start.1 = (bf16[80,256]{1,0:T(8,128)(2,1)S(1)}, bf16[80,256]{1,0:T(8,128)(2,1)S(1)}, u32[]{:S(2)}, u32[]{:S(2)}) collective-permute-start(bf16[80,256]{1,0:T(8,128)(2,1)S(1)} %get-tuple-element.36), channel_id=1, source_target_pairs={{0,4},{1,5},{2,6},{3,7},{4,0},{5,1},{6,2},{7,3},{8,12},{9,13},{10,... | collective-permute-start | bytes 122888 | tf_op jit(solution)/shard_map/ppermute | solution.py:281
  6.9 4.9 %collective-permute-start.2 = (bf16[80,256]{1,0:T(8,128)(2,1)S(1)}, bf16[80,256]{1,0:T(8,128)(2,1)S(1)}, u32[]{:S(2)}, u32[]{:S(2)}) collective-permute-start(bf16[80,256]{1,0:T(8,128)(2,1)S(1)} %get-tuple-element.37), channel_id=1, source_target_pairs={{0,2},{1,3},{2,0},{3,1},{4,6},{5,7},{6,4},{7,5},{8,10},{9,11},{10,... | collective-permute-start | bytes 122888 | tf_op jit(solution)/shard_map/ppermute | solution.py:281
  9.4 2.9 %collective-permute-start.7 = (bf16[80,256]{1,0:T(8,128)(2,1)S(1)}, bf16[80,256]{1,0:T(8,128)(2,1)S(1)}, u32[]{:S(2)}, u32[]{:S(2)}) collective-permute-start(bf16[80,256]{1,0:T(8,128)(2,1)S(1)} %get-tuple-element.41), channel_id=1, source_target_pairs={{0,1},{1,0},{2,3},{3,2},{4,5},{5,4},{6,7},{7,6},{8,9},{9,8},{10,11... | collective-permute-start | bytes 122888 | tf_op jit(solution)/shard_map/ppermute | solution.py:299
  9.5 2.9 %collective-permute-start.3 = (bf16[80,256]{1,0:T(8,128)(2,1)S(1)}, bf16[80,256]{1,0:T(8,128)(2,1)S(1)}, u32[]{:S(2)}, u32[]{:S(2)}) collective-permute-start(bf16[80,256]{1,0:T(8,128)(2,1)S(1)} %collective-permute-done.refs_0_), channel_id=1, source_target_pairs={{0,1},{1,0},{2,3},{3,2},{4,5},{5,4},{6,7},{7,6},{8,9},{9,8},{10,11... | collective-permute-start | bytes 122888 | tf_op jit(solution)/shard_map/ppermute | solution.py:285
  11.8 1.2 %collective-permute-start.4 = (bf16[80,256]{1,0:T(8,128)(2,1)S(1)}, bf16[80,256]{1,0:T(8,128)(2,1)S(1)}, u32[]{:S(2)}, u32[]{:S(2)}) collective-permute-start(bf16[80,256]{1,0:T(8,128)(2,1)S(1)} %collective-permute-done.1.refs_1_), channel_id=1, source_target_pairs={{0,1},{1,0},{2,3},{3,2},{4,5},{5,4},{6,7},{7,6},{8,9},{9,8},{10,11... | collective-permute-start | bytes 122888 | tf_op jit(solution)/shard_map/ppermute | solution.py:285
  11.8 1.4 %collective-permute-start.5 = (bf16[80,256]{1,0:T(8,128)(2,1)S(1)}, bf16[80,256]{1,0:T(8,128)(2,1)S(1)}, u32[]{:S(2)}, u32[]{:S(2)}) collective-permute-start(bf16[80,256]{1,0:T(8,128)(2,1)S(1)} %collective-permute-done.2.refs_2_), channel_id=1, source_target_pairs={{0,1},{1,0},{2,3},{3,2},{4,5},{5,4},{6,7},{7,6},{8,9},{9,8},{10,11... | collective-permute-start | bytes 122888 | tf_op jit(solution)/shard_map/ppermute | solution.py:285
  12.3 16.4 %copy-start.3 = (f32[1,4096]{1,0:T(1,128)S(1)}, f32[1,4096]{1,0:T(1,128)}, u32[]{:S(2)}) copy-start(f32[1,4096]{1,0:T(1,128)} %refs_4_.1) | copy-start | bytes 49156
  12.3 16.4 %copy-start.4 = (s32[1,16,1]{1,2,0:T(1,128)S(1)}, s32[1,16,1]{1,2,0:T(1,128)}, u32[]{:S(2)}) copy-start(s32[1,16,1]{1,2,0:T(1,128)} %param.13) | copy-start | bytes 196
  13.2 15.6 %collective-permute-start.12 = (bf16[352,256]{1,0:T(8,128)(2,1)S(1)}, bf16[352,256]{1,0:T(8,128)(2,1)S(1)}, u32[]{:S(2)}, u32[]{:S(2)}) collective-permute-start(bf16[352,256]{1,0:T(8,128)(2,1)S(1)} %shard_map.93), channel_id=1, source_target_pairs={{0,8},{8,16},{16,24},{24,0},{1,9},{9,17},{17,25},{25,1},{2,10},{10... | collective-permute-start | bytes 540680 | tf_op jit(solution)/shard_map/ppermute | solution.py:328
  17.1 1.4 %collective-permute-start.8 = (bf16[240,256]{1,0:T(8,128)(2,1)S(1)}, bf16[240,256]{1,0:T(8,128)(2,1)S(1)}, u32[]{:S(2)}, u32[]{:S(2)}) collective-permute-start(bf16[240,256]{1,0:T(8,128)(2,1)S(1)} %get-tuple-element.49), channel_id=1, source_target_pairs={{0,1},{1,0},{2,3},{3,2},{4,5},{5,4},{6,7},{7,6},{8,9},{9,8},{10,11... | collective-permute-start | bytes 368648 | tf_op jit(solution)/shard_map/ppermute | solution.py:299
  18.5 7.7 %collective-permute-start.9 = (bf16[80,256]{1,0:T(8,128)(2,1)S(1)}, bf16[80,256]{1,0:T(8,128)(2,1)S(1)}, u32[]{:S(2)}, u32[]{:S(2)}) collective-permute-start(bf16[80,256]{1,0:T(8,128)(2,1)S(1)} %get-tuple-element.50), channel_id=1, source_target_pairs={{0,14},{1,15},{2,12},{3,13},{4,10},{5,11},{6,8},{7,9},{8,22},{9,23... | collective-permute-start | bytes 122888 | tf_op jit(solution)/shard_map/ppermute | solution.py:330
  21.4 7.2 %collective-permute-start.10 = (bf16[80,256]{1,0:T(8,128)(2,1)S(1)}, bf16[80,256]{1,0:T(8,128)(2,1)S(1)}, u32[]{:S(2)}, u32[]{:S(2)}) collective-permute-start(bf16[80,256]{1,0:T(8,128)(2,1)S(1)} %get-tuple-element.51), channel_id=1, source_target_pairs={{0,12},{1,13},{2,14},{3,15},{4,8},{5,9},{6,10},{7,11},{8,20},{9,21... | collective-permute-start | bytes 122888 | tf_op jit(solution)/shard_map/ppermute | solution.py:330
  22.5 6.2 %collective-permute-start.11 = (bf16[80,256]{1,0:T(8,128)(2,1)S(1)}, bf16[80,256]{1,0:T(8,128)(2,1)S(1)}, u32[]{:S(2)}, u32[]{:S(2)}) collective-permute-start(bf16[80,256]{1,0:T(8,128)(2,1)S(1)} %get-tuple-element.52), channel_id=1, source_target_pairs={{0,10},{1,11},{2,8},{3,9},{4,14},{5,15},{6,12},{7,13},{8,18},{9,19... | collective-permute-start | bytes 122888 | tf_op jit(solution)/shard_map/ppermute | solution.py:330
  29.5 6.0 %collective-permute-start.13 = (bf16[80,256]{1,0:T(8,128)(2,1)S(1)}, bf16[80,256]{1,0:T(8,128)(2,1)S(1)}, u32[]{:S(2)}, u32[]{:S(2)}) collective-permute-start(bf16[80,256]{1,0:T(8,128)(2,1)S(1)} %get-tuple-element.55), channel_id=1, source_target_pairs={{0,6},{1,7},{2,4},{3,5},{4,2},{5,3},{6,0},{7,1},{8,14},{9,15},{10,... | collective-permute-start | bytes 122888 | tf_op jit(solution)/shard_map/ppermute | solution.py:281
  31.8 5.4 %collective-permute-start.14 = (bf16[80,256]{1,0:T(8,128)(2,1)S(1)}, bf16[80,256]{1,0:T(8,128)(2,1)S(1)}, u32[]{:S(2)}, u32[]{:S(2)}) collective-permute-start(bf16[80,256]{1,0:T(8,128)(2,1)S(1)} %get-tuple-element.56), channel_id=1, source_target_pairs={{0,4},{1,5},{2,6},{3,7},{4,0},{5,1},{6,2},{7,3},{8,12},{9,13},{10,... | collective-permute-start | bytes 122888 | tf_op jit(solution)/shard_map/ppermute | solution.py:281
  32.9 4.3 %collective-permute-start.15 = (bf16[80,256]{1,0:T(8,128)(2,1)S(1)}, bf16[80,256]{1,0:T(8,128)(2,1)S(1)}, u32[]{:S(2)}, u32[]{:S(2)}) collective-permute-start(bf16[80,256]{1,0:T(8,128)(2,1)S(1)} %get-tuple-element.57), channel_id=1, source_target_pairs={{0,2},{1,3},{2,0},{3,1},{4,6},{5,7},{6,4},{7,5},{8,10},{9,11},{10,... | collective-permute-start | bytes 122888 | tf_op jit(solution)/shard_map/ppermute | solution.py:281
  33.9 16.0 %copy-start.5 = (f32[1,16,1]{1,2,0:T(1,128)S(1)}, f32[1,16,1]{1,2,0:T(1,128)}, u32[]{:S(2)}) copy-start(f32[1,16,1]{1,2,0:T(1,128)} %param.14) | copy-start | bytes 196
  33.9 3.7 %collective-permute-start.19 = (bf16[80,256]{1,0:T(8,128)(2,1)S(1)}, bf16[80,256]{1,0:T(8,128)(2,1)S(1)}, u32[]{:S(2)}, u32[]{:S(2)}) collective-permute-start(bf16[80,256]{1,0:T(8,128)(2,1)S(1)} %get-tuple-element.58.refs_3_), channel_id=1, source_target_pairs={{0,1},{1,0},{2,3},{3,2},{4,5},{5,4},{6,7},{7,6},{8,9},{9,8},{10,11... | collective-permute-start | bytes 122888 | tf_op jit(solution)/shard_map/ppermute | solution.py:285
  35.5 2.2 %collective-permute-start.16 = (bf16[80,256]{1,0:T(8,128)(2,1)S(1)}, bf16[80,256]{1,0:T(8,128)(2,1)S(1)}, u32[]{:S(2)}, u32[]{:S(2)}) collective-permute-start(bf16[80,256]{1,0:T(8,128)(2,1)S(1)} %collective-permute-done.13.refs_0_), channel_id=1, source_target_pairs={{0,1},{1,0},{2,3},{3,2},{4,5},{5,4},{6,7},{7,6},{8,9},{9,8},{10,11... | collective-permute-start | bytes 122888 | tf_op jit(solution)/shard_map/ppermute | solution.py:285
  37.2 1.2 %collective-permute-start.17 = (bf16[80,256]{1,0:T(8,128)(2,1)S(1)}, bf16[80,256]{1,0:T(8,128)(2,1)S(1)}, u32[]{:S(2)}, u32[]{:S(2)}) collective-permute-start(bf16[80,256]{1,0:T(8,128)(2,1)S(1)} %collective-permute-done.14.refs_1_), channel_id=1, source_target_pairs={{0,1},{1,0},{2,3},{3,2},{4,5},{5,4},{6,7},{7,6},{8,9},{9,8},{10,11... | collective-permute-start | bytes 122888 | tf_op jit(solution)/shard_map/ppermute | solution.py:285
  37.2 1.4 %collective-permute-start.18 = (bf16[80,256]{1,0:T(8,128)(2,1)S(1)}, bf16[80,256]{1,0:T(8,128)(2,1)S(1)}, u32[]{:S(2)}, u32[]{:S(2)}) collective-permute-start(bf16[80,256]{1,0:T(8,128)(2,1)S(1)} %collective-permute-done.15.refs_2_), channel_id=1, source_target_pairs={{0,1},{1,0},{2,3},{3,2},{4,5},{5,4},{6,7},{7,6},{8,9},{9,8},{10,11... | collective-permute-start | bytes 122888 | tf_op jit(solution)/shard_map/ppermute | solution.py:285
  41.0 1.5 %collective-permute-start.20 = (bf16[320,256]{1,0:T(8,128)(2,1)S(1)}, bf16[320,256]{1,0:T(8,128)(2,1)S(1)}, u32[]{:S(2)}, u32[]{:S(2)}) collective-permute-start(bf16[320,256]{1,0:T(8,128)(2,1)S(1)} %get-tuple-element.60), channel_id=1, source_target_pairs={{0,1},{1,0},{2,3},{3,2},{4,5},{5,4},{6,7},{7,6},{8,9},{9,8},{10,11... | collective-permute-start | bytes 491528 | tf_op jit(solution)/shard_map/ppermute | solution.py:299
  42.5 6.2 %collective-permute-start.21 = (bf16[80,256]{1,0:T(8,128)(2,1)S(1)}, bf16[80,256]{1,0:T(8,128)(2,1)S(1)}, u32[]{:S(2)}, u32[]{:S(2)}) collective-permute-start(bf16[80,256]{1,0:T(8,128)(2,1)S(1)} %get-tuple-element.61), channel_id=1, source_target_pairs={{0,6},{1,7},{2,4},{3,5},{4,2},{5,3},{6,0},{7,1},{8,14},{9,15},{10,... | collective-permute-start | bytes 122888 | tf_op jit(solution)/shard_map/ppermute | solution.py:281
  44.0 5.9 %collective-permute-start.22 = (bf16[80,256]{1,0:T(8,128)(2,1)S(1)}, bf16[80,256]{1,0:T(8,128)(2,1)S(1)}, u32[]{:S(2)}, u32[]{:S(2)}) collective-permute-start(bf16[80,256]{1,0:T(8,128)(2,1)S(1)} %get-tuple-element.62), channel_id=1, source_target_pairs={{0,4},{1,5},{2,6},{3,7},{4,0},{5,1},{6,2},{7,3},{8,12},{9,13},{10,... | collective-permute-start | bytes 122888 | tf_op jit(solution)/shard_map/ppermute | solution.py:281
  44.6 5.3 %collective-permute-start.23 = (bf16[80,256]{1,0:T(8,128)(2,1)S(1)}, bf16[80,256]{1,0:T(8,128)(2,1)S(1)}, u32[]{:S(2)}, u32[]{:S(2)}) collective-permute-start(bf16[80,256]{1,0:T(8,128)(2,1)S(1)} %get-tuple-element.63), channel_id=1, source_target_pairs={{0,2},{1,3},{2,0},{3,1},{4,6},{5,7},{6,4},{7,5},{8,10},{9,11},{10,... | collective-permute-start | bytes 122888 | tf_op jit(solution)/shard_map/ppermute | solution.py:281

commit v2 on v1

--- a/solution.py
+++ b/solution.py
@@ -11,6 +11,8 @@
 CAP = 5
 ROWS = 16
 LANES = 256
+PIECE = 512
+PARTS = 4
 EPS = 1e-06
 F32 = jnp.float32
 BF16 = jnp.bfloat16
@@ -38,20 +40,20 @@
     return pltpu.VMEM((LANES // 128, rows * width // LANES, 128), F32)
 
 
-def spread(values, spread_ref):
-    rows, width = values.shape
+def spread(values, spread_ref, width, start=0):
+    rows, columns = values.shape
     pieces = width // LANES
-    for tile in range(width // 128):
-        piece, half = divmod(tile, LANES // 128)
+    for tile in range(columns // 128):
+        piece, half = divmod(start // 128 + tile, LANES // 128)
         spread_ref[half, pl.ds(piece, rows, stride=pieces), :] = values[
             :, tile * 128 : (tile + 1) * 128
         ]
 
 
-def gathered(spread_ref, rows, width):
+def gathered(spread_ref, rows, width, start=0, columns=None):
     pieces = width // LANES
     tiles = []
-    for tile in range(width // 128):
+    for tile in range(start // 128, (start + (columns or width)) // 128):
         piece, half = divmod(tile, LANES // 128)
         tiles.append(spread_ref[half, pl.ds(piece, rows, stride=pieces), :].astype(BF16))
     return jnp.concatenate(tiles, axis=1)
@@ -115,7 +117,7 @@
         (((0,), (0,)), ((), ())),
         preferred_element_type=F32,
     )
-    spread(packed, spread_ref)
+    spread(packed, spread_ref, normed.shape[1])
     to_blocks(spread_ref, block_refs)
 
 
@@ -163,19 +165,21 @@
     write_blocks(normed, slots, my_expert(group), spread_ref, block_refs)
 
 
-def residual(x, slots, gates, expert, blocks, spread_ref):
-    width = x.shape[1]
+def fill(blocks, spread_ref):
     filled = from_blocks(blocks, spread_ref)
     spread_ref[:, filled:, :] = jnp.zeros(
         (spread_ref.shape[0], spread_ref.shape[1] - filled, 128), F32
     )
+
+
+def residual(x, gates, chosen, spread_ref, width, start=0):
     found = jnp.dot(
-        block_map(slots, expert),
-        gathered(spread_ref, pad_rows(EXPERTS * CAP), width),
+        chosen,
+        gathered(spread_ref, chosen.shape[1], width, start, x.shape[1]),
         preferred_element_type=F32,
     )
     update = (gates * found).astype(BF16)
-    return x.astype(F32) + update.astype(F32)
+    return (x.astype(F32) + update.astype(F32)).astype(BF16)
 
 
 def middle_kernel(group, *refs):
@@ -190,19 +194,29 @@
     meta = carried_ref[pieces * rows : (pieces + 1) * rows].astype(F32)
     gates = meta[:, 1:2] + meta[:, 2:3] + meta[:, 3:4]
     blocks = [ref[...] for ref in block_ins] + [carried_ref[(pieces + 1) * rows :]]
-    first = residual(x, meta[:, 0:1], gates, expert, blocks, spread_ref).astype(BF16)
+    fill(blocks, spread_ref)
+    first = residual(x, gates, block_map(meta[:, 0:1], expert), spread_ref, width)
     first_ref[...] = first
     slots = slots_of(upright(routes_ref[...].astype(F32)))
     normed = normalize(first.astype(F32), gain_ref[...])
     write_blocks(normed, slots, expert, spread_ref, block_refs)
 
 
-def last_kernel(group, x_ref, b0, b1, b2, b3, routes_ref, gates_ref, out_ref, spread_ref):
-    slots = slots_of(upright(routes_ref[...].astype(F32)))
+def last_kernel(group, x_ref, b0, b1, b2, b3, routes_ref, gates_ref, out_ref, spread_ref, done_ref, sems):
+    chosen = block_map(slots_of(upright(routes_ref[...].astype(F32))), my_expert(group))
     gates = upright(gates_ref[...])
-    blocks = [ref[...] for ref in (b0, b1, b2, b3)]
-    mixed = residual(x_ref[...], slots, gates, my_expert(group), blocks, spread_ref)
-    out_ref[...] = mixed.astype(BF16)
+    fill([ref[...] for ref in (b0, b1, b2, b3)], spread_ref)
+    width = x_ref.shape[1]
+    copies = []
+    for i in range(PARTS):
+        span = slice(i * width // PARTS, (i + 1) * width // PARTS)
+        done_ref[:, span] = residual(x_ref[:, span], gates, chosen, spread_ref, width, span.start)
+        copies.append(
+            pltpu.make_async_copy(done_ref.at[:, span], out_ref.at[:, span], sems.at[i])
+        )
+        copies[-1].start()
+    for copy in copies:
+        copy.wait()
 
 
 def expert_kernel(given, w_gate, w_up, w_down, *refs):
@@ -214,7 +228,9 @@
     gate_val = jnp.dot(x, w_gate[...], preferred_element_type=F32)
     up_val = jnp.dot(x, w_up[...], preferred_element_type=F32)
     hidden = (gate_val / (1.0 + jnp.exp(-gate_val)) * up_val).astype(BF16)
-    spread(jnp.dot(hidden, w_down[...], preferred_element_type=F32), spread_ref)
+    for start in range(0, width, PIECE):
+        piece = jnp.dot(hidden, w_down[:, start : start + PIECE], preferred_element_type=F32)
+        spread(piece, spread_ref, width, start)
     to_blocks(spread_ref, outs)
 
 
@@ -236,13 +252,13 @@
     out_ref[rows:] = summed(ins)
 
 
-def call(body, outs, ins, megabytes, scratch=(), flops=0, space=VMEM):
+def call(body, outs, ins, megabytes, scratch=(), flops=0, space=VMEM, out_space=VMEM):
     moved = sum(a.size * a.dtype.itemsize for a in (*ins, *outs))
     return pl.pallas_call(
         body,
         out_shape=outs,
         in_specs=[space] * len(ins),
-        out_specs=[VMEM] * len(outs),
+        out_specs=[out_space] * len(outs),
         scratch_shapes=list(scratch),
         compiler_params=pltpu.CompilerParams(vmem_limit_bytes=megabytes << 20),
         cost_estimate=pl.CostEstimate(flops=flops, bytes_accessed=moved, transcendentals=0),
@@ -287,7 +303,7 @@
 
     def experts(ins):
         count = sum(a.shape[0] for a in ins) // tall
-        sums = call(
+        return call(
             functools.partial(expert_kernel, len(ins)),
             [jax.ShapeDtypeStruct((count // group * tall, wide), BF16)] * group,
             [*weights, *ins],
@@ -295,13 +311,17 @@
             [spread_scratch(pad_rows(count * CAP), width)],
             flops=6 * 256 * width * weights[0].shape[1],
         )
+
+    def exchanged(sums):
         return [sums[0]] + [
             lax.ppermute(sums[m], "expert", within(-m)) for m in range(1, group)
         ]
 
     def added(terms):
         parts = terms[0].shape[0] // tall
-        return call(functools.partial(sum_kernel, group), [block] * parts, terms, 8)
+        return call(
+            functools.partial(sum_kernel, group), [block] * parts, terms, 8, flops=10**9
+        )
 
     sources = [
         pltpu.with_memory_space_constraint(a, pltpu.HBM)
@@ -321,12 +341,14 @@
     (carry,) = call(
         carry_kernel,
         [jax.ShapeDtypeStruct((ahead + tall, LANES), BF16)],
-        [travelling, *experts(shared(blocks[-1:]))],
+        [travelling, *exchanged(experts(shared(blocks[-1:])))],
         8,
     )
     *ins, carry = lax.optimization_barrier((*shared(arrived), carry))
+    *sums, carry = lax.optimization_barrier((*experts(ins), carry))
+    terms = exchanged(sums)
     carried = lax.ppermute(carry, "section", [(i, (i + 1) % sections) for i in range(sections)])
-    sums = added(experts(ins))
+    sums = added(terms)
     home = [lax.ppermute(sums[i], ("section", "expert"), onward(i)) for i in range(EXPERTS - 1)]
     first, *blocks = call(
         functools.partial(middle_kernel, group),
@@ -335,14 +357,15 @@
         8,
         [packing],
     )
-    sums = added(experts(shared(across(blocks[:-1]) + blocks[-1:])))
+    sums = added(exchanged(experts(shared(across(blocks[:-1]) + blocks[-1:]))))
     home = across(sums[:-1])
     (mixed,) = call(
         functools.partial(last_kernel, group),
         [whole],
         [first, *home, sums[-1], routes_2, gates_2],
         8,
-        [packing],
+        [packing, pltpu.VMEM((rows, width), BF16), pltpu.SemaphoreType.DMA((PARTS,))],
+        out_space=HBM,
     )
     return mixed[None]
 

time: 51.2 us -> 50 us (0.977)
  waiting for transfers between devices: 16 us -> 14.1 us
  starting transfers between devices: 24.6 us -> 25.4 us
    ppermute x3, waiting for transfers between devices: 2.32 us -> 1.05 us  [exchanged(): lax.ppermute(sums[m], 'expert', within(-m))]
    ppermute x3, waiting for transfers between devices: 4.03 us -> 3.36 us  [on_device(): lax.ppermute(sums[i], ('section', 'expert'), onward(i))]
  transfers between devices with their start and end apart: 24 -> 24, of which waited for: 14 -> 13; matrix products, arithmetic and copies ran while one was open for 0% -> 0% of each run, Pallas kernels for 8% -> 4%
where the time goes in v2:
time: 50 us; the launch traced here: 49.9 us
  starting transfers between devices  25.4 us (51%)
  waiting for transfers between devices  14.1 us (28%)
  Pallas kernels  10.3 us (21%)
    ppermute x9, starting transfers between devices, across(): lax.ppermute(blocks[i], 'expert', to_expert(i))  14.2 us
    pallas_call x9, Pallas kernels, call(): pl.pallas_call(body, out_shape=outs, in_specs=[space] * len(ins), out_spe...  10.3 us
    ppermute x9, waiting for transfers between devices, across(): lax.ppermute(blocks[i], 'expert', to_expert(i))  7.99 us
    ppermute x3, starting transfers between devices, on_device(): lax.ppermute(sums[i], ('section', 'expert'), onward(i))  6.72 us
    ppermute x3, waiting for transfers between devices, on_device(): lax.ppermute(sums[i], ('section', 'expert'), onward(i))  3.36 us
    ppermute x8, starting transfers between devices, shared(): lax.ppermute(a, 'expert', within(m))  2.04 us
    ppermute x8, waiting for transfers between devices, shared(): lax.ppermute(a, 'expert', within(m))  1.68 us
    ppermute x1, starting transfers between devices, on_device(): lax.ppermute(carry, 'section', [(i, (i + 1) % sections) for i in range(se...  1.49 us
  transfers between devices with their start and end apart: 24, of which 13 were waited for; matrix products, arithmetic and copies ran while one was open for 0% of the time, Pallas kernels for 4%

profile of v2, /device:TPU:0, one launch (start us, length us, event | category | flops | bytes accessed | tf_op | source)
XLA Modules:
  0.0 49.9 jit_solution(4729799206501730911)
XLA Ops:
  0.0 1.7 %shard_map.91 = (bf16[80,256]{1,0:T(8,128)(2,1)S(1)}, bf16[80,256]{1,0:T(8,128)(2,1)S(1)}, bf16[80,256]{1,0:T(8,128)(2,1)S(1)}, bf16[80,256]{1,0:T(8,128)(2,1)S(1)}, bf16[272,256]{1,0:T(8,128)(2,1)S(1)}) custom-call(bf16[16,4096]{1,0:T(8,128)(2,1)} %bitcast.21, f32[1,4096]{1,0:T(1,128)} %refs_4_.1, s32[1,16]{1,0:T(1,128)} %bitcast.22, f32[1,16]{1,0:T(1,128)} %bitcast.23), custom_call_target="tpu_custom_call" | custom-call | flops 10000000000 | bytes 450688 | tf_op jit(solution)/shard_map/pallas_call | solution.py:257
  1.7 0.5 %collective-permute-start.6 = (bf16[80,256]{1,0:T(8,128)(2,1)S(1)}, bf16[80,256]{1,0:T(8,128)(2,1)S(1)}, u32[]{:S(2)}, u32[]{:S(2)}) collective-permute-start(bf16[80,256]{1,0:T(8,128)(2,1)S(1)} %get-tuple-element.42.refs_0_), channel_id=1, source_target_pairs={{0,1},{1,0},{2,3},{3,2},{4,5},{5,4},{6,7},{7,6},{8,9},{9,8},{10,11... | collective-permute-start | bytes 122888 | tf_op jit(solution)/shard_map/ppermute | solution.py:301
  2.2 4.7 %collective-permute-start = (bf16[80,256]{1,0:T(8,128)(2,1)S(1)}, bf16[80,256]{1,0:T(8,128)(2,1)S(1)}, u32[]{:S(2)}, u32[]{:S(2)}) collective-permute-start(bf16[80,256]{1,0:T(8,128)(2,1)S(1)} %get-tuple-element.38), channel_id=1, source_target_pairs={{0,6},{1,7},{2,4},{3,5},{4,2},{5,3},{6,0},{7,1},{8,14},{9,15},{10,... | collective-permute-start | bytes 122888 | tf_op jit(solution)/shard_map/ppermute | solution.py:297
  6.9 0.6 %collective-permute-start.2 = (bf16[80,256]{1,0:T(8,128)(2,1)S(1)}, bf16[80,256]{1,0:T(8,128)(2,1)S(1)}, u32[]{:S(2)}, u32[]{:S(2)}) collective-permute-start(bf16[80,256]{1,0:T(8,128)(2,1)S(1)} %get-tuple-element.40), channel_id=1, source_target_pairs={{0,2},{1,3},{2,0},{3,1},{4,6},{5,7},{6,4},{7,5},{8,10},{9,11},{10,... | collective-permute-start | bytes 122888 | tf_op jit(solution)/shard_map/ppermute | solution.py:297
  7.6 1.8 %shard_map.92 = (bf16[80,256]{1,0:T(8,128)(2,1)S(1)}, bf16[80,256]{1,0:T(8,128)(2,1)S(1)}) custom-call(bf16[4096,512]{1,0:T(8,128)(2,1)S(1)} %bitcast.9, bf16[4096,512]{1,0:T(8,128)(2,1)S(1)} %bitcast.12, bf16[512,4096]{1,0:T(8,128)(2,1)S(1)} %bitcast.15, bf16[80,256]{1,0:T(8,128)(2,1)S(1)} %get-tuple-element.42.refs_0_, ...), custom_call_target="tpu_custom_call" | custom-call | flops 3221225472 | bytes 12746752 | tf_op jit(solution)/shard_map/pallas_call | solution.py:257
  9.5 0.5 collective-permute-start.3
  10.0 1.8 %collective-permute-done.1.refs_1_ = bf16[80,256]{1,0:T(8,128)(2,1)S(1)} collective-permute-done((bf16[80,256]{1,0:T(8,128)(2,1)S(1)}, bf16[80,256]{1,0:T(8,128)(2,1)S(1)}, u32[]{:S(2)}, u32[]{:S(2)}) %collective-permute-start.1) | collective-permute-done | bytes 40992 | tf_op jit(solution)/shard_map/ppermute | solution.py:297
  11.8 0.5 %collective-permute-start.5 = (bf16[80,256]{1,0:T(8,128)(2,1)S(1)}, bf16[80,256]{1,0:T(8,128)(2,1)S(1)}, u32[]{:S(2)}, u32[]{:S(2)}) collective-permute-start(bf16[80,256]{1,0:T(8,128)(2,1)S(1)} %collective-permute-done.2.refs_2_), channel_id=1, source_target_pairs={{0,1},{1,0},{2,3},{3,2},{4,5},{5,4},{6,7},{7,6},{8,9},{9,8},{10,11... | collective-permute-start | bytes 122888 | tf_op jit(solution)/shard_map/ppermute | solution.py:301
  12.4 0.6 %collective-permute-done.4.refs_4_ = bf16[80,256]{1,0:T(8,128)(2,1)S(1)} collective-permute-done((bf16[80,256]{1,0:T(8,128)(2,1)S(1)}, bf16[80,256]{1,0:T(8,128)(2,1)S(1)}, u32[]{:S(2)}, u32[]{:S(2)}) %collective-permute-start.4) | collective-permute-done | bytes 40992 | tf_op jit(solution)/shard_map/ppermute | solution.py:301
  13.2 2.4 %shard_map.94 = (bf16[240,256]{1,0:T(8,128)(2,1)S(1)}, bf16[240,256]{1,0:T(8,128)(2,1)S(1)}) custom-call(bf16[4096,512]{1,0:T(8,128)(2,1)S(1)} %bitcast.10, bf16[4096,512]{1,0:T(8,128)(2,1)S(1)} %bitcast.13, bf16[512,4096]{1,0:T(8,128)(2,1)S(1)} %bitcast.16, bf16[80,256]{1,0:T(8,128)(2,1)S(1)} %collective-permute-done.refs_0_, ...), custom_call_target="tpu_custom_call" | custom-call | flops 3221225472 | bytes 13074432 | tf_op jit(solution)/shard_map/pallas_call | solution.py:257
  16.0 1.5 %collective-permute-start.12 = (bf16[352,256]{1,0:T(8,128)(2,1)S(1)}, bf16[352,256]{1,0:T(8,128)(2,1)S(1)}, u32[]{:S(2)}, u32[]{:S(2)}) collective-permute-start(bf16[352,256]{1,0:T(8,128)(2,1)S(1)} %shard_map.93), channel_id=1, source_target_pairs={{0,8},{8,16},{16,24},{24,0},{1,9},{9,17},{17,25},{25,1},{2,10},{10... | collective-permute-start | bytes 540680 | tf_op jit(solution)/shard_map/ppermute | solution.py:350
  17.5 2.9 %collective-permute-start.9 = (bf16[80,256]{1,0:T(8,128)(2,1)S(1)}, bf16[80,256]{1,0:T(8,128)(2,1)S(1)}, u32[]{:S(2)}, u32[]{:S(2)}) collective-permute-start(bf16[80,256]{1,0:T(8,128)(2,1)S(1)} %get-tuple-element.56), channel_id=1, source_target_pairs={{0,14},{1,15},{2,12},{3,13},{4,10},{5,11},{6,8},{7,9},{8,22},{9,23... | collective-permute-start | bytes 122888 | tf_op jit(solution)/shard_map/ppermute | solution.py:352
  20.4 0.9 %collective-permute-start.10 = (bf16[80,256]{1,0:T(8,128)(2,1)S(1)}, bf16[80,256]{1,0:T(8,128)(2,1)S(1)}, u32[]{:S(2)}, u32[]{:S(2)}) collective-permute-start(bf16[80,256]{1,0:T(8,128)(2,1)S(1)} %get-tuple-element.57), channel_id=1, source_target_pairs={{0,12},{1,13},{2,14},{3,15},{4,8},{5,9},{6,10},{7,11},{8,20},{9,21... | collective-permute-start | bytes 122888 | tf_op jit(solution)/shard_map/ppermute | solution.py:352
  21.3 2.9 %collective-permute-start.11 = (bf16[80,256]{1,0:T(8,128)(2,1)S(1)}, bf16[80,256]{1,0:T(8,128)(2,1)S(1)}, u32[]{:S(2)}, u32[]{:S(2)}) collective-permute-start(bf16[80,256]{1,0:T(8,128)(2,1)S(1)} %get-tuple-element.58), channel_id=1, source_target_pairs={{0,10},{1,11},{2,8},{3,9},{4,14},{5,15},{6,12},{7,13},{8,18},{9,19... | collective-permute-start | bytes 122888 | tf_op jit(solution)/shard_map/ppermute | solution.py:352
  24.2 0.9 %collective-permute-done.9.refs_0_ = bf16[80,256]{1,0:T(8,128)(2,1)S(1)} collective-permute-done((bf16[80,256]{1,0:T(8,128)(2,1)S(1)}, bf16[80,256]{1,0:T(8,128)(2,1)S(1)}, u32[]{:S(2)}, u32[]{:S(2)}) %collective-permute-start.9) | collective-permute-done | bytes 40992 | tf_op jit(solution)/shard_map/ppermute | solution.py:352
  25.2 2.2 %collective-permute-done.10.refs_1_ = bf16[80,256]{1,0:T(8,128)(2,1)S(1)} collective-permute-done((bf16[80,256]{1,0:T(8,128)(2,1)S(1)}, bf16[80,256]{1,0:T(8,128)(2,1)S(1)}, u32[]{:S(2)}, u32[]{:S(2)}) %collective-permute-start.10) | collective-permute-done | bytes 40992 | tf_op jit(solution)/shard_map/ppermute | solution.py:352
  27.6 0.7 %shard_map.96 = (bf16[16,4096]{1,0:T(8,128)(2,1)S(1)}, bf16[80,256]{1,0:T(8,128)(2,1)S(1)}, bf16[80,256]{1,0:T(8,128)(2,1)S(1)}, bf16[80,256]{1,0:T(8,128)(2,1)S(1)}, bf16[80,256]{1,0:T(8,128)(2,1)S(1)}) custom-call(bf16[80,256]{1,0:T(8,128)(2,1)S(1)} %collective-permute-done.9.refs_0_, bf16[80,256]{1,0:T(8,128)(2,1)S(1)} %collective-permute-done.10.refs_1_, ...), custom_call_target="tpu_custom_call" | custom-call | bytes 614464 | tf_op jit(solution)/shard_map/pallas_call | solution.py:257
  28.3 2.3 %collective-permute-start.13 = (bf16[80,256]{1,0:T(8,128)(2,1)S(1)}, bf16[80,256]{1,0:T(8,128)(2,1)S(1)}, u32[]{:S(2)}, u32[]{:S(2)}) collective-permute-start(bf16[80,256]{1,0:T(8,128)(2,1)S(1)} %get-tuple-element.61), channel_id=1, source_target_pairs={{0,6},{1,7},{2,4},{3,5},{4,2},{5,3},{6,0},{7,1},{8,14},{9,15},{10,... | collective-permute-start | bytes 122888 | tf_op jit(solution)/shard_map/ppermute | solution.py:297
  30.6 1.3 %collective-permute-start.14 = (bf16[80,256]{1,0:T(8,128)(2,1)S(1)}, bf16[80,256]{1,0:T(8,128)(2,1)S(1)}, u32[]{:S(2)}, u32[]{:S(2)}) collective-permute-start(bf16[80,256]{1,0:T(8,128)(2,1)S(1)} %get-tuple-element.62), channel_id=1, source_target_pairs={{0,4},{1,5},{2,6},{3,7},{4,0},{5,1},{6,2},{7,3},{8,12},{9,13},{10,... | collective-permute-start | bytes 122888 | tf_op jit(solution)/shard_map/ppermute | solution.py:297
  31.9 0.9 %collective-permute-start.15 = (bf16[80,256]{1,0:T(8,128)(2,1)S(1)}, bf16[80,256]{1,0:T(8,128)(2,1)S(1)}, u32[]{:S(2)}, u32[]{:S(2)}) collective-permute-start(bf16[80,256]{1,0:T(8,128)(2,1)S(1)} %get-tuple-element.63), channel_id=1, source_target_pairs={{0,2},{1,3},{2,0},{3,1},{4,6},{5,7},{6,4},{7,5},{8,10},{9,11},{10,... | collective-permute-start | bytes 122888 | tf_op jit(solution)/shard_map/ppermute | solution.py:297
  32.8 1.6 %collective-permute-done.13.refs_0_ = bf16[80,256]{1,0:T(8,128)(2,1)S(1)} collective-permute-done((bf16[80,256]{1,0:T(8,128)(2,1)S(1)}, bf16[80,256]{1,0:T(8,128)(2,1)S(1)}, u32[]{:S(2)}, u32[]{:S(2)}) %collective-permute-start.13) | collective-permute-done | bytes 40992 | tf_op jit(solution)/shard_map/ppermute | solution.py:297
  34.4 1.6 %collective-permute-done.14.refs_1_ = bf16[80,256]{1,0:T(8,128)(2,1)S(1)} collective-permute-done((bf16[80,256]{1,0:T(8,128)(2,1)S(1)}, bf16[80,256]{1,0:T(8,128)(2,1)S(1)}, u32[]{:S(2)}, u32[]{:S(2)}) %collective-permute-start.14) | collective-permute-done | bytes 40992 | tf_op jit(solution)/shard_map/ppermute | solution.py:297
  36.0 0.5 %collective-permute-start.18 = (bf16[80,256]{1,0:T(8,128)(2,1)S(1)}, bf16[80,256]{1,0:T(8,128)(2,1)S(1)}, u32[]{:S(2)}, u32[]{:S(2)}) collective-permute-start(bf16[80,256]{1,0:T(8,128)(2,1)S(1)} %collective-permute-done.15.refs_2_), channel_id=1, source_target_pairs={{0,1},{1,0},{2,3},{3,2},{4,5},{5,4},{6,7},{7,6},{8,9},{9,8},{10,11... | collective-permute-start | bytes 122888 | tf_op jit(solution)/shard_map/ppermute | solution.py:301
  36.5 0.7 %collective-permute-done.17.refs_5_ = bf16[80,256]{1,0:T(8,128)(2,1)S(1)} collective-permute-done((bf16[80,256]{1,0:T(8,128)(2,1)S(1)}, bf16[80,256]{1,0:T(8,128)(2,1)S(1)}, u32[]{:S(2)}, u32[]{:S(2)}) %collective-permute-start.17) | collective-permute-done | bytes 40992 | tf_op jit(solution)/shard_map/ppermute | solution.py:301
  37.4 2.4 %shard_map.97 = (bf16[320,256]{1,0:T(8,128)(2,1)S(1)}, bf16[320,256]{1,0:T(8,128)(2,1)S(1)}) custom-call(bf16[4096,512]{1,0:T(8,128)(2,1)S(1)} %bitcast.11, bf16[4096,512]{1,0:T(8,128)(2,1)S(1)} %bitcast.14, bf16[512,4096]{1,0:T(8,128)(2,1)S(1)} %bitcast.17, bf16[80,256]{1,0:T(8,128)(2,1)S(1)} %collective-permute-done.13.refs_0_, ...), custom_call_target="tpu_custom_call" | custom-call | flops 3221225472 | bytes 13238272 | tf_op jit(solution)/shard_map/pallas_call | solution.py:257
  40.2 1.0 %collective-permute-done.20.refs_1_ = bf16[320,256]{1,0:T(8,128)(2,1)S(1)} collective-permute-done((bf16[320,256]{1,0:T(8,128)(2,1)S(1)}, bf16[320,256]{1,0:T(8,128)(2,1)S(1)}, u32[]{:S(2)}, u32[]{:S(2)}) %collective-permute-start.20) | collective-permute-done | bytes 163872 | tf_op jit(solution)/shard_map/ppermute | solution.py:317
  41.3 1.8 %collective-permute-start.21 = (bf16[80,256]{1,0:T(8,128)(2,1)S(1)}, bf16[80,256]{1,0:T(8,128)(2,1)S(1)}, u32[]{:S(2)}, u32[]{:S(2)}) collective-permute-start(bf16[80,256]{1,0:T(8,128)(2,1)S(1)} %get-tuple-element.67), channel_id=1, source_target_pairs={{0,6},{1,7},{2,4},{3,5},{4,2},{5,3},{6,0},{7,1},{8,14},{9,15},{10,... | collective-permute-start | bytes 122888 | tf_op jit(solution)/shard_map/ppermute | solution.py:297
  43.0 0.4 collective-permute-start.22
  43.5 2.3 %collective-permute-start.23 = (bf16[80,256]{1,0:T(8,128)(2,1)S(1)}, bf16[80,256]{1,0:T(8,128)(2,1)S(1)}, u32[]{:S(2)}, u32[]{:S(2)}) collective-permute-start(bf16[80,256]{1,0:T(8,128)(2,1)S(1)} %get-tuple-element.69), channel_id=1, source_target_pairs={{0,2},{1,3},{2,0},{3,1},{4,6},{5,7},{6,4},{7,5},{8,10},{9,11},{10,... | collective-permute-start | bytes 122888 | tf_op jit(solution)/shard_map/ppermute | solution.py:297
  45.7 1.8 %collective-permute-done.21.b0 = bf16[80,256]{1,0:T(8,128)(2,1)S(1)} collective-permute-done((bf16[80,256]{1,0:T(8,128)(2,1)S(1)}, bf16[80,256]{1,0:T(8,128)(2,1)S(1)}, u32[]{:S(2)}, u32[]{:S(2)}) %collective-permute-start.21) | collective-permute-done | bytes 40992 | tf_op jit(solution)/shard_map/ppermute | solution.py:297
  47.5 1.2 %collective-permute-done.22.b1 = bf16[80,256]{1,0:T(8,128)(2,1)S(1)} collective-permute-done((bf16[80,256]{1,0:T(8,128)(2,1)S(1)}, bf16[80,256]{1,0:T(8,128)(2,1)S(1)}, u32[]{:S(2)}, u32[]{:S(2)}) %collective-permute-start.22) | collective-permute-done | bytes 40992 | tf_op jit(solution)/shard_map/ppermute | solution.py:297
  48.7 1.1 %shard_map.99 = bf16[16,4096]{1,0:T(8,128)(2,1)} custom-call(bf16[16,4096]{1,0:T(8,128)(2,1)S(1)} %get-tuple-element.60.x_ref, bf16[80,256]{1,0:T(8,128)(2,1)S(1)} %collective-permute-done.21.b0, bf16[80,256]{1,0:T(8,128)(2,1)S(1)} %collective-permute-done.22.b1, bf16[80,256]{1,0:T(8,128)(2,1)S(1)} %collective-permute-done.23.b2, ...), custom_call_target="tpu_custom_call" | custom-call | bytes 426112 | tf_op jit(solution)/shard_map/pallas_call | solution.py:257
  (37 shorter events, 1.6 us)
Async XLA Ops:
  0.0 7.5 %copy-start = (bf16[1,1,4096,512]{3,2,1,0:T(8,128)(2,1)S(1)}, bf16[1,1,4096,512]{3,2,1,0:T(8,128)(2,1)}, u32[]{:S(2)}) copy-start(bf16[1,1,4096,512]{3,2,1,0:T(8,128)(2,1)} %param.15) | copy-start | bytes 12582916
  0.0 7.5 %copy-start.1 = (bf16[1,1,4096,512]{3,2,1,0:T(8,128)(2,1)S(1)}, bf16[1,1,4096,512]{3,2,1,0:T(8,128)(2,1)}, u32[]{:S(2)}) copy-start(bf16[1,1,4096,512]{3,2,1,0:T(8,128)(2,1)} %param.16) | copy-start | bytes 12582916
  0.0 7.5 %copy-start.2 = (bf16[1,1,512,4096]{3,2,1,0:T(8,128)(2,1)S(1)}, bf16[1,1,512,4096]{3,2,1,0:T(8,128)(2,1)}, u32[]{:S(2)}) copy-start(bf16[1,1,512,4096]{3,2,1,0:T(8,128)(2,1)} %param.17) | copy-start | bytes 12582916
  1.7 5.8 %collective-permute-start.6 = (bf16[80,256]{1,0:T(8,128)(2,1)S(1)}, bf16[80,256]{1,0:T(8,128)(2,1)S(1)}, u32[]{:S(2)}, u32[]{:S(2)}) collective-permute-start(bf16[80,256]{1,0:T(8,128)(2,1)S(1)} %get-tuple-element.42.refs_0_), channel_id=1, source_target_pairs={{0,1},{1,0},{2,3},{3,2},{4,5},{5,4},{6,7},{7,6},{8,9},{9,8},{10,11... | collective-permute-start | bytes 122888 | tf_op jit(solution)/shard_map/ppermute | solution.py:301
  2.2 7.3 %collective-permute-start = (bf16[80,256]{1,0:T(8,128)(2,1)S(1)}, bf16[80,256]{1,0:T(8,128)(2,1)S(1)}, u32[]{:S(2)}, u32[]{:S(2)}) collective-permute-start(bf16[80,256]{1,0:T(8,128)(2,1)S(1)} %get-tuple-element.38), channel_id=1, source_target_pairs={{0,6},{1,7},{2,4},{3,5},{4,2},{5,3},{6,0},{7,1},{8,14},{9,15},{10,... | collective-permute-start | bytes 122888 | tf_op jit(solution)/shard_map/ppermute | solution.py:297
  6.9 4.9 %collective-permute-start.1 = (bf16[80,256]{1,0:T(8,128)(2,1)S(1)}, bf16[80,256]{1,0:T(8,128)(2,1)S(1)}, u32[]{:S(2)}, u32[]{:S(2)}) collective-permute-start(bf16[80,256]{1,0:T(8,128)(2,1)S(1)} %get-tuple-element.39), channel_id=1, source_target_pairs={{0,4},{1,5},{2,6},{3,7},{4,0},{5,1},{6,2},{7,3},{8,12},{9,13},{10,... | collective-permute-start | bytes 122888 | tf_op jit(solution)/shard_map/ppermute | solution.py:297
  6.9 4.9 %collective-permute-start.2 = (bf16[80,256]{1,0:T(8,128)(2,1)S(1)}, bf16[80,256]{1,0:T(8,128)(2,1)S(1)}, u32[]{:S(2)}, u32[]{:S(2)}) collective-permute-start(bf16[80,256]{1,0:T(8,128)(2,1)S(1)} %get-tuple-element.40), channel_id=1, source_target_pairs={{0,2},{1,3},{2,0},{3,1},{4,6},{5,7},{6,4},{7,5},{8,10},{9,11},{10,... | collective-permute-start | bytes 122888 | tf_op jit(solution)/shard_map/ppermute | solution.py:297
  9.4 2.9 %collective-permute-start.7 = (bf16[80,256]{1,0:T(8,128)(2,1)S(1)}, bf16[80,256]{1,0:T(8,128)(2,1)S(1)}, u32[]{:S(2)}, u32[]{:S(2)}) collective-permute-start(bf16[80,256]{1,0:T(8,128)(2,1)S(1)} %get-tuple-element.44), channel_id=1, source_target_pairs={{0,1},{1,0},{2,3},{3,2},{4,5},{5,4},{6,7},{7,6},{8,9},{9,8},{10,11... | collective-permute-start | bytes 122888 | tf_op jit(solution)/shard_map/ppermute | solution.py:317
  9.5 2.9 %collective-permute-start.3 = (bf16[80,256]{1,0:T(8,128)(2,1)S(1)}, bf16[80,256]{1,0:T(8,128)(2,1)S(1)}, u32[]{:S(2)}, u32[]{:S(2)}) collective-permute-start(bf16[80,256]{1,0:T(8,128)(2,1)S(1)} %collective-permute-done.refs_0_), channel_id=1, source_target_pairs={{0,1},{1,0},{2,3},{3,2},{4,5},{5,4},{6,7},{7,6},{8,9},{9,8},{10,11... | collective-permute-start | bytes 122888 | tf_op jit(solution)/shard_map/ppermute | solution.py:301
  11.8 1.2 %collective-permute-start.4 = (bf16[80,256]{1,0:T(8,128)(2,1)S(1)}, bf16[80,256]{1,0:T(8,128)(2,1)S(1)}, u32[]{:S(2)}, u32[]{:S(2)}) collective-permute-start(bf16[80,256]{1,0:T(8,128)(2,1)S(1)} %collective-permute-done.1.refs_1_), channel_id=1, source_target_pairs={{0,1},{1,0},{2,3},{3,2},{4,5},{5,4},{6,7},{7,6},{8,9},{9,8},{10,11... | collective-permute-start | bytes 122888 | tf_op jit(solution)/shard_map/ppermute | solution.py:301
  11.8 1.4 %collective-permute-start.5 = (bf16[80,256]{1,0:T(8,128)(2,1)S(1)}, bf16[80,256]{1,0:T(8,128)(2,1)S(1)}, u32[]{:S(2)}, u32[]{:S(2)}) collective-permute-start(bf16[80,256]{1,0:T(8,128)(2,1)S(1)} %collective-permute-done.2.refs_2_), channel_id=1, source_target_pairs={{0,1},{1,0},{2,3},{3,2},{4,5},{5,4},{6,7},{7,6},{8,9},{9,8},{10,11... | collective-permute-start | bytes 122888 | tf_op jit(solution)/shard_map/ppermute | solution.py:301
  12.3 15.2 %copy-start.3 = (f32[1,4096]{1,0:T(1,128)S(1)}, f32[1,4096]{1,0:T(1,128)}, u32[]{:S(2)}) copy-start(f32[1,4096]{1,0:T(1,128)} %refs_4_.1) | copy-start | bytes 49156
  12.3 15.2 %copy-start.4 = (s32[1,16,1]{1,2,0:T(1,128)S(1)}, s32[1,16,1]{1,2,0:T(1,128)}, u32[]{:S(2)}) copy-start(s32[1,16,1]{1,2,0:T(1,128)} %param.13) | copy-start | bytes 196
  15.6 1.9 %collective-permute-start.8 = (bf16[240,256]{1,0:T(8,128)(2,1)S(1)}, bf16[240,256]{1,0:T(8,128)(2,1)S(1)}, u32[]{:S(2)}, u32[]{:S(2)}) collective-permute-start(bf16[240,256]{1,0:T(8,128)(2,1)S(1)} %get-tuple-element.55), channel_id=1, source_target_pairs={{0,1},{1,0},{2,3},{3,2},{4,5},{5,4},{6,7},{7,6},{8,9},{9,8},{10,11... | collective-permute-start | bytes 368648 | tf_op jit(solution)/shard_map/ppermute | solution.py:317
  16.0 11.6 %collective-permute-start.12 = (bf16[352,256]{1,0:T(8,128)(2,1)S(1)}, bf16[352,256]{1,0:T(8,128)(2,1)S(1)}, u32[]{:S(2)}, u32[]{:S(2)}) collective-permute-start(bf16[352,256]{1,0:T(8,128)(2,1)S(1)} %shard_map.93), channel_id=1, source_target_pairs={{0,8},{8,16},{16,24},{24,0},{1,9},{9,17},{17,25},{25,1},{2,10},{10... | collective-permute-start | bytes 540680 | tf_op jit(solution)/shard_map/ppermute | solution.py:350
  17.5 7.7 %collective-permute-start.9 = (bf16[80,256]{1,0:T(8,128)(2,1)S(1)}, bf16[80,256]{1,0:T(8,128)(2,1)S(1)}, u32[]{:S(2)}, u32[]{:S(2)}) collective-permute-start(bf16[80,256]{1,0:T(8,128)(2,1)S(1)} %get-tuple-element.56), channel_id=1, source_target_pairs={{0,14},{1,15},{2,12},{3,13},{4,10},{5,11},{6,8},{7,9},{8,22},{9,23... | collective-permute-start | bytes 122888 | tf_op jit(solution)/shard_map/ppermute | solution.py:352
  20.4 7.0 %collective-permute-start.10 = (bf16[80,256]{1,0:T(8,128)(2,1)S(1)}, bf16[80,256]{1,0:T(8,128)(2,1)S(1)}, u32[]{:S(2)}, u32[]{:S(2)}) collective-permute-start(bf16[80,256]{1,0:T(8,128)(2,1)S(1)} %get-tuple-element.57), channel_id=1, source_target_pairs={{0,12},{1,13},{2,14},{3,15},{4,8},{5,9},{6,10},{7,11},{8,20},{9,21... | collective-permute-start | bytes 122888 | tf_op jit(solution)/shard_map/ppermute | solution.py:352
  21.3 6.2 %collective-permute-start.11 = (bf16[80,256]{1,0:T(8,128)(2,1)S(1)}, bf16[80,256]{1,0:T(8,128)(2,1)S(1)}, u32[]{:S(2)}, u32[]{:S(2)}) collective-permute-start(bf16[80,256]{1,0:T(8,128)(2,1)S(1)} %get-tuple-element.58), channel_id=1, source_target_pairs={{0,10},{1,11},{2,8},{3,9},{4,14},{5,15},{6,12},{7,13},{8,18},{9,19... | collective-permute-start | bytes 122888 | tf_op jit(solution)/shard_map/ppermute | solution.py:352
  28.3 6.1 %collective-permute-start.13 = (bf16[80,256]{1,0:T(8,128)(2,1)S(1)}, bf16[80,256]{1,0:T(8,128)(2,1)S(1)}, u32[]{:S(2)}, u32[]{:S(2)}) collective-permute-start(bf16[80,256]{1,0:T(8,128)(2,1)S(1)} %get-tuple-element.61), channel_id=1, source_target_pairs={{0,6},{1,7},{2,4},{3,5},{4,2},{5,3},{6,0},{7,1},{8,14},{9,15},{10,... | collective-permute-start | bytes 122888 | tf_op jit(solution)/shard_map/ppermute | solution.py:297
  30.6 5.3 %collective-permute-start.14 = (bf16[80,256]{1,0:T(8,128)(2,1)S(1)}, bf16[80,256]{1,0:T(8,128)(2,1)S(1)}, u32[]{:S(2)}, u32[]{:S(2)}) collective-permute-start(bf16[80,256]{1,0:T(8,128)(2,1)S(1)} %get-tuple-element.62), channel_id=1, source_target_pairs={{0,4},{1,5},{2,6},{3,7},{4,0},{5,1},{6,2},{7,3},{8,12},{9,13},{10,... | collective-permute-start | bytes 122888 | tf_op jit(solution)/shard_map/ppermute | solution.py:297
  31.9 4.1 %collective-permute-start.15 = (bf16[80,256]{1,0:T(8,128)(2,1)S(1)}, bf16[80,256]{1,0:T(8,128)(2,1)S(1)}, u32[]{:S(2)}, u32[]{:S(2)}) collective-permute-start(bf16[80,256]{1,0:T(8,128)(2,1)S(1)} %get-tuple-element.63), channel_id=1, source_target_pairs={{0,2},{1,3},{2,0},{3,1},{4,6},{5,7},{6,4},{7,5},{8,10},{9,11},{10,... | collective-permute-start | bytes 122888 | tf_op jit(solution)/shard_map/ppermute | solution.py:297
  32.8 15.9 %copy-start.5 = (f32[1,16,1]{1,2,0:T(1,128)S(1)}, f32[1,16,1]{1,2,0:T(1,128)}, u32[]{:S(2)}) copy-start(f32[1,16,1]{1,2,0:T(1,128)} %param.14) | copy-start | bytes 196
  32.8 3.7 %collective-permute-start.19 = (bf16[80,256]{1,0:T(8,128)(2,1)S(1)}, bf16[80,256]{1,0:T(8,128)(2,1)S(1)}, u32[]{:S(2)}, u32[]{:S(2)}) collective-permute-start(bf16[80,256]{1,0:T(8,128)(2,1)S(1)} %get-tuple-element.64.refs_3_), channel_id=1, source_target_pairs={{0,1},{1,0},{2,3},{3,2},{4,5},{5,4},{6,7},{7,6},{8,9},{9,8},{10,11... | collective-permute-start | bytes 122888 | tf_op jit(solution)/shard_map/ppermute | solution.py:301
  34.4 2.1 %collective-permute-start.16 = (bf16[80,256]{1,0:T(8,128)(2,1)S(1)}, bf16[80,256]{1,0:T(8,128)(2,1)S(1)}, u32[]{:S(2)}, u32[]{:S(2)}) collective-permute-start(bf16[80,256]{1,0:T(8,128)(2,1)S(1)} %collective-permute-done.13.refs_0_), channel_id=1, source_target_pairs={{0,1},{1,0},{2,3},{3,2},{4,5},{5,4},{6,7},{7,6},{8,9},{9,8},{10,11... | collective-permute-start | bytes 122888 | tf_op jit(solution)/shard_map/ppermute | solution.py:301
  36.0 1.2 %collective-permute-start.17 = (bf16[80,256]{1,0:T(8,128)(2,1)S(1)}, bf16[80,256]{1,0:T(8,128)(2,1)S(1)}, u32[]{:S(2)}, u32[]{:S(2)}) collective-permute-start(bf16[80,256]{1,0:T(8,128)(2,1)S(1)} %collective-permute-done.14.refs_1_), channel_id=1, source_target_pairs={{0,1},{1,0},{2,3},{3,2},{4,5},{5,4},{6,7},{7,6},{8,9},{9,8},{10,11... | collective-permute-start | bytes 122888 | tf_op jit(solution)/shard_map/ppermute | solution.py:301
  36.0 1.4 %collective-permute-start.18 = (bf16[80,256]{1,0:T(8,128)(2,1)S(1)}, bf16[80,256]{1,0:T(8,128)(2,1)S(1)}, u32[]{:S(2)}, u32[]{:S(2)}) collective-permute-start(bf16[80,256]{1,0:T(8,128)(2,1)S(1)} %collective-permute-done.15.refs_2_), channel_id=1, source_target_pairs={{0,1},{1,0},{2,3},{3,2},{4,5},{5,4},{6,7},{7,6},{8,9},{9,8},{10,11... | collective-permute-start | bytes 122888 | tf_op jit(solution)/shard_map/ppermute | solution.py:301
  39.8 1.5 %collective-permute-start.20 = (bf16[320,256]{1,0:T(8,128)(2,1)S(1)}, bf16[320,256]{1,0:T(8,128)(2,1)S(1)}, u32[]{:S(2)}, u32[]{:S(2)}) collective-permute-start(bf16[320,256]{1,0:T(8,128)(2,1)S(1)} %get-tuple-element.66), channel_id=1, source_target_pairs={{0,1},{1,0},{2,3},{3,2},{4,5},{5,4},{6,7},{7,6},{8,9},{9,8},{10,11... | collective-permute-start | bytes 491528 | tf_op jit(solution)/shard_map/ppermute | solution.py:317
  41.3 6.2 %collective-permute-start.21 = (bf16[80,256]{1,0:T(8,128)(2,1)S(1)}, bf16[80,256]{1,0:T(8,128)(2,1)S(1)}, u32[]{:S(2)}, u32[]{:S(2)}) collective-permute-start(bf16[80,256]{1,0:T(8,128)(2,1)S(1)} %get-tuple-element.67), channel_id=1, source_target_pairs={{0,6},{1,7},{2,4},{3,5},{4,2},{5,3},{6,0},{7,1},{8,14},{9,15},{10,... | collective-permute-start | bytes 122888 | tf_op jit(solution)/shard_map/ppermute | solution.py:297
  43.0 5.7 %collective-permute-start.22 = (bf16[80,256]{1,0:T(8,128)(2,1)S(1)}, bf16[80,256]{1,0:T(8,128)(2,1)S(1)}, u32[]{:S(2)}, u32[]{:S(2)}) collective-permute-start(bf16[80,256]{1,0:T(8,128)(2,1)S(1)} %get-tuple-element.68), channel_id=1, source_target_pairs={{0,4},{1,5},{2,6},{3,7},{4,0},{5,1},{6,2},{7,3},{8,12},{9,13},{10,... | collective-permute-start | bytes 122888 | tf_op jit(solution)/shard_map/ppermute | solution.py:297
  43.5 5.3 %collective-permute-start.23 = (bf16[80,256]{1,0:T(8,128)(2,1)S(1)}, bf16[80,256]{1,0:T(8,128)(2,1)S(1)}, u32[]{:S(2)}, u32[]{:S(2)}) collective-permute-start(bf16[80,256]{1,0:T(8,128)(2,1)S(1)} %get-tuple-element.69), channel_id=1, source_target_pairs={{0,2},{1,3},{2,0},{3,1},{4,6},{5,7},{6,4},{7,5},{8,10},{9,11},{10,... | collective-permute-start | bytes 122888 | tf_op jit(solution)/shard_map/ppermute | solution.py:297

commit v3 on v2

--- a/solution.py
+++ b/solution.py
@@ -21,7 +21,7 @@
 
 
 def distance(place):
-    return EXPERTS - 1 - place
+    return place ^ (2 + (place >> 1))
 
 
 def fifth(value):
@@ -110,12 +110,9 @@
     return (values * inv_scale * gain).astype(BF16)
 
 
-def write_blocks(normed, slots, expert, spread_ref, block_refs):
+def write_blocks(normed, chosen, spread_ref, block_refs):
     packed = lax.dot_general(
-        block_map(slots, expert),
-        normed,
-        (((0,), (0,)), ((), ())),
-        preferred_element_type=F32,
+        chosen, normed, (((0,), (0,)), ((), ())), preferred_element_type=F32
     )
     spread(packed, spread_ref, normed.shape[1])
     to_blocks(spread_ref, block_refs)
@@ -149,20 +146,23 @@
     ]
     for copy in copies:
         copy.start()
-    for copy in copies:
-        copy.wait()
     x_ref, gain_ref, routes_ref, gates_ref = held
     rows, width = x_ref.shape
+    for copy in copies[2:]:
+        copy.wait()
     slots = slots_of(upright(routes_ref[...].astype(F32)))
     lane = lax.broadcasted_iota(jnp.int32, (rows, LANES), 1)
     meta = jnp.zeros((rows, LANES), F32)
     for i, column in enumerate([slots, *split_parts(upright(gates_ref[...]))]):
         meta = jnp.where(lane == i, column.astype(F32), meta)
+    chosen = block_map(slots, my_expert(group))
+    for copy in copies[:2]:
+        copy.wait()
     for piece in range(width // LANES):
         ahead_ref[piece * rows : (piece + 1) * rows] = x_ref[:, piece * LANES : (piece + 1) * LANES]
     ahead_ref[width // LANES * rows :] = meta.astype(BF16)
     normed = normalize(x_ref[...].astype(F32), gain_ref[...])
-    write_blocks(normed, slots, my_expert(group), spread_ref, block_refs)
+    write_blocks(normed, chosen, spread_ref, block_refs)
 
 
 def fill(blocks, spread_ref):
@@ -183,7 +183,7 @@
 
 
 def middle_kernel(group, *refs):
-    block_ins, carried_ref, gain_ref, routes_ref = refs[: EXPERTS - 1], *refs[EXPERTS - 1 : EXPERTS + 2]
+    block_ins, carried_ref, gain_ref, map_ref = refs[: EXPERTS - 1], *refs[EXPERTS - 1 : EXPERTS + 2]
     first_ref, block_refs, spread_ref = refs[EXPERTS + 2], refs[EXPERTS + 3 : -1], refs[-1]
     expert = my_expert(group)
     rows, width = first_ref.shape
@@ -197,14 +197,13 @@
     fill(blocks, spread_ref)
     first = residual(x, gates, block_map(meta[:, 0:1], expert), spread_ref, width)
     first_ref[...] = first
-    slots = slots_of(upright(routes_ref[...].astype(F32)))
     normed = normalize(first.astype(F32), gain_ref[...])
-    write_blocks(normed, slots, expert, spread_ref, block_refs)
-
-
-def last_kernel(group, x_ref, b0, b1, b2, b3, routes_ref, gates_ref, out_ref, spread_ref, done_ref, sems):
-    chosen = block_map(slots_of(upright(routes_ref[...].astype(F32))), my_expert(group))
-    gates = upright(gates_ref[...])
+    write_blocks(normed, map_ref[...], spread_ref, block_refs)
+
+
+def last_kernel(x_ref, b0, b1, b2, b3, map_ref, gates_ref, out_ref, spread_ref, done_ref, sems):
+    chosen = map_ref[...]
+    gates = gates_ref[:, 0:1]
     fill([ref[...] for ref in (b0, b1, b2, b3)], spread_ref)
     width = x_ref.shape[1]
     copies = []
@@ -245,11 +244,14 @@
     hand_out(summed(refs[:given]), refs[given:])
 
 
-def carry_kernel(ahead_ref, *refs):
-    ins, out_ref = refs[:-1], refs[-1]
+def carry_kernel(group, routes_ref, gates_ref, ahead_ref, *refs):
+    ins, (out_ref, map_ref, column_ref) = refs[:-3], refs[-3:]
     rows = ahead_ref.shape[0]
     out_ref[:rows] = ahead_ref[...]
     out_ref[rows:] = summed(ins)
+    slots = slots_of(upright(routes_ref[...].astype(F32)))
+    map_ref[...] = block_map(slots, my_expert(group))
+    column_ref[...] = jnp.broadcast_to(upright(gates_ref[...]), column_ref.shape)
 
 
 def call(body, outs, ins, megabytes, scratch=(), flops=0, space=VMEM, out_space=VMEM):
@@ -338,10 +340,14 @@
         space=HBM,
     )
     arrived = across(blocks[:-1])
-    (carry,) = call(
-        carry_kernel,
-        [jax.ShapeDtypeStruct((ahead + tall, LANES), BF16)],
-        [travelling, *exchanged(experts(shared(blocks[-1:])))],
+    carry, second_map, second_gates = call(
+        functools.partial(carry_kernel, group),
+        [
+            jax.ShapeDtypeStruct((ahead + tall, LANES), BF16),
+            jax.ShapeDtypeStruct((rows, pad_rows(EXPERTS * CAP)), BF16),
+            jax.ShapeDtypeStruct((rows, 128), F32),
+        ],
+        [routes_2, gates_2, travelling, *exchanged(experts(shared(blocks[-1:])))],
         8,
     )
     *ins, carry = lax.optimization_barrier((*shared(arrived), carry))
@@ -353,16 +359,16 @@
     first, *blocks = call(
         functools.partial(middle_kernel, group),
         [whole] + [block] * EXPERTS,
-        [*home, carried, gain, routes_2],
+        [*home, carried, gain, second_map],
         8,
         [packing],
     )
     sums = added(exchanged(experts(shared(across(blocks[:-1]) + blocks[-1:]))))
     home = across(sums[:-1])
     (mixed,) = call(
-        functools.partial(last_kernel, group),
+        last_kernel,
         [whole],
-        [first, *home, sums[-1], routes_2, gates_2],
+        [first, *home, sums[-1], second_map, second_gates],
         8,
         [packing, pltpu.VMEM((rows, width), BF16), pltpu.SemaphoreType.DMA((PARTS,))],
         out_space=HBM,

time: 50 us -> 49.4 us (0.988)
  starting transfers between devices: 25.4 us -> 22.2 us
  waiting for transfers between devices: 14.1 us -> 16.7 us
    ppermute x9, starting transfers between devices: 14.2 us -> 12.3 us  [across(): lax.ppermute(blocks[i], 'expert', to_expert(i))]
    ppermute x3, waiting for transfers between devices: 3.36 us -> 4.81 us  [on_device(): lax.ppermute(sums[i], ('section', 'expert'), onward(i))]
    ppermute x9, waiting for transfers between devices: 7.99 us -> 9.17 us  [across(): lax.ppermute(blocks[i], 'expert', to_expert(i))]
    ppermute x3, starting transfers between devices: 6.72 us -> 5.81 us  [on_device(): lax.ppermute(sums[i], ('section', 'expert'), onward(i))]
  transfers between devices with their start and end apart: 24 -> 24, of which waited for: 13 -> 14; matrix products, arithmetic and copies ran while one was open for 0% -> 0% of each run, Pallas kernels for 4% -> 4%
where the time goes in v3:
time: 49.4 us; the launch traced here: 49.3 us
  starting transfers between devices  22.2 us (45%)
  waiting for transfers between devices  16.7 us (34%)
  Pallas kernels  10.2 us (21%)
    ppermute x9, starting transfers between devices, across(): lax.ppermute(blocks[i], 'expert', to_expert(i))  12.3 us
    pallas_call x9, Pallas kernels, call(): pl.pallas_call(body, out_shape=outs, in_specs=[space] * len(ins), out_spe...  10.2 us
    ppermute x9, waiting for transfers between devices, across(): lax.ppermute(blocks[i], 'expert', to_expert(i))  9.17 us
    ppermute x3, starting transfers between devices, on_device(): lax.ppermute(sums[i], ('section', 'expert'), onward(i))  5.81 us
    ppermute x3, waiting for transfers between devices, on_device(): lax.ppermute(sums[i], ('section', 'expert'), onward(i))  4.81 us
    ppermute x8, starting transfers between devices, shared(): lax.ppermute(a, 'expert', within(m))  1.78 us
    ppermute x8, waiting for transfers between devices, shared(): lax.ppermute(a, 'expert', within(m))  1.55 us
    ppermute x1, starting transfers between devices, on_device(): lax.ppermute(carry, 'section', [(i, (i + 1) % sections) for i in range(se...  1.49 us
  transfers between devices with their start and end apart: 24, of which 14 were waited for; matrix products, arithmetic and copies ran while one was open for 0% of the time, Pallas kernels for 4%

profile of v3, /device:TPU:0, one launch (start us, length us, event | category | flops | bytes accessed | tf_op | source)
XLA Modules:
  0.0 49.3 jit_solution(9410300588647417357)
XLA Ops:
  0.0 1.6 %shard_map.91 = (bf16[80,256]{1,0:T(8,128)(2,1)S(1)}, bf16[80,256]{1,0:T(8,128)(2,1)S(1)}, bf16[80,256]{1,0:T(8,128)(2,1)S(1)}, bf16[80,256]{1,0:T(8,128)(2,1)S(1)}, bf16[272,256]{1,0:T(8,128)(2,1)S(1)}) custom-call(bf16[16,4096]{1,0:T(8,128)(2,1)} %bitcast.20, f32[1,4096]{1,0:T(1,128)} %refs_4_.1, s32[1,16]{1,0:T(1,128)} %bitcast.21, f32[1,16]{1,0:T(1,128)} %bitcast.22), custom_call_target="tpu_custom_call" | custom-call | flops 10000000000 | bytes 450688 | tf_op jit(solution)/shard_map/pallas_call | solution.py:259
  1.6 0.5 %collective-permute-start.6 = (bf16[80,256]{1,0:T(8,128)(2,1)S(1)}, bf16[80,256]{1,0:T(8,128)(2,1)S(1)}, u32[]{:S(2)}, u32[]{:S(2)}) collective-permute-start(bf16[80,256]{1,0:T(8,128)(2,1)S(1)} %get-tuple-element.45.refs_0_), channel_id=1, source_target_pairs={{0,1},{1,0},{2,3},{3,2},{4,5},{5,4},{6,7},{7,6},{8,9},{9,8},{10,11... | collective-permute-start | bytes 122888 | tf_op jit(solution)/shard_map/ppermute | solution.py:303
  2.1 3.7 %collective-permute-start = (bf16[80,256]{1,0:T(8,128)(2,1)S(1)}, bf16[80,256]{1,0:T(8,128)(2,1)S(1)}, u32[]{:S(2)}, u32[]{:S(2)}) collective-permute-start(bf16[80,256]{1,0:T(8,128)(2,1)S(1)} %get-tuple-element.41), channel_id=1, source_target_pairs={{0,4},{1,5},{2,6},{3,7},{4,0},{5,1},{6,2},{7,3},{8,12},{9,13},{10,... | collective-permute-start | bytes 122888 | tf_op jit(solution)/shard_map/ppermute | solution.py:299
  5.8 1.3 %collective-permute-start.1 = (bf16[80,256]{1,0:T(8,128)(2,1)S(1)}, bf16[80,256]{1,0:T(8,128)(2,1)S(1)}, u32[]{:S(2)}, u32[]{:S(2)}) collective-permute-start(bf16[80,256]{1,0:T(8,128)(2,1)S(1)} %get-tuple-element.42), channel_id=1, source_target_pairs={{0,6},{1,7},{2,4},{3,5},{4,2},{5,3},{6,0},{7,1},{8,14},{9,15},{10,... | collective-permute-start | bytes 122888 | tf_op jit(solution)/shard_map/ppermute | solution.py:299
  7.4 1.8 %shard_map.92 = (bf16[80,256]{1,0:T(8,128)(2,1)S(1)}, bf16[80,256]{1,0:T(8,128)(2,1)S(1)}) custom-call(bf16[4096,512]{1,0:T(8,128)(2,1)S(1)} %bitcast.9, bf16[4096,512]{1,0:T(8,128)(2,1)S(1)} %bitcast.12, bf16[512,4096]{1,0:T(8,128)(2,1)S(1)} %bitcast.15, bf16[80,256]{1,0:T(8,128)(2,1)S(1)} %get-tuple-element.45.refs_0_, ...), custom_call_target="tpu_custom_call" | custom-call | flops 3221225472 | bytes 12746752 | tf_op jit(solution)/shard_map/pallas_call | solution.py:259
  9.4 0.5 collective-permute-start.3
  9.8 1.9 %collective-permute-done.1.refs_1_ = bf16[80,256]{1,0:T(8,128)(2,1)S(1)} collective-permute-done((bf16[80,256]{1,0:T(8,128)(2,1)S(1)}, bf16[80,256]{1,0:T(8,128)(2,1)S(1)}, u32[]{:S(2)}, u32[]{:S(2)}) %collective-permute-start.1) | collective-permute-done | bytes 40992 | tf_op jit(solution)/shard_map/ppermute | solution.py:299
  11.7 0.5 %collective-permute-start.5 = (bf16[80,256]{1,0:T(8,128)(2,1)S(1)}, bf16[80,256]{1,0:T(8,128)(2,1)S(1)}, u32[]{:S(2)}, u32[]{:S(2)}) collective-permute-start(bf16[80,256]{1,0:T(8,128)(2,1)S(1)} %collective-permute-done.2.refs_2_), channel_id=1, source_target_pairs={{0,1},{1,0},{2,3},{3,2},{4,5},{5,4},{6,7},{7,6},{8,9},{9,8},{10,11... | collective-permute-start | bytes 122888 | tf_op jit(solution)/shard_map/ppermute | solution.py:303
  12.5 0.4 collective-permute-done.4.refs_4_
  13.1 2.4 %shard_map.94 = (bf16[240,256]{1,0:T(8,128)(2,1)S(1)}, bf16[240,256]{1,0:T(8,128)(2,1)S(1)}) custom-call(bf16[4096,512]{1,0:T(8,128)(2,1)S(1)} %bitcast.10, bf16[4096,512]{1,0:T(8,128)(2,1)S(1)} %bitcast.13, bf16[512,4096]{1,0:T(8,128)(2,1)S(1)} %bitcast.16, bf16[80,256]{1,0:T(8,128)(2,1)S(1)} %collective-permute-done.refs_0_, ...), custom_call_target="tpu_custom_call" | custom-call | flops 3221225472 | bytes 13074432 | tf_op jit(solution)/shard_map/pallas_call | solution.py:259
  15.5 0.4 collective-permute-start.8
  15.9 1.5 %collective-permute-start.12 = (bf16[352,256]{1,0:T(8,128)(2,1)S(1)}, bf16[352,256]{1,0:T(8,128)(2,1)S(1)}, u32[]{:S(2)}, u32[]{:S(2)}) collective-permute-start(bf16[352,256]{1,0:T(8,128)(2,1)S(1)} %get-tuple-element.63), channel_id=1, source_target_pairs={{0,8},{8,16},{16,24},{24,0},{1,9},{9,17},{17,25},{25,1},{2,10},{10... | collective-permute-start | bytes 540680 | tf_op jit(solution)/shard_map/ppermute | solution.py:356
  17.4 2.5 %collective-permute-start.9 = (bf16[80,256]{1,0:T(8,128)(2,1)S(1)}, bf16[80,256]{1,0:T(8,128)(2,1)S(1)}, u32[]{:S(2)}, u32[]{:S(2)}) collective-permute-start(bf16[80,256]{1,0:T(8,128)(2,1)S(1)} %get-tuple-element.60), channel_id=1, source_target_pairs={{0,12},{1,13},{2,14},{3,15},{4,8},{5,9},{6,10},{7,11},{8,20},{9,21... | collective-permute-start | bytes 122888 | tf_op jit(solution)/shard_map/ppermute | solution.py:358
  19.9 1.9 %collective-permute-start.10 = (bf16[80,256]{1,0:T(8,128)(2,1)S(1)}, bf16[80,256]{1,0:T(8,128)(2,1)S(1)}, u32[]{:S(2)}, u32[]{:S(2)}) collective-permute-start(bf16[80,256]{1,0:T(8,128)(2,1)S(1)} %get-tuple-element.61), channel_id=1, source_target_pairs={{0,14},{1,15},{2,12},{3,13},{4,10},{5,11},{6,8},{7,9},{8,22},{9,23... | collective-permute-start | bytes 122888 | tf_op jit(solution)/shard_map/ppermute | solution.py:358
  21.9 1.4 %collective-permute-start.11 = (bf16[80,256]{1,0:T(8,128)(2,1)S(1)}, bf16[80,256]{1,0:T(8,128)(2,1)S(1)}, u32[]{:S(2)}, u32[]{:S(2)}) collective-permute-start(bf16[80,256]{1,0:T(8,128)(2,1)S(1)} %get-tuple-element.62), channel_id=1, source_target_pairs={{0,10},{1,11},{2,8},{3,9},{4,14},{5,15},{6,12},{7,13},{8,18},{9,19... | collective-permute-start | bytes 122888 | tf_op jit(solution)/shard_map/ppermute | solution.py:358
  23.2 1.0 %collective-permute-done.9.refs_0_ = bf16[80,256]{1,0:T(8,128)(2,1)S(1)} collective-permute-done((bf16[80,256]{1,0:T(8,128)(2,1)S(1)}, bf16[80,256]{1,0:T(8,128)(2,1)S(1)}, u32[]{:S(2)}, u32[]{:S(2)}) %collective-permute-start.9) | collective-permute-done | bytes 40992 | tf_op jit(solution)/shard_map/ppermute | solution.py:358
  24.3 3.5 %collective-permute-done.10.refs_1_ = bf16[80,256]{1,0:T(8,128)(2,1)S(1)} collective-permute-done((bf16[80,256]{1,0:T(8,128)(2,1)S(1)}, bf16[80,256]{1,0:T(8,128)(2,1)S(1)}, u32[]{:S(2)}, u32[]{:S(2)}) %collective-permute-start.10) | collective-permute-done | bytes 40992 | tf_op jit(solution)/shard_map/ppermute | solution.py:358
  28.0 0.7 %shard_map.96 = (bf16[16,4096]{1,0:T(8,128)(2,1)S(1)}, bf16[80,256]{1,0:T(8,128)(2,1)S(1)}, bf16[80,256]{1,0:T(8,128)(2,1)S(1)}, bf16[80,256]{1,0:T(8,128)(2,1)S(1)}, bf16[80,256]{1,0:T(8,128)(2,1)S(1)}) custom-call(bf16[80,256]{1,0:T(8,128)(2,1)S(1)} %collective-permute-done.9.refs_0_, bf16[80,256]{1,0:T(8,128)(2,1)S(1)} %collective-permute-done.10.refs_1_, ...), custom_call_target="tpu_custom_call" | custom-call | bytes 615424 | tf_op jit(solution)/shard_map/pallas_call | solution.py:259
  28.8 1.3 %collective-permute-start.13 = (bf16[80,256]{1,0:T(8,128)(2,1)S(1)}, bf16[80,256]{1,0:T(8,128)(2,1)S(1)}, u32[]{:S(2)}, u32[]{:S(2)}) collective-permute-start(bf16[80,256]{1,0:T(8,128)(2,1)S(1)} %get-tuple-element.66), channel_id=1, source_target_pairs={{0,4},{1,5},{2,6},{3,7},{4,0},{5,1},{6,2},{7,3},{8,12},{9,13},{10,... | collective-permute-start | bytes 122888 | tf_op jit(solution)/shard_map/ppermute | solution.py:299
  30.0 1.7 %collective-permute-start.14 = (bf16[80,256]{1,0:T(8,128)(2,1)S(1)}, bf16[80,256]{1,0:T(8,128)(2,1)S(1)}, u32[]{:S(2)}, u32[]{:S(2)}) collective-permute-start(bf16[80,256]{1,0:T(8,128)(2,1)S(1)} %get-tuple-element.67), channel_id=1, source_target_pairs={{0,6},{1,7},{2,4},{3,5},{4,2},{5,3},{6,0},{7,1},{8,14},{9,15},{10,... | collective-permute-start | bytes 122888 | tf_op jit(solution)/shard_map/ppermute | solution.py:299
  31.8 0.6 %collective-permute-start.15 = (bf16[80,256]{1,0:T(8,128)(2,1)S(1)}, bf16[80,256]{1,0:T(8,128)(2,1)S(1)}, u32[]{:S(2)}, u32[]{:S(2)}) collective-permute-start(bf16[80,256]{1,0:T(8,128)(2,1)S(1)} %get-tuple-element.68), channel_id=1, source_target_pairs={{0,2},{1,3},{2,0},{3,1},{4,6},{5,7},{6,4},{7,5},{8,10},{9,11},{10,... | collective-permute-start | bytes 122888 | tf_op jit(solution)/shard_map/ppermute | solution.py:299
  32.3 1.8 %collective-permute-done.13.refs_0_ = bf16[80,256]{1,0:T(8,128)(2,1)S(1)} collective-permute-done((bf16[80,256]{1,0:T(8,128)(2,1)S(1)}, bf16[80,256]{1,0:T(8,128)(2,1)S(1)}, u32[]{:S(2)}, u32[]{:S(2)}) %collective-permute-start.13) | collective-permute-done | bytes 40992 | tf_op jit(solution)/shard_map/ppermute | solution.py:299
  34.2 1.8 %collective-permute-done.14.refs_1_ = bf16[80,256]{1,0:T(8,128)(2,1)S(1)} collective-permute-done((bf16[80,256]{1,0:T(8,128)(2,1)S(1)}, bf16[80,256]{1,0:T(8,128)(2,1)S(1)}, u32[]{:S(2)}, u32[]{:S(2)}) %collective-permute-start.14) | collective-permute-done | bytes 40992 | tf_op jit(solution)/shard_map/ppermute | solution.py:299
  36.4 0.7 %collective-permute-done.17.refs_5_ = bf16[80,256]{1,0:T(8,128)(2,1)S(1)} collective-permute-done((bf16[80,256]{1,0:T(8,128)(2,1)S(1)}, bf16[80,256]{1,0:T(8,128)(2,1)S(1)}, u32[]{:S(2)}, u32[]{:S(2)}) %collective-permute-start.17) | collective-permute-done | bytes 40992 | tf_op jit(solution)/shard_map/ppermute | solution.py:303
  37.4 2.4 %shard_map.97 = (bf16[320,256]{1,0:T(8,128)(2,1)S(1)}, bf16[320,256]{1,0:T(8,128)(2,1)S(1)}) custom-call(bf16[4096,512]{1,0:T(8,128)(2,1)S(1)} %bitcast.11, bf16[4096,512]{1,0:T(8,128)(2,1)S(1)} %bitcast.14, bf16[512,4096]{1,0:T(8,128)(2,1)S(1)} %bitcast.17, bf16[80,256]{1,0:T(8,128)(2,1)S(1)} %collective-permute-done.13.refs_0_, ...), custom_call_target="tpu_custom_call" | custom-call | flops 3221225472 | bytes 13238272 | tf_op jit(solution)/shard_map/pallas_call | solution.py:259
  40.1 1.1 %collective-permute-done.20.refs_1_ = bf16[320,256]{1,0:T(8,128)(2,1)S(1)} collective-permute-done((bf16[320,256]{1,0:T(8,128)(2,1)S(1)}, bf16[320,256]{1,0:T(8,128)(2,1)S(1)}, u32[]{:S(2)}, u32[]{:S(2)}) %collective-permute-start.20) | collective-permute-done | bytes 163872 | tf_op jit(solution)/shard_map/ppermute | solution.py:319
  41.3 1.2 %collective-permute-start.21 = (bf16[80,256]{1,0:T(8,128)(2,1)S(1)}, bf16[80,256]{1,0:T(8,128)(2,1)S(1)}, u32[]{:S(2)}, u32[]{:S(2)}) collective-permute-start(bf16[80,256]{1,0:T(8,128)(2,1)S(1)} %get-tuple-element.72), channel_id=1, source_target_pairs={{0,4},{1,5},{2,6},{3,7},{4,0},{5,1},{6,2},{7,3},{8,12},{9,13},{10,... | collective-permute-start | bytes 122888 | tf_op jit(solution)/shard_map/ppermute | solution.py:299
  42.5 1.4 %collective-permute-start.22 = (bf16[80,256]{1,0:T(8,128)(2,1)S(1)}, bf16[80,256]{1,0:T(8,128)(2,1)S(1)}, u32[]{:S(2)}, u32[]{:S(2)}) collective-permute-start(bf16[80,256]{1,0:T(8,128)(2,1)S(1)} %get-tuple-element.73), channel_id=1, source_target_pairs={{0,6},{1,7},{2,4},{3,5},{4,2},{5,3},{6,0},{7,1},{8,14},{9,15},{10,... | collective-permute-start | bytes 122888 | tf_op jit(solution)/shard_map/ppermute | solution.py:299
  43.9 1.0 %collective-permute-start.23 = (bf16[80,256]{1,0:T(8,128)(2,1)S(1)}, bf16[80,256]{1,0:T(8,128)(2,1)S(1)}, u32[]{:S(2)}, u32[]{:S(2)}) collective-permute-start(bf16[80,256]{1,0:T(8,128)(2,1)S(1)} %get-tuple-element.74), channel_id=1, source_target_pairs={{0,2},{1,3},{2,0},{3,1},{4,6},{5,7},{6,4},{7,5},{8,10},{9,11},{10,... | collective-permute-start | bytes 122888 | tf_op jit(solution)/shard_map/ppermute | solution.py:299
  44.9 1.9 %collective-permute-done.21.b0 = bf16[80,256]{1,0:T(8,128)(2,1)S(1)} collective-permute-done((bf16[80,256]{1,0:T(8,128)(2,1)S(1)}, bf16[80,256]{1,0:T(8,128)(2,1)S(1)}, u32[]{:S(2)}, u32[]{:S(2)}) %collective-permute-start.21) | collective-permute-done | bytes 40992 | tf_op jit(solution)/shard_map/ppermute | solution.py:299
  46.8 1.5 %collective-permute-done.22.b1 = bf16[80,256]{1,0:T(8,128)(2,1)S(1)} collective-permute-done((bf16[80,256]{1,0:T(8,128)(2,1)S(1)}, bf16[80,256]{1,0:T(8,128)(2,1)S(1)}, u32[]{:S(2)}, u32[]{:S(2)}) %collective-permute-start.22) | collective-permute-done | bytes 40992 | tf_op jit(solution)/shard_map/ppermute | solution.py:299
  48.3 1.0 %shard_map.99 = bf16[16,4096]{1,0:T(8,128)(2,1)} custom-call(bf16[16,4096]{1,0:T(8,128)(2,1)S(1)} %get-tuple-element.65.x_ref, bf16[80,256]{1,0:T(8,128)(2,1)S(1)} %collective-permute-done.21.b0, bf16[80,256]{1,0:T(8,128)(2,1)S(1)} %collective-permute-done.22.b1, bf16[80,256]{1,0:T(8,128)(2,1)S(1)} %collective-permute-done.23.b2, ...), custom_call_target="tpu_custom_call" | custom-call | bytes 435200 | tf_op jit(solution)/shard_map/pallas_call | solution.py:259
  (37 shorter events, 2.3 us)
Async XLA Ops:
  0.0 7.4 %copy-start = (bf16[1,1,4096,512]{3,2,1,0:T(8,128)(2,1)S(1)}, bf16[1,1,4096,512]{3,2,1,0:T(8,128)(2,1)}, u32[]{:S(2)}) copy-start(bf16[1,1,4096,512]{3,2,1,0:T(8,128)(2,1)} %param.15) | copy-start | bytes 12582916
  0.0 7.4 %copy-start.1 = (bf16[1,1,4096,512]{3,2,1,0:T(8,128)(2,1)S(1)}, bf16[1,1,4096,512]{3,2,1,0:T(8,128)(2,1)}, u32[]{:S(2)}) copy-start(bf16[1,1,4096,512]{3,2,1,0:T(8,128)(2,1)} %param.16) | copy-start | bytes 12582916
  0.0 7.4 %copy-start.2 = (bf16[1,1,512,4096]{3,2,1,0:T(8,128)(2,1)S(1)}, bf16[1,1,512,4096]{3,2,1,0:T(8,128)(2,1)}, u32[]{:S(2)}) copy-start(bf16[1,1,512,4096]{3,2,1,0:T(8,128)(2,1)} %param.17) | copy-start | bytes 12582916
  1.6 5.8 %collective-permute-start.6 = (bf16[80,256]{1,0:T(8,128)(2,1)S(1)}, bf16[80,256]{1,0:T(8,128)(2,1)S(1)}, u32[]{:S(2)}, u32[]{:S(2)}) collective-permute-start(bf16[80,256]{1,0:T(8,128)(2,1)S(1)} %get-tuple-element.45.refs_0_), channel_id=1, source_target_pairs={{0,1},{1,0},{2,3},{3,2},{4,5},{5,4},{6,7},{7,6},{8,9},{9,8},{10,11... | collective-permute-start | bytes 122888 | tf_op jit(solution)/shard_map/ppermute | solution.py:303
  2.1 7.2 %collective-permute-start = (bf16[80,256]{1,0:T(8,128)(2,1)S(1)}, bf16[80,256]{1,0:T(8,128)(2,1)S(1)}, u32[]{:S(2)}, u32[]{:S(2)}) collective-permute-start(bf16[80,256]{1,0:T(8,128)(2,1)S(1)} %get-tuple-element.41), channel_id=1, source_target_pairs={{0,4},{1,5},{2,6},{3,7},{4,0},{5,1},{6,2},{7,3},{8,12},{9,13},{10,... | collective-permute-start | bytes 122888 | tf_op jit(solution)/shard_map/ppermute | solution.py:299
  5.8 5.9 %collective-permute-start.1 = (bf16[80,256]{1,0:T(8,128)(2,1)S(1)}, bf16[80,256]{1,0:T(8,128)(2,1)S(1)}, u32[]{:S(2)}, u32[]{:S(2)}) collective-permute-start(bf16[80,256]{1,0:T(8,128)(2,1)S(1)} %get-tuple-element.42), channel_id=1, source_target_pairs={{0,6},{1,7},{2,4},{3,5},{4,2},{5,3},{6,0},{7,1},{8,14},{9,15},{10,... | collective-permute-start | bytes 122888 | tf_op jit(solution)/shard_map/ppermute | solution.py:299
  7.1 4.6 %collective-permute-start.2 = (bf16[80,256]{1,0:T(8,128)(2,1)S(1)}, bf16[80,256]{1,0:T(8,128)(2,1)S(1)}, u32[]{:S(2)}, u32[]{:S(2)}) collective-permute-start(bf16[80,256]{1,0:T(8,128)(2,1)S(1)} %get-tuple-element.43), channel_id=1, source_target_pairs={{0,2},{1,3},{2,0},{3,1},{4,6},{5,7},{6,4},{7,5},{8,10},{9,11},{10,... | collective-permute-start | bytes 122888 | tf_op jit(solution)/shard_map/ppermute | solution.py:299
  7.4 4.8 %copy-start.4 = (s32[1,16,1]{1,2,0:T(1,128)S(1)}, s32[1,16,1]{1,2,0:T(1,128)}, u32[]{:S(2)}) copy-start(s32[1,16,1]{1,2,0:T(1,128)} %param.13) | copy-start | bytes 196
  7.4 4.8 %copy-start.5 = (f32[1,16,1]{1,2,0:T(1,128)S(1)}, f32[1,16,1]{1,2,0:T(1,128)}, u32[]{:S(2)}) copy-start(f32[1,16,1]{1,2,0:T(1,128)} %param.14) | copy-start | bytes 196
  9.3 3.0 %collective-permute-start.7 = (bf16[80,256]{1,0:T(8,128)(2,1)S(1)}, bf16[80,256]{1,0:T(8,128)(2,1)S(1)}, u32[]{:S(2)}, u32[]{:S(2)}) collective-permute-start(bf16[80,256]{1,0:T(8,128)(2,1)S(1)} %get-tuple-element.47), channel_id=1, source_target_pairs={{0,1},{1,0},{2,3},{3,2},{4,5},{5,4},{6,7},{7,6},{8,9},{9,8},{10,11... | collective-permute-start | bytes 122888 | tf_op jit(solution)/shard_map/ppermute | solution.py:319
  9.4 3.2 %collective-permute-start.3 = (bf16[80,256]{1,0:T(8,128)(2,1)S(1)}, bf16[80,256]{1,0:T(8,128)(2,1)S(1)}, u32[]{:S(2)}, u32[]{:S(2)}) collective-permute-start(bf16[80,256]{1,0:T(8,128)(2,1)S(1)} %collective-permute-done.refs_0_), channel_id=1, source_target_pairs={{0,1},{1,0},{2,3},{3,2},{4,5},{5,4},{6,7},{7,6},{8,9},{9,8},{10,11... | collective-permute-start | bytes 122888 | tf_op jit(solution)/shard_map/ppermute | solution.py:303
  11.7 1.2 %collective-permute-start.4 = (bf16[80,256]{1,0:T(8,128)(2,1)S(1)}, bf16[80,256]{1,0:T(8,128)(2,1)S(1)}, u32[]{:S(2)}, u32[]{:S(2)}) collective-permute-start(bf16[80,256]{1,0:T(8,128)(2,1)S(1)} %collective-permute-done.1.refs_1_), channel_id=1, source_target_pairs={{0,1},{1,0},{2,3},{3,2},{4,5},{5,4},{6,7},{7,6},{8,9},{9,8},{10,11... | collective-permute-start | bytes 122888 | tf_op jit(solution)/shard_map/ppermute | solution.py:303
  11.7 1.4 %collective-permute-start.5 = (bf16[80,256]{1,0:T(8,128)(2,1)S(1)}, bf16[80,256]{1,0:T(8,128)(2,1)S(1)}, u32[]{:S(2)}, u32[]{:S(2)}) collective-permute-start(bf16[80,256]{1,0:T(8,128)(2,1)S(1)} %collective-permute-done.2.refs_2_), channel_id=1, source_target_pairs={{0,1},{1,0},{2,3},{3,2},{4,5},{5,4},{6,7},{7,6},{8,9},{9,8},{10,11... | collective-permute-start | bytes 122888 | tf_op jit(solution)/shard_map/ppermute | solution.py:303
  13.1 15.0 %copy-start.3 = (f32[1,4096]{1,0:T(1,128)S(1)}, f32[1,4096]{1,0:T(1,128)}, u32[]{:S(2)}) copy-start(f32[1,4096]{1,0:T(1,128)} %refs_4_.1) | copy-start | bytes 49156
  15.5 1.9 %collective-permute-start.8 = (bf16[240,256]{1,0:T(8,128)(2,1)S(1)}, bf16[240,256]{1,0:T(8,128)(2,1)S(1)}, u32[]{:S(2)}, u32[]{:S(2)}) collective-permute-start(bf16[240,256]{1,0:T(8,128)(2,1)S(1)} %get-tuple-element.59), channel_id=1, source_target_pairs={{0,1},{1,0},{2,3},{3,2},{4,5},{5,4},{6,7},{7,6},{8,9},{9,8},{10,11... | collective-permute-start | bytes 368648 | tf_op jit(solution)/shard_map/ppermute | solution.py:319
  15.9 12.2 %collective-permute-start.12 = (bf16[352,256]{1,0:T(8,128)(2,1)S(1)}, bf16[352,256]{1,0:T(8,128)(2,1)S(1)}, u32[]{:S(2)}, u32[]{:S(2)}) collective-permute-start(bf16[352,256]{1,0:T(8,128)(2,1)S(1)} %get-tuple-element.63), channel_id=1, source_target_pairs={{0,8},{8,16},{16,24},{24,0},{1,9},{9,17},{17,25},{25,1},{2,10},{10... | collective-permute-start | bytes 540680 | tf_op jit(solution)/shard_map/ppermute | solution.py:356
  17.4 6.9 %collective-permute-start.9 = (bf16[80,256]{1,0:T(8,128)(2,1)S(1)}, bf16[80,256]{1,0:T(8,128)(2,1)S(1)}, u32[]{:S(2)}, u32[]{:S(2)}) collective-permute-start(bf16[80,256]{1,0:T(8,128)(2,1)S(1)} %get-tuple-element.60), channel_id=1, source_target_pairs={{0,12},{1,13},{2,14},{3,15},{4,8},{5,9},{6,10},{7,11},{8,20},{9,21... | collective-permute-start | bytes 122888 | tf_op jit(solution)/shard_map/ppermute | solution.py:358
  19.9 7.8 %collective-permute-start.10 = (bf16[80,256]{1,0:T(8,128)(2,1)S(1)}, bf16[80,256]{1,0:T(8,128)(2,1)S(1)}, u32[]{:S(2)}, u32[]{:S(2)}) collective-permute-start(bf16[80,256]{1,0:T(8,128)(2,1)S(1)} %get-tuple-element.61), channel_id=1, source_target_pairs={{0,14},{1,15},{2,12},{3,13},{4,10},{5,11},{6,8},{7,9},{8,22},{9,23... | collective-permute-start | bytes 122888 | tf_op jit(solution)/shard_map/ppermute | solution.py:358
  21.9 6.2 %collective-permute-start.11 = (bf16[80,256]{1,0:T(8,128)(2,1)S(1)}, bf16[80,256]{1,0:T(8,128)(2,1)S(1)}, u32[]{:S(2)}, u32[]{:S(2)}) collective-permute-start(bf16[80,256]{1,0:T(8,128)(2,1)S(1)} %get-tuple-element.62), channel_id=1, source_target_pairs={{0,10},{1,11},{2,8},{3,9},{4,14},{5,15},{6,12},{7,13},{8,18},{9,19... | collective-permute-start | bytes 122888 | tf_op jit(solution)/shard_map/ppermute | solution.py:358
  28.8 5.4 %collective-permute-start.13 = (bf16[80,256]{1,0:T(8,128)(2,1)S(1)}, bf16[80,256]{1,0:T(8,128)(2,1)S(1)}, u32[]{:S(2)}, u32[]{:S(2)}) collective-permute-start(bf16[80,256]{1,0:T(8,128)(2,1)S(1)} %get-tuple-element.66), channel_id=1, source_target_pairs={{0,4},{1,5},{2,6},{3,7},{4,0},{5,1},{6,2},{7,3},{8,12},{9,13},{10,... | collective-permute-start | bytes 122888 | tf_op jit(solution)/shard_map/ppermute | solution.py:299
  30.0 5.9 %collective-permute-start.14 = (bf16[80,256]{1,0:T(8,128)(2,1)S(1)}, bf16[80,256]{1,0:T(8,128)(2,1)S(1)}, u32[]{:S(2)}, u32[]{:S(2)}) collective-permute-start(bf16[80,256]{1,0:T(8,128)(2,1)S(1)} %get-tuple-element.67), channel_id=1, source_target_pairs={{0,6},{1,7},{2,4},{3,5},{4,2},{5,3},{6,0},{7,1},{8,14},{9,15},{10,... | collective-permute-start | bytes 122888 | tf_op jit(solution)/shard_map/ppermute | solution.py:299
  31.8 4.4 %collective-permute-start.15 = (bf16[80,256]{1,0:T(8,128)(2,1)S(1)}, bf16[80,256]{1,0:T(8,128)(2,1)S(1)}, u32[]{:S(2)}, u32[]{:S(2)}) collective-permute-start(bf16[80,256]{1,0:T(8,128)(2,1)S(1)} %get-tuple-element.68), channel_id=1, source_target_pairs={{0,2},{1,3},{2,0},{3,1},{4,6},{5,7},{6,4},{7,5},{8,10},{9,11},{10,... | collective-permute-start | bytes 122888 | tf_op jit(solution)/shard_map/ppermute | solution.py:299
  32.3 4.1 %collective-permute-start.19 = (bf16[80,256]{1,0:T(8,128)(2,1)S(1)}, bf16[80,256]{1,0:T(8,128)(2,1)S(1)}, u32[]{:S(2)}, u32[]{:S(2)}) collective-permute-start(bf16[80,256]{1,0:T(8,128)(2,1)S(1)} %get-tuple-element.69.refs_3_), channel_id=1, source_target_pairs={{0,1},{1,0},{2,3},{3,2},{4,5},{5,4},{6,7},{7,6},{8,9},{9,8},{10,11... | collective-permute-start | bytes 122888 | tf_op jit(solution)/shard_map/ppermute | solution.py:303
  34.2 2.3 %collective-permute-start.16 = (bf16[80,256]{1,0:T(8,128)(2,1)S(1)}, bf16[80,256]{1,0:T(8,128)(2,1)S(1)}, u32[]{:S(2)}, u32[]{:S(2)}) collective-permute-start(bf16[80,256]{1,0:T(8,128)(2,1)S(1)} %collective-permute-done.13.refs_0_), channel_id=1, source_target_pairs={{0,1},{1,0},{2,3},{3,2},{4,5},{5,4},{6,7},{7,6},{8,9},{9,8},{10,11... | collective-permute-start | bytes 122888 | tf_op jit(solution)/shard_map/ppermute | solution.py:303
  35.9 1.2 %collective-permute-start.17 = (bf16[80,256]{1,0:T(8,128)(2,1)S(1)}, bf16[80,256]{1,0:T(8,128)(2,1)S(1)}, u32[]{:S(2)}, u32[]{:S(2)}) collective-permute-start(bf16[80,256]{1,0:T(8,128)(2,1)S(1)} %collective-permute-done.14.refs_1_), channel_id=1, source_target_pairs={{0,1},{1,0},{2,3},{3,2},{4,5},{5,4},{6,7},{7,6},{8,9},{9,8},{10,11... | collective-permute-start | bytes 122888 | tf_op jit(solution)/shard_map/ppermute | solution.py:303
  36.2 1.2 %collective-permute-start.18 = (bf16[80,256]{1,0:T(8,128)(2,1)S(1)}, bf16[80,256]{1,0:T(8,128)(2,1)S(1)}, u32[]{:S(2)}, u32[]{:S(2)}) collective-permute-start(bf16[80,256]{1,0:T(8,128)(2,1)S(1)} %collective-permute-done.15.refs_2_), channel_id=1, source_target_pairs={{0,1},{1,0},{2,3},{3,2},{4,5},{5,4},{6,7},{7,6},{8,9},{9,8},{10,11... | collective-permute-start | bytes 122888 | tf_op jit(solution)/shard_map/ppermute | solution.py:303
  39.8 1.5 %collective-permute-start.20 = (bf16[320,256]{1,0:T(8,128)(2,1)S(1)}, bf16[320,256]{1,0:T(8,128)(2,1)S(1)}, u32[]{:S(2)}, u32[]{:S(2)}) collective-permute-start(bf16[320,256]{1,0:T(8,128)(2,1)S(1)} %get-tuple-element.71), channel_id=1, source_target_pairs={{0,1},{1,0},{2,3},{3,2},{4,5},{5,4},{6,7},{7,6},{8,9},{9,8},{10,11... | collective-permute-start | bytes 491528 | tf_op jit(solution)/shard_map/ppermute | solution.py:319
  41.3 5.5 %collective-permute-start.21 = (bf16[80,256]{1,0:T(8,128)(2,1)S(1)}, bf16[80,256]{1,0:T(8,128)(2,1)S(1)}, u32[]{:S(2)}, u32[]{:S(2)}) collective-permute-start(bf16[80,256]{1,0:T(8,128)(2,1)S(1)} %get-tuple-element.72), channel_id=1, source_target_pairs={{0,4},{1,5},{2,6},{3,7},{4,0},{5,1},{6,2},{7,3},{8,12},{9,13},{10,... | collective-permute-start | bytes 122888 | tf_op jit(solution)/shard_map/ppermute | solution.py:299
  42.5 5.8 %collective-permute-start.22 = (bf16[80,256]{1,0:T(8,128)(2,1)S(1)}, bf16[80,256]{1,0:T(8,128)(2,1)S(1)}, u32[]{:S(2)}, u32[]{:S(2)}) collective-permute-start(bf16[80,256]{1,0:T(8,128)(2,1)S(1)} %get-tuple-element.73), channel_id=1, source_target_pairs={{0,6},{1,7},{2,4},{3,5},{4,2},{5,3},{6,0},{7,1},{8,14},{9,15},{10,... | collective-permute-start | bytes 122888 | tf_op jit(solution)/shard_map/ppermute | solution.py:299
  43.9 4.4 %collective-permute-start.23 = (bf16[80,256]{1,0:T(8,128)(2,1)S(1)}, bf16[80,256]{1,0:T(8,128)(2,1)S(1)}, u32[]{:S(2)}, u32[]{:S(2)}) collective-permute-start(bf16[80,256]{1,0:T(8,128)(2,1)S(1)} %get-tuple-element.74), channel_id=1, source_target_pairs={{0,2},{1,3},{2,0},{3,1},{4,6},{5,7},{6,4},{7,5},{8,10},{9,11},{10,... | collective-permute-start | bytes 122888 | tf_op jit(solution)/shard_map/ppermute | solution.py:299

commit v4 on v3

--- a/solution.py
+++ b/solution.py
@@ -295,8 +295,12 @@
             for i, j in to_expert(place)
         ]
 
-    def across(blocks):
-        return [lax.ppermute(blocks[i], "expert", to_expert(i)) for i in range(EXPERTS - 1)]
+    def across(blocks, order=(0, 1, 2)):
+        sent = {i: lax.ppermute(blocks[i], "expert", to_expert(i)) for i in order}
+        return [sent[i] for i in range(EXPERTS - 1)]
+
+    def swapped(parts):
+        return [parts[0], parts[2], parts[1], *parts[3:]]
 
     def shared(arrived):
         return arrived + [
@@ -339,7 +343,7 @@
         flops=10**10,
         space=HBM,
     )
-    arrived = across(blocks[:-1])
+    arrived = swapped(across(blocks, (0, 2, 1)))
     carry, second_map, second_gates = call(
         functools.partial(carry_kernel, group),
         [
@@ -354,7 +358,7 @@
     *sums, carry = lax.optimization_barrier((*experts(ins), carry))
     terms = exchanged(sums)
     carried = lax.ppermute(carry, "section", [(i, (i + 1) % sections) for i in range(sections)])
-    sums = added(terms)
+    sums = swapped(added(terms))
     home = [lax.ppermute(sums[i], ("section", "expert"), onward(i)) for i in range(EXPERTS - 1)]
     first, *blocks = call(
         functools.partial(middle_kernel, group),
@@ -363,8 +367,9 @@
         8,
         [packing],
     )
-    sums = added(exchanged(experts(shared(across(blocks[:-1]) + blocks[-1:]))))
-    home = across(sums[:-1])
+    ins = shared(swapped(across(blocks, (0, 2, 1)) + blocks[-1:]))
+    sums = swapped(added(exchanged(experts(ins))))
+    home = across(sums)
     (mixed,) = call(
         last_kernel,
         [whole],

time: 49.4 us -> 49.9 us (1.010)
    ppermute x3, waiting for transfers between devices: 4.81 us -> 3.12 us  [on_device(): lax.ppermute(sums[i], ('section', 'expert'), onward(i))]
    ppermute x9, waiting for transfers between devices: 9.17 us -> 10.4 us  [across(): sent = {i: lax.ppermute(blocks[i], 'expert', to_expert(i)) for i in order}]
    ppermute x9, starting transfers between devices: 12.3 us -> 13.3 us  [across(): sent = {i: lax.ppermute(blocks[i], 'expert', to_expert(i)) for i in order}]
    ppermute x8, starting transfers between devices: 1.78 us -> 1.16 us  [shared(): lax.ppermute(a, 'expert', within(m))]
    ppermute x8, waiting for transfers between devices: 1.55 us -> 2.12 us  [shared(): lax.ppermute(a, 'expert', within(m))]
  transfers between devices with their start and end apart: 24 -> 24, of which waited for: 14 -> 13; matrix products, arithmetic and copies ran while one was open for 0% -> 0% of each run, Pallas kernels for 4% -> 4%
where the time goes in v4:
time: 49.9 us; the launch traced here: 49.7 us
  starting transfers between devices  22.5 us (45%)
  waiting for transfers between devices  16.9 us (34%)
  Pallas kernels  10.2 us (20%)
    ppermute x9, starting transfers between devices, across(): sent = {i: lax.ppermute(blocks[i], 'expert', to_expert(i)) for i in order}  13.3 us
    ppermute x9, waiting for transfers between devices, across(): sent = {i: lax.ppermute(blocks[i], 'expert', to_expert(i)) for i in order}  10.4 us
    pallas_call x9, Pallas kernels, call(): pl.pallas_call(body, out_shape=outs, in_specs=[space] * len(ins), out_spe...  10.2 us
    ppermute x3, starting transfers between devices, on_device(): lax.ppermute(sums[i], ('section', 'expert'), onward(i))  6 us
    ppermute x3, waiting for transfers between devices, on_device(): lax.ppermute(sums[i], ('section', 'expert'), onward(i))  3.12 us
    ppermute x8, waiting for transfers between devices, shared(): lax.ppermute(a, 'expert', within(m))  2.12 us
    ppermute x1, starting transfers between devices, on_device(): lax.ppermute(carry, 'section', [(i, (i + 1) % sections) for i in range(se...  1.49 us
    ppermute x3, waiting for transfers between devices, exchanged(): lax.ppermute(sums[m], 'expert', within(-m))  1.24 us
  transfers between devices with their start and end apart: 24, of which 13 were waited for; matrix products, arithmetic and copies ran while one was open for 0% of the time, Pallas kernels for 4%

profile of v4, /device:TPU:0, one launch (start us, length us, event | category | flops | bytes accessed | tf_op | source)
XLA Modules:
  0.0 49.7 jit_solution(5133775399626841330)
XLA Ops:
  0.0 1.6 %shard_map.91 = (bf16[80,256]{1,0:T(8,128)(2,1)S(1)}, bf16[80,256]{1,0:T(8,128)(2,1)S(1)}, bf16[80,256]{1,0:T(8,128)(2,1)S(1)}, bf16[80,256]{1,0:T(8,128)(2,1)S(1)}, bf16[272,256]{1,0:T(8,128)(2,1)S(1)}) custom-call(bf16[16,4096]{1,0:T(8,128)(2,1)} %bitcast.20, f32[1,4096]{1,0:T(1,128)} %refs_4_.1, s32[1,16]{1,0:T(1,128)} %bitcast.21, f32[1,16]{1,0:T(1,128)} %bitcast.22), custom_call_target="tpu_custom_call" | custom-call | flops 10000000000 | bytes 450688 | tf_op jit(solution)/shard_map/pallas_call | solution.py:259
  1.6 0.5 %collective-permute-start.6 = (bf16[80,256]{1,0:T(8,128)(2,1)S(1)}, bf16[80,256]{1,0:T(8,128)(2,1)S(1)}, u32[]{:S(2)}, u32[]{:S(2)}) collective-permute-start(bf16[80,256]{1,0:T(8,128)(2,1)S(1)} %get-tuple-element.45.refs_0_), channel_id=1, source_target_pairs={{0,1},{1,0},{2,3},{3,2},{4,5},{5,4},{6,7},{7,6},{8,9},{9,8},{10,11... | collective-permute-start | bytes 122888 | tf_op jit(solution)/shard_map/ppermute | solution.py:307
  2.1 3.7 %collective-permute-start = (bf16[80,256]{1,0:T(8,128)(2,1)S(1)}, bf16[80,256]{1,0:T(8,128)(2,1)S(1)}, u32[]{:S(2)}, u32[]{:S(2)}) collective-permute-start(bf16[80,256]{1,0:T(8,128)(2,1)S(1)} %get-tuple-element.41), channel_id=1, source_target_pairs={{0,4},{1,5},{2,6},{3,7},{4,0},{5,1},{6,2},{7,3},{8,12},{9,13},{10,... | collective-permute-start | bytes 122888 | tf_op jit(solution)/shard_map/ppermute | solution.py:299
  5.8 1.6 %collective-permute-start.1 = (bf16[80,256]{1,0:T(8,128)(2,1)S(1)}, bf16[80,256]{1,0:T(8,128)(2,1)S(1)}, u32[]{:S(2)}, u32[]{:S(2)}) collective-permute-start(bf16[80,256]{1,0:T(8,128)(2,1)S(1)} %get-tuple-element.42), channel_id=1, source_target_pairs={{0,2},{1,3},{2,0},{3,1},{4,6},{5,7},{6,4},{7,5},{8,10},{9,11},{10,... | collective-permute-start | bytes 122888 | tf_op jit(solution)/shard_map/ppermute | solution.py:299
  7.4 1.8 %shard_map.92 = (bf16[80,256]{1,0:T(8,128)(2,1)S(1)}, bf16[80,256]{1,0:T(8,128)(2,1)S(1)}) custom-call(bf16[4096,512]{1,0:T(8,128)(2,1)S(1)} %bitcast.9, bf16[4096,512]{1,0:T(8,128)(2,1)S(1)} %bitcast.12, bf16[512,4096]{1,0:T(8,128)(2,1)S(1)} %bitcast.15, bf16[80,256]{1,0:T(8,128)(2,1)S(1)} %get-tuple-element.45.refs_0_, ...), custom_call_target="tpu_custom_call" | custom-call | flops 3221225472 | bytes 12746752 | tf_op jit(solution)/shard_map/pallas_call | solution.py:259
  9.4 0.5 collective-permute-start.3
  9.9 3.2 %collective-permute-done.2.refs_2_ = bf16[80,256]{1,0:T(8,128)(2,1)S(1)} collective-permute-done((bf16[80,256]{1,0:T(8,128)(2,1)S(1)}, bf16[80,256]{1,0:T(8,128)(2,1)S(1)}, u32[]{:S(2)}, u32[]{:S(2)}) %collective-permute-start.2) | collective-permute-done | bytes 40992 | tf_op jit(solution)/shard_map/ppermute | solution.py:299
  13.2 0.3 shard_map.93
  13.5 0.9 %collective-permute-done.5.refs_5_ = bf16[80,256]{1,0:T(8,128)(2,1)S(1)} collective-permute-done((bf16[80,256]{1,0:T(8,128)(2,1)S(1)}, bf16[80,256]{1,0:T(8,128)(2,1)S(1)}, u32[]{:S(2)}, u32[]{:S(2)}) %collective-permute-start.5) | collective-permute-done | bytes 40992 | tf_op jit(solution)/shard_map/ppermute | solution.py:307
  14.4 2.4 %shard_map.94 = (bf16[240,256]{1,0:T(8,128)(2,1)S(1)}, bf16[240,256]{1,0:T(8,128)(2,1)S(1)}) custom-call(bf16[4096,512]{1,0:T(8,128)(2,1)S(1)} %bitcast.10, bf16[4096,512]{1,0:T(8,128)(2,1)S(1)} %bitcast.13, bf16[512,4096]{1,0:T(8,128)(2,1)S(1)} %bitcast.16, bf16[80,256]{1,0:T(8,128)(2,1)S(1)} %collective-permute-done.refs_0_, ...), custom_call_target="tpu_custom_call" | custom-call | flops 3221225472 | bytes 13074432 | tf_op jit(solution)/shard_map/pallas_call | solution.py:259
  17.0 1.5 %collective-permute-start.12 = (bf16[352,256]{1,0:T(8,128)(2,1)S(1)}, bf16[352,256]{1,0:T(8,128)(2,1)S(1)}, u32[]{:S(2)}, u32[]{:S(2)}) collective-permute-start(bf16[352,256]{1,0:T(8,128)(2,1)S(1)} %get-tuple-element.63), channel_id=1, source_target_pairs={{0,8},{8,16},{16,24},{24,0},{1,9},{9,17},{17,25},{25,1},{2,10},{10... | collective-permute-start | bytes 540680 | tf_op jit(solution)/shard_map/ppermute | solution.py:360
  18.5 1.0 %collective-permute-start.9 = (bf16[80,256]{1,0:T(8,128)(2,1)S(1)}, bf16[80,256]{1,0:T(8,128)(2,1)S(1)}, u32[]{:S(2)}, u32[]{:S(2)}) collective-permute-start(bf16[80,256]{1,0:T(8,128)(2,1)S(1)} %get-tuple-element.60), channel_id=1, source_target_pairs={{0,12},{1,13},{2,14},{3,15},{4,8},{5,9},{6,10},{7,11},{8,20},{9,21... | collective-permute-start | bytes 122888 | tf_op jit(solution)/shard_map/ppermute | solution.py:362
  19.6 1.9 %collective-permute-start.10 = (bf16[80,256]{1,0:T(8,128)(2,1)S(1)}, bf16[80,256]{1,0:T(8,128)(2,1)S(1)}, u32[]{:S(2)}, u32[]{:S(2)}) collective-permute-start(bf16[80,256]{1,0:T(8,128)(2,1)S(1)} %get-tuple-element.61), channel_id=1, source_target_pairs={{0,14},{1,15},{2,12},{3,13},{4,10},{5,11},{6,8},{7,9},{8,22},{9,23... | collective-permute-start | bytes 122888 | tf_op jit(solution)/shard_map/ppermute | solution.py:362
  21.5 3.1 %collective-permute-start.11 = (bf16[80,256]{1,0:T(8,128)(2,1)S(1)}, bf16[80,256]{1,0:T(8,128)(2,1)S(1)}, u32[]{:S(2)}, u32[]{:S(2)}) collective-permute-start(bf16[80,256]{1,0:T(8,128)(2,1)S(1)} %get-tuple-element.62), channel_id=1, source_target_pairs={{0,10},{1,11},{2,8},{3,9},{4,14},{5,15},{6,12},{7,13},{8,18},{9,19... | collective-permute-start | bytes 122888 | tf_op jit(solution)/shard_map/ppermute | solution.py:362
  24.5 0.8 %collective-permute-done.9.refs_0_ = bf16[80,256]{1,0:T(8,128)(2,1)S(1)} collective-permute-done((bf16[80,256]{1,0:T(8,128)(2,1)S(1)}, bf16[80,256]{1,0:T(8,128)(2,1)S(1)}, u32[]{:S(2)}, u32[]{:S(2)}) %collective-permute-start.9) | collective-permute-done | bytes 40992 | tf_op jit(solution)/shard_map/ppermute | solution.py:362
  25.3 2.2 %collective-permute-done.10.refs_1_ = bf16[80,256]{1,0:T(8,128)(2,1)S(1)} collective-permute-done((bf16[80,256]{1,0:T(8,128)(2,1)S(1)}, bf16[80,256]{1,0:T(8,128)(2,1)S(1)}, u32[]{:S(2)}, u32[]{:S(2)}) %collective-permute-start.10) | collective-permute-done | bytes 40992 | tf_op jit(solution)/shard_map/ppermute | solution.py:362
  27.7 0.7 %shard_map.96 = (bf16[16,4096]{1,0:T(8,128)(2,1)S(1)}, bf16[80,256]{1,0:T(8,128)(2,1)S(1)}, bf16[80,256]{1,0:T(8,128)(2,1)S(1)}, bf16[80,256]{1,0:T(8,128)(2,1)S(1)}, bf16[80,256]{1,0:T(8,128)(2,1)S(1)}) custom-call(bf16[80,256]{1,0:T(8,128)(2,1)S(1)} %collective-permute-done.9.refs_0_, bf16[80,256]{1,0:T(8,128)(2,1)S(1)} %collective-permute-done.10.refs_1_, ...), custom_call_target="tpu_custom_call" | custom-call | bytes 615424 | tf_op jit(solution)/shard_map/pallas_call | solution.py:259
  28.4 1.5 %collective-permute-start.13 = (bf16[80,256]{1,0:T(8,128)(2,1)S(1)}, bf16[80,256]{1,0:T(8,128)(2,1)S(1)}, u32[]{:S(2)}, u32[]{:S(2)}) collective-permute-start(bf16[80,256]{1,0:T(8,128)(2,1)S(1)} %get-tuple-element.66), channel_id=1, source_target_pairs={{0,4},{1,5},{2,6},{3,7},{4,0},{5,1},{6,2},{7,3},{8,12},{9,13},{10,... | collective-permute-start | bytes 122888 | tf_op jit(solution)/shard_map/ppermute | solution.py:299
  29.9 1.6 %collective-permute-start.14 = (bf16[80,256]{1,0:T(8,128)(2,1)S(1)}, bf16[80,256]{1,0:T(8,128)(2,1)S(1)}, u32[]{:S(2)}, u32[]{:S(2)}) collective-permute-start(bf16[80,256]{1,0:T(8,128)(2,1)S(1)} %get-tuple-element.67), channel_id=1, source_target_pairs={{0,2},{1,3},{2,0},{3,1},{4,6},{5,7},{6,4},{7,5},{8,10},{9,11},{10,... | collective-permute-start | bytes 122888 | tf_op jit(solution)/shard_map/ppermute | solution.py:299
  31.5 1.4 %collective-permute-start.15 = (bf16[80,256]{1,0:T(8,128)(2,1)S(1)}, bf16[80,256]{1,0:T(8,128)(2,1)S(1)}, u32[]{:S(2)}, u32[]{:S(2)}) collective-permute-start(bf16[80,256]{1,0:T(8,128)(2,1)S(1)} %get-tuple-element.68), channel_id=1, source_target_pairs={{0,6},{1,7},{2,4},{3,5},{4,2},{5,3},{6,0},{7,1},{8,14},{9,15},{10,... | collective-permute-start | bytes 122888 | tf_op jit(solution)/shard_map/ppermute | solution.py:299
  32.9 0.5 collective-permute-done.13.refs_0_
  33.4 0.9 %collective-permute-done.14.refs_1_ = bf16[80,256]{1,0:T(8,128)(2,1)S(1)} collective-permute-done((bf16[80,256]{1,0:T(8,128)(2,1)S(1)}, bf16[80,256]{1,0:T(8,128)(2,1)S(1)}, u32[]{:S(2)}, u32[]{:S(2)}) %collective-permute-start.14) | collective-permute-done | bytes 40992 | tf_op jit(solution)/shard_map/ppermute | solution.py:299
  34.3 2.9 %collective-permute-done.15.refs_2_ = bf16[80,256]{1,0:T(8,128)(2,1)S(1)} collective-permute-done((bf16[80,256]{1,0:T(8,128)(2,1)S(1)}, bf16[80,256]{1,0:T(8,128)(2,1)S(1)}, u32[]{:S(2)}, u32[]{:S(2)}) %collective-permute-start.15) | collective-permute-done | bytes 40992 | tf_op jit(solution)/shard_map/ppermute | solution.py:299
  37.3 1.2 %collective-permute-done.18.refs_6_ = bf16[80,256]{1,0:T(8,128)(2,1)S(1)} collective-permute-done((bf16[80,256]{1,0:T(8,128)(2,1)S(1)}, bf16[80,256]{1,0:T(8,128)(2,1)S(1)}, u32[]{:S(2)}, u32[]{:S(2)}) %collective-permute-start.18) | collective-permute-done | bytes 40992 | tf_op jit(solution)/shard_map/ppermute | solution.py:307
  38.5 2.4 %shard_map.97 = (bf16[320,256]{1,0:T(8,128)(2,1)S(1)}, bf16[320,256]{1,0:T(8,128)(2,1)S(1)}) custom-call(bf16[4096,512]{1,0:T(8,128)(2,1)S(1)} %bitcast.11, bf16[4096,512]{1,0:T(8,128)(2,1)S(1)} %bitcast.14, bf16[512,4096]{1,0:T(8,128)(2,1)S(1)} %bitcast.17, bf16[80,256]{1,0:T(8,128)(2,1)S(1)} %collective-permute-done.13.refs_0_, ...), custom_call_target="tpu_custom_call" | custom-call | flops 3221225472 | bytes 13238272 | tf_op jit(solution)/shard_map/pallas_call | solution.py:259
  41.1 1.2 %collective-permute-done.20.refs_1_ = bf16[320,256]{1,0:T(8,128)(2,1)S(1)} collective-permute-done((bf16[320,256]{1,0:T(8,128)(2,1)S(1)}, bf16[320,256]{1,0:T(8,128)(2,1)S(1)}, u32[]{:S(2)}, u32[]{:S(2)}) %collective-permute-start.20) | collective-permute-done | bytes 163872 | tf_op jit(solution)/shard_map/ppermute | solution.py:323
  42.4 0.2 collective-permute-start.21
  42.7 1.4 %collective-permute-start.22 = (bf16[80,256]{1,0:T(8,128)(2,1)S(1)}, bf16[80,256]{1,0:T(8,128)(2,1)S(1)}, u32[]{:S(2)}, u32[]{:S(2)}) collective-permute-start(bf16[80,256]{1,0:T(8,128)(2,1)S(1)} %get-tuple-element.73), channel_id=1, source_target_pairs={{0,6},{1,7},{2,4},{3,5},{4,2},{5,3},{6,0},{7,1},{8,14},{9,15},{10,... | collective-permute-start | bytes 122888 | tf_op jit(solution)/shard_map/ppermute | solution.py:299
  44.1 1.9 %collective-permute-start.23 = (bf16[80,256]{1,0:T(8,128)(2,1)S(1)}, bf16[80,256]{1,0:T(8,128)(2,1)S(1)}, u32[]{:S(2)}, u32[]{:S(2)}) collective-permute-start(bf16[80,256]{1,0:T(8,128)(2,1)S(1)} %get-tuple-element.74), channel_id=1, source_target_pairs={{0,2},{1,3},{2,0},{3,1},{4,6},{5,7},{6,4},{7,5},{8,10},{9,11},{10,... | collective-permute-start | bytes 122888 | tf_op jit(solution)/shard_map/ppermute | solution.py:299
  46.0 1.9 %collective-permute-done.21.b0 = bf16[80,256]{1,0:T(8,128)(2,1)S(1)} collective-permute-done((bf16[80,256]{1,0:T(8,128)(2,1)S(1)}, bf16[80,256]{1,0:T(8,128)(2,1)S(1)}, u32[]{:S(2)}, u32[]{:S(2)}) %collective-permute-start.21) | collective-permute-done | bytes 40992 | tf_op jit(solution)/shard_map/ppermute | solution.py:299
  47.9 0.6 %collective-permute-done.22.b1 = bf16[80,256]{1,0:T(8,128)(2,1)S(1)} collective-permute-done((bf16[80,256]{1,0:T(8,128)(2,1)S(1)}, bf16[80,256]{1,0:T(8,128)(2,1)S(1)}, u32[]{:S(2)}, u32[]{:S(2)}) %collective-permute-start.22) | collective-permute-done | bytes 40992 | tf_op jit(solution)/shard_map/ppermute | solution.py:299
  48.8 1.0 %shard_map.99 = bf16[16,4096]{1,0:T(8,128)(2,1)} custom-call(bf16[16,4096]{1,0:T(8,128)(2,1)S(1)} %get-tuple-element.65.x_ref, bf16[80,256]{1,0:T(8,128)(2,1)S(1)} %collective-permute-done.21.b0, bf16[80,256]{1,0:T(8,128)(2,1)S(1)} %collective-permute-done.22.b1, bf16[80,256]{1,0:T(8,128)(2,1)S(1)} %collective-permute-done.23.b2, ...), custom_call_target="tpu_custom_call" | custom-call | bytes 435200 | tf_op jit(solution)/shard_map/pallas_call | solution.py:259
  (37 shorter events, 1.2 us)
Async XLA Ops:
  0.0 7.4 %copy-start = (bf16[1,1,4096,512]{3,2,1,0:T(8,128)(2,1)S(1)}, bf16[1,1,4096,512]{3,2,1,0:T(8,128)(2,1)}, u32[]{:S(2)}) copy-start(bf16[1,1,4096,512]{3,2,1,0:T(8,128)(2,1)} %param.15) | copy-start | bytes 12582916
  0.0 7.4 %copy-start.1 = (bf16[1,1,4096,512]{3,2,1,0:T(8,128)(2,1)S(1)}, bf16[1,1,4096,512]{3,2,1,0:T(8,128)(2,1)}, u32[]{:S(2)}) copy-start(bf16[1,1,4096,512]{3,2,1,0:T(8,128)(2,1)} %param.16) | copy-start | bytes 12582916
  0.0 7.4 %copy-start.2 = (bf16[1,1,512,4096]{3,2,1,0:T(8,128)(2,1)S(1)}, bf16[1,1,512,4096]{3,2,1,0:T(8,128)(2,1)}, u32[]{:S(2)}) copy-start(bf16[1,1,512,4096]{3,2,1,0:T(8,128)(2,1)} %param.17) | copy-start | bytes 12582916
  1.6 5.8 %collective-permute-start.6 = (bf16[80,256]{1,0:T(8,128)(2,1)S(1)}, bf16[80,256]{1,0:T(8,128)(2,1)S(1)}, u32[]{:S(2)}, u32[]{:S(2)}) collective-permute-start(bf16[80,256]{1,0:T(8,128)(2,1)S(1)} %get-tuple-element.45.refs_0_), channel_id=1, source_target_pairs={{0,1},{1,0},{2,3},{3,2},{4,5},{5,4},{6,7},{7,6},{8,9},{9,8},{10,11... | collective-permute-start | bytes 122888 | tf_op jit(solution)/shard_map/ppermute | solution.py:307
  2.1 7.2 %collective-permute-start = (bf16[80,256]{1,0:T(8,128)(2,1)S(1)}, bf16[80,256]{1,0:T(8,128)(2,1)S(1)}, u32[]{:S(2)}, u32[]{:S(2)}) collective-permute-start(bf16[80,256]{1,0:T(8,128)(2,1)S(1)} %get-tuple-element.41), channel_id=1, source_target_pairs={{0,4},{1,5},{2,6},{3,7},{4,0},{5,1},{6,2},{7,3},{8,12},{9,13},{10,... | collective-permute-start | bytes 122888 | tf_op jit(solution)/shard_map/ppermute | solution.py:299
  5.8 4.1 %collective-permute-start.1 = (bf16[80,256]{1,0:T(8,128)(2,1)S(1)}, bf16[80,256]{1,0:T(8,128)(2,1)S(1)}, u32[]{:S(2)}, u32[]{:S(2)}) collective-permute-start(bf16[80,256]{1,0:T(8,128)(2,1)S(1)} %get-tuple-element.42), channel_id=1, source_target_pairs={{0,2},{1,3},{2,0},{3,1},{4,6},{5,7},{6,4},{7,5},{8,10},{9,11},{10,... | collective-permute-start | bytes 122888 | tf_op jit(solution)/shard_map/ppermute | solution.py:299
  7.4 5.8 %collective-permute-start.2 = (bf16[80,256]{1,0:T(8,128)(2,1)S(1)}, bf16[80,256]{1,0:T(8,128)(2,1)S(1)}, u32[]{:S(2)}, u32[]{:S(2)}) collective-permute-start(bf16[80,256]{1,0:T(8,128)(2,1)S(1)} %get-tuple-element.43), channel_id=1, source_target_pairs={{0,6},{1,7},{2,4},{3,5},{4,2},{5,3},{6,0},{7,1},{8,14},{9,15},{10,... | collective-permute-start | bytes 122888 | tf_op jit(solution)/shard_map/ppermute | solution.py:299
  7.4 5.8 %copy-start.4 = (s32[1,16,1]{1,2,0:T(1,128)S(1)}, s32[1,16,1]{1,2,0:T(1,128)}, u32[]{:S(2)}) copy-start(s32[1,16,1]{1,2,0:T(1,128)} %param.13) | copy-start | bytes 196
  7.4 5.8 %copy-start.5 = (f32[1,16,1]{1,2,0:T(1,128)S(1)}, f32[1,16,1]{1,2,0:T(1,128)}, u32[]{:S(2)}) copy-start(f32[1,16,1]{1,2,0:T(1,128)} %param.14) | copy-start | bytes 196
  9.3 3.9 %collective-permute-start.7 = (bf16[80,256]{1,0:T(8,128)(2,1)S(1)}, bf16[80,256]{1,0:T(8,128)(2,1)S(1)}, u32[]{:S(2)}, u32[]{:S(2)}) collective-permute-start(bf16[80,256]{1,0:T(8,128)(2,1)S(1)} %get-tuple-element.47), channel_id=1, source_target_pairs={{0,1},{1,0},{2,3},{3,2},{4,5},{5,4},{6,7},{7,6},{8,9},{9,8},{10,11... | collective-permute-start | bytes 122888 | tf_op jit(solution)/shard_map/ppermute | solution.py:323
  9.4 4.1 %collective-permute-start.3 = (bf16[80,256]{1,0:T(8,128)(2,1)S(1)}, bf16[80,256]{1,0:T(8,128)(2,1)S(1)}, u32[]{:S(2)}, u32[]{:S(2)}) collective-permute-start(bf16[80,256]{1,0:T(8,128)(2,1)S(1)} %collective-permute-done.refs_0_), channel_id=1, source_target_pairs={{0,1},{1,0},{2,3},{3,2},{4,5},{5,4},{6,7},{7,6},{8,9},{9,8},{10,11... | collective-permute-start | bytes 122888 | tf_op jit(solution)/shard_map/ppermute | solution.py:307
  9.9 3.6 %collective-permute-start.4 = (bf16[80,256]{1,0:T(8,128)(2,1)S(1)}, bf16[80,256]{1,0:T(8,128)(2,1)S(1)}, u32[]{:S(2)}, u32[]{:S(2)}) collective-permute-start(bf16[80,256]{1,0:T(8,128)(2,1)S(1)} %collective-permute-done.1.refs_1_), channel_id=1, source_target_pairs={{0,1},{1,0},{2,3},{3,2},{4,5},{5,4},{6,7},{7,6},{8,9},{9,8},{10,11... | collective-permute-start | bytes 122888 | tf_op jit(solution)/shard_map/ppermute | solution.py:307
  13.2 1.2 %collective-permute-start.5 = (bf16[80,256]{1,0:T(8,128)(2,1)S(1)}, bf16[80,256]{1,0:T(8,128)(2,1)S(1)}, u32[]{:S(2)}, u32[]{:S(2)}) collective-permute-start(bf16[80,256]{1,0:T(8,128)(2,1)S(1)} %collective-permute-done.2.refs_2_), channel_id=1, source_target_pairs={{0,1},{1,0},{2,3},{3,2},{4,5},{5,4},{6,7},{7,6},{8,9},{9,8},{10,11... | collective-permute-start | bytes 122888 | tf_op jit(solution)/shard_map/ppermute | solution.py:307
  14.4 13.3 %copy-start.3 = (f32[1,4096]{1,0:T(1,128)S(1)}, f32[1,4096]{1,0:T(1,128)}, u32[]{:S(2)}) copy-start(f32[1,4096]{1,0:T(1,128)} %refs_4_.1) | copy-start | bytes 49156
  16.8 1.7 %collective-permute-start.8 = (bf16[240,256]{1,0:T(8,128)(2,1)S(1)}, bf16[240,256]{1,0:T(8,128)(2,1)S(1)}, u32[]{:S(2)}, u32[]{:S(2)}) collective-permute-start(bf16[240,256]{1,0:T(8,128)(2,1)S(1)} %get-tuple-element.59), channel_id=1, source_target_pairs={{0,1},{1,0},{2,3},{3,2},{4,5},{5,4},{6,7},{7,6},{8,9},{9,8},{10,11... | collective-permute-start | bytes 368648 | tf_op jit(solution)/shard_map/ppermute | solution.py:323
  17.0 10.7 %collective-permute-start.12 = (bf16[352,256]{1,0:T(8,128)(2,1)S(1)}, bf16[352,256]{1,0:T(8,128)(2,1)S(1)}, u32[]{:S(2)}, u32[]{:S(2)}) collective-permute-start(bf16[352,256]{1,0:T(8,128)(2,1)S(1)} %get-tuple-element.63), channel_id=1, source_target_pairs={{0,8},{8,16},{16,24},{24,0},{1,9},{9,17},{17,25},{25,1},{2,10},{10... | collective-permute-start | bytes 540680 | tf_op jit(solution)/shard_map/ppermute | solution.py:360
  18.5 6.8 %collective-permute-start.9 = (bf16[80,256]{1,0:T(8,128)(2,1)S(1)}, bf16[80,256]{1,0:T(8,128)(2,1)S(1)}, u32[]{:S(2)}, u32[]{:S(2)}) collective-permute-start(bf16[80,256]{1,0:T(8,128)(2,1)S(1)} %get-tuple-element.60), channel_id=1, source_target_pairs={{0,12},{1,13},{2,14},{3,15},{4,8},{5,9},{6,10},{7,11},{8,20},{9,21... | collective-permute-start | bytes 122888 | tf_op jit(solution)/shard_map/ppermute | solution.py:362
  19.6 7.9 %collective-permute-start.10 = (bf16[80,256]{1,0:T(8,128)(2,1)S(1)}, bf16[80,256]{1,0:T(8,128)(2,1)S(1)}, u32[]{:S(2)}, u32[]{:S(2)}) collective-permute-start(bf16[80,256]{1,0:T(8,128)(2,1)S(1)} %get-tuple-element.61), channel_id=1, source_target_pairs={{0,14},{1,15},{2,12},{3,13},{4,10},{5,11},{6,8},{7,9},{8,22},{9,23... | collective-permute-start | bytes 122888 | tf_op jit(solution)/shard_map/ppermute | solution.py:362
  21.5 6.2 %collective-permute-start.11 = (bf16[80,256]{1,0:T(8,128)(2,1)S(1)}, bf16[80,256]{1,0:T(8,128)(2,1)S(1)}, u32[]{:S(2)}, u32[]{:S(2)}) collective-permute-start(bf16[80,256]{1,0:T(8,128)(2,1)S(1)} %get-tuple-element.62), channel_id=1, source_target_pairs={{0,10},{1,11},{2,8},{3,9},{4,14},{5,15},{6,12},{7,13},{8,18},{9,19... | collective-permute-start | bytes 122888 | tf_op jit(solution)/shard_map/ppermute | solution.py:362
  28.4 5.0 %collective-permute-start.13 = (bf16[80,256]{1,0:T(8,128)(2,1)S(1)}, bf16[80,256]{1,0:T(8,128)(2,1)S(1)}, u32[]{:S(2)}, u32[]{:S(2)}) collective-permute-start(bf16[80,256]{1,0:T(8,128)(2,1)S(1)} %get-tuple-element.66), channel_id=1, source_target_pairs={{0,4},{1,5},{2,6},{3,7},{4,0},{5,1},{6,2},{7,3},{8,12},{9,13},{10,... | collective-permute-start | bytes 122888 | tf_op jit(solution)/shard_map/ppermute | solution.py:299
  29.9 4.4 %collective-permute-start.14 = (bf16[80,256]{1,0:T(8,128)(2,1)S(1)}, bf16[80,256]{1,0:T(8,128)(2,1)S(1)}, u32[]{:S(2)}, u32[]{:S(2)}) collective-permute-start(bf16[80,256]{1,0:T(8,128)(2,1)S(1)} %get-tuple-element.67), channel_id=1, source_target_pairs={{0,2},{1,3},{2,0},{3,1},{4,6},{5,7},{6,4},{7,5},{8,10},{9,11},{10,... | collective-permute-start | bytes 122888 | tf_op jit(solution)/shard_map/ppermute | solution.py:299
  31.5 5.8 %collective-permute-start.15 = (bf16[80,256]{1,0:T(8,128)(2,1)S(1)}, bf16[80,256]{1,0:T(8,128)(2,1)S(1)}, u32[]{:S(2)}, u32[]{:S(2)}) collective-permute-start(bf16[80,256]{1,0:T(8,128)(2,1)S(1)} %get-tuple-element.68), channel_id=1, source_target_pairs={{0,6},{1,7},{2,4},{3,5},{4,2},{5,3},{6,0},{7,1},{8,14},{9,15},{10,... | collective-permute-start | bytes 122888 | tf_op jit(solution)/shard_map/ppermute | solution.py:299
  32.9 4.4 %collective-permute-start.19 = (bf16[80,256]{1,0:T(8,128)(2,1)S(1)}, bf16[80,256]{1,0:T(8,128)(2,1)S(1)}, u32[]{:S(2)}, u32[]{:S(2)}) collective-permute-start(bf16[80,256]{1,0:T(8,128)(2,1)S(1)} %get-tuple-element.69.refs_3_), channel_id=1, source_target_pairs={{0,1},{1,0},{2,3},{3,2},{4,5},{5,4},{6,7},{7,6},{8,9},{9,8},{10,11... | collective-permute-start | bytes 122888 | tf_op jit(solution)/shard_map/ppermute | solution.py:307
  33.3 4.0 %collective-permute-start.16 = (bf16[80,256]{1,0:T(8,128)(2,1)S(1)}, bf16[80,256]{1,0:T(8,128)(2,1)S(1)}, u32[]{:S(2)}, u32[]{:S(2)}) collective-permute-start(bf16[80,256]{1,0:T(8,128)(2,1)S(1)} %collective-permute-done.13.refs_0_), channel_id=1, source_target_pairs={{0,1},{1,0},{2,3},{3,2},{4,5},{5,4},{6,7},{7,6},{8,9},{9,8},{10,11... | collective-permute-start | bytes 122888 | tf_op jit(solution)/shard_map/ppermute | solution.py:307
  34.3 3.0 %collective-permute-start.17 = (bf16[80,256]{1,0:T(8,128)(2,1)S(1)}, bf16[80,256]{1,0:T(8,128)(2,1)S(1)}, u32[]{:S(2)}, u32[]{:S(2)}) collective-permute-start(bf16[80,256]{1,0:T(8,128)(2,1)S(1)} %collective-permute-done.14.refs_1_), channel_id=1, source_target_pairs={{0,1},{1,0},{2,3},{3,2},{4,5},{5,4},{6,7},{7,6},{8,9},{9,8},{10,11... | collective-permute-start | bytes 122888 | tf_op jit(solution)/shard_map/ppermute | solution.py:307
  37.3 1.2 %collective-permute-start.18 = (bf16[80,256]{1,0:T(8,128)(2,1)S(1)}, bf16[80,256]{1,0:T(8,128)(2,1)S(1)}, u32[]{:S(2)}, u32[]{:S(2)}) collective-permute-start(bf16[80,256]{1,0:T(8,128)(2,1)S(1)} %collective-permute-done.15.refs_2_), channel_id=1, source_target_pairs={{0,1},{1,0},{2,3},{3,2},{4,5},{5,4},{6,7},{7,6},{8,9},{9,8},{10,11... | collective-permute-start | bytes 122888 | tf_op jit(solution)/shard_map/ppermute | solution.py:307
  40.9 1.5 %collective-permute-start.20 = (bf16[320,256]{1,0:T(8,128)(2,1)S(1)}, bf16[320,256]{1,0:T(8,128)(2,1)S(1)}, u32[]{:S(2)}, u32[]{:S(2)}) collective-permute-start(bf16[320,256]{1,0:T(8,128)(2,1)S(1)} %get-tuple-element.71), channel_id=1, source_target_pairs={{0,1},{1,0},{2,3},{3,2},{4,5},{5,4},{6,7},{7,6},{8,9},{9,8},{10,11... | collective-permute-start | bytes 491528 | tf_op jit(solution)/shard_map/ppermute | solution.py:323
  42.4 5.5 %collective-permute-start.21 = (bf16[80,256]{1,0:T(8,128)(2,1)S(1)}, bf16[80,256]{1,0:T(8,128)(2,1)S(1)}, u32[]{:S(2)}, u32[]{:S(2)}) collective-permute-start(bf16[80,256]{1,0:T(8,128)(2,1)S(1)} %get-tuple-element.72), channel_id=1, source_target_pairs={{0,4},{1,5},{2,6},{3,7},{4,0},{5,1},{6,2},{7,3},{8,12},{9,13},{10,... | collective-permute-start | bytes 122888 | tf_op jit(solution)/shard_map/ppermute | solution.py:299
  42.7 5.9 %collective-permute-start.22 = (bf16[80,256]{1,0:T(8,128)(2,1)S(1)}, bf16[80,256]{1,0:T(8,128)(2,1)S(1)}, u32[]{:S(2)}, u32[]{:S(2)}) collective-permute-start(bf16[80,256]{1,0:T(8,128)(2,1)S(1)} %get-tuple-element.73), channel_id=1, source_target_pairs={{0,6},{1,7},{2,4},{3,5},{4,2},{5,3},{6,0},{7,1},{8,14},{9,15},{10,... | collective-permute-start | bytes 122888 | tf_op jit(solution)/shard_map/ppermute | solution.py:299
  44.1 4.7 %collective-permute-start.23 = (bf16[80,256]{1,0:T(8,128)(2,1)S(1)}, bf16[80,256]{1,0:T(8,128)(2,1)S(1)}, u32[]{:S(2)}, u32[]{:S(2)}) collective-permute-start(bf16[80,256]{1,0:T(8,128)(2,1)S(1)} %get-tuple-element.74), channel_id=1, source_target_pairs={{0,2},{1,3},{2,0},{3,1},{4,6},{5,7},{6,4},{7,5},{8,10},{9,11},{10,... | collective-permute-start | bytes 122888 | tf_op jit(solution)/shard_map/ppermute | solution.py:299

commit v5 on v3

--- a/solution.py
+++ b/solution.py
@@ -12,6 +12,7 @@
 ROWS = 16
 LANES = 256
 PIECE = 512
+DEPTH = 1024
 PARTS = 4
 EPS = 1e-06
 F32 = jnp.float32
@@ -223,9 +224,11 @@
     width = w_gate.shape[0]
     rows = spread_ref.shape[1] * LANES // width
     from_blocks([ref[...] for ref in ins], spread_ref)
-    x = gathered(spread_ref, rows, width)
-    gate_val = jnp.dot(x, w_gate[...], preferred_element_type=F32)
-    up_val = jnp.dot(x, w_up[...], preferred_element_type=F32)
+    gate_val = up_val = jnp.zeros((rows, w_gate.shape[1]), F32)
+    for start in range(0, width, DEPTH):
+        x = gathered(spread_ref, rows, width, start, DEPTH)
+        gate_val += jnp.dot(x, w_gate[start : start + DEPTH], preferred_element_type=F32)
+        up_val += jnp.dot(x, w_up[start : start + DEPTH], preferred_element_type=F32)
     hidden = (gate_val / (1.0 + jnp.exp(-gate_val)) * up_val).astype(BF16)
     for start in range(0, width, PIECE):
         piece = jnp.dot(hidden, w_down[:, start : start + PIECE], preferred_element_type=F32)

time: 49.4 us -> 49.4 us (level)
  no operation moved by 1% of the time
where the time goes in v5:
time: 49.4 us; the launch traced here: 49.3 us
  starting transfers between devices  22.2 us (45%)
  waiting for transfers between devices  16.7 us (34%)
  Pallas kernels  10.2 us (21%)
    ppermute x9, starting transfers between devices, across(): lax.ppermute(blocks[i], 'expert', to_expert(i))  12.3 us
    pallas_call x9, Pallas kernels, call(): pl.pallas_call(body, out_shape=outs, in_specs=[space] * len(ins), out_spe...  10.2 us
    ppermute x9, waiting for transfers between devices, across(): lax.ppermute(blocks[i], 'expert', to_expert(i))  9.16 us
    ppermute x3, starting transfers between devices, on_device(): lax.ppermute(sums[i], ('section', 'expert'), onward(i))  5.81 us
    ppermute x3, waiting for transfers between devices, on_device(): lax.ppermute(sums[i], ('section', 'expert'), onward(i))  4.81 us
    ppermute x8, starting transfers between devices, shared(): lax.ppermute(a, 'expert', within(m))  1.78 us
    ppermute x8, waiting for transfers between devices, shared(): lax.ppermute(a, 'expert', within(m))  1.55 us
    ppermute x1, starting transfers between devices, on_device(): lax.ppermute(carry, 'section', [(i, (i + 1) % sections) for i in range(se...  1.49 us
  transfers between devices with their start and end apart: 24, of which 14 were waited for; matrix products, arithmetic and copies ran while one was open for 0% of the time, Pallas kernels for 4%

profile of v5, /device:TPU:0, one launch (start us, length us, event | category | flops | bytes accessed | tf_op | source)
XLA Modules:
  0.0 49.3 jit_solution(14987957545096253732)
XLA Ops:
  0.0 1.6 %shard_map.91 = (bf16[80,256]{1,0:T(8,128)(2,1)S(1)}, bf16[80,256]{1,0:T(8,128)(2,1)S(1)}, bf16[80,256]{1,0:T(8,128)(2,1)S(1)}, bf16[80,256]{1,0:T(8,128)(2,1)S(1)}, bf16[272,256]{1,0:T(8,128)(2,1)S(1)}) custom-call(bf16[16,4096]{1,0:T(8,128)(2,1)} %bitcast.20, f32[1,4096]{1,0:T(1,128)} %refs_4_.1, s32[1,16]{1,0:T(1,128)} %bitcast.21, f32[1,16]{1,0:T(1,128)} %bitcast.22), custom_call_target="tpu_custom_call" | custom-call | flops 10000000000 | bytes 450688 | tf_op jit(solution)/shard_map/pallas_call | solution.py:262
  1.6 0.5 %collective-permute-start.6 = (bf16[80,256]{1,0:T(8,128)(2,1)S(1)}, bf16[80,256]{1,0:T(8,128)(2,1)S(1)}, u32[]{:S(2)}, u32[]{:S(2)}) collective-permute-start(bf16[80,256]{1,0:T(8,128)(2,1)S(1)} %get-tuple-element.45.refs_0_), channel_id=1, source_target_pairs={{0,1},{1,0},{2,3},{3,2},{4,5},{5,4},{6,7},{7,6},{8,9},{9,8},{10,11... | collective-permute-start | bytes 122888 | tf_op jit(solution)/shard_map/ppermute | solution.py:306
  2.1 3.7 %collective-permute-start = (bf16[80,256]{1,0:T(8,128)(2,1)S(1)}, bf16[80,256]{1,0:T(8,128)(2,1)S(1)}, u32[]{:S(2)}, u32[]{:S(2)}) collective-permute-start(bf16[80,256]{1,0:T(8,128)(2,1)S(1)} %get-tuple-element.41), channel_id=1, source_target_pairs={{0,4},{1,5},{2,6},{3,7},{4,0},{5,1},{6,2},{7,3},{8,12},{9,13},{10,... | collective-permute-start | bytes 122888 | tf_op jit(solution)/shard_map/ppermute | solution.py:302
  5.8 1.3 %collective-permute-start.1 = (bf16[80,256]{1,0:T(8,128)(2,1)S(1)}, bf16[80,256]{1,0:T(8,128)(2,1)S(1)}, u32[]{:S(2)}, u32[]{:S(2)}) collective-permute-start(bf16[80,256]{1,0:T(8,128)(2,1)S(1)} %get-tuple-element.42), channel_id=1, source_target_pairs={{0,6},{1,7},{2,4},{3,5},{4,2},{5,3},{6,0},{7,1},{8,14},{9,15},{10,... | collective-permute-start | bytes 122888 | tf_op jit(solution)/shard_map/ppermute | solution.py:302
  7.4 1.8 %shard_map.92 = (bf16[80,256]{1,0:T(8,128)(2,1)S(1)}, bf16[80,256]{1,0:T(8,128)(2,1)S(1)}) custom-call(bf16[4096,512]{1,0:T(8,128)(2,1)S(1)} %bitcast.9, bf16[4096,512]{1,0:T(8,128)(2,1)S(1)} %bitcast.12, bf16[512,4096]{1,0:T(8,128)(2,1)S(1)} %bitcast.15, bf16[80,256]{1,0:T(8,128)(2,1)S(1)} %get-tuple-element.45.refs_0_, ...), custom_call_target="tpu_custom_call" | custom-call | flops 3221225472 | bytes 12746752 | tf_op jit(solution)/shard_map/pallas_call | solution.py:262
  9.4 0.5 collective-permute-start.3
  9.8 1.9 %collective-permute-done.1.refs_1_ = bf16[80,256]{1,0:T(8,128)(2,1)S(1)} collective-permute-done((bf16[80,256]{1,0:T(8,128)(2,1)S(1)}, bf16[80,256]{1,0:T(8,128)(2,1)S(1)}, u32[]{:S(2)}, u32[]{:S(2)}) %collective-permute-start.1) | collective-permute-done | bytes 40992 | tf_op jit(solution)/shard_map/ppermute | solution.py:302
  11.7 0.5 %collective-permute-start.5 = (bf16[80,256]{1,0:T(8,128)(2,1)S(1)}, bf16[80,256]{1,0:T(8,128)(2,1)S(1)}, u32[]{:S(2)}, u32[]{:S(2)}) collective-permute-start(bf16[80,256]{1,0:T(8,128)(2,1)S(1)} %collective-permute-done.2.refs_2_), channel_id=1, source_target_pairs={{0,1},{1,0},{2,3},{3,2},{4,5},{5,4},{6,7},{7,6},{8,9},{9,8},{10,11... | collective-permute-start | bytes 122888 | tf_op jit(solution)/shard_map/ppermute | solution.py:306
  12.5 0.4 collective-permute-done.4.refs_4_
  13.1 2.4 %shard_map.94 = (bf16[240,256]{1,0:T(8,128)(2,1)S(1)}, bf16[240,256]{1,0:T(8,128)(2,1)S(1)}) custom-call(bf16[4096,512]{1,0:T(8,128)(2,1)S(1)} %bitcast.10, bf16[4096,512]{1,0:T(8,128)(2,1)S(1)} %bitcast.13, bf16[512,4096]{1,0:T(8,128)(2,1)S(1)} %bitcast.16, bf16[80,256]{1,0:T(8,128)(2,1)S(1)} %collective-permute-done.refs_0_, ...), custom_call_target="tpu_custom_call" | custom-call | flops 3221225472 | bytes 13074432 | tf_op jit(solution)/shard_map/pallas_call | solution.py:262
  15.5 0.4 collective-permute-start.8
  15.9 1.5 %collective-permute-start.12 = (bf16[352,256]{1,0:T(8,128)(2,1)S(1)}, bf16[352,256]{1,0:T(8,128)(2,1)S(1)}, u32[]{:S(2)}, u32[]{:S(2)}) collective-permute-start(bf16[352,256]{1,0:T(8,128)(2,1)S(1)} %get-tuple-element.63), channel_id=1, source_target_pairs={{0,8},{8,16},{16,24},{24,0},{1,9},{9,17},{17,25},{25,1},{2,10},{10... | collective-permute-start | bytes 540680 | tf_op jit(solution)/shard_map/ppermute | solution.py:359
  17.4 2.5 %collective-permute-start.9 = (bf16[80,256]{1,0:T(8,128)(2,1)S(1)}, bf16[80,256]{1,0:T(8,128)(2,1)S(1)}, u32[]{:S(2)}, u32[]{:S(2)}) collective-permute-start(bf16[80,256]{1,0:T(8,128)(2,1)S(1)} %get-tuple-element.60), channel_id=1, source_target_pairs={{0,12},{1,13},{2,14},{3,15},{4,8},{5,9},{6,10},{7,11},{8,20},{9,21... | collective-permute-start | bytes 122888 | tf_op jit(solution)/shard_map/ppermute | solution.py:361
  19.9 1.9 %collective-permute-start.10 = (bf16[80,256]{1,0:T(8,128)(2,1)S(1)}, bf16[80,256]{1,0:T(8,128)(2,1)S(1)}, u32[]{:S(2)}, u32[]{:S(2)}) collective-permute-start(bf16[80,256]{1,0:T(8,128)(2,1)S(1)} %get-tuple-element.61), channel_id=1, source_target_pairs={{0,14},{1,15},{2,12},{3,13},{4,10},{5,11},{6,8},{7,9},{8,22},{9,23... | collective-permute-start | bytes 122888 | tf_op jit(solution)/shard_map/ppermute | solution.py:361
  21.9 1.4 %collective-permute-start.11 = (bf16[80,256]{1,0:T(8,128)(2,1)S(1)}, bf16[80,256]{1,0:T(8,128)(2,1)S(1)}, u32[]{:S(2)}, u32[]{:S(2)}) collective-permute-start(bf16[80,256]{1,0:T(8,128)(2,1)S(1)} %get-tuple-element.62), channel_id=1, source_target_pairs={{0,10},{1,11},{2,8},{3,9},{4,14},{5,15},{6,12},{7,13},{8,18},{9,19... | collective-permute-start | bytes 122888 | tf_op jit(solution)/shard_map/ppermute | solution.py:361
  23.2 1.0 %collective-permute-done.9.refs_0_ = bf16[80,256]{1,0:T(8,128)(2,1)S(1)} collective-permute-done((bf16[80,256]{1,0:T(8,128)(2,1)S(1)}, bf16[80,256]{1,0:T(8,128)(2,1)S(1)}, u32[]{:S(2)}, u32[]{:S(2)}) %collective-permute-start.9) | collective-permute-done | bytes 40992 | tf_op jit(solution)/shard_map/ppermute | solution.py:361
  24.3 3.5 %collective-permute-done.10.refs_1_ = bf16[80,256]{1,0:T(8,128)(2,1)S(1)} collective-permute-done((bf16[80,256]{1,0:T(8,128)(2,1)S(1)}, bf16[80,256]{1,0:T(8,128)(2,1)S(1)}, u32[]{:S(2)}, u32[]{:S(2)}) %collective-permute-start.10) | collective-permute-done | bytes 40992 | tf_op jit(solution)/shard_map/ppermute | solution.py:361
  28.1 0.7 %shard_map.96 = (bf16[16,4096]{1,0:T(8,128)(2,1)S(1)}, bf16[80,256]{1,0:T(8,128)(2,1)S(1)}, bf16[80,256]{1,0:T(8,128)(2,1)S(1)}, bf16[80,256]{1,0:T(8,128)(2,1)S(1)}, bf16[80,256]{1,0:T(8,128)(2,1)S(1)}) custom-call(bf16[80,256]{1,0:T(8,128)(2,1)S(1)} %collective-permute-done.9.refs_0_, bf16[80,256]{1,0:T(8,128)(2,1)S(1)} %collective-permute-done.10.refs_1_, ...), custom_call_target="tpu_custom_call" | custom-call | bytes 615424 | tf_op jit(solution)/shard_map/pallas_call | solution.py:262
  28.8 1.3 %collective-permute-start.13 = (bf16[80,256]{1,0:T(8,128)(2,1)S(1)}, bf16[80,256]{1,0:T(8,128)(2,1)S(1)}, u32[]{:S(2)}, u32[]{:S(2)}) collective-permute-start(bf16[80,256]{1,0:T(8,128)(2,1)S(1)} %get-tuple-element.66), channel_id=1, source_target_pairs={{0,4},{1,5},{2,6},{3,7},{4,0},{5,1},{6,2},{7,3},{8,12},{9,13},{10,... | collective-permute-start | bytes 122888 | tf_op jit(solution)/shard_map/ppermute | solution.py:302
  30.0 1.7 %collective-permute-start.14 = (bf16[80,256]{1,0:T(8,128)(2,1)S(1)}, bf16[80,256]{1,0:T(8,128)(2,1)S(1)}, u32[]{:S(2)}, u32[]{:S(2)}) collective-permute-start(bf16[80,256]{1,0:T(8,128)(2,1)S(1)} %get-tuple-element.67), channel_id=1, source_target_pairs={{0,6},{1,7},{2,4},{3,5},{4,2},{5,3},{6,0},{7,1},{8,14},{9,15},{10,... | collective-permute-start | bytes 122888 | tf_op jit(solution)/shard_map/ppermute | solution.py:302
  31.8 0.6 %collective-permute-start.15 = (bf16[80,256]{1,0:T(8,128)(2,1)S(1)}, bf16[80,256]{1,0:T(8,128)(2,1)S(1)}, u32[]{:S(2)}, u32[]{:S(2)}) collective-permute-start(bf16[80,256]{1,0:T(8,128)(2,1)S(1)} %get-tuple-element.68), channel_id=1, source_target_pairs={{0,2},{1,3},{2,0},{3,1},{4,6},{5,7},{6,4},{7,5},{8,10},{9,11},{10,... | collective-permute-start | bytes 122888 | tf_op jit(solution)/shard_map/ppermute | solution.py:302
  32.3 1.8 %collective-permute-done.13.refs_0_ = bf16[80,256]{1,0:T(8,128)(2,1)S(1)} collective-permute-done((bf16[80,256]{1,0:T(8,128)(2,1)S(1)}, bf16[80,256]{1,0:T(8,128)(2,1)S(1)}, u32[]{:S(2)}, u32[]{:S(2)}) %collective-permute-start.13) | collective-permute-done | bytes 40992 | tf_op jit(solution)/shard_map/ppermute | solution.py:302
  34.2 1.8 %collective-permute-done.14.refs_1_ = bf16[80,256]{1,0:T(8,128)(2,1)S(1)} collective-permute-done((bf16[80,256]{1,0:T(8,128)(2,1)S(1)}, bf16[80,256]{1,0:T(8,128)(2,1)S(1)}, u32[]{:S(2)}, u32[]{:S(2)}) %collective-permute-start.14) | collective-permute-done | bytes 40992 | tf_op jit(solution)/shard_map/ppermute | solution.py:302
  36.5 0.7 %collective-permute-done.17.refs_5_ = bf16[80,256]{1,0:T(8,128)(2,1)S(1)} collective-permute-done((bf16[80,256]{1,0:T(8,128)(2,1)S(1)}, bf16[80,256]{1,0:T(8,128)(2,1)S(1)}, u32[]{:S(2)}, u32[]{:S(2)}) %collective-permute-start.17) | collective-permute-done | bytes 40992 | tf_op jit(solution)/shard_map/ppermute | solution.py:306
  37.4 2.4 %shard_map.97 = (bf16[320,256]{1,0:T(8,128)(2,1)S(1)}, bf16[320,256]{1,0:T(8,128)(2,1)S(1)}) custom-call(bf16[4096,512]{1,0:T(8,128)(2,1)S(1)} %bitcast.11, bf16[4096,512]{1,0:T(8,128)(2,1)S(1)} %bitcast.14, bf16[512,4096]{1,0:T(8,128)(2,1)S(1)} %bitcast.17, bf16[80,256]{1,0:T(8,128)(2,1)S(1)} %collective-permute-done.13.refs_0_, ...), custom_call_target="tpu_custom_call" | custom-call | flops 3221225472 | bytes 13238272 | tf_op jit(solution)/shard_map/pallas_call | solution.py:262
  40.1 1.2 %collective-permute-done.20.refs_1_ = bf16[320,256]{1,0:T(8,128)(2,1)S(1)} collective-permute-done((bf16[320,256]{1,0:T(8,128)(2,1)S(1)}, bf16[320,256]{1,0:T(8,128)(2,1)S(1)}, u32[]{:S(2)}, u32[]{:S(2)}) %collective-permute-start.20) | collective-permute-done | bytes 163872 | tf_op jit(solution)/shard_map/ppermute | solution.py:322
  41.3 1.2 %collective-permute-start.21 = (bf16[80,256]{1,0:T(8,128)(2,1)S(1)}, bf16[80,256]{1,0:T(8,128)(2,1)S(1)}, u32[]{:S(2)}, u32[]{:S(2)}) collective-permute-start(bf16[80,256]{1,0:T(8,128)(2,1)S(1)} %get-tuple-element.72), channel_id=1, source_target_pairs={{0,4},{1,5},{2,6},{3,7},{4,0},{5,1},{6,2},{7,3},{8,12},{9,13},{10,... | collective-permute-start | bytes 122888 | tf_op jit(solution)/shard_map/ppermute | solution.py:302
  42.5 1.4 %collective-permute-start.22 = (bf16[80,256]{1,0:T(8,128)(2,1)S(1)}, bf16[80,256]{1,0:T(8,128)(2,1)S(1)}, u32[]{:S(2)}, u32[]{:S(2)}) collective-permute-start(bf16[80,256]{1,0:T(8,128)(2,1)S(1)} %get-tuple-element.73), channel_id=1, source_target_pairs={{0,6},{1,7},{2,4},{3,5},{4,2},{5,3},{6,0},{7,1},{8,14},{9,15},{10,... | collective-permute-start | bytes 122888 | tf_op jit(solution)/shard_map/ppermute | solution.py:302
  43.9 1.0 %collective-permute-start.23 = (bf16[80,256]{1,0:T(8,128)(2,1)S(1)}, bf16[80,256]{1,0:T(8,128)(2,1)S(1)}, u32[]{:S(2)}, u32[]{:S(2)}) collective-permute-start(bf16[80,256]{1,0:T(8,128)(2,1)S(1)} %get-tuple-element.74), channel_id=1, source_target_pairs={{0,2},{1,3},{2,0},{3,1},{4,6},{5,7},{6,4},{7,5},{8,10},{9,11},{10,... | collective-permute-start | bytes 122888 | tf_op jit(solution)/shard_map/ppermute | solution.py:302
  44.9 1.9 %collective-permute-done.21.b0 = bf16[80,256]{1,0:T(8,128)(2,1)S(1)} collective-permute-done((bf16[80,256]{1,0:T(8,128)(2,1)S(1)}, bf16[80,256]{1,0:T(8,128)(2,1)S(1)}, u32[]{:S(2)}, u32[]{:S(2)}) %collective-permute-start.21) | collective-permute-done | bytes 40992 | tf_op jit(solution)/shard_map/ppermute | solution.py:302
  46.8 1.5 %collective-permute-done.22.b1 = bf16[80,256]{1,0:T(8,128)(2,1)S(1)} collective-permute-done((bf16[80,256]{1,0:T(8,128)(2,1)S(1)}, bf16[80,256]{1,0:T(8,128)(2,1)S(1)}, u32[]{:S(2)}, u32[]{:S(2)}) %collective-permute-start.22) | collective-permute-done | bytes 40992 | tf_op jit(solution)/shard_map/ppermute | solution.py:302
  48.3 1.0 %shard_map.99 = bf16[16,4096]{1,0:T(8,128)(2,1)} custom-call(bf16[16,4096]{1,0:T(8,128)(2,1)S(1)} %get-tuple-element.65.x_ref, bf16[80,256]{1,0:T(8,128)(2,1)S(1)} %collective-permute-done.21.b0, bf16[80,256]{1,0:T(8,128)(2,1)S(1)} %collective-permute-done.22.b1, bf16[80,256]{1,0:T(8,128)(2,1)S(1)} %collective-permute-done.23.b2, ...), custom_call_target="tpu_custom_call" | custom-call | bytes 435200 | tf_op jit(solution)/shard_map/pallas_call | solution.py:262
  (37 shorter events, 2.3 us)
Async XLA Ops:
  0.0 7.4 %copy-start = (bf16[1,1,4096,512]{3,2,1,0:T(8,128)(2,1)S(1)}, bf16[1,1,4096,512]{3,2,1,0:T(8,128)(2,1)}, u32[]{:S(2)}) copy-start(bf16[1,1,4096,512]{3,2,1,0:T(8,128)(2,1)} %param.15) | copy-start | bytes 12582916
  0.0 7.4 %copy-start.1 = (bf16[1,1,4096,512]{3,2,1,0:T(8,128)(2,1)S(1)}, bf16[1,1,4096,512]{3,2,1,0:T(8,128)(2,1)}, u32[]{:S(2)}) copy-start(bf16[1,1,4096,512]{3,2,1,0:T(8,128)(2,1)} %param.16) | copy-start | bytes 12582916
  0.0 7.4 %copy-start.2 = (bf16[1,1,512,4096]{3,2,1,0:T(8,128)(2,1)S(1)}, bf16[1,1,512,4096]{3,2,1,0:T(8,128)(2,1)}, u32[]{:S(2)}) copy-start(bf16[1,1,512,4096]{3,2,1,0:T(8,128)(2,1)} %param.17) | copy-start | bytes 12582916
  1.6 5.8 %collective-permute-start.6 = (bf16[80,256]{1,0:T(8,128)(2,1)S(1)}, bf16[80,256]{1,0:T(8,128)(2,1)S(1)}, u32[]{:S(2)}, u32[]{:S(2)}) collective-permute-start(bf16[80,256]{1,0:T(8,128)(2,1)S(1)} %get-tuple-element.45.refs_0_), channel_id=1, source_target_pairs={{0,1},{1,0},{2,3},{3,2},{4,5},{5,4},{6,7},{7,6},{8,9},{9,8},{10,11... | collective-permute-start | bytes 122888 | tf_op jit(solution)/shard_map/ppermute | solution.py:306
  2.1 7.2 %collective-permute-start = (bf16[80,256]{1,0:T(8,128)(2,1)S(1)}, bf16[80,256]{1,0:T(8,128)(2,1)S(1)}, u32[]{:S(2)}, u32[]{:S(2)}) collective-permute-start(bf16[80,256]{1,0:T(8,128)(2,1)S(1)} %get-tuple-element.41), channel_id=1, source_target_pairs={{0,4},{1,5},{2,6},{3,7},{4,0},{5,1},{6,2},{7,3},{8,12},{9,13},{10,... | collective-permute-start | bytes 122888 | tf_op jit(solution)/shard_map/ppermute | solution.py:302
  5.8 5.9 %collective-permute-start.1 = (bf16[80,256]{1,0:T(8,128)(2,1)S(1)}, bf16[80,256]{1,0:T(8,128)(2,1)S(1)}, u32[]{:S(2)}, u32[]{:S(2)}) collective-permute-start(bf16[80,256]{1,0:T(8,128)(2,1)S(1)} %get-tuple-element.42), channel_id=1, source_target_pairs={{0,6},{1,7},{2,4},{3,5},{4,2},{5,3},{6,0},{7,1},{8,14},{9,15},{10,... | collective-permute-start | bytes 122888 | tf_op jit(solution)/shard_map/ppermute | solution.py:302
  7.1 4.6 %collective-permute-start.2 = (bf16[80,256]{1,0:T(8,128)(2,1)S(1)}, bf16[80,256]{1,0:T(8,128)(2,1)S(1)}, u32[]{:S(2)}, u32[]{:S(2)}) collective-permute-start(bf16[80,256]{1,0:T(8,128)(2,1)S(1)} %get-tuple-element.43), channel_id=1, source_target_pairs={{0,2},{1,3},{2,0},{3,1},{4,6},{5,7},{6,4},{7,5},{8,10},{9,11},{10,... | collective-permute-start | bytes 122888 | tf_op jit(solution)/shard_map/ppermute | solution.py:302
  7.4 4.8 %copy-start.4 = (s32[1,16,1]{1,2,0:T(1,128)S(1)}, s32[1,16,1]{1,2,0:T(1,128)}, u32[]{:S(2)}) copy-start(s32[1,16,1]{1,2,0:T(1,128)} %param.13) | copy-start | bytes 196
  7.4 4.8 %copy-start.5 = (f32[1,16,1]{1,2,0:T(1,128)S(1)}, f32[1,16,1]{1,2,0:T(1,128)}, u32[]{:S(2)}) copy-start(f32[1,16,1]{1,2,0:T(1,128)} %param.14) | copy-start | bytes 196
  9.3 3.0 %collective-permute-start.7 = (bf16[80,256]{1,0:T(8,128)(2,1)S(1)}, bf16[80,256]{1,0:T(8,128)(2,1)S(1)}, u32[]{:S(2)}, u32[]{:S(2)}) collective-permute-start(bf16[80,256]{1,0:T(8,128)(2,1)S(1)} %get-tuple-element.47), channel_id=1, source_target_pairs={{0,1},{1,0},{2,3},{3,2},{4,5},{5,4},{6,7},{7,6},{8,9},{9,8},{10,11... | collective-permute-start | bytes 122888 | tf_op jit(solution)/shard_map/ppermute | solution.py:322
  9.4 3.1 %collective-permute-start.3 = (bf16[80,256]{1,0:T(8,128)(2,1)S(1)}, bf16[80,256]{1,0:T(8,128)(2,1)S(1)}, u32[]{:S(2)}, u32[]{:S(2)}) collective-permute-start(bf16[80,256]{1,0:T(8,128)(2,1)S(1)} %collective-permute-done.refs_0_), channel_id=1, source_target_pairs={{0,1},{1,0},{2,3},{3,2},{4,5},{5,4},{6,7},{7,6},{8,9},{9,8},{10,11... | collective-permute-start | bytes 122888 | tf_op jit(solution)/shard_map/ppermute | solution.py:306
  11.7 1.2 %collective-permute-start.4 = (bf16[80,256]{1,0:T(8,128)(2,1)S(1)}, bf16[80,256]{1,0:T(8,128)(2,1)S(1)}, u32[]{:S(2)}, u32[]{:S(2)}) collective-permute-start(bf16[80,256]{1,0:T(8,128)(2,1)S(1)} %collective-permute-done.1.refs_1_), channel_id=1, source_target_pairs={{0,1},{1,0},{2,3},{3,2},{4,5},{5,4},{6,7},{7,6},{8,9},{9,8},{10,11... | collective-permute-start | bytes 122888 | tf_op jit(solution)/shard_map/ppermute | solution.py:306
  11.7 1.4 %collective-permute-start.5 = (bf16[80,256]{1,0:T(8,128)(2,1)S(1)}, bf16[80,256]{1,0:T(8,128)(2,1)S(1)}, u32[]{:S(2)}, u32[]{:S(2)}) collective-permute-start(bf16[80,256]{1,0:T(8,128)(2,1)S(1)} %collective-permute-done.2.refs_2_), channel_id=1, source_target_pairs={{0,1},{1,0},{2,3},{3,2},{4,5},{5,4},{6,7},{7,6},{8,9},{9,8},{10,11... | collective-permute-start | bytes 122888 | tf_op jit(solution)/shard_map/ppermute | solution.py:306
  13.1 15.0 %copy-start.3 = (f32[1,4096]{1,0:T(1,128)S(1)}, f32[1,4096]{1,0:T(1,128)}, u32[]{:S(2)}) copy-start(f32[1,4096]{1,0:T(1,128)} %refs_4_.1) | copy-start | bytes 49156
  15.5 1.9 %collective-permute-start.8 = (bf16[240,256]{1,0:T(8,128)(2,1)S(1)}, bf16[240,256]{1,0:T(8,128)(2,1)S(1)}, u32[]{:S(2)}, u32[]{:S(2)}) collective-permute-start(bf16[240,256]{1,0:T(8,128)(2,1)S(1)} %get-tuple-element.59), channel_id=1, source_target_pairs={{0,1},{1,0},{2,3},{3,2},{4,5},{5,4},{6,7},{7,6},{8,9},{9,8},{10,11... | collective-permute-start | bytes 368648 | tf_op jit(solution)/shard_map/ppermute | solution.py:322
  15.9 12.2 %collective-permute-start.12 = (bf16[352,256]{1,0:T(8,128)(2,1)S(1)}, bf16[352,256]{1,0:T(8,128)(2,1)S(1)}, u32[]{:S(2)}, u32[]{:S(2)}) collective-permute-start(bf16[352,256]{1,0:T(8,128)(2,1)S(1)} %get-tuple-element.63), channel_id=1, source_target_pairs={{0,8},{8,16},{16,24},{24,0},{1,9},{9,17},{17,25},{25,1},{2,10},{10... | collective-permute-start | bytes 540680 | tf_op jit(solution)/shard_map/ppermute | solution.py:359
  17.4 6.9 %collective-permute-start.9 = (bf16[80,256]{1,0:T(8,128)(2,1)S(1)}, bf16[80,256]{1,0:T(8,128)(2,1)S(1)}, u32[]{:S(2)}, u32[]{:S(2)}) collective-permute-start(bf16[80,256]{1,0:T(8,128)(2,1)S(1)} %get-tuple-element.60), channel_id=1, source_target_pairs={{0,12},{1,13},{2,14},{3,15},{4,8},{5,9},{6,10},{7,11},{8,20},{9,21... | collective-permute-start | bytes 122888 | tf_op jit(solution)/shard_map/ppermute | solution.py:361
  19.9 7.8 %collective-permute-start.10 = (bf16[80,256]{1,0:T(8,128)(2,1)S(1)}, bf16[80,256]{1,0:T(8,128)(2,1)S(1)}, u32[]{:S(2)}, u32[]{:S(2)}) collective-permute-start(bf16[80,256]{1,0:T(8,128)(2,1)S(1)} %get-tuple-element.61), channel_id=1, source_target_pairs={{0,14},{1,15},{2,12},{3,13},{4,10},{5,11},{6,8},{7,9},{8,22},{9,23... | collective-permute-start | bytes 122888 | tf_op jit(solution)/shard_map/ppermute | solution.py:361
  21.9 6.2 %collective-permute-start.11 = (bf16[80,256]{1,0:T(8,128)(2,1)S(1)}, bf16[80,256]{1,0:T(8,128)(2,1)S(1)}, u32[]{:S(2)}, u32[]{:S(2)}) collective-permute-start(bf16[80,256]{1,0:T(8,128)(2,1)S(1)} %get-tuple-element.62), channel_id=1, source_target_pairs={{0,10},{1,11},{2,8},{3,9},{4,14},{5,15},{6,12},{7,13},{8,18},{9,19... | collective-permute-start | bytes 122888 | tf_op jit(solution)/shard_map/ppermute | solution.py:361
  28.8 5.4 %collective-permute-start.13 = (bf16[80,256]{1,0:T(8,128)(2,1)S(1)}, bf16[80,256]{1,0:T(8,128)(2,1)S(1)}, u32[]{:S(2)}, u32[]{:S(2)}) collective-permute-start(bf16[80,256]{1,0:T(8,128)(2,1)S(1)} %get-tuple-element.66), channel_id=1, source_target_pairs={{0,4},{1,5},{2,6},{3,7},{4,0},{5,1},{6,2},{7,3},{8,12},{9,13},{10,... | collective-permute-start | bytes 122888 | tf_op jit(solution)/shard_map/ppermute | solution.py:302
  30.0 5.9 %collective-permute-start.14 = (bf16[80,256]{1,0:T(8,128)(2,1)S(1)}, bf16[80,256]{1,0:T(8,128)(2,1)S(1)}, u32[]{:S(2)}, u32[]{:S(2)}) collective-permute-start(bf16[80,256]{1,0:T(8,128)(2,1)S(1)} %get-tuple-element.67), channel_id=1, source_target_pairs={{0,6},{1,7},{2,4},{3,5},{4,2},{5,3},{6,0},{7,1},{8,14},{9,15},{10,... | collective-permute-start | bytes 122888 | tf_op jit(solution)/shard_map/ppermute | solution.py:302
  31.8 4.4 %collective-permute-start.15 = (bf16[80,256]{1,0:T(8,128)(2,1)S(1)}, bf16[80,256]{1,0:T(8,128)(2,1)S(1)}, u32[]{:S(2)}, u32[]{:S(2)}) collective-permute-start(bf16[80,256]{1,0:T(8,128)(2,1)S(1)} %get-tuple-element.68), channel_id=1, source_target_pairs={{0,2},{1,3},{2,0},{3,1},{4,6},{5,7},{6,4},{7,5},{8,10},{9,11},{10,... | collective-permute-start | bytes 122888 | tf_op jit(solution)/shard_map/ppermute | solution.py:302
  32.3 4.1 %collective-permute-start.19 = (bf16[80,256]{1,0:T(8,128)(2,1)S(1)}, bf16[80,256]{1,0:T(8,128)(2,1)S(1)}, u32[]{:S(2)}, u32[]{:S(2)}) collective-permute-start(bf16[80,256]{1,0:T(8,128)(2,1)S(1)} %get-tuple-element.69.refs_3_), channel_id=1, source_target_pairs={{0,1},{1,0},{2,3},{3,2},{4,5},{5,4},{6,7},{7,6},{8,9},{9,8},{10,11... | collective-permute-start | bytes 122888 | tf_op jit(solution)/shard_map/ppermute | solution.py:306
  34.2 2.3 %collective-permute-start.16 = (bf16[80,256]{1,0:T(8,128)(2,1)S(1)}, bf16[80,256]{1,0:T(8,128)(2,1)S(1)}, u32[]{:S(2)}, u32[]{:S(2)}) collective-permute-start(bf16[80,256]{1,0:T(8,128)(2,1)S(1)} %collective-permute-done.13.refs_0_), channel_id=1, source_target_pairs={{0,1},{1,0},{2,3},{3,2},{4,5},{5,4},{6,7},{7,6},{8,9},{9,8},{10,11... | collective-permute-start | bytes 122888 | tf_op jit(solution)/shard_map/ppermute | solution.py:306
  35.9 1.2 %collective-permute-start.17 = (bf16[80,256]{1,0:T(8,128)(2,1)S(1)}, bf16[80,256]{1,0:T(8,128)(2,1)S(1)}, u32[]{:S(2)}, u32[]{:S(2)}) collective-permute-start(bf16[80,256]{1,0:T(8,128)(2,1)S(1)} %collective-permute-done.14.refs_1_), channel_id=1, source_target_pairs={{0,1},{1,0},{2,3},{3,2},{4,5},{5,4},{6,7},{7,6},{8,9},{9,8},{10,11... | collective-permute-start | bytes 122888 | tf_op jit(solution)/shard_map/ppermute | solution.py:306
  36.2 1.2 %collective-permute-start.18 = (bf16[80,256]{1,0:T(8,128)(2,1)S(1)}, bf16[80,256]{1,0:T(8,128)(2,1)S(1)}, u32[]{:S(2)}, u32[]{:S(2)}) collective-permute-start(bf16[80,256]{1,0:T(8,128)(2,1)S(1)} %collective-permute-done.15.refs_2_), channel_id=1, source_target_pairs={{0,1},{1,0},{2,3},{3,2},{4,5},{5,4},{6,7},{7,6},{8,9},{9,8},{10,11... | collective-permute-start | bytes 122888 | tf_op jit(solution)/shard_map/ppermute | solution.py:306
  39.8 1.5 %collective-permute-start.20 = (bf16[320,256]{1,0:T(8,128)(2,1)S(1)}, bf16[320,256]{1,0:T(8,128)(2,1)S(1)}, u32[]{:S(2)}, u32[]{:S(2)}) collective-permute-start(bf16[320,256]{1,0:T(8,128)(2,1)S(1)} %get-tuple-element.71), channel_id=1, source_target_pairs={{0,1},{1,0},{2,3},{3,2},{4,5},{5,4},{6,7},{7,6},{8,9},{9,8},{10,11... | collective-permute-start | bytes 491528 | tf_op jit(solution)/shard_map/ppermute | solution.py:322
  41.3 5.5 %collective-permute-start.21 = (bf16[80,256]{1,0:T(8,128)(2,1)S(1)}, bf16[80,256]{1,0:T(8,128)(2,1)S(1)}, u32[]{:S(2)}, u32[]{:S(2)}) collective-permute-start(bf16[80,256]{1,0:T(8,128)(2,1)S(1)} %get-tuple-element.72), channel_id=1, source_target_pairs={{0,4},{1,5},{2,6},{3,7},{4,0},{5,1},{6,2},{7,3},{8,12},{9,13},{10,... | collective-permute-start | bytes 122888 | tf_op jit(solution)/shard_map/ppermute | solution.py:302
  42.5 5.8 %collective-permute-start.22 = (bf16[80,256]{1,0:T(8,128)(2,1)S(1)}, bf16[80,256]{1,0:T(8,128)(2,1)S(1)}, u32[]{:S(2)}, u32[]{:S(2)}) collective-permute-start(bf16[80,256]{1,0:T(8,128)(2,1)S(1)} %get-tuple-element.73), channel_id=1, source_target_pairs={{0,6},{1,7},{2,4},{3,5},{4,2},{5,3},{6,0},{7,1},{8,14},{9,15},{10,... | collective-permute-start | bytes 122888 | tf_op jit(solution)/shard_map/ppermute | solution.py:302
  43.9 4.4 %collective-permute-start.23 = (bf16[80,256]{1,0:T(8,128)(2,1)S(1)}, bf16[80,256]{1,0:T(8,128)(2,1)S(1)}, u32[]{:S(2)}, u32[]{:S(2)}) collective-permute-start(bf16[80,256]{1,0:T(8,128)(2,1)S(1)} %get-tuple-element.74), channel_id=1, source_target_pairs={{0,2},{1,3},{2,0},{3,1},{4,6},{5,7},{6,4},{7,5},{8,10},{9,11},{10,... | collective-permute-start | bytes 122888 | tf_op jit(solution)/shard_map/ppermute | solution.py:302

commit v6 on v5

--- a/solution.py
+++ b/solution.py
@@ -139,29 +139,20 @@
 
 
 def pack_kernel(group, *refs):
-    sources, block_refs, ahead_ref = refs[:4], refs[4 : 4 + EXPERTS], refs[4 + EXPERTS]
-    held, spread_ref, sems = refs[5 + EXPERTS : -2], refs[-2], refs[-1]
+    sources, block_refs = refs[:3], refs[3 : 3 + EXPERTS]
+    held, spread_ref, sems = refs[3 + EXPERTS : -2], refs[-2], refs[-1]
     copies = [
         pltpu.make_async_copy(source, place, sems.at[i])
         for i, (source, place) in enumerate(zip(sources, held))
     ]
     for copy in copies:
         copy.start()
-    x_ref, gain_ref, routes_ref, gates_ref = held
-    rows, width = x_ref.shape
-    for copy in copies[2:]:
-        copy.wait()
+    x_ref, gain_ref, routes_ref = held
+    copies[2].wait()
     slots = slots_of(upright(routes_ref[...].astype(F32)))
-    lane = lax.broadcasted_iota(jnp.int32, (rows, LANES), 1)
-    meta = jnp.zeros((rows, LANES), F32)
-    for i, column in enumerate([slots, *split_parts(upright(gates_ref[...]))]):
-        meta = jnp.where(lane == i, column.astype(F32), meta)
     chosen = block_map(slots, my_expert(group))
     for copy in copies[:2]:
         copy.wait()
-    for piece in range(width // LANES):
-        ahead_ref[piece * rows : (piece + 1) * rows] = x_ref[:, piece * LANES : (piece + 1) * LANES]
-    ahead_ref[width // LANES * rows :] = meta.astype(BF16)
     normed = normalize(x_ref[...].astype(F32), gain_ref[...])
     write_blocks(normed, chosen, spread_ref, block_refs)
 
@@ -247,11 +238,19 @@
     hand_out(summed(refs[:given]), refs[given:])
 
 
-def carry_kernel(group, routes_ref, gates_ref, ahead_ref, *refs):
+def carry_kernel(group, x_ref, first_routes, first_gates, routes_ref, gates_ref, *refs):
     ins, (out_ref, map_ref, column_ref) = refs[:-3], refs[-3:]
-    rows = ahead_ref.shape[0]
-    out_ref[:rows] = ahead_ref[...]
-    out_ref[rows:] = summed(ins)
+    rows, width = x_ref.shape
+    for piece in range(width // LANES):
+        out_ref[piece * rows : (piece + 1) * rows] = x_ref[:, piece * LANES : (piece + 1) * LANES]
+    filled = width // LANES * rows
+    slots = slots_of(upright(first_routes[...].astype(F32)))
+    lane = lax.broadcasted_iota(jnp.int32, (rows, LANES), 1)
+    meta = jnp.zeros((rows, LANES), F32)
+    for i, column in enumerate([slots, *split_parts(upright(first_gates[...]))]):
+        meta = jnp.where(lane == i, column.astype(F32), meta)
+    out_ref[filled : filled + rows] = meta.astype(BF16)
+    out_ref[filled + rows :] = summed(ins)
     slots = slots_of(upright(routes_ref[...].astype(F32)))
     map_ref[...] = block_map(slots, my_expert(group))
     column_ref[...] = jnp.broadcast_to(upright(gates_ref[...]), column_ref.shape)
@@ -330,11 +329,11 @@
 
     sources = [
         pltpu.with_memory_space_constraint(a, pltpu.HBM)
-        for a in (tokens[0], gain, routes_1, gates_1)
+        for a in (tokens[0], gain, routes_1)
     ]
-    *blocks, travelling = call(
+    *blocks, own = call(
         functools.partial(pack_kernel, group),
-        [block] * EXPERTS + [jax.ShapeDtypeStruct((ahead, LANES), BF16)],
+        [block] * EXPERTS,
         sources,
         8,
         [pltpu.VMEM(a.shape, a.dtype) for a in sources]
@@ -342,7 +341,7 @@
         flops=10**10,
         space=HBM,
     )
-    arrived = across(blocks[:-1])
+    arrived = across(blocks)
     carry, second_map, second_gates = call(
         functools.partial(carry_kernel, group),
         [
@@ -350,7 +349,7 @@
             jax.ShapeDtypeStruct((rows, pad_rows(EXPERTS * CAP)), BF16),
             jax.ShapeDtypeStruct((rows, 128), F32),
         ],
-        [routes_2, gates_2, travelling, *exchanged(experts(shared(blocks[-1:])))],
+        [tokens[0], routes_1, gates_1, routes_2, gates_2, *exchanged(experts(shared([own])))],
         8,
     )
     *ins, carry = lax.optimization_barrier((*shared(arrived), carry))

time: 49.4 us -> 49.4 us (level)
  no operation moved by 1% of the time
where the time goes in v6:
time: 49.4 us; the launch traced here: 49.3 us
  starting transfers between devices  22.2 us (45%)
  waiting for transfers between devices  16.6 us (34%)
  Pallas kernels  10.2 us (21%)
    ppermute x9, starting transfers between devices, across(): lax.ppermute(blocks[i], 'expert', to_expert(i))  12.3 us
    pallas_call x9, Pallas kernels, call(): pl.pallas_call(body, out_shape=outs, in_specs=[space] * len(ins), out_spe...  10.2 us
    ppermute x9, waiting for transfers between devices, across(): lax.ppermute(blocks[i], 'expert', to_expert(i))  9.13 us
    ppermute x3, starting transfers between devices, on_device(): lax.ppermute(sums[i], ('section', 'expert'), onward(i))  5.81 us
    ppermute x3, waiting for transfers between devices, on_device(): lax.ppermute(sums[i], ('section', 'expert'), onward(i))  4.81 us
    ppermute x8, starting transfers between devices, shared(): lax.ppermute(a, 'expert', within(m))  1.78 us
    ppermute x8, waiting for transfers between devices, shared(): lax.ppermute(a, 'expert', within(m))  1.52 us
    ppermute x1, starting transfers between devices, on_device(): lax.ppermute(carry, 'section', [(i, (i + 1) % sections) for i in range(se...  1.49 us
  transfers between devices with their start and end apart: 24, of which 14 were waited for; matrix products, arithmetic and copies ran while one was open for 0% of the time, Pallas kernels for 4%

profile of v6, /device:TPU:0, one launch (start us, length us, event | category | flops | bytes accessed | tf_op | source)
XLA Modules:
  0.0 49.3 jit_solution(8582127123347527867)
XLA Ops:
  0.0 1.6 %shard_map.91 = (bf16[80,256]{1,0:T(8,128)(2,1)S(1)}, bf16[80,256]{1,0:T(8,128)(2,1)S(1)}, bf16[80,256]{1,0:T(8,128)(2,1)S(1)}, bf16[80,256]{1,0:T(8,128)(2,1)S(1)}) custom-call(bf16[16,4096]{1,0:T(8,128)(2,1)} %bitcast.18, f32[1,4096]{1,0:T(1,128)} %refs_4_.1, s32[1,16]{1,0:T(1,128)} %bitcast.20), custom_call_target="tpu_custom_call" | custom-call | flops 10000000000 | bytes 311360 | tf_op jit(solution)/shard_map/pallas_call | solution.py:261
  1.6 0.5 %collective-permute-start.6 = (bf16[80,256]{1,0:T(8,128)(2,1)S(1)}, bf16[80,256]{1,0:T(8,128)(2,1)S(1)}, u32[]{:S(2)}, u32[]{:S(2)}) collective-permute-start(bf16[80,256]{1,0:T(8,128)(2,1)S(1)} %get-tuple-element.43.refs_0_), channel_id=1, source_target_pairs={{0,1},{1,0},{2,3},{3,2},{4,5},{5,4},{6,7},{7,6},{8,9},{9,8},{10,11... | collective-permute-start | bytes 122888 | tf_op jit(solution)/shard_map/ppermute | solution.py:305
  2.1 3.7 %collective-permute-start = (bf16[80,256]{1,0:T(8,128)(2,1)S(1)}, bf16[80,256]{1,0:T(8,128)(2,1)S(1)}, u32[]{:S(2)}, u32[]{:S(2)}) collective-permute-start(bf16[80,256]{1,0:T(8,128)(2,1)S(1)} %get-tuple-element.40), channel_id=1, source_target_pairs={{0,4},{1,5},{2,6},{3,7},{4,0},{5,1},{6,2},{7,3},{8,12},{9,13},{10,... | collective-permute-start | bytes 122888 | tf_op jit(solution)/shard_map/ppermute | solution.py:301
  5.8 1.3 %collective-permute-start.1 = (bf16[80,256]{1,0:T(8,128)(2,1)S(1)}, bf16[80,256]{1,0:T(8,128)(2,1)S(1)}, u32[]{:S(2)}, u32[]{:S(2)}) collective-permute-start(bf16[80,256]{1,0:T(8,128)(2,1)S(1)} %get-tuple-element.41), channel_id=1, source_target_pairs={{0,6},{1,7},{2,4},{3,5},{4,2},{5,3},{6,0},{7,1},{8,14},{9,15},{10,... | collective-permute-start | bytes 122888 | tf_op jit(solution)/shard_map/ppermute | solution.py:301
  7.4 1.8 %shard_map.92 = (bf16[80,256]{1,0:T(8,128)(2,1)S(1)}, bf16[80,256]{1,0:T(8,128)(2,1)S(1)}) custom-call(bf16[4096,512]{1,0:T(8,128)(2,1)S(1)} %bitcast.9, bf16[4096,512]{1,0:T(8,128)(2,1)S(1)} %bitcast.12, bf16[512,4096]{1,0:T(8,128)(2,1)S(1)} %bitcast.15, bf16[80,256]{1,0:T(8,128)(2,1)S(1)} %get-tuple-element.43.refs_0_, ...), custom_call_target="tpu_custom_call" | custom-call | flops 3221225472 | bytes 12746752 | tf_op jit(solution)/shard_map/pallas_call | solution.py:261
  9.4 0.5 collective-permute-start.3
  9.9 1.8 %collective-permute-done.1.refs_1_ = bf16[80,256]{1,0:T(8,128)(2,1)S(1)} collective-permute-done((bf16[80,256]{1,0:T(8,128)(2,1)S(1)}, bf16[80,256]{1,0:T(8,128)(2,1)S(1)}, u32[]{:S(2)}, u32[]{:S(2)}) %collective-permute-start.1) | collective-permute-done | bytes 40992 | tf_op jit(solution)/shard_map/ppermute | solution.py:301
  11.7 0.5 %collective-permute-start.5 = (bf16[80,256]{1,0:T(8,128)(2,1)S(1)}, bf16[80,256]{1,0:T(8,128)(2,1)S(1)}, u32[]{:S(2)}, u32[]{:S(2)}) collective-permute-start(bf16[80,256]{1,0:T(8,128)(2,1)S(1)} %collective-permute-done.2.refs_2_), channel_id=1, source_target_pairs={{0,1},{1,0},{2,3},{3,2},{4,5},{5,4},{6,7},{7,6},{8,9},{9,8},{10,11... | collective-permute-start | bytes 122888 | tf_op jit(solution)/shard_map/ppermute | solution.py:305
  12.5 0.4 collective-permute-done.4.refs_4_
  13.1 2.4 %shard_map.94 = (bf16[240,256]{1,0:T(8,128)(2,1)S(1)}, bf16[240,256]{1,0:T(8,128)(2,1)S(1)}) custom-call(bf16[4096,512]{1,0:T(8,128)(2,1)S(1)} %bitcast.10, bf16[4096,512]{1,0:T(8,128)(2,1)S(1)} %bitcast.13, bf16[512,4096]{1,0:T(8,128)(2,1)S(1)} %bitcast.16, bf16[80,256]{1,0:T(8,128)(2,1)S(1)} %collective-permute-done.refs_0_, ...), custom_call_target="tpu_custom_call" | custom-call | flops 3221225472 | bytes 13074432 | tf_op jit(solution)/shard_map/pallas_call | solution.py:261
  15.4 0.4 collective-permute-start.8
  15.9 1.5 %collective-permute-start.12 = (bf16[352,256]{1,0:T(8,128)(2,1)S(1)}, bf16[352,256]{1,0:T(8,128)(2,1)S(1)}, u32[]{:S(2)}, u32[]{:S(2)}) collective-permute-start(bf16[352,256]{1,0:T(8,128)(2,1)S(1)} %get-tuple-element.61), channel_id=1, source_target_pairs={{0,8},{8,16},{16,24},{24,0},{1,9},{9,17},{17,25},{25,1},{2,10},{10... | collective-permute-start | bytes 540680 | tf_op jit(solution)/shard_map/ppermute | solution.py:358
  17.4 2.5 %collective-permute-start.9 = (bf16[80,256]{1,0:T(8,128)(2,1)S(1)}, bf16[80,256]{1,0:T(8,128)(2,1)S(1)}, u32[]{:S(2)}, u32[]{:S(2)}) collective-permute-start(bf16[80,256]{1,0:T(8,128)(2,1)S(1)} %get-tuple-element.58), channel_id=1, source_target_pairs={{0,12},{1,13},{2,14},{3,15},{4,8},{5,9},{6,10},{7,11},{8,20},{9,21... | collective-permute-start | bytes 122888 | tf_op jit(solution)/shard_map/ppermute | solution.py:360
  19.9 1.9 %collective-permute-start.10 = (bf16[80,256]{1,0:T(8,128)(2,1)S(1)}, bf16[80,256]{1,0:T(8,128)(2,1)S(1)}, u32[]{:S(2)}, u32[]{:S(2)}) collective-permute-start(bf16[80,256]{1,0:T(8,128)(2,1)S(1)} %get-tuple-element.59), channel_id=1, source_target_pairs={{0,14},{1,15},{2,12},{3,13},{4,10},{5,11},{6,8},{7,9},{8,22},{9,23... | collective-permute-start | bytes 122888 | tf_op jit(solution)/shard_map/ppermute | solution.py:360
  21.9 1.4 %collective-permute-start.11 = (bf16[80,256]{1,0:T(8,128)(2,1)S(1)}, bf16[80,256]{1,0:T(8,128)(2,1)S(1)}, u32[]{:S(2)}, u32[]{:S(2)}) collective-permute-start(bf16[80,256]{1,0:T(8,128)(2,1)S(1)} %get-tuple-element.60), channel_id=1, source_target_pairs={{0,10},{1,11},{2,8},{3,9},{4,14},{5,15},{6,12},{7,13},{8,18},{9,19... | collective-permute-start | bytes 122888 | tf_op jit(solution)/shard_map/ppermute | solution.py:360
  23.2 1.0 %collective-permute-done.9.refs_0_ = bf16[80,256]{1,0:T(8,128)(2,1)S(1)} collective-permute-done((bf16[80,256]{1,0:T(8,128)(2,1)S(1)}, bf16[80,256]{1,0:T(8,128)(2,1)S(1)}, u32[]{:S(2)}, u32[]{:S(2)}) %collective-permute-start.9) | collective-permute-done | bytes 40992 | tf_op jit(solution)/shard_map/ppermute | solution.py:360
  24.3 3.5 %collective-permute-done.10.refs_1_ = bf16[80,256]{1,0:T(8,128)(2,1)S(1)} collective-permute-done((bf16[80,256]{1,0:T(8,128)(2,1)S(1)}, bf16[80,256]{1,0:T(8,128)(2,1)S(1)}, u32[]{:S(2)}, u32[]{:S(2)}) %collective-permute-start.10) | collective-permute-done | bytes 40992 | tf_op jit(solution)/shard_map/ppermute | solution.py:360
  28.0 0.7 %shard_map.96 = (bf16[16,4096]{1,0:T(8,128)(2,1)S(1)}, bf16[80,256]{1,0:T(8,128)(2,1)S(1)}, bf16[80,256]{1,0:T(8,128)(2,1)S(1)}, bf16[80,256]{1,0:T(8,128)(2,1)S(1)}, bf16[80,256]{1,0:T(8,128)(2,1)S(1)}) custom-call(bf16[80,256]{1,0:T(8,128)(2,1)S(1)} %collective-permute-done.9.refs_0_, bf16[80,256]{1,0:T(8,128)(2,1)S(1)} %collective-permute-done.10.refs_1_, ...), custom_call_target="tpu_custom_call" | custom-call | bytes 615424 | tf_op jit(solution)/shard_map/pallas_call | solution.py:261
  28.7 1.3 %collective-permute-start.13 = (bf16[80,256]{1,0:T(8,128)(2,1)S(1)}, bf16[80,256]{1,0:T(8,128)(2,1)S(1)}, u32[]{:S(2)}, u32[]{:S(2)}) collective-permute-start(bf16[80,256]{1,0:T(8,128)(2,1)S(1)} %get-tuple-element.64), channel_id=1, source_target_pairs={{0,4},{1,5},{2,6},{3,7},{4,0},{5,1},{6,2},{7,3},{8,12},{9,13},{10,... | collective-permute-start | bytes 122888 | tf_op jit(solution)/shard_map/ppermute | solution.py:301
  30.0 1.7 %collective-permute-start.14 = (bf16[80,256]{1,0:T(8,128)(2,1)S(1)}, bf16[80,256]{1,0:T(8,128)(2,1)S(1)}, u32[]{:S(2)}, u32[]{:S(2)}) collective-permute-start(bf16[80,256]{1,0:T(8,128)(2,1)S(1)} %get-tuple-element.65), channel_id=1, source_target_pairs={{0,6},{1,7},{2,4},{3,5},{4,2},{5,3},{6,0},{7,1},{8,14},{9,15},{10,... | collective-permute-start | bytes 122888 | tf_op jit(solution)/shard_map/ppermute | solution.py:301
  31.7 0.6 %collective-permute-start.15 = (bf16[80,256]{1,0:T(8,128)(2,1)S(1)}, bf16[80,256]{1,0:T(8,128)(2,1)S(1)}, u32[]{:S(2)}, u32[]{:S(2)}) collective-permute-start(bf16[80,256]{1,0:T(8,128)(2,1)S(1)} %get-tuple-element.66), channel_id=1, source_target_pairs={{0,2},{1,3},{2,0},{3,1},{4,6},{5,7},{6,4},{7,5},{8,10},{9,11},{10,... | collective-permute-start | bytes 122888 | tf_op jit(solution)/shard_map/ppermute | solution.py:301
  32.3 1.8 %collective-permute-done.13.refs_0_ = bf16[80,256]{1,0:T(8,128)(2,1)S(1)} collective-permute-done((bf16[80,256]{1,0:T(8,128)(2,1)S(1)}, bf16[80,256]{1,0:T(8,128)(2,1)S(1)}, u32[]{:S(2)}, u32[]{:S(2)}) %collective-permute-start.13) | collective-permute-done | bytes 40992 | tf_op jit(solution)/shard_map/ppermute | solution.py:301
  34.2 1.8 %collective-permute-done.14.refs_1_ = bf16[80,256]{1,0:T(8,128)(2,1)S(1)} collective-permute-done((bf16[80,256]{1,0:T(8,128)(2,1)S(1)}, bf16[80,256]{1,0:T(8,128)(2,1)S(1)}, u32[]{:S(2)}, u32[]{:S(2)}) %collective-permute-start.14) | collective-permute-done | bytes 40992 | tf_op jit(solution)/shard_map/ppermute | solution.py:301
  36.4 0.7 %collective-permute-done.17.refs_5_ = bf16[80,256]{1,0:T(8,128)(2,1)S(1)} collective-permute-done((bf16[80,256]{1,0:T(8,128)(2,1)S(1)}, bf16[80,256]{1,0:T(8,128)(2,1)S(1)}, u32[]{:S(2)}, u32[]{:S(2)}) %collective-permute-start.17) | collective-permute-done | bytes 40992 | tf_op jit(solution)/shard_map/ppermute | solution.py:305
  37.4 2.4 %shard_map.97 = (bf16[320,256]{1,0:T(8,128)(2,1)S(1)}, bf16[320,256]{1,0:T(8,128)(2,1)S(1)}) custom-call(bf16[4096,512]{1,0:T(8,128)(2,1)S(1)} %bitcast.11, bf16[4096,512]{1,0:T(8,128)(2,1)S(1)} %bitcast.14, bf16[512,4096]{1,0:T(8,128)(2,1)S(1)} %bitcast.17, bf16[80,256]{1,0:T(8,128)(2,1)S(1)} %collective-permute-done.13.refs_0_, ...), custom_call_target="tpu_custom_call" | custom-call | flops 3221225472 | bytes 13238272 | tf_op jit(solution)/shard_map/pallas_call | solution.py:261
  40.1 1.1 %collective-permute-done.20.refs_1_ = bf16[320,256]{1,0:T(8,128)(2,1)S(1)} collective-permute-done((bf16[320,256]{1,0:T(8,128)(2,1)S(1)}, bf16[320,256]{1,0:T(8,128)(2,1)S(1)}, u32[]{:S(2)}, u32[]{:S(2)}) %collective-permute-start.20) | collective-permute-done | bytes 163872 | tf_op jit(solution)/shard_map/ppermute | solution.py:321
  41.3 1.2 %collective-permute-start.21 = (bf16[80,256]{1,0:T(8,128)(2,1)S(1)}, bf16[80,256]{1,0:T(8,128)(2,1)S(1)}, u32[]{:S(2)}, u32[]{:S(2)}) collective-permute-start(bf16[80,256]{1,0:T(8,128)(2,1)S(1)} %get-tuple-element.70), channel_id=1, source_target_pairs={{0,4},{1,5},{2,6},{3,7},{4,0},{5,1},{6,2},{7,3},{8,12},{9,13},{10,... | collective-permute-start | bytes 122888 | tf_op jit(solution)/shard_map/ppermute | solution.py:301
  42.5 1.4 %collective-permute-start.22 = (bf16[80,256]{1,0:T(8,128)(2,1)S(1)}, bf16[80,256]{1,0:T(8,128)(2,1)S(1)}, u32[]{:S(2)}, u32[]{:S(2)}) collective-permute-start(bf16[80,256]{1,0:T(8,128)(2,1)S(1)} %get-tuple-element.71), channel_id=1, source_target_pairs={{0,6},{1,7},{2,4},{3,5},{4,2},{5,3},{6,0},{7,1},{8,14},{9,15},{10,... | collective-permute-start | bytes 122888 | tf_op jit(solution)/shard_map/ppermute | solution.py:301
  43.9 1.0 %collective-permute-start.23 = (bf16[80,256]{1,0:T(8,128)(2,1)S(1)}, bf16[80,256]{1,0:T(8,128)(2,1)S(1)}, u32[]{:S(2)}, u32[]{:S(2)}) collective-permute-start(bf16[80,256]{1,0:T(8,128)(2,1)S(1)} %get-tuple-element.72), channel_id=1, source_target_pairs={{0,2},{1,3},{2,0},{3,1},{4,6},{5,7},{6,4},{7,5},{8,10},{9,11},{10,... | collective-permute-start | bytes 122888 | tf_op jit(solution)/shard_map/ppermute | solution.py:301
  44.9 1.9 %collective-permute-done.21.b0 = bf16[80,256]{1,0:T(8,128)(2,1)S(1)} collective-permute-done((bf16[80,256]{1,0:T(8,128)(2,1)S(1)}, bf16[80,256]{1,0:T(8,128)(2,1)S(1)}, u32[]{:S(2)}, u32[]{:S(2)}) %collective-permute-start.21) | collective-permute-done | bytes 40992 | tf_op jit(solution)/shard_map/ppermute | solution.py:301
  46.8 1.5 %collective-permute-done.22.b1 = bf16[80,256]{1,0:T(8,128)(2,1)S(1)} collective-permute-done((bf16[80,256]{1,0:T(8,128)(2,1)S(1)}, bf16[80,256]{1,0:T(8,128)(2,1)S(1)}, u32[]{:S(2)}, u32[]{:S(2)}) %collective-permute-start.22) | collective-permute-done | bytes 40992 | tf_op jit(solution)/shard_map/ppermute | solution.py:301
  48.3 1.0 %shard_map.99 = bf16[16,4096]{1,0:T(8,128)(2,1)} custom-call(bf16[16,4096]{1,0:T(8,128)(2,1)S(1)} %get-tuple-element.63.x_ref, bf16[80,256]{1,0:T(8,128)(2,1)S(1)} %collective-permute-done.21.b0, bf16[80,256]{1,0:T(8,128)(2,1)S(1)} %collective-permute-done.22.b1, bf16[80,256]{1,0:T(8,128)(2,1)S(1)} %collective-permute-done.23.b2, ...), custom_call_target="tpu_custom_call" | custom-call | bytes 435200 | tf_op jit(solution)/shard_map/pallas_call | solution.py:261
  (43 shorter events, 2.3 us)
Async XLA Ops:
  0.0 7.4 %copy-start = (bf16[1,1,4096,512]{3,2,1,0:T(8,128)(2,1)S(1)}, bf16[1,1,4096,512]{3,2,1,0:T(8,128)(2,1)}, u32[]{:S(2)}) copy-start(bf16[1,1,4096,512]{3,2,1,0:T(8,128)(2,1)} %param.15) | copy-start | bytes 12582916
  0.0 7.4 %copy-start.1 = (bf16[1,1,4096,512]{3,2,1,0:T(8,128)(2,1)S(1)}, bf16[1,1,4096,512]{3,2,1,0:T(8,128)(2,1)}, u32[]{:S(2)}) copy-start(bf16[1,1,4096,512]{3,2,1,0:T(8,128)(2,1)} %param.16) | copy-start | bytes 12582916
  0.0 7.4 %copy-start.2 = (bf16[1,1,512,4096]{3,2,1,0:T(8,128)(2,1)S(1)}, bf16[1,1,512,4096]{3,2,1,0:T(8,128)(2,1)}, u32[]{:S(2)}) copy-start(bf16[1,1,512,4096]{3,2,1,0:T(8,128)(2,1)} %param.17) | copy-start | bytes 12582916
  1.6 5.8 %collective-permute-start.6 = (bf16[80,256]{1,0:T(8,128)(2,1)S(1)}, bf16[80,256]{1,0:T(8,128)(2,1)S(1)}, u32[]{:S(2)}, u32[]{:S(2)}) collective-permute-start(bf16[80,256]{1,0:T(8,128)(2,1)S(1)} %get-tuple-element.43.refs_0_), channel_id=1, source_target_pairs={{0,1},{1,0},{2,3},{3,2},{4,5},{5,4},{6,7},{7,6},{8,9},{9,8},{10,11... | collective-permute-start | bytes 122888 | tf_op jit(solution)/shard_map/ppermute | solution.py:305
  2.1 7.3 %collective-permute-start = (bf16[80,256]{1,0:T(8,128)(2,1)S(1)}, bf16[80,256]{1,0:T(8,128)(2,1)S(1)}, u32[]{:S(2)}, u32[]{:S(2)}) collective-permute-start(bf16[80,256]{1,0:T(8,128)(2,1)S(1)} %get-tuple-element.40), channel_id=1, source_target_pairs={{0,4},{1,5},{2,6},{3,7},{4,0},{5,1},{6,2},{7,3},{8,12},{9,13},{10,... | collective-permute-start | bytes 122888 | tf_op jit(solution)/shard_map/ppermute | solution.py:301
  5.8 5.9 %collective-permute-start.1 = (bf16[80,256]{1,0:T(8,128)(2,1)S(1)}, bf16[80,256]{1,0:T(8,128)(2,1)S(1)}, u32[]{:S(2)}, u32[]{:S(2)}) collective-permute-start(bf16[80,256]{1,0:T(8,128)(2,1)S(1)} %get-tuple-element.41), channel_id=1, source_target_pairs={{0,6},{1,7},{2,4},{3,5},{4,2},{5,3},{6,0},{7,1},{8,14},{9,15},{10,... | collective-permute-start | bytes 122888 | tf_op jit(solution)/shard_map/ppermute | solution.py:301
  7.1 4.6 %collective-permute-start.2 = (bf16[80,256]{1,0:T(8,128)(2,1)S(1)}, bf16[80,256]{1,0:T(8,128)(2,1)S(1)}, u32[]{:S(2)}, u32[]{:S(2)}) collective-permute-start(bf16[80,256]{1,0:T(8,128)(2,1)S(1)} %get-tuple-element.42), channel_id=1, source_target_pairs={{0,2},{1,3},{2,0},{3,1},{4,6},{5,7},{6,4},{7,5},{8,10},{9,11},{10,... | collective-permute-start | bytes 122888 | tf_op jit(solution)/shard_map/ppermute | solution.py:301
  7.4 4.8 %copy-start.3 = (bf16[1,16,4096]{2,1,0:T(8,128)(2,1)S(1)}, bf16[1,16,4096]{2,1,0:T(8,128)(2,1)}, u32[]{:S(2)}) copy-start(bf16[1,16,4096]{2,1,0:T(8,128)(2,1)} %param.9) | copy-start | bytes 393220
  7.4 4.8 %copy-start.5 = (s32[1,16,1]{1,2,0:T(1,128)S(1)}, s32[1,16,1]{1,2,0:T(1,128)}, u32[]{:S(2)}) copy-start(s32[1,16,1]{1,2,0:T(1,128)} %param.11) | copy-start | bytes 196
  7.4 4.8 %copy-start.6 = (f32[1,16,1]{1,2,0:T(1,128)S(1)}, f32[1,16,1]{1,2,0:T(1,128)}, u32[]{:S(2)}) copy-start(f32[1,16,1]{1,2,0:T(1,128)} %param.12) | copy-start | bytes 196
  7.4 4.8 %copy-start.7 = (s32[1,16,1]{1,2,0:T(1,128)S(1)}, s32[1,16,1]{1,2,0:T(1,128)}, u32[]{:S(2)}) copy-start(s32[1,16,1]{1,2,0:T(1,128)} %param.13) | copy-start | bytes 196
  9.3 2.9 %collective-permute-start.7 = (bf16[80,256]{1,0:T(8,128)(2,1)S(1)}, bf16[80,256]{1,0:T(8,128)(2,1)S(1)}, u32[]{:S(2)}, u32[]{:S(2)}) collective-permute-start(bf16[80,256]{1,0:T(8,128)(2,1)S(1)} %get-tuple-element.45), channel_id=1, source_target_pairs={{0,1},{1,0},{2,3},{3,2},{4,5},{5,4},{6,7},{7,6},{8,9},{9,8},{10,11... | collective-permute-start | bytes 122888 | tf_op jit(solution)/shard_map/ppermute | solution.py:321
  9.4 3.1 %collective-permute-start.3 = (bf16[80,256]{1,0:T(8,128)(2,1)S(1)}, bf16[80,256]{1,0:T(8,128)(2,1)S(1)}, u32[]{:S(2)}, u32[]{:S(2)}) collective-permute-start(bf16[80,256]{1,0:T(8,128)(2,1)S(1)} %collective-permute-done.refs_0_), channel_id=1, source_target_pairs={{0,1},{1,0},{2,3},{3,2},{4,5},{5,4},{6,7},{7,6},{8,9},{9,8},{10,11... | collective-permute-start | bytes 122888 | tf_op jit(solution)/shard_map/ppermute | solution.py:305
  11.7 1.2 %collective-permute-start.4 = (bf16[80,256]{1,0:T(8,128)(2,1)S(1)}, bf16[80,256]{1,0:T(8,128)(2,1)S(1)}, u32[]{:S(2)}, u32[]{:S(2)}) collective-permute-start(bf16[80,256]{1,0:T(8,128)(2,1)S(1)} %collective-permute-done.1.refs_1_), channel_id=1, source_target_pairs={{0,1},{1,0},{2,3},{3,2},{4,5},{5,4},{6,7},{7,6},{8,9},{9,8},{10,11... | collective-permute-start | bytes 122888 | tf_op jit(solution)/shard_map/ppermute | solution.py:305
  11.7 1.4 %collective-permute-start.5 = (bf16[80,256]{1,0:T(8,128)(2,1)S(1)}, bf16[80,256]{1,0:T(8,128)(2,1)S(1)}, u32[]{:S(2)}, u32[]{:S(2)}) collective-permute-start(bf16[80,256]{1,0:T(8,128)(2,1)S(1)} %collective-permute-done.2.refs_2_), channel_id=1, source_target_pairs={{0,1},{1,0},{2,3},{3,2},{4,5},{5,4},{6,7},{7,6},{8,9},{9,8},{10,11... | collective-permute-start | bytes 122888 | tf_op jit(solution)/shard_map/ppermute | solution.py:305
  13.1 15.0 %copy-start.4 = (f32[1,4096]{1,0:T(1,128)S(1)}, f32[1,4096]{1,0:T(1,128)}, u32[]{:S(2)}) copy-start(f32[1,4096]{1,0:T(1,128)} %refs_4_.1) | copy-start | bytes 49156
  15.4 1.9 %collective-permute-start.8 = (bf16[240,256]{1,0:T(8,128)(2,1)S(1)}, bf16[240,256]{1,0:T(8,128)(2,1)S(1)}, u32[]{:S(2)}, u32[]{:S(2)}) collective-permute-start(bf16[240,256]{1,0:T(8,128)(2,1)S(1)} %get-tuple-element.57), channel_id=1, source_target_pairs={{0,1},{1,0},{2,3},{3,2},{4,5},{5,4},{6,7},{7,6},{8,9},{9,8},{10,11... | collective-permute-start | bytes 368648 | tf_op jit(solution)/shard_map/ppermute | solution.py:321
  15.9 12.2 %collective-permute-start.12 = (bf16[352,256]{1,0:T(8,128)(2,1)S(1)}, bf16[352,256]{1,0:T(8,128)(2,1)S(1)}, u32[]{:S(2)}, u32[]{:S(2)}) collective-permute-start(bf16[352,256]{1,0:T(8,128)(2,1)S(1)} %get-tuple-element.61), channel_id=1, source_target_pairs={{0,8},{8,16},{16,24},{24,0},{1,9},{9,17},{17,25},{25,1},{2,10},{10... | collective-permute-start | bytes 540680 | tf_op jit(solution)/shard_map/ppermute | solution.py:358
  17.4 6.9 %collective-permute-start.9 = (bf16[80,256]{1,0:T(8,128)(2,1)S(1)}, bf16[80,256]{1,0:T(8,128)(2,1)S(1)}, u32[]{:S(2)}, u32[]{:S(2)}) collective-permute-start(bf16[80,256]{1,0:T(8,128)(2,1)S(1)} %get-tuple-element.58), channel_id=1, source_target_pairs={{0,12},{1,13},{2,14},{3,15},{4,8},{5,9},{6,10},{7,11},{8,20},{9,21... | collective-permute-start | bytes 122888 | tf_op jit(solution)/shard_map/ppermute | solution.py:360
  19.9 7.8 %collective-permute-start.10 = (bf16[80,256]{1,0:T(8,128)(2,1)S(1)}, bf16[80,256]{1,0:T(8,128)(2,1)S(1)}, u32[]{:S(2)}, u32[]{:S(2)}) collective-permute-start(bf16[80,256]{1,0:T(8,128)(2,1)S(1)} %get-tuple-element.59), channel_id=1, source_target_pairs={{0,14},{1,15},{2,12},{3,13},{4,10},{5,11},{6,8},{7,9},{8,22},{9,23... | collective-permute-start | bytes 122888 | tf_op jit(solution)/shard_map/ppermute | solution.py:360
  21.9 6.2 %collective-permute-start.11 = (bf16[80,256]{1,0:T(8,128)(2,1)S(1)}, bf16[80,256]{1,0:T(8,128)(2,1)S(1)}, u32[]{:S(2)}, u32[]{:S(2)}) collective-permute-start(bf16[80,256]{1,0:T(8,128)(2,1)S(1)} %get-tuple-element.60), channel_id=1, source_target_pairs={{0,10},{1,11},{2,8},{3,9},{4,14},{5,15},{6,12},{7,13},{8,18},{9,19... | collective-permute-start | bytes 122888 | tf_op jit(solution)/shard_map/ppermute | solution.py:360
  28.7 5.4 %collective-permute-start.13 = (bf16[80,256]{1,0:T(8,128)(2,1)S(1)}, bf16[80,256]{1,0:T(8,128)(2,1)S(1)}, u32[]{:S(2)}, u32[]{:S(2)}) collective-permute-start(bf16[80,256]{1,0:T(8,128)(2,1)S(1)} %get-tuple-element.64), channel_id=1, source_target_pairs={{0,4},{1,5},{2,6},{3,7},{4,0},{5,1},{6,2},{7,3},{8,12},{9,13},{10,... | collective-permute-start | bytes 122888 | tf_op jit(solution)/shard_map/ppermute | solution.py:301
  30.0 5.9 %collective-permute-start.14 = (bf16[80,256]{1,0:T(8,128)(2,1)S(1)}, bf16[80,256]{1,0:T(8,128)(2,1)S(1)}, u32[]{:S(2)}, u32[]{:S(2)}) collective-permute-start(bf16[80,256]{1,0:T(8,128)(2,1)S(1)} %get-tuple-element.65), channel_id=1, source_target_pairs={{0,6},{1,7},{2,4},{3,5},{4,2},{5,3},{6,0},{7,1},{8,14},{9,15},{10,... | collective-permute-start | bytes 122888 | tf_op jit(solution)/shard_map/ppermute | solution.py:301
  31.7 4.4 %collective-permute-start.15 = (bf16[80,256]{1,0:T(8,128)(2,1)S(1)}, bf16[80,256]{1,0:T(8,128)(2,1)S(1)}, u32[]{:S(2)}, u32[]{:S(2)}) collective-permute-start(bf16[80,256]{1,0:T(8,128)(2,1)S(1)} %get-tuple-element.66), channel_id=1, source_target_pairs={{0,2},{1,3},{2,0},{3,1},{4,6},{5,7},{6,4},{7,5},{8,10},{9,11},{10,... | collective-permute-start | bytes 122888 | tf_op jit(solution)/shard_map/ppermute | solution.py:301
  32.3 4.1 %collective-permute-start.19 = (bf16[80,256]{1,0:T(8,128)(2,1)S(1)}, bf16[80,256]{1,0:T(8,128)(2,1)S(1)}, u32[]{:S(2)}, u32[]{:S(2)}) collective-permute-start(bf16[80,256]{1,0:T(8,128)(2,1)S(1)} %get-tuple-element.67.refs_3_), channel_id=1, source_target_pairs={{0,1},{1,0},{2,3},{3,2},{4,5},{5,4},{6,7},{7,6},{8,9},{9,8},{10,11... | collective-permute-start | bytes 122888 | tf_op jit(solution)/shard_map/ppermute | solution.py:305
  34.2 2.3 %collective-permute-start.16 = (bf16[80,256]{1,0:T(8,128)(2,1)S(1)}, bf16[80,256]{1,0:T(8,128)(2,1)S(1)}, u32[]{:S(2)}, u32[]{:S(2)}) collective-permute-start(bf16[80,256]{1,0:T(8,128)(2,1)S(1)} %collective-permute-done.13.refs_0_), channel_id=1, source_target_pairs={{0,1},{1,0},{2,3},{3,2},{4,5},{5,4},{6,7},{7,6},{8,9},{9,8},{10,11... | collective-permute-start | bytes 122888 | tf_op jit(solution)/shard_map/ppermute | solution.py:305
  35.9 1.2 %collective-permute-start.17 = (bf16[80,256]{1,0:T(8,128)(2,1)S(1)}, bf16[80,256]{1,0:T(8,128)(2,1)S(1)}, u32[]{:S(2)}, u32[]{:S(2)}) collective-permute-start(bf16[80,256]{1,0:T(8,128)(2,1)S(1)} %collective-permute-done.14.refs_1_), channel_id=1, source_target_pairs={{0,1},{1,0},{2,3},{3,2},{4,5},{5,4},{6,7},{7,6},{8,9},{9,8},{10,11... | collective-permute-start | bytes 122888 | tf_op jit(solution)/shard_map/ppermute | solution.py:305
  36.2 1.2 %collective-permute-start.18 = (bf16[80,256]{1,0:T(8,128)(2,1)S(1)}, bf16[80,256]{1,0:T(8,128)(2,1)S(1)}, u32[]{:S(2)}, u32[]{:S(2)}) collective-permute-start(bf16[80,256]{1,0:T(8,128)(2,1)S(1)} %collective-permute-done.15.refs_2_), channel_id=1, source_target_pairs={{0,1},{1,0},{2,3},{3,2},{4,5},{5,4},{6,7},{7,6},{8,9},{9,8},{10,11... | collective-permute-start | bytes 122888 | tf_op jit(solution)/shard_map/ppermute | solution.py:305
  39.8 1.5 %collective-permute-start.20 = (bf16[320,256]{1,0:T(8,128)(2,1)S(1)}, bf16[320,256]{1,0:T(8,128)(2,1)S(1)}, u32[]{:S(2)}, u32[]{:S(2)}) collective-permute-start(bf16[320,256]{1,0:T(8,128)(2,1)S(1)} %get-tuple-element.69), channel_id=1, source_target_pairs={{0,1},{1,0},{2,3},{3,2},{4,5},{5,4},{6,7},{7,6},{8,9},{9,8},{10,11... | collective-permute-start | bytes 491528 | tf_op jit(solution)/shard_map/ppermute | solution.py:321
  41.3 5.5 %collective-permute-start.21 = (bf16[80,256]{1,0:T(8,128)(2,1)S(1)}, bf16[80,256]{1,0:T(8,128)(2,1)S(1)}, u32[]{:S(2)}, u32[]{:S(2)}) collective-permute-start(bf16[80,256]{1,0:T(8,128)(2,1)S(1)} %get-tuple-element.70), channel_id=1, source_target_pairs={{0,4},{1,5},{2,6},{3,7},{4,0},{5,1},{6,2},{7,3},{8,12},{9,13},{10,... | collective-permute-start | bytes 122888 | tf_op jit(solution)/shard_map/ppermute | solution.py:301
  42.5 5.8 %collective-permute-start.22 = (bf16[80,256]{1,0:T(8,128)(2,1)S(1)}, bf16[80,256]{1,0:T(8,128)(2,1)S(1)}, u32[]{:S(2)}, u32[]{:S(2)}) collective-permute-start(bf16[80,256]{1,0:T(8,128)(2,1)S(1)} %get-tuple-element.71), channel_id=1, source_target_pairs={{0,6},{1,7},{2,4},{3,5},{4,2},{5,3},{6,0},{7,1},{8,14},{9,15},{10,... | collective-permute-start | bytes 122888 | tf_op jit(solution)/shard_map/ppermute | solution.py:301
  43.9 4.4 %collective-permute-start.23 = (bf16[80,256]{1,0:T(8,128)(2,1)S(1)}, bf16[80,256]{1,0:T(8,128)(2,1)S(1)}, u32[]{:S(2)}, u32[]{:S(2)}) collective-permute-start(bf16[80,256]{1,0:T(8,128)(2,1)S(1)} %get-tuple-element.72), channel_id=1, source_target_pairs={{0,2},{1,3},{2,0},{3,1},{4,6},{5,7},{6,4},{7,5},{8,10},{9,11},{10,... | collective-permute-start | bytes 122888 | tf_op jit(solution)/shard_map/ppermute | solution.py:301
  (1 other events, 4.8 us)

commit v7 on v3

--- a/solution.py
+++ b/solution.py
@@ -37,7 +37,7 @@
 
 
 def spread_scratch(rows, width):
-    return pltpu.VMEM((LANES // 128, rows * width // LANES, 128), F32)
+    return pltpu.VMEM((LANES // 128, (rows + 1) * width // LANES, 128), F32)
 
 
 def spread(values, spread_ref, width, start=0):
@@ -221,7 +221,7 @@
 def expert_kernel(given, w_gate, w_up, w_down, *refs):
     ins, outs, spread_ref = refs[:given], refs[given:-1], refs[-1]
     width = w_gate.shape[0]
-    rows = spread_ref.shape[1] * LANES // width
+    rows = spread_ref.shape[1] * LANES // width - 1
     from_blocks([ref[...] for ref in ins], spread_ref)
     x = gathered(spread_ref, rows, width)
     gate_val = jnp.dot(x, w_gate[...], preferred_element_type=F32)

time: 49.4 us -> 49.4 us (level)
  no operation moved by 1% of the time
where the time goes in v7:
time: 49.4 us; the launch traced here: 49.3 us
  starting transfers between devices  22.2 us (45%)
  waiting for transfers between devices  16.7 us (34%)
  Pallas kernels  10.2 us (21%)
    ppermute x9, starting transfers between devices, across(): lax.ppermute(blocks[i], 'expert', to_expert(i))  12.3 us
    pallas_call x9, Pallas kernels, call(): pl.pallas_call(body, out_shape=outs, in_specs=[space] * len(ins), out_spe...  10.2 us
    ppermute x9, waiting for transfers between devices, across(): lax.ppermute(blocks[i], 'expert', to_expert(i))  9.17 us
    ppermute x3, starting transfers between devices, on_device(): lax.ppermute(sums[i], ('section', 'expert'), onward(i))  5.81 us
    ppermute x3, waiting for transfers between devices, on_device(): lax.ppermute(sums[i], ('section', 'expert'), onward(i))  4.81 us
    ppermute x8, starting transfers between devices, shared(): lax.ppermute(a, 'expert', within(m))  1.78 us
    ppermute x8, waiting for transfers between devices, shared(): lax.ppermute(a, 'expert', within(m))  1.55 us
    ppermute x1, starting transfers between devices, on_device(): lax.ppermute(carry, 'section', [(i, (i + 1) % sections) for i in range(se...  1.49 us
  transfers between devices with their start and end apart: 24, of which 14 were waited for; matrix products, arithmetic and copies ran while one was open for 0% of the time, Pallas kernels for 4%

profile of v7, /device:TPU:0, one launch (start us, length us, event | category | flops | bytes accessed | tf_op | source)
XLA Modules:
  0.0 49.3 jit_solution(17768604241797679552)
XLA Ops:
  0.0 1.6 %shard_map.91 = (bf16[80,256]{1,0:T(8,128)(2,1)S(1)}, bf16[80,256]{1,0:T(8,128)(2,1)S(1)}, bf16[80,256]{1,0:T(8,128)(2,1)S(1)}, bf16[80,256]{1,0:T(8,128)(2,1)S(1)}, bf16[272,256]{1,0:T(8,128)(2,1)S(1)}) custom-call(bf16[16,4096]{1,0:T(8,128)(2,1)} %bitcast.20, f32[1,4096]{1,0:T(1,128)} %refs_4_.1, s32[1,16]{1,0:T(1,128)} %bitcast.21, f32[1,16]{1,0:T(1,128)} %bitcast.22), custom_call_target="tpu_custom_call" | custom-call | flops 10000000000 | bytes 450688 | tf_op jit(solution)/shard_map/pallas_call | solution.py:259
  1.6 0.5 %collective-permute-start.6 = (bf16[80,256]{1,0:T(8,128)(2,1)S(1)}, bf16[80,256]{1,0:T(8,128)(2,1)S(1)}, u32[]{:S(2)}, u32[]{:S(2)}) collective-permute-start(bf16[80,256]{1,0:T(8,128)(2,1)S(1)} %get-tuple-element.45.refs_0_), channel_id=1, source_target_pairs={{0,1},{1,0},{2,3},{3,2},{4,5},{5,4},{6,7},{7,6},{8,9},{9,8},{10,11... | collective-permute-start | bytes 122888 | tf_op jit(solution)/shard_map/ppermute | solution.py:303
  2.1 3.7 %collective-permute-start = (bf16[80,256]{1,0:T(8,128)(2,1)S(1)}, bf16[80,256]{1,0:T(8,128)(2,1)S(1)}, u32[]{:S(2)}, u32[]{:S(2)}) collective-permute-start(bf16[80,256]{1,0:T(8,128)(2,1)S(1)} %get-tuple-element.41), channel_id=1, source_target_pairs={{0,4},{1,5},{2,6},{3,7},{4,0},{5,1},{6,2},{7,3},{8,12},{9,13},{10,... | collective-permute-start | bytes 122888 | tf_op jit(solution)/shard_map/ppermute | solution.py:299
  5.8 1.3 %collective-permute-start.1 = (bf16[80,256]{1,0:T(8,128)(2,1)S(1)}, bf16[80,256]{1,0:T(8,128)(2,1)S(1)}, u32[]{:S(2)}, u32[]{:S(2)}) collective-permute-start(bf16[80,256]{1,0:T(8,128)(2,1)S(1)} %get-tuple-element.42), channel_id=1, source_target_pairs={{0,6},{1,7},{2,4},{3,5},{4,2},{5,3},{6,0},{7,1},{8,14},{9,15},{10,... | collective-permute-start | bytes 122888 | tf_op jit(solution)/shard_map/ppermute | solution.py:299
  7.4 1.8 %shard_map.92 = (bf16[80,256]{1,0:T(8,128)(2,1)S(1)}, bf16[80,256]{1,0:T(8,128)(2,1)S(1)}) custom-call(bf16[4096,512]{1,0:T(8,128)(2,1)S(1)} %bitcast.9, bf16[4096,512]{1,0:T(8,128)(2,1)S(1)} %bitcast.12, bf16[512,4096]{1,0:T(8,128)(2,1)S(1)} %bitcast.15, bf16[80,256]{1,0:T(8,128)(2,1)S(1)} %get-tuple-element.45.refs_0_, ...), custom_call_target="tpu_custom_call" | custom-call | flops 3221225472 | bytes 12746752 | tf_op jit(solution)/shard_map/pallas_call | solution.py:259
  9.4 0.5 collective-permute-start.3
  9.8 1.9 %collective-permute-done.1.refs_1_ = bf16[80,256]{1,0:T(8,128)(2,1)S(1)} collective-permute-done((bf16[80,256]{1,0:T(8,128)(2,1)S(1)}, bf16[80,256]{1,0:T(8,128)(2,1)S(1)}, u32[]{:S(2)}, u32[]{:S(2)}) %collective-permute-start.1) | collective-permute-done | bytes 40992 | tf_op jit(solution)/shard_map/ppermute | solution.py:299
  11.7 0.5 %collective-permute-start.5 = (bf16[80,256]{1,0:T(8,128)(2,1)S(1)}, bf16[80,256]{1,0:T(8,128)(2,1)S(1)}, u32[]{:S(2)}, u32[]{:S(2)}) collective-permute-start(bf16[80,256]{1,0:T(8,128)(2,1)S(1)} %collective-permute-done.2.refs_2_), channel_id=1, source_target_pairs={{0,1},{1,0},{2,3},{3,2},{4,5},{5,4},{6,7},{7,6},{8,9},{9,8},{10,11... | collective-permute-start | bytes 122888 | tf_op jit(solution)/shard_map/ppermute | solution.py:303
  12.5 0.4 collective-permute-done.4.refs_4_
  13.1 2.4 %shard_map.94 = (bf16[240,256]{1,0:T(8,128)(2,1)S(1)}, bf16[240,256]{1,0:T(8,128)(2,1)S(1)}) custom-call(bf16[4096,512]{1,0:T(8,128)(2,1)S(1)} %bitcast.10, bf16[4096,512]{1,0:T(8,128)(2,1)S(1)} %bitcast.13, bf16[512,4096]{1,0:T(8,128)(2,1)S(1)} %bitcast.16, bf16[80,256]{1,0:T(8,128)(2,1)S(1)} %collective-permute-done.refs_0_, ...), custom_call_target="tpu_custom_call" | custom-call | flops 3221225472 | bytes 13074432 | tf_op jit(solution)/shard_map/pallas_call | solution.py:259
  15.5 0.4 collective-permute-start.8
  15.9 1.5 %collective-permute-start.12 = (bf16[352,256]{1,0:T(8,128)(2,1)S(1)}, bf16[352,256]{1,0:T(8,128)(2,1)S(1)}, u32[]{:S(2)}, u32[]{:S(2)}) collective-permute-start(bf16[352,256]{1,0:T(8,128)(2,1)S(1)} %get-tuple-element.63), channel_id=1, source_target_pairs={{0,8},{8,16},{16,24},{24,0},{1,9},{9,17},{17,25},{25,1},{2,10},{10... | collective-permute-start | bytes 540680 | tf_op jit(solution)/shard_map/ppermute | solution.py:356
  17.4 2.5 %collective-permute-start.9 = (bf16[80,256]{1,0:T(8,128)(2,1)S(1)}, bf16[80,256]{1,0:T(8,128)(2,1)S(1)}, u32[]{:S(2)}, u32[]{:S(2)}) collective-permute-start(bf16[80,256]{1,0:T(8,128)(2,1)S(1)} %get-tuple-element.60), channel_id=1, source_target_pairs={{0,12},{1,13},{2,14},{3,15},{4,8},{5,9},{6,10},{7,11},{8,20},{9,21... | collective-permute-start | bytes 122888 | tf_op jit(solution)/shard_map/ppermute | solution.py:358
  19.9 1.9 %collective-permute-start.10 = (bf16[80,256]{1,0:T(8,128)(2,1)S(1)}, bf16[80,256]{1,0:T(8,128)(2,1)S(1)}, u32[]{:S(2)}, u32[]{:S(2)}) collective-permute-start(bf16[80,256]{1,0:T(8,128)(2,1)S(1)} %get-tuple-element.61), channel_id=1, source_target_pairs={{0,14},{1,15},{2,12},{3,13},{4,10},{5,11},{6,8},{7,9},{8,22},{9,23... | collective-permute-start | bytes 122888 | tf_op jit(solution)/shard_map/ppermute | solution.py:358
  21.9 1.4 %collective-permute-start.11 = (bf16[80,256]{1,0:T(8,128)(2,1)S(1)}, bf16[80,256]{1,0:T(8,128)(2,1)S(1)}, u32[]{:S(2)}, u32[]{:S(2)}) collective-permute-start(bf16[80,256]{1,0:T(8,128)(2,1)S(1)} %get-tuple-element.62), channel_id=1, source_target_pairs={{0,10},{1,11},{2,8},{3,9},{4,14},{5,15},{6,12},{7,13},{8,18},{9,19... | collective-permute-start | bytes 122888 | tf_op jit(solution)/shard_map/ppermute | solution.py:358
  23.2 1.0 %collective-permute-done.9.refs_0_ = bf16[80,256]{1,0:T(8,128)(2,1)S(1)} collective-permute-done((bf16[80,256]{1,0:T(8,128)(2,1)S(1)}, bf16[80,256]{1,0:T(8,128)(2,1)S(1)}, u32[]{:S(2)}, u32[]{:S(2)}) %collective-permute-start.9) | collective-permute-done | bytes 40992 | tf_op jit(solution)/shard_map/ppermute | solution.py:358
  24.3 3.5 %collective-permute-done.10.refs_1_ = bf16[80,256]{1,0:T(8,128)(2,1)S(1)} collective-permute-done((bf16[80,256]{1,0:T(8,128)(2,1)S(1)}, bf16[80,256]{1,0:T(8,128)(2,1)S(1)}, u32[]{:S(2)}, u32[]{:S(2)}) %collective-permute-start.10) | collective-permute-done | bytes 40992 | tf_op jit(solution)/shard_map/ppermute | solution.py:358
  28.0 0.7 %shard_map.96 = (bf16[16,4096]{1,0:T(8,128)(2,1)S(1)}, bf16[80,256]{1,0:T(8,128)(2,1)S(1)}, bf16[80,256]{1,0:T(8,128)(2,1)S(1)}, bf16[80,256]{1,0:T(8,128)(2,1)S(1)}, bf16[80,256]{1,0:T(8,128)(2,1)S(1)}) custom-call(bf16[80,256]{1,0:T(8,128)(2,1)S(1)} %collective-permute-done.9.refs_0_, bf16[80,256]{1,0:T(8,128)(2,1)S(1)} %collective-permute-done.10.refs_1_, ...), custom_call_target="tpu_custom_call" | custom-call | bytes 615424 | tf_op jit(solution)/shard_map/pallas_call | solution.py:259
  28.8 1.3 %collective-permute-start.13 = (bf16[80,256]{1,0:T(8,128)(2,1)S(1)}, bf16[80,256]{1,0:T(8,128)(2,1)S(1)}, u32[]{:S(2)}, u32[]{:S(2)}) collective-permute-start(bf16[80,256]{1,0:T(8,128)(2,1)S(1)} %get-tuple-element.66), channel_id=1, source_target_pairs={{0,4},{1,5},{2,6},{3,7},{4,0},{5,1},{6,2},{7,3},{8,12},{9,13},{10,... | collective-permute-start | bytes 122888 | tf_op jit(solution)/shard_map/ppermute | solution.py:299
  30.0 1.7 %collective-permute-start.14 = (bf16[80,256]{1,0:T(8,128)(2,1)S(1)}, bf16[80,256]{1,0:T(8,128)(2,1)S(1)}, u32[]{:S(2)}, u32[]{:S(2)}) collective-permute-start(bf16[80,256]{1,0:T(8,128)(2,1)S(1)} %get-tuple-element.67), channel_id=1, source_target_pairs={{0,6},{1,7},{2,4},{3,5},{4,2},{5,3},{6,0},{7,1},{8,14},{9,15},{10,... | collective-permute-start | bytes 122888 | tf_op jit(solution)/shard_map/ppermute | solution.py:299
  31.7 0.6 %collective-permute-start.15 = (bf16[80,256]{1,0:T(8,128)(2,1)S(1)}, bf16[80,256]{1,0:T(8,128)(2,1)S(1)}, u32[]{:S(2)}, u32[]{:S(2)}) collective-permute-start(bf16[80,256]{1,0:T(8,128)(2,1)S(1)} %get-tuple-element.68), channel_id=1, source_target_pairs={{0,2},{1,3},{2,0},{3,1},{4,6},{5,7},{6,4},{7,5},{8,10},{9,11},{10,... | collective-permute-start | bytes 122888 | tf_op jit(solution)/shard_map/ppermute | solution.py:299
  32.3 1.8 %collective-permute-done.13.refs_0_ = bf16[80,256]{1,0:T(8,128)(2,1)S(1)} collective-permute-done((bf16[80,256]{1,0:T(8,128)(2,1)S(1)}, bf16[80,256]{1,0:T(8,128)(2,1)S(1)}, u32[]{:S(2)}, u32[]{:S(2)}) %collective-permute-start.13) | collective-permute-done | bytes 40992 | tf_op jit(solution)/shard_map/ppermute | solution.py:299
  34.2 1.8 %collective-permute-done.14.refs_1_ = bf16[80,256]{1,0:T(8,128)(2,1)S(1)} collective-permute-done((bf16[80,256]{1,0:T(8,128)(2,1)S(1)}, bf16[80,256]{1,0:T(8,128)(2,1)S(1)}, u32[]{:S(2)}, u32[]{:S(2)}) %collective-permute-start.14) | collective-permute-done | bytes 40992 | tf_op jit(solution)/shard_map/ppermute | solution.py:299
  36.4 0.7 %collective-permute-done.17.refs_5_ = bf16[80,256]{1,0:T(8,128)(2,1)S(1)} collective-permute-done((bf16[80,256]{1,0:T(8,128)(2,1)S(1)}, bf16[80,256]{1,0:T(8,128)(2,1)S(1)}, u32[]{:S(2)}, u32[]{:S(2)}) %collective-permute-start.17) | collective-permute-done | bytes 40992 | tf_op jit(solution)/shard_map/ppermute | solution.py:303
  37.4 2.4 %shard_map.97 = (bf16[320,256]{1,0:T(8,128)(2,1)S(1)}, bf16[320,256]{1,0:T(8,128)(2,1)S(1)}) custom-call(bf16[4096,512]{1,0:T(8,128)(2,1)S(1)} %bitcast.11, bf16[4096,512]{1,0:T(8,128)(2,1)S(1)} %bitcast.14, bf16[512,4096]{1,0:T(8,128)(2,1)S(1)} %bitcast.17, bf16[80,256]{1,0:T(8,128)(2,1)S(1)} %collective-permute-done.13.refs_0_, ...), custom_call_target="tpu_custom_call" | custom-call | flops 3221225472 | bytes 13238272 | tf_op jit(solution)/shard_map/pallas_call | solution.py:259
  40.1 1.1 %collective-permute-done.20.refs_1_ = bf16[320,256]{1,0:T(8,128)(2,1)S(1)} collective-permute-done((bf16[320,256]{1,0:T(8,128)(2,1)S(1)}, bf16[320,256]{1,0:T(8,128)(2,1)S(1)}, u32[]{:S(2)}, u32[]{:S(2)}) %collective-permute-start.20) | collective-permute-done | bytes 163872 | tf_op jit(solution)/shard_map/ppermute | solution.py:319
  41.3 1.2 %collective-permute-start.21 = (bf16[80,256]{1,0:T(8,128)(2,1)S(1)}, bf16[80,256]{1,0:T(8,128)(2,1)S(1)}, u32[]{:S(2)}, u32[]{:S(2)}) collective-permute-start(bf16[80,256]{1,0:T(8,128)(2,1)S(1)} %get-tuple-element.72), channel_id=1, source_target_pairs={{0,4},{1,5},{2,6},{3,7},{4,0},{5,1},{6,2},{7,3},{8,12},{9,13},{10,... | collective-permute-start | bytes 122888 | tf_op jit(solution)/shard_map/ppermute | solution.py:299
  42.5 1.4 %collective-permute-start.22 = (bf16[80,256]{1,0:T(8,128)(2,1)S(1)}, bf16[80,256]{1,0:T(8,128)(2,1)S(1)}, u32[]{:S(2)}, u32[]{:S(2)}) collective-permute-start(bf16[80,256]{1,0:T(8,128)(2,1)S(1)} %get-tuple-element.73), channel_id=1, source_target_pairs={{0,6},{1,7},{2,4},{3,5},{4,2},{5,3},{6,0},{7,1},{8,14},{9,15},{10,... | collective-permute-start | bytes 122888 | tf_op jit(solution)/shard_map/ppermute | solution.py:299
  43.9 1.0 %collective-permute-start.23 = (bf16[80,256]{1,0:T(8,128)(2,1)S(1)}, bf16[80,256]{1,0:T(8,128)(2,1)S(1)}, u32[]{:S(2)}, u32[]{:S(2)}) collective-permute-start(bf16[80,256]{1,0:T(8,128)(2,1)S(1)} %get-tuple-element.74), channel_id=1, source_target_pairs={{0,2},{1,3},{2,0},{3,1},{4,6},{5,7},{6,4},{7,5},{8,10},{9,11},{10,... | collective-permute-start | bytes 122888 | tf_op jit(solution)/shard_map/ppermute | solution.py:299
  44.9 1.9 %collective-permute-done.21.b0 = bf16[80,256]{1,0:T(8,128)(2,1)S(1)} collective-permute-done((bf16[80,256]{1,0:T(8,128)(2,1)S(1)}, bf16[80,256]{1,0:T(8,128)(2,1)S(1)}, u32[]{:S(2)}, u32[]{:S(2)}) %collective-permute-start.21) | collective-permute-done | bytes 40992 | tf_op jit(solution)/shard_map/ppermute | solution.py:299
  46.8 1.5 %collective-permute-done.22.b1 = bf16[80,256]{1,0:T(8,128)(2,1)S(1)} collective-permute-done((bf16[80,256]{1,0:T(8,128)(2,1)S(1)}, bf16[80,256]{1,0:T(8,128)(2,1)S(1)}, u32[]{:S(2)}, u32[]{:S(2)}) %collective-permute-start.22) | collective-permute-done | bytes 40992 | tf_op jit(solution)/shard_map/ppermute | solution.py:299
  48.3 1.0 %shard_map.99 = bf16[16,4096]{1,0:T(8,128)(2,1)} custom-call(bf16[16,4096]{1,0:T(8,128)(2,1)S(1)} %get-tuple-element.65.x_ref, bf16[80,256]{1,0:T(8,128)(2,1)S(1)} %collective-permute-done.21.b0, bf16[80,256]{1,0:T(8,128)(2,1)S(1)} %collective-permute-done.22.b1, bf16[80,256]{1,0:T(8,128)(2,1)S(1)} %collective-permute-done.23.b2, ...), custom_call_target="tpu_custom_call" | custom-call | bytes 435200 | tf_op jit(solution)/shard_map/pallas_call | solution.py:259
  (37 shorter events, 2.3 us)
Async XLA Ops:
  0.0 7.4 %copy-start = (bf16[1,1,4096,512]{3,2,1,0:T(8,128)(2,1)S(1)}, bf16[1,1,4096,512]{3,2,1,0:T(8,128)(2,1)}, u32[]{:S(2)}) copy-start(bf16[1,1,4096,512]{3,2,1,0:T(8,128)(2,1)} %param.15) | copy-start | bytes 12582916
  0.0 7.4 %copy-start.1 = (bf16[1,1,4096,512]{3,2,1,0:T(8,128)(2,1)S(1)}, bf16[1,1,4096,512]{3,2,1,0:T(8,128)(2,1)}, u32[]{:S(2)}) copy-start(bf16[1,1,4096,512]{3,2,1,0:T(8,128)(2,1)} %param.16) | copy-start | bytes 12582916
  0.0 7.4 %copy-start.2 = (bf16[1,1,512,4096]{3,2,1,0:T(8,128)(2,1)S(1)}, bf16[1,1,512,4096]{3,2,1,0:T(8,128)(2,1)}, u32[]{:S(2)}) copy-start(bf16[1,1,512,4096]{3,2,1,0:T(8,128)(2,1)} %param.17) | copy-start | bytes 12582916
  1.6 5.8 %collective-permute-start.6 = (bf16[80,256]{1,0:T(8,128)(2,1)S(1)}, bf16[80,256]{1,0:T(8,128)(2,1)S(1)}, u32[]{:S(2)}, u32[]{:S(2)}) collective-permute-start(bf16[80,256]{1,0:T(8,128)(2,1)S(1)} %get-tuple-element.45.refs_0_), channel_id=1, source_target_pairs={{0,1},{1,0},{2,3},{3,2},{4,5},{5,4},{6,7},{7,6},{8,9},{9,8},{10,11... | collective-permute-start | bytes 122888 | tf_op jit(solution)/shard_map/ppermute | solution.py:303
  2.1 7.2 %collective-permute-start = (bf16[80,256]{1,0:T(8,128)(2,1)S(1)}, bf16[80,256]{1,0:T(8,128)(2,1)S(1)}, u32[]{:S(2)}, u32[]{:S(2)}) collective-permute-start(bf16[80,256]{1,0:T(8,128)(2,1)S(1)} %get-tuple-element.41), channel_id=1, source_target_pairs={{0,4},{1,5},{2,6},{3,7},{4,0},{5,1},{6,2},{7,3},{8,12},{9,13},{10,... | collective-permute-start | bytes 122888 | tf_op jit(solution)/shard_map/ppermute | solution.py:299
  5.8 5.9 %collective-permute-start.1 = (bf16[80,256]{1,0:T(8,128)(2,1)S(1)}, bf16[80,256]{1,0:T(8,128)(2,1)S(1)}, u32[]{:S(2)}, u32[]{:S(2)}) collective-permute-start(bf16[80,256]{1,0:T(8,128)(2,1)S(1)} %get-tuple-element.42), channel_id=1, source_target_pairs={{0,6},{1,7},{2,4},{3,5},{4,2},{5,3},{6,0},{7,1},{8,14},{9,15},{10,... | collective-permute-start | bytes 122888 | tf_op jit(solution)/shard_map/ppermute | solution.py:299
  7.1 4.6 %collective-permute-start.2 = (bf16[80,256]{1,0:T(8,128)(2,1)S(1)}, bf16[80,256]{1,0:T(8,128)(2,1)S(1)}, u32[]{:S(2)}, u32[]{:S(2)}) collective-permute-start(bf16[80,256]{1,0:T(8,128)(2,1)S(1)} %get-tuple-element.43), channel_id=1, source_target_pairs={{0,2},{1,3},{2,0},{3,1},{4,6},{5,7},{6,4},{7,5},{8,10},{9,11},{10,... | collective-permute-start | bytes 122888 | tf_op jit(solution)/shard_map/ppermute | solution.py:299
  7.4 4.8 %copy-start.4 = (s32[1,16,1]{1,2,0:T(1,128)S(1)}, s32[1,16,1]{1,2,0:T(1,128)}, u32[]{:S(2)}) copy-start(s32[1,16,1]{1,2,0:T(1,128)} %param.13) | copy-start | bytes 196
  7.4 4.8 %copy-start.5 = (f32[1,16,1]{1,2,0:T(1,128)S(1)}, f32[1,16,1]{1,2,0:T(1,128)}, u32[]{:S(2)}) copy-start(f32[1,16,1]{1,2,0:T(1,128)} %param.14) | copy-start | bytes 196
  9.3 3.0 %collective-permute-start.7 = (bf16[80,256]{1,0:T(8,128)(2,1)S(1)}, bf16[80,256]{1,0:T(8,128)(2,1)S(1)}, u32[]{:S(2)}, u32[]{:S(2)}) collective-permute-start(bf16[80,256]{1,0:T(8,128)(2,1)S(1)} %get-tuple-element.47), channel_id=1, source_target_pairs={{0,1},{1,0},{2,3},{3,2},{4,5},{5,4},{6,7},{7,6},{8,9},{9,8},{10,11... | collective-permute-start | bytes 122888 | tf_op jit(solution)/shard_map/ppermute | solution.py:319
  9.4 3.2 %collective-permute-start.3 = (bf16[80,256]{1,0:T(8,128)(2,1)S(1)}, bf16[80,256]{1,0:T(8,128)(2,1)S(1)}, u32[]{:S(2)}, u32[]{:S(2)}) collective-permute-start(bf16[80,256]{1,0:T(8,128)(2,1)S(1)} %collective-permute-done.refs_0_), channel_id=1, source_target_pairs={{0,1},{1,0},{2,3},{3,2},{4,5},{5,4},{6,7},{7,6},{8,9},{9,8},{10,11... | collective-permute-start | bytes 122888 | tf_op jit(solution)/shard_map/ppermute | solution.py:303
  11.7 1.2 %collective-permute-start.4 = (bf16[80,256]{1,0:T(8,128)(2,1)S(1)}, bf16[80,256]{1,0:T(8,128)(2,1)S(1)}, u32[]{:S(2)}, u32[]{:S(2)}) collective-permute-start(bf16[80,256]{1,0:T(8,128)(2,1)S(1)} %collective-permute-done.1.refs_1_), channel_id=1, source_target_pairs={{0,1},{1,0},{2,3},{3,2},{4,5},{5,4},{6,7},{7,6},{8,9},{9,8},{10,11... | collective-permute-start | bytes 122888 | tf_op jit(solution)/shard_map/ppermute | solution.py:303
  11.7 1.4 %collective-permute-start.5 = (bf16[80,256]{1,0:T(8,128)(2,1)S(1)}, bf16[80,256]{1,0:T(8,128)(2,1)S(1)}, u32[]{:S(2)}, u32[]{:S(2)}) collective-permute-start(bf16[80,256]{1,0:T(8,128)(2,1)S(1)} %collective-permute-done.2.refs_2_), channel_id=1, source_target_pairs={{0,1},{1,0},{2,3},{3,2},{4,5},{5,4},{6,7},{7,6},{8,9},{9,8},{10,11... | collective-permute-start | bytes 122888 | tf_op jit(solution)/shard_map/ppermute | solution.py:303
  13.1 15.0 %copy-start.3 = (f32[1,4096]{1,0:T(1,128)S(1)}, f32[1,4096]{1,0:T(1,128)}, u32[]{:S(2)}) copy-start(f32[1,4096]{1,0:T(1,128)} %refs_4_.1) | copy-start | bytes 49156
  15.5 1.9 %collective-permute-start.8 = (bf16[240,256]{1,0:T(8,128)(2,1)S(1)}, bf16[240,256]{1,0:T(8,128)(2,1)S(1)}, u32[]{:S(2)}, u32[]{:S(2)}) collective-permute-start(bf16[240,256]{1,0:T(8,128)(2,1)S(1)} %get-tuple-element.59), channel_id=1, source_target_pairs={{0,1},{1,0},{2,3},{3,2},{4,5},{5,4},{6,7},{7,6},{8,9},{9,8},{10,11... | collective-permute-start | bytes 368648 | tf_op jit(solution)/shard_map/ppermute | solution.py:319
  15.9 12.2 %collective-permute-start.12 = (bf16[352,256]{1,0:T(8,128)(2,1)S(1)}, bf16[352,256]{1,0:T(8,128)(2,1)S(1)}, u32[]{:S(2)}, u32[]{:S(2)}) collective-permute-start(bf16[352,256]{1,0:T(8,128)(2,1)S(1)} %get-tuple-element.63), channel_id=1, source_target_pairs={{0,8},{8,16},{16,24},{24,0},{1,9},{9,17},{17,25},{25,1},{2,10},{10... | collective-permute-start | bytes 540680 | tf_op jit(solution)/shard_map/ppermute | solution.py:356
  17.4 6.9 %collective-permute-start.9 = (bf16[80,256]{1,0:T(8,128)(2,1)S(1)}, bf16[80,256]{1,0:T(8,128)(2,1)S(1)}, u32[]{:S(2)}, u32[]{:S(2)}) collective-permute-start(bf16[80,256]{1,0:T(8,128)(2,1)S(1)} %get-tuple-element.60), channel_id=1, source_target_pairs={{0,12},{1,13},{2,14},{3,15},{4,8},{5,9},{6,10},{7,11},{8,20},{9,21... | collective-permute-start | bytes 122888 | tf_op jit(solution)/shard_map/ppermute | solution.py:358
  19.9 7.8 %collective-permute-start.10 = (bf16[80,256]{1,0:T(8,128)(2,1)S(1)}, bf16[80,256]{1,0:T(8,128)(2,1)S(1)}, u32[]{:S(2)}, u32[]{:S(2)}) collective-permute-start(bf16[80,256]{1,0:T(8,128)(2,1)S(1)} %get-tuple-element.61), channel_id=1, source_target_pairs={{0,14},{1,15},{2,12},{3,13},{4,10},{5,11},{6,8},{7,9},{8,22},{9,23... | collective-permute-start | bytes 122888 | tf_op jit(solution)/shard_map/ppermute | solution.py:358
  21.9 6.2 %collective-permute-start.11 = (bf16[80,256]{1,0:T(8,128)(2,1)S(1)}, bf16[80,256]{1,0:T(8,128)(2,1)S(1)}, u32[]{:S(2)}, u32[]{:S(2)}) collective-permute-start(bf16[80,256]{1,0:T(8,128)(2,1)S(1)} %get-tuple-element.62), channel_id=1, source_target_pairs={{0,10},{1,11},{2,8},{3,9},{4,14},{5,15},{6,12},{7,13},{8,18},{9,19... | collective-permute-start | bytes 122888 | tf_op jit(solution)/shard_map/ppermute | solution.py:358
  28.8 5.4 %collective-permute-start.13 = (bf16[80,256]{1,0:T(8,128)(2,1)S(1)}, bf16[80,256]{1,0:T(8,128)(2,1)S(1)}, u32[]{:S(2)}, u32[]{:S(2)}) collective-permute-start(bf16[80,256]{1,0:T(8,128)(2,1)S(1)} %get-tuple-element.66), channel_id=1, source_target_pairs={{0,4},{1,5},{2,6},{3,7},{4,0},{5,1},{6,2},{7,3},{8,12},{9,13},{10,... | collective-permute-start | bytes 122888 | tf_op jit(solution)/shard_map/ppermute | solution.py:299
  30.0 5.9 %collective-permute-start.14 = (bf16[80,256]{1,0:T(8,128)(2,1)S(1)}, bf16[80,256]{1,0:T(8,128)(2,1)S(1)}, u32[]{:S(2)}, u32[]{:S(2)}) collective-permute-start(bf16[80,256]{1,0:T(8,128)(2,1)S(1)} %get-tuple-element.67), channel_id=1, source_target_pairs={{0,6},{1,7},{2,4},{3,5},{4,2},{5,3},{6,0},{7,1},{8,14},{9,15},{10,... | collective-permute-start | bytes 122888 | tf_op jit(solution)/shard_map/ppermute | solution.py:299
  31.7 4.4 %collective-permute-start.15 = (bf16[80,256]{1,0:T(8,128)(2,1)S(1)}, bf16[80,256]{1,0:T(8,128)(2,1)S(1)}, u32[]{:S(2)}, u32[]{:S(2)}) collective-permute-start(bf16[80,256]{1,0:T(8,128)(2,1)S(1)} %get-tuple-element.68), channel_id=1, source_target_pairs={{0,2},{1,3},{2,0},{3,1},{4,6},{5,7},{6,4},{7,5},{8,10},{9,11},{10,... | collective-permute-start | bytes 122888 | tf_op jit(solution)/shard_map/ppermute | solution.py:299
  32.3 4.1 %collective-permute-start.19 = (bf16[80,256]{1,0:T(8,128)(2,1)S(1)}, bf16[80,256]{1,0:T(8,128)(2,1)S(1)}, u32[]{:S(2)}, u32[]{:S(2)}) collective-permute-start(bf16[80,256]{1,0:T(8,128)(2,1)S(1)} %get-tuple-element.69.refs_3_), channel_id=1, source_target_pairs={{0,1},{1,0},{2,3},{3,2},{4,5},{5,4},{6,7},{7,6},{8,9},{9,8},{10,11... | collective-permute-start | bytes 122888 | tf_op jit(solution)/shard_map/ppermute | solution.py:303
  34.2 2.3 %collective-permute-start.16 = (bf16[80,256]{1,0:T(8,128)(2,1)S(1)}, bf16[80,256]{1,0:T(8,128)(2,1)S(1)}, u32[]{:S(2)}, u32[]{:S(2)}) collective-permute-start(bf16[80,256]{1,0:T(8,128)(2,1)S(1)} %collective-permute-done.13.refs_0_), channel_id=1, source_target_pairs={{0,1},{1,0},{2,3},{3,2},{4,5},{5,4},{6,7},{7,6},{8,9},{9,8},{10,11... | collective-permute-start | bytes 122888 | tf_op jit(solution)/shard_map/ppermute | solution.py:303
  35.9 1.2 %collective-permute-start.17 = (bf16[80,256]{1,0:T(8,128)(2,1)S(1)}, bf16[80,256]{1,0:T(8,128)(2,1)S(1)}, u32[]{:S(2)}, u32[]{:S(2)}) collective-permute-start(bf16[80,256]{1,0:T(8,128)(2,1)S(1)} %collective-permute-done.14.refs_1_), channel_id=1, source_target_pairs={{0,1},{1,0},{2,3},{3,2},{4,5},{5,4},{6,7},{7,6},{8,9},{9,8},{10,11... | collective-permute-start | bytes 122888 | tf_op jit(solution)/shard_map/ppermute | solution.py:303
  36.2 1.2 %collective-permute-start.18 = (bf16[80,256]{1,0:T(8,128)(2,1)S(1)}, bf16[80,256]{1,0:T(8,128)(2,1)S(1)}, u32[]{:S(2)}, u32[]{:S(2)}) collective-permute-start(bf16[80,256]{1,0:T(8,128)(2,1)S(1)} %collective-permute-done.15.refs_2_), channel_id=1, source_target_pairs={{0,1},{1,0},{2,3},{3,2},{4,5},{5,4},{6,7},{7,6},{8,9},{9,8},{10,11... | collective-permute-start | bytes 122888 | tf_op jit(solution)/shard_map/ppermute | solution.py:303
  39.8 1.5 %collective-permute-start.20 = (bf16[320,256]{1,0:T(8,128)(2,1)S(1)}, bf16[320,256]{1,0:T(8,128)(2,1)S(1)}, u32[]{:S(2)}, u32[]{:S(2)}) collective-permute-start(bf16[320,256]{1,0:T(8,128)(2,1)S(1)} %get-tuple-element.71), channel_id=1, source_target_pairs={{0,1},{1,0},{2,3},{3,2},{4,5},{5,4},{6,7},{7,6},{8,9},{9,8},{10,11... | collective-permute-start | bytes 491528 | tf_op jit(solution)/shard_map/ppermute | solution.py:319
  41.3 5.5 %collective-permute-start.21 = (bf16[80,256]{1,0:T(8,128)(2,1)S(1)}, bf16[80,256]{1,0:T(8,128)(2,1)S(1)}, u32[]{:S(2)}, u32[]{:S(2)}) collective-permute-start(bf16[80,256]{1,0:T(8,128)(2,1)S(1)} %get-tuple-element.72), channel_id=1, source_target_pairs={{0,4},{1,5},{2,6},{3,7},{4,0},{5,1},{6,2},{7,3},{8,12},{9,13},{10,... | collective-permute-start | bytes 122888 | tf_op jit(solution)/shard_map/ppermute | solution.py:299
  42.5 5.8 %collective-permute-start.22 = (bf16[80,256]{1,0:T(8,128)(2,1)S(1)}, bf16[80,256]{1,0:T(8,128)(2,1)S(1)}, u32[]{:S(2)}, u32[]{:S(2)}) collective-permute-start(bf16[80,256]{1,0:T(8,128)(2,1)S(1)} %get-tuple-element.73), channel_id=1, source_target_pairs={{0,6},{1,7},{2,4},{3,5},{4,2},{5,3},{6,0},{7,1},{8,14},{9,15},{10,... | collective-permute-start | bytes 122888 | tf_op jit(solution)/shard_map/ppermute | solution.py:299
  43.9 4.4 %collective-permute-start.23 = (bf16[80,256]{1,0:T(8,128)(2,1)S(1)}, bf16[80,256]{1,0:T(8,128)(2,1)S(1)}, u32[]{:S(2)}, u32[]{:S(2)}) collective-permute-start(bf16[80,256]{1,0:T(8,128)(2,1)S(1)} %get-tuple-element.74), channel_id=1, source_target_pairs={{0,2},{1,3},{2,0},{3,1},{4,6},{5,7},{6,4},{7,5},{8,10},{9,11},{10,... | collective-permute-start | bytes 122888 | tf_op jit(solution)/shard_map/ppermute | solution.py:299

commit v8 on v7

--- a/solution.py
+++ b/solution.py
@@ -11,7 +11,7 @@
 CAP = 5
 ROWS = 16
 LANES = 256
-PIECE = 512
+PIECE = 256
 PARTS = 4
 EPS = 1e-06
 F32 = jnp.float32
@@ -224,9 +224,12 @@
     rows = spread_ref.shape[1] * LANES // width - 1
     from_blocks([ref[...] for ref in ins], spread_ref)
     x = gathered(spread_ref, rows, width)
-    gate_val = jnp.dot(x, w_gate[...], preferred_element_type=F32)
-    up_val = jnp.dot(x, w_up[...], preferred_element_type=F32)
-    hidden = (gate_val / (1.0 + jnp.exp(-gate_val)) * up_val).astype(BF16)
+    hidden = []
+    for start in range(0, w_gate.shape[1], PIECE):
+        gate_val = jnp.dot(x, w_gate[:, start : start + PIECE], preferred_element_type=F32)
+        up_val = jnp.dot(x, w_up[:, start : start + PIECE], preferred_element_type=F32)
+        hidden.append((gate_val / (1.0 + jnp.exp(-gate_val)) * up_val).astype(BF16))
+    hidden = jnp.concatenate(hidden, axis=1)
     for start in range(0, width, PIECE):
         piece = jnp.dot(hidden, w_down[:, start : start + PIECE], preferred_element_type=F32)
         spread(piece, spread_ref, width, start)

time: 49.4 us -> 49.4 us (level)
  no operation moved by 1% of the time
where the time goes in v8:
time: 49.4 us; the launch traced here: 49.2 us
  starting transfers between devices  22.2 us (45%)
  waiting for transfers between devices  16.7 us (34%)
  Pallas kernels  10.1 us (20%)
    ppermute x9, starting transfers between devices, across(): lax.ppermute(blocks[i], 'expert', to_expert(i))  12.3 us
    pallas_call x9, Pallas kernels, call(): pl.pallas_call(body, out_shape=outs, in_specs=[space] * len(ins), out_spe...  10.1 us
    ppermute x9, waiting for transfers between devices, across(): lax.ppermute(blocks[i], 'expert', to_expert(i))  9.18 us
    ppermute x3, starting transfers between devices, on_device(): lax.ppermute(sums[i], ('section', 'expert'), onward(i))  5.82 us
    ppermute x3, waiting for transfers between devices, on_device(): lax.ppermute(sums[i], ('section', 'expert'), onward(i))  4.82 us
    ppermute x8, starting transfers between devices, shared(): lax.ppermute(a, 'expert', within(m))  1.78 us
    ppermute x8, waiting for transfers between devices, shared(): lax.ppermute(a, 'expert', within(m))  1.55 us
    ppermute x1, starting transfers between devices, on_device(): lax.ppermute(carry, 'section', [(i, (i + 1) % sections) for i in range(se...  1.49 us
  transfers between devices with their start and end apart: 24, of which 14 were waited for; matrix products, arithmetic and copies ran while one was open for 0% of the time, Pallas kernels for 4%

profile of v8, /device:TPU:0, one launch (start us, length us, event | category | flops | bytes accessed | tf_op | source)
XLA Modules:
  0.0 49.2 jit_solution(3478655229185429585)
XLA Ops:
  0.0 1.6 %shard_map.91 = (bf16[80,256]{1,0:T(8,128)(2,1)S(1)}, bf16[80,256]{1,0:T(8,128)(2,1)S(1)}, bf16[80,256]{1,0:T(8,128)(2,1)S(1)}, bf16[80,256]{1,0:T(8,128)(2,1)S(1)}, bf16[272,256]{1,0:T(8,128)(2,1)S(1)}) custom-call(bf16[16,4096]{1,0:T(8,128)(2,1)} %bitcast.20, f32[1,4096]{1,0:T(1,128)} %refs_4_.1, s32[1,16]{1,0:T(1,128)} %bitcast.21, f32[1,16]{1,0:T(1,128)} %bitcast.22), custom_call_target="tpu_custom_call" | custom-call | flops 10000000000 | bytes 450688 | tf_op jit(solution)/shard_map/pallas_call | solution.py:262
  1.6 0.5 %collective-permute-start.6 = (bf16[80,256]{1,0:T(8,128)(2,1)S(1)}, bf16[80,256]{1,0:T(8,128)(2,1)S(1)}, u32[]{:S(2)}, u32[]{:S(2)}) collective-permute-start(bf16[80,256]{1,0:T(8,128)(2,1)S(1)} %get-tuple-element.45.refs_0_), channel_id=1, source_target_pairs={{0,1},{1,0},{2,3},{3,2},{4,5},{5,4},{6,7},{7,6},{8,9},{9,8},{10,11... | collective-permute-start | bytes 122888 | tf_op jit(solution)/shard_map/ppermute | solution.py:306
  2.1 3.7 %collective-permute-start = (bf16[80,256]{1,0:T(8,128)(2,1)S(1)}, bf16[80,256]{1,0:T(8,128)(2,1)S(1)}, u32[]{:S(2)}, u32[]{:S(2)}) collective-permute-start(bf16[80,256]{1,0:T(8,128)(2,1)S(1)} %get-tuple-element.41), channel_id=1, source_target_pairs={{0,4},{1,5},{2,6},{3,7},{4,0},{5,1},{6,2},{7,3},{8,12},{9,13},{10,... | collective-permute-start | bytes 122888 | tf_op jit(solution)/shard_map/ppermute | solution.py:302
  5.8 1.3 %collective-permute-start.1 = (bf16[80,256]{1,0:T(8,128)(2,1)S(1)}, bf16[80,256]{1,0:T(8,128)(2,1)S(1)}, u32[]{:S(2)}, u32[]{:S(2)}) collective-permute-start(bf16[80,256]{1,0:T(8,128)(2,1)S(1)} %get-tuple-element.42), channel_id=1, source_target_pairs={{0,6},{1,7},{2,4},{3,5},{4,2},{5,3},{6,0},{7,1},{8,14},{9,15},{10,... | collective-permute-start | bytes 122888 | tf_op jit(solution)/shard_map/ppermute | solution.py:302
  7.4 1.8 %shard_map.92 = (bf16[80,256]{1,0:T(8,128)(2,1)S(1)}, bf16[80,256]{1,0:T(8,128)(2,1)S(1)}) custom-call(bf16[4096,512]{1,0:T(8,128)(2,1)S(1)} %bitcast.9, bf16[4096,512]{1,0:T(8,128)(2,1)S(1)} %bitcast.12, bf16[512,4096]{1,0:T(8,128)(2,1)S(1)} %bitcast.15, bf16[80,256]{1,0:T(8,128)(2,1)S(1)} %get-tuple-element.45.refs_0_, ...), custom_call_target="tpu_custom_call" | custom-call | flops 3221225472 | bytes 12746752 | tf_op jit(solution)/shard_map/pallas_call | solution.py:262
  9.3 0.5 collective-permute-start.3
  9.8 1.9 %collective-permute-done.1.refs_1_ = bf16[80,256]{1,0:T(8,128)(2,1)S(1)} collective-permute-done((bf16[80,256]{1,0:T(8,128)(2,1)S(1)}, bf16[80,256]{1,0:T(8,128)(2,1)S(1)}, u32[]{:S(2)}, u32[]{:S(2)}) %collective-permute-start.1) | collective-permute-done | bytes 40992 | tf_op jit(solution)/shard_map/ppermute | solution.py:302
  11.7 0.5 %collective-permute-start.5 = (bf16[80,256]{1,0:T(8,128)(2,1)S(1)}, bf16[80,256]{1,0:T(8,128)(2,1)S(1)}, u32[]{:S(2)}, u32[]{:S(2)}) collective-permute-start(bf16[80,256]{1,0:T(8,128)(2,1)S(1)} %collective-permute-done.2.refs_2_), channel_id=1, source_target_pairs={{0,1},{1,0},{2,3},{3,2},{4,5},{5,4},{6,7},{7,6},{8,9},{9,8},{10,11... | collective-permute-start | bytes 122888 | tf_op jit(solution)/shard_map/ppermute | solution.py:306
  12.5 0.4 collective-permute-done.4.refs_4_
  13.1 2.3 %shard_map.94 = (bf16[240,256]{1,0:T(8,128)(2,1)S(1)}, bf16[240,256]{1,0:T(8,128)(2,1)S(1)}) custom-call(bf16[4096,512]{1,0:T(8,128)(2,1)S(1)} %bitcast.10, bf16[4096,512]{1,0:T(8,128)(2,1)S(1)} %bitcast.13, bf16[512,4096]{1,0:T(8,128)(2,1)S(1)} %bitcast.16, bf16[80,256]{1,0:T(8,128)(2,1)S(1)} %collective-permute-done.refs_0_, ...), custom_call_target="tpu_custom_call" | custom-call | flops 3221225472 | bytes 13074432 | tf_op jit(solution)/shard_map/pallas_call | solution.py:262
  15.4 0.4 collective-permute-start.8
  15.8 1.5 %collective-permute-start.12 = (bf16[352,256]{1,0:T(8,128)(2,1)S(1)}, bf16[352,256]{1,0:T(8,128)(2,1)S(1)}, u32[]{:S(2)}, u32[]{:S(2)}) collective-permute-start(bf16[352,256]{1,0:T(8,128)(2,1)S(1)} %get-tuple-element.63), channel_id=1, source_target_pairs={{0,8},{8,16},{16,24},{24,0},{1,9},{9,17},{17,25},{25,1},{2,10},{10... | collective-permute-start | bytes 540680 | tf_op jit(solution)/shard_map/ppermute | solution.py:359
  17.4 2.5 %collective-permute-start.9 = (bf16[80,256]{1,0:T(8,128)(2,1)S(1)}, bf16[80,256]{1,0:T(8,128)(2,1)S(1)}, u32[]{:S(2)}, u32[]{:S(2)}) collective-permute-start(bf16[80,256]{1,0:T(8,128)(2,1)S(1)} %get-tuple-element.60), channel_id=1, source_target_pairs={{0,12},{1,13},{2,14},{3,15},{4,8},{5,9},{6,10},{7,11},{8,20},{9,21... | collective-permute-start | bytes 122888 | tf_op jit(solution)/shard_map/ppermute | solution.py:361
  19.9 1.9 %collective-permute-start.10 = (bf16[80,256]{1,0:T(8,128)(2,1)S(1)}, bf16[80,256]{1,0:T(8,128)(2,1)S(1)}, u32[]{:S(2)}, u32[]{:S(2)}) collective-permute-start(bf16[80,256]{1,0:T(8,128)(2,1)S(1)} %get-tuple-element.61), channel_id=1, source_target_pairs={{0,14},{1,15},{2,12},{3,13},{4,10},{5,11},{6,8},{7,9},{8,22},{9,23... | collective-permute-start | bytes 122888 | tf_op jit(solution)/shard_map/ppermute | solution.py:361
  21.8 1.4 %collective-permute-start.11 = (bf16[80,256]{1,0:T(8,128)(2,1)S(1)}, bf16[80,256]{1,0:T(8,128)(2,1)S(1)}, u32[]{:S(2)}, u32[]{:S(2)}) collective-permute-start(bf16[80,256]{1,0:T(8,128)(2,1)S(1)} %get-tuple-element.62), channel_id=1, source_target_pairs={{0,10},{1,11},{2,8},{3,9},{4,14},{5,15},{6,12},{7,13},{8,18},{9,19... | collective-permute-start | bytes 122888 | tf_op jit(solution)/shard_map/ppermute | solution.py:361
  23.2 1.0 %collective-permute-done.9.refs_0_ = bf16[80,256]{1,0:T(8,128)(2,1)S(1)} collective-permute-done((bf16[80,256]{1,0:T(8,128)(2,1)S(1)}, bf16[80,256]{1,0:T(8,128)(2,1)S(1)}, u32[]{:S(2)}, u32[]{:S(2)}) %collective-permute-start.9) | collective-permute-done | bytes 40992 | tf_op jit(solution)/shard_map/ppermute | solution.py:361
  24.2 3.5 %collective-permute-done.10.refs_1_ = bf16[80,256]{1,0:T(8,128)(2,1)S(1)} collective-permute-done((bf16[80,256]{1,0:T(8,128)(2,1)S(1)}, bf16[80,256]{1,0:T(8,128)(2,1)S(1)}, u32[]{:S(2)}, u32[]{:S(2)}) %collective-permute-start.10) | collective-permute-done | bytes 40992 | tf_op jit(solution)/shard_map/ppermute | solution.py:361
  28.0 0.7 %shard_map.96 = (bf16[16,4096]{1,0:T(8,128)(2,1)S(1)}, bf16[80,256]{1,0:T(8,128)(2,1)S(1)}, bf16[80,256]{1,0:T(8,128)(2,1)S(1)}, bf16[80,256]{1,0:T(8,128)(2,1)S(1)}, bf16[80,256]{1,0:T(8,128)(2,1)S(1)}) custom-call(bf16[80,256]{1,0:T(8,128)(2,1)S(1)} %collective-permute-done.9.refs_0_, bf16[80,256]{1,0:T(8,128)(2,1)S(1)} %collective-permute-done.10.refs_1_, ...), custom_call_target="tpu_custom_call" | custom-call | bytes 615424 | tf_op jit(solution)/shard_map/pallas_call | solution.py:262
  28.7 1.3 %collective-permute-start.13 = (bf16[80,256]{1,0:T(8,128)(2,1)S(1)}, bf16[80,256]{1,0:T(8,128)(2,1)S(1)}, u32[]{:S(2)}, u32[]{:S(2)}) collective-permute-start(bf16[80,256]{1,0:T(8,128)(2,1)S(1)} %get-tuple-element.66), channel_id=1, source_target_pairs={{0,4},{1,5},{2,6},{3,7},{4,0},{5,1},{6,2},{7,3},{8,12},{9,13},{10,... | collective-permute-start | bytes 122888 | tf_op jit(solution)/shard_map/ppermute | solution.py:302
  30.0 1.7 %collective-permute-start.14 = (bf16[80,256]{1,0:T(8,128)(2,1)S(1)}, bf16[80,256]{1,0:T(8,128)(2,1)S(1)}, u32[]{:S(2)}, u32[]{:S(2)}) collective-permute-start(bf16[80,256]{1,0:T(8,128)(2,1)S(1)} %get-tuple-element.67), channel_id=1, source_target_pairs={{0,6},{1,7},{2,4},{3,5},{4,2},{5,3},{6,0},{7,1},{8,14},{9,15},{10,... | collective-permute-start | bytes 122888 | tf_op jit(solution)/shard_map/ppermute | solution.py:302
  31.7 0.6 %collective-permute-start.15 = (bf16[80,256]{1,0:T(8,128)(2,1)S(1)}, bf16[80,256]{1,0:T(8,128)(2,1)S(1)}, u32[]{:S(2)}, u32[]{:S(2)}) collective-permute-start(bf16[80,256]{1,0:T(8,128)(2,1)S(1)} %get-tuple-element.68), channel_id=1, source_target_pairs={{0,2},{1,3},{2,0},{3,1},{4,6},{5,7},{6,4},{7,5},{8,10},{9,11},{10,... | collective-permute-start | bytes 122888 | tf_op jit(solution)/shard_map/ppermute | solution.py:302
  32.3 1.8 %collective-permute-done.13.refs_0_ = bf16[80,256]{1,0:T(8,128)(2,1)S(1)} collective-permute-done((bf16[80,256]{1,0:T(8,128)(2,1)S(1)}, bf16[80,256]{1,0:T(8,128)(2,1)S(1)}, u32[]{:S(2)}, u32[]{:S(2)}) %collective-permute-start.13) | collective-permute-done | bytes 40992 | tf_op jit(solution)/shard_map/ppermute | solution.py:302
  34.1 1.8 %collective-permute-done.14.refs_1_ = bf16[80,256]{1,0:T(8,128)(2,1)S(1)} collective-permute-done((bf16[80,256]{1,0:T(8,128)(2,1)S(1)}, bf16[80,256]{1,0:T(8,128)(2,1)S(1)}, u32[]{:S(2)}, u32[]{:S(2)}) %collective-permute-start.14) | collective-permute-done | bytes 40992 | tf_op jit(solution)/shard_map/ppermute | solution.py:302
  36.4 0.7 %collective-permute-done.17.refs_5_ = bf16[80,256]{1,0:T(8,128)(2,1)S(1)} collective-permute-done((bf16[80,256]{1,0:T(8,128)(2,1)S(1)}, bf16[80,256]{1,0:T(8,128)(2,1)S(1)}, u32[]{:S(2)}, u32[]{:S(2)}) %collective-permute-start.17) | collective-permute-done | bytes 40992 | tf_op jit(solution)/shard_map/ppermute | solution.py:306
  37.4 2.4 %shard_map.97 = (bf16[320,256]{1,0:T(8,128)(2,1)S(1)}, bf16[320,256]{1,0:T(8,128)(2,1)S(1)}) custom-call(bf16[4096,512]{1,0:T(8,128)(2,1)S(1)} %bitcast.11, bf16[4096,512]{1,0:T(8,128)(2,1)S(1)} %bitcast.14, bf16[512,4096]{1,0:T(8,128)(2,1)S(1)} %bitcast.17, bf16[80,256]{1,0:T(8,128)(2,1)S(1)} %collective-permute-done.13.refs_0_, ...), custom_call_target="tpu_custom_call" | custom-call | flops 3221225472 | bytes 13238272 | tf_op jit(solution)/shard_map/pallas_call | solution.py:262
  40.1 1.2 %collective-permute-done.20.refs_1_ = bf16[320,256]{1,0:T(8,128)(2,1)S(1)} collective-permute-done((bf16[320,256]{1,0:T(8,128)(2,1)S(1)}, bf16[320,256]{1,0:T(8,128)(2,1)S(1)}, u32[]{:S(2)}, u32[]{:S(2)}) %collective-permute-start.20) | collective-permute-done | bytes 163872 | tf_op jit(solution)/shard_map/ppermute | solution.py:322
  41.3 1.2 %collective-permute-start.21 = (bf16[80,256]{1,0:T(8,128)(2,1)S(1)}, bf16[80,256]{1,0:T(8,128)(2,1)S(1)}, u32[]{:S(2)}, u32[]{:S(2)}) collective-permute-start(bf16[80,256]{1,0:T(8,128)(2,1)S(1)} %get-tuple-element.72), channel_id=1, source_target_pairs={{0,4},{1,5},{2,6},{3,7},{4,0},{5,1},{6,2},{7,3},{8,12},{9,13},{10,... | collective-permute-start | bytes 122888 | tf_op jit(solution)/shard_map/ppermute | solution.py:302
  42.4 1.4 %collective-permute-start.22 = (bf16[80,256]{1,0:T(8,128)(2,1)S(1)}, bf16[80,256]{1,0:T(8,128)(2,1)S(1)}, u32[]{:S(2)}, u32[]{:S(2)}) collective-permute-start(bf16[80,256]{1,0:T(8,128)(2,1)S(1)} %get-tuple-element.73), channel_id=1, source_target_pairs={{0,6},{1,7},{2,4},{3,5},{4,2},{5,3},{6,0},{7,1},{8,14},{9,15},{10,... | collective-permute-start | bytes 122888 | tf_op jit(solution)/shard_map/ppermute | solution.py:302
  43.8 1.0 %collective-permute-start.23 = (bf16[80,256]{1,0:T(8,128)(2,1)S(1)}, bf16[80,256]{1,0:T(8,128)(2,1)S(1)}, u32[]{:S(2)}, u32[]{:S(2)}) collective-permute-start(bf16[80,256]{1,0:T(8,128)(2,1)S(1)} %get-tuple-element.74), channel_id=1, source_target_pairs={{0,2},{1,3},{2,0},{3,1},{4,6},{5,7},{6,4},{7,5},{8,10},{9,11},{10,... | collective-permute-start | bytes 122888 | tf_op jit(solution)/shard_map/ppermute | solution.py:302
  44.8 1.9 %collective-permute-done.21.b0 = bf16[80,256]{1,0:T(8,128)(2,1)S(1)} collective-permute-done((bf16[80,256]{1,0:T(8,128)(2,1)S(1)}, bf16[80,256]{1,0:T(8,128)(2,1)S(1)}, u32[]{:S(2)}, u32[]{:S(2)}) %collective-permute-start.21) | collective-permute-done | bytes 40992 | tf_op jit(solution)/shard_map/ppermute | solution.py:302
  46.8 1.5 %collective-permute-done.22.b1 = bf16[80,256]{1,0:T(8,128)(2,1)S(1)} collective-permute-done((bf16[80,256]{1,0:T(8,128)(2,1)S(1)}, bf16[80,256]{1,0:T(8,128)(2,1)S(1)}, u32[]{:S(2)}, u32[]{:S(2)}) %collective-permute-start.22) | collective-permute-done | bytes 40992 | tf_op jit(solution)/shard_map/ppermute | solution.py:302
  48.3 1.0 %shard_map.99 = bf16[16,4096]{1,0:T(8,128)(2,1)} custom-call(bf16[16,4096]{1,0:T(8,128)(2,1)S(1)} %get-tuple-element.65.x_ref, bf16[80,256]{1,0:T(8,128)(2,1)S(1)} %collective-permute-done.21.b0, bf16[80,256]{1,0:T(8,128)(2,1)S(1)} %collective-permute-done.22.b1, bf16[80,256]{1,0:T(8,128)(2,1)S(1)} %collective-permute-done.23.b2, ...), custom_call_target="tpu_custom_call" | custom-call | bytes 435200 | tf_op jit(solution)/shard_map/pallas_call | solution.py:262
  (37 shorter events, 2.3 us)
Async XLA Ops:
  0.0 7.4 %copy-start = (bf16[1,1,4096,512]{3,2,1,0:T(8,128)(2,1)S(1)}, bf16[1,1,4096,512]{3,2,1,0:T(8,128)(2,1)}, u32[]{:S(2)}) copy-start(bf16[1,1,4096,512]{3,2,1,0:T(8,128)(2,1)} %param.15) | copy-start | bytes 12582916
  0.0 7.4 %copy-start.1 = (bf16[1,1,4096,512]{3,2,1,0:T(8,128)(2,1)S(1)}, bf16[1,1,4096,512]{3,2,1,0:T(8,128)(2,1)}, u32[]{:S(2)}) copy-start(bf16[1,1,4096,512]{3,2,1,0:T(8,128)(2,1)} %param.16) | copy-start | bytes 12582916
  0.0 7.4 %copy-start.2 = (bf16[1,1,512,4096]{3,2,1,0:T(8,128)(2,1)S(1)}, bf16[1,1,512,4096]{3,2,1,0:T(8,128)(2,1)}, u32[]{:S(2)}) copy-start(bf16[1,1,512,4096]{3,2,1,0:T(8,128)(2,1)} %param.17) | copy-start | bytes 12582916
  1.6 5.8 %collective-permute-start.6 = (bf16[80,256]{1,0:T(8,128)(2,1)S(1)}, bf16[80,256]{1,0:T(8,128)(2,1)S(1)}, u32[]{:S(2)}, u32[]{:S(2)}) collective-permute-start(bf16[80,256]{1,0:T(8,128)(2,1)S(1)} %get-tuple-element.45.refs_0_), channel_id=1, source_target_pairs={{0,1},{1,0},{2,3},{3,2},{4,5},{5,4},{6,7},{7,6},{8,9},{9,8},{10,11... | collective-permute-start | bytes 122888 | tf_op jit(solution)/shard_map/ppermute | solution.py:306
  2.1 7.2 %collective-permute-start = (bf16[80,256]{1,0:T(8,128)(2,1)S(1)}, bf16[80,256]{1,0:T(8,128)(2,1)S(1)}, u32[]{:S(2)}, u32[]{:S(2)}) collective-permute-start(bf16[80,256]{1,0:T(8,128)(2,1)S(1)} %get-tuple-element.41), channel_id=1, source_target_pairs={{0,4},{1,5},{2,6},{3,7},{4,0},{5,1},{6,2},{7,3},{8,12},{9,13},{10,... | collective-permute-start | bytes 122888 | tf_op jit(solution)/shard_map/ppermute | solution.py:302
  5.8 5.9 %collective-permute-start.1 = (bf16[80,256]{1,0:T(8,128)(2,1)S(1)}, bf16[80,256]{1,0:T(8,128)(2,1)S(1)}, u32[]{:S(2)}, u32[]{:S(2)}) collective-permute-start(bf16[80,256]{1,0:T(8,128)(2,1)S(1)} %get-tuple-element.42), channel_id=1, source_target_pairs={{0,6},{1,7},{2,4},{3,5},{4,2},{5,3},{6,0},{7,1},{8,14},{9,15},{10,... | collective-permute-start | bytes 122888 | tf_op jit(solution)/shard_map/ppermute | solution.py:302
  7.1 4.6 %collective-permute-start.2 = (bf16[80,256]{1,0:T(8,128)(2,1)S(1)}, bf16[80,256]{1,0:T(8,128)(2,1)S(1)}, u32[]{:S(2)}, u32[]{:S(2)}) collective-permute-start(bf16[80,256]{1,0:T(8,128)(2,1)S(1)} %get-tuple-element.43), channel_id=1, source_target_pairs={{0,2},{1,3},{2,0},{3,1},{4,6},{5,7},{6,4},{7,5},{8,10},{9,11},{10,... | collective-permute-start | bytes 122888 | tf_op jit(solution)/shard_map/ppermute | solution.py:302
  7.4 4.8 %copy-start.4 = (s32[1,16,1]{1,2,0:T(1,128)S(1)}, s32[1,16,1]{1,2,0:T(1,128)}, u32[]{:S(2)}) copy-start(s32[1,16,1]{1,2,0:T(1,128)} %param.13) | copy-start | bytes 196
  7.4 4.8 %copy-start.5 = (f32[1,16,1]{1,2,0:T(1,128)S(1)}, f32[1,16,1]{1,2,0:T(1,128)}, u32[]{:S(2)}) copy-start(f32[1,16,1]{1,2,0:T(1,128)} %param.14) | copy-start | bytes 196
  9.2 3.0 %collective-permute-start.7 = (bf16[80,256]{1,0:T(8,128)(2,1)S(1)}, bf16[80,256]{1,0:T(8,128)(2,1)S(1)}, u32[]{:S(2)}, u32[]{:S(2)}) collective-permute-start(bf16[80,256]{1,0:T(8,128)(2,1)S(1)} %get-tuple-element.47), channel_id=1, source_target_pairs={{0,1},{1,0},{2,3},{3,2},{4,5},{5,4},{6,7},{7,6},{8,9},{9,8},{10,11... | collective-permute-start | bytes 122888 | tf_op jit(solution)/shard_map/ppermute | solution.py:322
  9.3 3.2 %collective-permute-start.3 = (bf16[80,256]{1,0:T(8,128)(2,1)S(1)}, bf16[80,256]{1,0:T(8,128)(2,1)S(1)}, u32[]{:S(2)}, u32[]{:S(2)}) collective-permute-start(bf16[80,256]{1,0:T(8,128)(2,1)S(1)} %collective-permute-done.refs_0_), channel_id=1, source_target_pairs={{0,1},{1,0},{2,3},{3,2},{4,5},{5,4},{6,7},{7,6},{8,9},{9,8},{10,11... | collective-permute-start | bytes 122888 | tf_op jit(solution)/shard_map/ppermute | solution.py:306
  11.7 1.2 %collective-permute-start.4 = (bf16[80,256]{1,0:T(8,128)(2,1)S(1)}, bf16[80,256]{1,0:T(8,128)(2,1)S(1)}, u32[]{:S(2)}, u32[]{:S(2)}) collective-permute-start(bf16[80,256]{1,0:T(8,128)(2,1)S(1)} %collective-permute-done.1.refs_1_), channel_id=1, source_target_pairs={{0,1},{1,0},{2,3},{3,2},{4,5},{5,4},{6,7},{7,6},{8,9},{9,8},{10,11... | collective-permute-start | bytes 122888 | tf_op jit(solution)/shard_map/ppermute | solution.py:306
  11.7 1.4 %collective-permute-start.5 = (bf16[80,256]{1,0:T(8,128)(2,1)S(1)}, bf16[80,256]{1,0:T(8,128)(2,1)S(1)}, u32[]{:S(2)}, u32[]{:S(2)}) collective-permute-start(bf16[80,256]{1,0:T(8,128)(2,1)S(1)} %collective-permute-done.2.refs_2_), channel_id=1, source_target_pairs={{0,1},{1,0},{2,3},{3,2},{4,5},{5,4},{6,7},{7,6},{8,9},{9,8},{10,11... | collective-permute-start | bytes 122888 | tf_op jit(solution)/shard_map/ppermute | solution.py:306
  13.1 14.9 %copy-start.3 = (f32[1,4096]{1,0:T(1,128)S(1)}, f32[1,4096]{1,0:T(1,128)}, u32[]{:S(2)}) copy-start(f32[1,4096]{1,0:T(1,128)} %refs_4_.1) | copy-start | bytes 49156
  15.4 1.9 %collective-permute-start.8 = (bf16[240,256]{1,0:T(8,128)(2,1)S(1)}, bf16[240,256]{1,0:T(8,128)(2,1)S(1)}, u32[]{:S(2)}, u32[]{:S(2)}) collective-permute-start(bf16[240,256]{1,0:T(8,128)(2,1)S(1)} %get-tuple-element.59), channel_id=1, source_target_pairs={{0,1},{1,0},{2,3},{3,2},{4,5},{5,4},{6,7},{7,6},{8,9},{9,8},{10,11... | collective-permute-start | bytes 368648 | tf_op jit(solution)/shard_map/ppermute | solution.py:322
  15.8 12.2 %collective-permute-start.12 = (bf16[352,256]{1,0:T(8,128)(2,1)S(1)}, bf16[352,256]{1,0:T(8,128)(2,1)S(1)}, u32[]{:S(2)}, u32[]{:S(2)}) collective-permute-start(bf16[352,256]{1,0:T(8,128)(2,1)S(1)} %get-tuple-element.63), channel_id=1, source_target_pairs={{0,8},{8,16},{16,24},{24,0},{1,9},{9,17},{17,25},{25,1},{2,10},{10... | collective-permute-start | bytes 540680 | tf_op jit(solution)/shard_map/ppermute | solution.py:359
  17.4 6.9 %collective-permute-start.9 = (bf16[80,256]{1,0:T(8,128)(2,1)S(1)}, bf16[80,256]{1,0:T(8,128)(2,1)S(1)}, u32[]{:S(2)}, u32[]{:S(2)}) collective-permute-start(bf16[80,256]{1,0:T(8,128)(2,1)S(1)} %get-tuple-element.60), channel_id=1, source_target_pairs={{0,12},{1,13},{2,14},{3,15},{4,8},{5,9},{6,10},{7,11},{8,20},{9,21... | collective-permute-start | bytes 122888 | tf_op jit(solution)/shard_map/ppermute | solution.py:361
  19.9 7.8 %collective-permute-start.10 = (bf16[80,256]{1,0:T(8,128)(2,1)S(1)}, bf16[80,256]{1,0:T(8,128)(2,1)S(1)}, u32[]{:S(2)}, u32[]{:S(2)}) collective-permute-start(bf16[80,256]{1,0:T(8,128)(2,1)S(1)} %get-tuple-element.61), channel_id=1, source_target_pairs={{0,14},{1,15},{2,12},{3,13},{4,10},{5,11},{6,8},{7,9},{8,22},{9,23... | collective-permute-start | bytes 122888 | tf_op jit(solution)/shard_map/ppermute | solution.py:361
  21.8 6.2 %collective-permute-start.11 = (bf16[80,256]{1,0:T(8,128)(2,1)S(1)}, bf16[80,256]{1,0:T(8,128)(2,1)S(1)}, u32[]{:S(2)}, u32[]{:S(2)}) collective-permute-start(bf16[80,256]{1,0:T(8,128)(2,1)S(1)} %get-tuple-element.62), channel_id=1, source_target_pairs={{0,10},{1,11},{2,8},{3,9},{4,14},{5,15},{6,12},{7,13},{8,18},{9,19... | collective-permute-start | bytes 122888 | tf_op jit(solution)/shard_map/ppermute | solution.py:361
  28.7 5.4 %collective-permute-start.13 = (bf16[80,256]{1,0:T(8,128)(2,1)S(1)}, bf16[80,256]{1,0:T(8,128)(2,1)S(1)}, u32[]{:S(2)}, u32[]{:S(2)}) collective-permute-start(bf16[80,256]{1,0:T(8,128)(2,1)S(1)} %get-tuple-element.66), channel_id=1, source_target_pairs={{0,4},{1,5},{2,6},{3,7},{4,0},{5,1},{6,2},{7,3},{8,12},{9,13},{10,... | collective-permute-start | bytes 122888 | tf_op jit(solution)/shard_map/ppermute | solution.py:302
  30.0 5.9 %collective-permute-start.14 = (bf16[80,256]{1,0:T(8,128)(2,1)S(1)}, bf16[80,256]{1,0:T(8,128)(2,1)S(1)}, u32[]{:S(2)}, u32[]{:S(2)}) collective-permute-start(bf16[80,256]{1,0:T(8,128)(2,1)S(1)} %get-tuple-element.67), channel_id=1, source_target_pairs={{0,6},{1,7},{2,4},{3,5},{4,2},{5,3},{6,0},{7,1},{8,14},{9,15},{10,... | collective-permute-start | bytes 122888 | tf_op jit(solution)/shard_map/ppermute | solution.py:302
  31.7 4.4 %collective-permute-start.15 = (bf16[80,256]{1,0:T(8,128)(2,1)S(1)}, bf16[80,256]{1,0:T(8,128)(2,1)S(1)}, u32[]{:S(2)}, u32[]{:S(2)}) collective-permute-start(bf16[80,256]{1,0:T(8,128)(2,1)S(1)} %get-tuple-element.68), channel_id=1, source_target_pairs={{0,2},{1,3},{2,0},{3,1},{4,6},{5,7},{6,4},{7,5},{8,10},{9,11},{10,... | collective-permute-start | bytes 122888 | tf_op jit(solution)/shard_map/ppermute | solution.py:302
  32.3 4.1 %collective-permute-start.19 = (bf16[80,256]{1,0:T(8,128)(2,1)S(1)}, bf16[80,256]{1,0:T(8,128)(2,1)S(1)}, u32[]{:S(2)}, u32[]{:S(2)}) collective-permute-start(bf16[80,256]{1,0:T(8,128)(2,1)S(1)} %get-tuple-element.69.refs_3_), channel_id=1, source_target_pairs={{0,1},{1,0},{2,3},{3,2},{4,5},{5,4},{6,7},{7,6},{8,9},{9,8},{10,11... | collective-permute-start | bytes 122888 | tf_op jit(solution)/shard_map/ppermute | solution.py:306
  34.1 2.3 %collective-permute-start.16 = (bf16[80,256]{1,0:T(8,128)(2,1)S(1)}, bf16[80,256]{1,0:T(8,128)(2,1)S(1)}, u32[]{:S(2)}, u32[]{:S(2)}) collective-permute-start(bf16[80,256]{1,0:T(8,128)(2,1)S(1)} %collective-permute-done.13.refs_0_), channel_id=1, source_target_pairs={{0,1},{1,0},{2,3},{3,2},{4,5},{5,4},{6,7},{7,6},{8,9},{9,8},{10,11... | collective-permute-start | bytes 122888 | tf_op jit(solution)/shard_map/ppermute | solution.py:306
  35.9 1.2 %collective-permute-start.17 = (bf16[80,256]{1,0:T(8,128)(2,1)S(1)}, bf16[80,256]{1,0:T(8,128)(2,1)S(1)}, u32[]{:S(2)}, u32[]{:S(2)}) collective-permute-start(bf16[80,256]{1,0:T(8,128)(2,1)S(1)} %collective-permute-done.14.refs_1_), channel_id=1, source_target_pairs={{0,1},{1,0},{2,3},{3,2},{4,5},{5,4},{6,7},{7,6},{8,9},{9,8},{10,11... | collective-permute-start | bytes 122888 | tf_op jit(solution)/shard_map/ppermute | solution.py:306
  36.2 1.2 %collective-permute-start.18 = (bf16[80,256]{1,0:T(8,128)(2,1)S(1)}, bf16[80,256]{1,0:T(8,128)(2,1)S(1)}, u32[]{:S(2)}, u32[]{:S(2)}) collective-permute-start(bf16[80,256]{1,0:T(8,128)(2,1)S(1)} %collective-permute-done.15.refs_2_), channel_id=1, source_target_pairs={{0,1},{1,0},{2,3},{3,2},{4,5},{5,4},{6,7},{7,6},{8,9},{9,8},{10,11... | collective-permute-start | bytes 122888 | tf_op jit(solution)/shard_map/ppermute | solution.py:306
  39.8 1.5 %collective-permute-start.20 = (bf16[320,256]{1,0:T(8,128)(2,1)S(1)}, bf16[320,256]{1,0:T(8,128)(2,1)S(1)}, u32[]{:S(2)}, u32[]{:S(2)}) collective-permute-start(bf16[320,256]{1,0:T(8,128)(2,1)S(1)} %get-tuple-element.71), channel_id=1, source_target_pairs={{0,1},{1,0},{2,3},{3,2},{4,5},{5,4},{6,7},{7,6},{8,9},{9,8},{10,11... | collective-permute-start | bytes 491528 | tf_op jit(solution)/shard_map/ppermute | solution.py:322
  41.3 5.5 %collective-permute-start.21 = (bf16[80,256]{1,0:T(8,128)(2,1)S(1)}, bf16[80,256]{1,0:T(8,128)(2,1)S(1)}, u32[]{:S(2)}, u32[]{:S(2)}) collective-permute-start(bf16[80,256]{1,0:T(8,128)(2,1)S(1)} %get-tuple-element.72), channel_id=1, source_target_pairs={{0,4},{1,5},{2,6},{3,7},{4,0},{5,1},{6,2},{7,3},{8,12},{9,13},{10,... | collective-permute-start | bytes 122888 | tf_op jit(solution)/shard_map/ppermute | solution.py:302
  42.4 5.8 %collective-permute-start.22 = (bf16[80,256]{1,0:T(8,128)(2,1)S(1)}, bf16[80,256]{1,0:T(8,128)(2,1)S(1)}, u32[]{:S(2)}, u32[]{:S(2)}) collective-permute-start(bf16[80,256]{1,0:T(8,128)(2,1)S(1)} %get-tuple-element.73), channel_id=1, source_target_pairs={{0,6},{1,7},{2,4},{3,5},{4,2},{5,3},{6,0},{7,1},{8,14},{9,15},{10,... | collective-permute-start | bytes 122888 | tf_op jit(solution)/shard_map/ppermute | solution.py:302
  43.8 4.4 %collective-permute-start.23 = (bf16[80,256]{1,0:T(8,128)(2,1)S(1)}, bf16[80,256]{1,0:T(8,128)(2,1)S(1)}, u32[]{:S(2)}, u32[]{:S(2)}) collective-permute-start(bf16[80,256]{1,0:T(8,128)(2,1)S(1)} %get-tuple-element.74), channel_id=1, source_target_pairs={{0,2},{1,3},{2,0},{3,1},{4,6},{5,7},{6,4},{7,5},{8,10},{9,11},{10,... | collective-permute-start | bytes 122888 | tf_op jit(solution)/shard_map/ppermute | solution.py:302

commit v9 on v8

--- a/solution.py
+++ b/solution.py
@@ -153,14 +153,15 @@
     slots = slots_of(upright(routes_ref[...].astype(F32)))
     lane = lax.broadcasted_iota(jnp.int32, (rows, LANES), 1)
     meta = jnp.zeros((rows, LANES), F32)
-    for i, column in enumerate([slots, *split_parts(upright(gates_ref[...]))]):
-        meta = jnp.where(lane == i, column.astype(F32), meta)
+    for i, column in enumerate(split_parts(upright(gates_ref[...]))):
+        meta = jnp.where(lane == 128 + i, column.astype(F32), meta)
     chosen = block_map(slots, my_expert(group))
     for copy in copies[:2]:
         copy.wait()
     for piece in range(width // LANES):
         ahead_ref[piece * rows : (piece + 1) * rows] = x_ref[:, piece * LANES : (piece + 1) * LANES]
     ahead_ref[width // LANES * rows :] = meta.astype(BF16)
+    ahead_ref[width // LANES * rows :, : chosen.shape[1]] = chosen
     normed = normalize(x_ref[...].astype(F32), gain_ref[...])
     write_blocks(normed, chosen, spread_ref, block_refs)
 
@@ -182,20 +183,20 @@
     return (x.astype(F32) + update.astype(F32)).astype(BF16)
 
 
-def middle_kernel(group, *refs):
+def middle_kernel(*refs):
     block_ins, carried_ref, gain_ref, map_ref = refs[: EXPERTS - 1], *refs[EXPERTS - 1 : EXPERTS + 2]
     first_ref, block_refs, spread_ref = refs[EXPERTS + 2], refs[EXPERTS + 3 : -1], refs[-1]
-    expert = my_expert(group)
     rows, width = first_ref.shape
     pieces = width // LANES
     x = jnp.concatenate(
         [carried_ref[piece * rows : (piece + 1) * rows] for piece in range(pieces)], axis=1
     )
     meta = carried_ref[pieces * rows : (pieces + 1) * rows].astype(F32)
-    gates = meta[:, 1:2] + meta[:, 2:3] + meta[:, 3:4]
+    gates = meta[:, 128:129] + meta[:, 129:130] + meta[:, 130:131]
+    chosen = meta[:, : pad_rows(EXPERTS * CAP)].astype(BF16)
     blocks = [ref[...] for ref in block_ins] + [carried_ref[(pieces + 1) * rows :]]
     fill(blocks, spread_ref)
-    first = residual(x, gates, block_map(meta[:, 0:1], expert), spread_ref, width)
+    first = residual(x, gates, chosen, spread_ref, width)
     first_ref[...] = first
     normed = normalize(first.astype(F32), gain_ref[...])
     write_blocks(normed, map_ref[...], spread_ref, block_refs)
@@ -360,7 +361,7 @@
     sums = added(terms)
     home = [lax.ppermute(sums[i], ("section", "expert"), onward(i)) for i in range(EXPERTS - 1)]
     first, *blocks = call(
-        functools.partial(middle_kernel, group),
+        middle_kernel,
         [whole] + [block] * EXPERTS,
         [*home, carried, gain, second_map],
         8,

time: 49.4 us -> 49.4 us (level)
  no operation moved by 1% of the time
where the time goes in v9:
time: 49.4 us; the launch traced here: 49.2 us
  starting transfers between devices  22.2 us (45%)
  waiting for transfers between devices  16.7 us (34%)
  Pallas kernels  10.1 us (20%)
    ppermute x9, starting transfers between devices, across(): lax.ppermute(blocks[i], 'expert', to_expert(i))  12.3 us
    pallas_call x9, Pallas kernels, call(): pl.pallas_call(body, out_shape=outs, in_specs=[space] * len(ins), out_spe...  10.1 us
    ppermute x9, waiting for transfers between devices, across(): lax.ppermute(blocks[i], 'expert', to_expert(i))  9.18 us
    ppermute x3, starting transfers between devices, on_device(): lax.ppermute(sums[i], ('section', 'expert'), onward(i))  5.81 us
    ppermute x3, waiting for transfers between devices, on_device(): lax.ppermute(sums[i], ('section', 'expert'), onward(i))  4.82 us
    ppermute x8, starting transfers between devices, shared(): lax.ppermute(a, 'expert', within(m))  1.78 us
    ppermute x8, waiting for transfers between devices, shared(): lax.ppermute(a, 'expert', within(m))  1.55 us
    ppermute x1, starting transfers between devices, on_device(): lax.ppermute(carry, 'section', [(i, (i + 1) % sections) for i in range(se...  1.49 us
  transfers between devices with their start and end apart: 24, of which 14 were waited for; matrix products, arithmetic and copies ran while one was open for 0% of the time, Pallas kernels for 4%

profile of v9, /device:TPU:0, one launch (start us, length us, event | category | flops | bytes accessed | tf_op | source)
XLA Modules:
  0.0 49.2 jit_solution(10378902539161899211)
XLA Ops:
  0.0 1.6 %shard_map.91 = (bf16[80,256]{1,0:T(8,128)(2,1)S(1)}, bf16[80,256]{1,0:T(8,128)(2,1)S(1)}, bf16[80,256]{1,0:T(8,128)(2,1)S(1)}, bf16[80,256]{1,0:T(8,128)(2,1)S(1)}, bf16[272,256]{1,0:T(8,128)(2,1)S(1)}) custom-call(bf16[16,4096]{1,0:T(8,128)(2,1)} %bitcast.20, f32[1,4096]{1,0:T(1,128)} %refs_4_.1, s32[1,16]{1,0:T(1,128)} %bitcast.21, f32[1,16]{1,0:T(1,128)} %bitcast.22), custom_call_target="tpu_custom_call" | custom-call | flops 10000000000 | bytes 450688 | tf_op jit(solution)/shard_map/pallas_call | solution.py:263
  1.6 0.5 %collective-permute-start.6 = (bf16[80,256]{1,0:T(8,128)(2,1)S(1)}, bf16[80,256]{1,0:T(8,128)(2,1)S(1)}, u32[]{:S(2)}, u32[]{:S(2)}) collective-permute-start(bf16[80,256]{1,0:T(8,128)(2,1)S(1)} %get-tuple-element.45.refs_0_), channel_id=1, source_target_pairs={{0,1},{1,0},{2,3},{3,2},{4,5},{5,4},{6,7},{7,6},{8,9},{9,8},{10,11... | collective-permute-start | bytes 122888 | tf_op jit(solution)/shard_map/ppermute | solution.py:307
  2.1 3.7 %collective-permute-start = (bf16[80,256]{1,0:T(8,128)(2,1)S(1)}, bf16[80,256]{1,0:T(8,128)(2,1)S(1)}, u32[]{:S(2)}, u32[]{:S(2)}) collective-permute-start(bf16[80,256]{1,0:T(8,128)(2,1)S(1)} %get-tuple-element.41), channel_id=1, source_target_pairs={{0,4},{1,5},{2,6},{3,7},{4,0},{5,1},{6,2},{7,3},{8,12},{9,13},{10,... | collective-permute-start | bytes 122888 | tf_op jit(solution)/shard_map/ppermute | solution.py:303
  5.8 1.3 %collective-permute-start.1 = (bf16[80,256]{1,0:T(8,128)(2,1)S(1)}, bf16[80,256]{1,0:T(8,128)(2,1)S(1)}, u32[]{:S(2)}, u32[]{:S(2)}) collective-permute-start(bf16[80,256]{1,0:T(8,128)(2,1)S(1)} %get-tuple-element.42), channel_id=1, source_target_pairs={{0,6},{1,7},{2,4},{3,5},{4,2},{5,3},{6,0},{7,1},{8,14},{9,15},{10,... | collective-permute-start | bytes 122888 | tf_op jit(solution)/shard_map/ppermute | solution.py:303
  7.4 1.8 %shard_map.92 = (bf16[80,256]{1,0:T(8,128)(2,1)S(1)}, bf16[80,256]{1,0:T(8,128)(2,1)S(1)}) custom-call(bf16[4096,512]{1,0:T(8,128)(2,1)S(1)} %bitcast.9, bf16[4096,512]{1,0:T(8,128)(2,1)S(1)} %bitcast.12, bf16[512,4096]{1,0:T(8,128)(2,1)S(1)} %bitcast.15, bf16[80,256]{1,0:T(8,128)(2,1)S(1)} %get-tuple-element.45.refs_0_, ...), custom_call_target="tpu_custom_call" | custom-call | flops 3221225472 | bytes 12746752 | tf_op jit(solution)/shard_map/pallas_call | solution.py:263
  9.3 0.5 collective-permute-start.3
  9.8 1.9 %collective-permute-done.1.refs_1_ = bf16[80,256]{1,0:T(8,128)(2,1)S(1)} collective-permute-done((bf16[80,256]{1,0:T(8,128)(2,1)S(1)}, bf16[80,256]{1,0:T(8,128)(2,1)S(1)}, u32[]{:S(2)}, u32[]{:S(2)}) %collective-permute-start.1) | collective-permute-done | bytes 40992 | tf_op jit(solution)/shard_map/ppermute | solution.py:303
  11.7 0.5 %collective-permute-start.5 = (bf16[80,256]{1,0:T(8,128)(2,1)S(1)}, bf16[80,256]{1,0:T(8,128)(2,1)S(1)}, u32[]{:S(2)}, u32[]{:S(2)}) collective-permute-start(bf16[80,256]{1,0:T(8,128)(2,1)S(1)} %collective-permute-done.2.refs_2_), channel_id=1, source_target_pairs={{0,1},{1,0},{2,3},{3,2},{4,5},{5,4},{6,7},{7,6},{8,9},{9,8},{10,11... | collective-permute-start | bytes 122888 | tf_op jit(solution)/shard_map/ppermute | solution.py:307
  12.5 0.4 collective-permute-done.4.refs_4_
  13.1 2.3 %shard_map.94 = (bf16[240,256]{1,0:T(8,128)(2,1)S(1)}, bf16[240,256]{1,0:T(8,128)(2,1)S(1)}) custom-call(bf16[4096,512]{1,0:T(8,128)(2,1)S(1)} %bitcast.10, bf16[4096,512]{1,0:T(8,128)(2,1)S(1)} %bitcast.13, bf16[512,4096]{1,0:T(8,128)(2,1)S(1)} %bitcast.16, bf16[80,256]{1,0:T(8,128)(2,1)S(1)} %collective-permute-done.refs_0_, ...), custom_call_target="tpu_custom_call" | custom-call | flops 3221225472 | bytes 13074432 | tf_op jit(solution)/shard_map/pallas_call | solution.py:263
  15.4 0.4 collective-permute-start.8
  15.8 1.5 %collective-permute-start.12 = (bf16[352,256]{1,0:T(8,128)(2,1)S(1)}, bf16[352,256]{1,0:T(8,128)(2,1)S(1)}, u32[]{:S(2)}, u32[]{:S(2)}) collective-permute-start(bf16[352,256]{1,0:T(8,128)(2,1)S(1)} %get-tuple-element.63), channel_id=1, source_target_pairs={{0,8},{8,16},{16,24},{24,0},{1,9},{9,17},{17,25},{25,1},{2,10},{10... | collective-permute-start | bytes 540680 | tf_op jit(solution)/shard_map/ppermute | solution.py:360
  17.4 2.5 %collective-permute-start.9 = (bf16[80,256]{1,0:T(8,128)(2,1)S(1)}, bf16[80,256]{1,0:T(8,128)(2,1)S(1)}, u32[]{:S(2)}, u32[]{:S(2)}) collective-permute-start(bf16[80,256]{1,0:T(8,128)(2,1)S(1)} %get-tuple-element.60), channel_id=1, source_target_pairs={{0,12},{1,13},{2,14},{3,15},{4,8},{5,9},{6,10},{7,11},{8,20},{9,21... | collective-permute-start | bytes 122888 | tf_op jit(solution)/shard_map/ppermute | solution.py:362
  19.9 1.9 %collective-permute-start.10 = (bf16[80,256]{1,0:T(8,128)(2,1)S(1)}, bf16[80,256]{1,0:T(8,128)(2,1)S(1)}, u32[]{:S(2)}, u32[]{:S(2)}) collective-permute-start(bf16[80,256]{1,0:T(8,128)(2,1)S(1)} %get-tuple-element.61), channel_id=1, source_target_pairs={{0,14},{1,15},{2,12},{3,13},{4,10},{5,11},{6,8},{7,9},{8,22},{9,23... | collective-permute-start | bytes 122888 | tf_op jit(solution)/shard_map/ppermute | solution.py:362
  21.8 1.4 %collective-permute-start.11 = (bf16[80,256]{1,0:T(8,128)(2,1)S(1)}, bf16[80,256]{1,0:T(8,128)(2,1)S(1)}, u32[]{:S(2)}, u32[]{:S(2)}) collective-permute-start(bf16[80,256]{1,0:T(8,128)(2,1)S(1)} %get-tuple-element.62), channel_id=1, source_target_pairs={{0,10},{1,11},{2,8},{3,9},{4,14},{5,15},{6,12},{7,13},{8,18},{9,19... | collective-permute-start | bytes 122888 | tf_op jit(solution)/shard_map/ppermute | solution.py:362
  23.2 1.0 %collective-permute-done.9.refs_0_ = bf16[80,256]{1,0:T(8,128)(2,1)S(1)} collective-permute-done((bf16[80,256]{1,0:T(8,128)(2,1)S(1)}, bf16[80,256]{1,0:T(8,128)(2,1)S(1)}, u32[]{:S(2)}, u32[]{:S(2)}) %collective-permute-start.9) | collective-permute-done | bytes 40992 | tf_op jit(solution)/shard_map/ppermute | solution.py:362
  24.2 3.5 %collective-permute-done.10.refs_1_ = bf16[80,256]{1,0:T(8,128)(2,1)S(1)} collective-permute-done((bf16[80,256]{1,0:T(8,128)(2,1)S(1)}, bf16[80,256]{1,0:T(8,128)(2,1)S(1)}, u32[]{:S(2)}, u32[]{:S(2)}) %collective-permute-start.10) | collective-permute-done | bytes 40992 | tf_op jit(solution)/shard_map/ppermute | solution.py:362
  28.0 0.7 %shard_map.96 = (bf16[16,4096]{1,0:T(8,128)(2,1)S(1)}, bf16[80,256]{1,0:T(8,128)(2,1)S(1)}, bf16[80,256]{1,0:T(8,128)(2,1)S(1)}, bf16[80,256]{1,0:T(8,128)(2,1)S(1)}, bf16[80,256]{1,0:T(8,128)(2,1)S(1)}) custom-call(bf16[80,256]{1,0:T(8,128)(2,1)S(1)} %collective-permute-done.9.refs_0_, bf16[80,256]{1,0:T(8,128)(2,1)S(1)} %collective-permute-done.10.refs_1_, ...), custom_call_target="tpu_custom_call" | custom-call | bytes 615424 | tf_op jit(solution)/shard_map/pallas_call | solution.py:263
  28.7 1.3 %collective-permute-start.13 = (bf16[80,256]{1,0:T(8,128)(2,1)S(1)}, bf16[80,256]{1,0:T(8,128)(2,1)S(1)}, u32[]{:S(2)}, u32[]{:S(2)}) collective-permute-start(bf16[80,256]{1,0:T(8,128)(2,1)S(1)} %get-tuple-element.66), channel_id=1, source_target_pairs={{0,4},{1,5},{2,6},{3,7},{4,0},{5,1},{6,2},{7,3},{8,12},{9,13},{10,... | collective-permute-start | bytes 122888 | tf_op jit(solution)/shard_map/ppermute | solution.py:303
  30.0 1.7 %collective-permute-start.14 = (bf16[80,256]{1,0:T(8,128)(2,1)S(1)}, bf16[80,256]{1,0:T(8,128)(2,1)S(1)}, u32[]{:S(2)}, u32[]{:S(2)}) collective-permute-start(bf16[80,256]{1,0:T(8,128)(2,1)S(1)} %get-tuple-element.67), channel_id=1, source_target_pairs={{0,6},{1,7},{2,4},{3,5},{4,2},{5,3},{6,0},{7,1},{8,14},{9,15},{10,... | collective-permute-start | bytes 122888 | tf_op jit(solution)/shard_map/ppermute | solution.py:303
  31.7 0.6 %collective-permute-start.15 = (bf16[80,256]{1,0:T(8,128)(2,1)S(1)}, bf16[80,256]{1,0:T(8,128)(2,1)S(1)}, u32[]{:S(2)}, u32[]{:S(2)}) collective-permute-start(bf16[80,256]{1,0:T(8,128)(2,1)S(1)} %get-tuple-element.68), channel_id=1, source_target_pairs={{0,2},{1,3},{2,0},{3,1},{4,6},{5,7},{6,4},{7,5},{8,10},{9,11},{10,... | collective-permute-start | bytes 122888 | tf_op jit(solution)/shard_map/ppermute | solution.py:303
  32.3 1.8 %collective-permute-done.13.refs_0_ = bf16[80,256]{1,0:T(8,128)(2,1)S(1)} collective-permute-done((bf16[80,256]{1,0:T(8,128)(2,1)S(1)}, bf16[80,256]{1,0:T(8,128)(2,1)S(1)}, u32[]{:S(2)}, u32[]{:S(2)}) %collective-permute-start.13) | collective-permute-done | bytes 40992 | tf_op jit(solution)/shard_map/ppermute | solution.py:303
  34.1 1.8 %collective-permute-done.14.refs_1_ = bf16[80,256]{1,0:T(8,128)(2,1)S(1)} collective-permute-done((bf16[80,256]{1,0:T(8,128)(2,1)S(1)}, bf16[80,256]{1,0:T(8,128)(2,1)S(1)}, u32[]{:S(2)}, u32[]{:S(2)}) %collective-permute-start.14) | collective-permute-done | bytes 40992 | tf_op jit(solution)/shard_map/ppermute | solution.py:303
  36.4 0.7 %collective-permute-done.17.refs_5_ = bf16[80,256]{1,0:T(8,128)(2,1)S(1)} collective-permute-done((bf16[80,256]{1,0:T(8,128)(2,1)S(1)}, bf16[80,256]{1,0:T(8,128)(2,1)S(1)}, u32[]{:S(2)}, u32[]{:S(2)}) %collective-permute-start.17) | collective-permute-done | bytes 40992 | tf_op jit(solution)/shard_map/ppermute | solution.py:307
  37.4 2.4 %shard_map.97 = (bf16[320,256]{1,0:T(8,128)(2,1)S(1)}, bf16[320,256]{1,0:T(8,128)(2,1)S(1)}) custom-call(bf16[4096,512]{1,0:T(8,128)(2,1)S(1)} %bitcast.11, bf16[4096,512]{1,0:T(8,128)(2,1)S(1)} %bitcast.14, bf16[512,4096]{1,0:T(8,128)(2,1)S(1)} %bitcast.17, bf16[80,256]{1,0:T(8,128)(2,1)S(1)} %collective-permute-done.13.refs_0_, ...), custom_call_target="tpu_custom_call" | custom-call | flops 3221225472 | bytes 13238272 | tf_op jit(solution)/shard_map/pallas_call | solution.py:263
  40.1 1.2 %collective-permute-done.20.refs_1_ = bf16[320,256]{1,0:T(8,128)(2,1)S(1)} collective-permute-done((bf16[320,256]{1,0:T(8,128)(2,1)S(1)}, bf16[320,256]{1,0:T(8,128)(2,1)S(1)}, u32[]{:S(2)}, u32[]{:S(2)}) %collective-permute-start.20) | collective-permute-done | bytes 163872 | tf_op jit(solution)/shard_map/ppermute | solution.py:323
  41.3 1.2 %collective-permute-start.21 = (bf16[80,256]{1,0:T(8,128)(2,1)S(1)}, bf16[80,256]{1,0:T(8,128)(2,1)S(1)}, u32[]{:S(2)}, u32[]{:S(2)}) collective-permute-start(bf16[80,256]{1,0:T(8,128)(2,1)S(1)} %get-tuple-element.72), channel_id=1, source_target_pairs={{0,4},{1,5},{2,6},{3,7},{4,0},{5,1},{6,2},{7,3},{8,12},{9,13},{10,... | collective-permute-start | bytes 122888 | tf_op jit(solution)/shard_map/ppermute | solution.py:303
  42.4 1.4 %collective-permute-start.22 = (bf16[80,256]{1,0:T(8,128)(2,1)S(1)}, bf16[80,256]{1,0:T(8,128)(2,1)S(1)}, u32[]{:S(2)}, u32[]{:S(2)}) collective-permute-start(bf16[80,256]{1,0:T(8,128)(2,1)S(1)} %get-tuple-element.73), channel_id=1, source_target_pairs={{0,6},{1,7},{2,4},{3,5},{4,2},{5,3},{6,0},{7,1},{8,14},{9,15},{10,... | collective-permute-start | bytes 122888 | tf_op jit(solution)/shard_map/ppermute | solution.py:303
  43.8 1.0 %collective-permute-start.23 = (bf16[80,256]{1,0:T(8,128)(2,1)S(1)}, bf16[80,256]{1,0:T(8,128)(2,1)S(1)}, u32[]{:S(2)}, u32[]{:S(2)}) collective-permute-start(bf16[80,256]{1,0:T(8,128)(2,1)S(1)} %get-tuple-element.74), channel_id=1, source_target_pairs={{0,2},{1,3},{2,0},{3,1},{4,6},{5,7},{6,4},{7,5},{8,10},{9,11},{10,... | collective-permute-start | bytes 122888 | tf_op jit(solution)/shard_map/ppermute | solution.py:303
  44.8 1.9 %collective-permute-done.21.b0 = bf16[80,256]{1,0:T(8,128)(2,1)S(1)} collective-permute-done((bf16[80,256]{1,0:T(8,128)(2,1)S(1)}, bf16[80,256]{1,0:T(8,128)(2,1)S(1)}, u32[]{:S(2)}, u32[]{:S(2)}) %collective-permute-start.21) | collective-permute-done | bytes 40992 | tf_op jit(solution)/shard_map/ppermute | solution.py:303
  46.7 1.5 %collective-permute-done.22.b1 = bf16[80,256]{1,0:T(8,128)(2,1)S(1)} collective-permute-done((bf16[80,256]{1,0:T(8,128)(2,1)S(1)}, bf16[80,256]{1,0:T(8,128)(2,1)S(1)}, u32[]{:S(2)}, u32[]{:S(2)}) %collective-permute-start.22) | collective-permute-done | bytes 40992 | tf_op jit(solution)/shard_map/ppermute | solution.py:303
  48.3 1.0 %shard_map.99 = bf16[16,4096]{1,0:T(8,128)(2,1)} custom-call(bf16[16,4096]{1,0:T(8,128)(2,1)S(1)} %get-tuple-element.65.x_ref, bf16[80,256]{1,0:T(8,128)(2,1)S(1)} %collective-permute-done.21.b0, bf16[80,256]{1,0:T(8,128)(2,1)S(1)} %collective-permute-done.22.b1, bf16[80,256]{1,0:T(8,128)(2,1)S(1)} %collective-permute-done.23.b2, ...), custom_call_target="tpu_custom_call" | custom-call | bytes 435200 | tf_op jit(solution)/shard_map/pallas_call | solution.py:263
  (37 shorter events, 2.3 us)
Async XLA Ops:
  0.0 7.4 %copy-start = (bf16[1,1,4096,512]{3,2,1,0:T(8,128)(2,1)S(1)}, bf16[1,1,4096,512]{3,2,1,0:T(8,128)(2,1)}, u32[]{:S(2)}) copy-start(bf16[1,1,4096,512]{3,2,1,0:T(8,128)(2,1)} %param.15) | copy-start | bytes 12582916
  0.0 7.4 %copy-start.1 = (bf16[1,1,4096,512]{3,2,1,0:T(8,128)(2,1)S(1)}, bf16[1,1,4096,512]{3,2,1,0:T(8,128)(2,1)}, u32[]{:S(2)}) copy-start(bf16[1,1,4096,512]{3,2,1,0:T(8,128)(2,1)} %param.16) | copy-start | bytes 12582916
  0.0 7.4 %copy-start.2 = (bf16[1,1,512,4096]{3,2,1,0:T(8,128)(2,1)S(1)}, bf16[1,1,512,4096]{3,2,1,0:T(8,128)(2,1)}, u32[]{:S(2)}) copy-start(bf16[1,1,512,4096]{3,2,1,0:T(8,128)(2,1)} %param.17) | copy-start | bytes 12582916
  1.6 5.8 %collective-permute-start.6 = (bf16[80,256]{1,0:T(8,128)(2,1)S(1)}, bf16[80,256]{1,0:T(8,128)(2,1)S(1)}, u32[]{:S(2)}, u32[]{:S(2)}) collective-permute-start(bf16[80,256]{1,0:T(8,128)(2,1)S(1)} %get-tuple-element.45.refs_0_), channel_id=1, source_target_pairs={{0,1},{1,0},{2,3},{3,2},{4,5},{5,4},{6,7},{7,6},{8,9},{9,8},{10,11... | collective-permute-start | bytes 122888 | tf_op jit(solution)/shard_map/ppermute | solution.py:307
  2.1 7.2 %collective-permute-start = (bf16[80,256]{1,0:T(8,128)(2,1)S(1)}, bf16[80,256]{1,0:T(8,128)(2,1)S(1)}, u32[]{:S(2)}, u32[]{:S(2)}) collective-permute-start(bf16[80,256]{1,0:T(8,128)(2,1)S(1)} %get-tuple-element.41), channel_id=1, source_target_pairs={{0,4},{1,5},{2,6},{3,7},{4,0},{5,1},{6,2},{7,3},{8,12},{9,13},{10,... | collective-permute-start | bytes 122888 | tf_op jit(solution)/shard_map/ppermute | solution.py:303
  5.8 5.9 %collective-permute-start.1 = (bf16[80,256]{1,0:T(8,128)(2,1)S(1)}, bf16[80,256]{1,0:T(8,128)(2,1)S(1)}, u32[]{:S(2)}, u32[]{:S(2)}) collective-permute-start(bf16[80,256]{1,0:T(8,128)(2,1)S(1)} %get-tuple-element.42), channel_id=1, source_target_pairs={{0,6},{1,7},{2,4},{3,5},{4,2},{5,3},{6,0},{7,1},{8,14},{9,15},{10,... | collective-permute-start | bytes 122888 | tf_op jit(solution)/shard_map/ppermute | solution.py:303
  7.1 4.6 %collective-permute-start.2 = (bf16[80,256]{1,0:T(8,128)(2,1)S(1)}, bf16[80,256]{1,0:T(8,128)(2,1)S(1)}, u32[]{:S(2)}, u32[]{:S(2)}) collective-permute-start(bf16[80,256]{1,0:T(8,128)(2,1)S(1)} %get-tuple-element.43), channel_id=1, source_target_pairs={{0,2},{1,3},{2,0},{3,1},{4,6},{5,7},{6,4},{7,5},{8,10},{9,11},{10,... | collective-permute-start | bytes 122888 | tf_op jit(solution)/shard_map/ppermute | solution.py:303
  7.4 4.8 %copy-start.4 = (s32[1,16,1]{1,2,0:T(1,128)S(1)}, s32[1,16,1]{1,2,0:T(1,128)}, u32[]{:S(2)}) copy-start(s32[1,16,1]{1,2,0:T(1,128)} %param.13) | copy-start | bytes 196
  7.4 4.8 %copy-start.5 = (f32[1,16,1]{1,2,0:T(1,128)S(1)}, f32[1,16,1]{1,2,0:T(1,128)}, u32[]{:S(2)}) copy-start(f32[1,16,1]{1,2,0:T(1,128)} %param.14) | copy-start | bytes 196
  9.2 3.0 %collective-permute-start.7 = (bf16[80,256]{1,0:T(8,128)(2,1)S(1)}, bf16[80,256]{1,0:T(8,128)(2,1)S(1)}, u32[]{:S(2)}, u32[]{:S(2)}) collective-permute-start(bf16[80,256]{1,0:T(8,128)(2,1)S(1)} %get-tuple-element.47), channel_id=1, source_target_pairs={{0,1},{1,0},{2,3},{3,2},{4,5},{5,4},{6,7},{7,6},{8,9},{9,8},{10,11... | collective-permute-start | bytes 122888 | tf_op jit(solution)/shard_map/ppermute | solution.py:323
  9.3 3.2 %collective-permute-start.3 = (bf16[80,256]{1,0:T(8,128)(2,1)S(1)}, bf16[80,256]{1,0:T(8,128)(2,1)S(1)}, u32[]{:S(2)}, u32[]{:S(2)}) collective-permute-start(bf16[80,256]{1,0:T(8,128)(2,1)S(1)} %collective-permute-done.refs_0_), channel_id=1, source_target_pairs={{0,1},{1,0},{2,3},{3,2},{4,5},{5,4},{6,7},{7,6},{8,9},{9,8},{10,11... | collective-permute-start | bytes 122888 | tf_op jit(solution)/shard_map/ppermute | solution.py:307
  11.7 1.2 %collective-permute-start.4 = (bf16[80,256]{1,0:T(8,128)(2,1)S(1)}, bf16[80,256]{1,0:T(8,128)(2,1)S(1)}, u32[]{:S(2)}, u32[]{:S(2)}) collective-permute-start(bf16[80,256]{1,0:T(8,128)(2,1)S(1)} %collective-permute-done.1.refs_1_), channel_id=1, source_target_pairs={{0,1},{1,0},{2,3},{3,2},{4,5},{5,4},{6,7},{7,6},{8,9},{9,8},{10,11... | collective-permute-start | bytes 122888 | tf_op jit(solution)/shard_map/ppermute | solution.py:307
  11.7 1.4 %collective-permute-start.5 = (bf16[80,256]{1,0:T(8,128)(2,1)S(1)}, bf16[80,256]{1,0:T(8,128)(2,1)S(1)}, u32[]{:S(2)}, u32[]{:S(2)}) collective-permute-start(bf16[80,256]{1,0:T(8,128)(2,1)S(1)} %collective-permute-done.2.refs_2_), channel_id=1, source_target_pairs={{0,1},{1,0},{2,3},{3,2},{4,5},{5,4},{6,7},{7,6},{8,9},{9,8},{10,11... | collective-permute-start | bytes 122888 | tf_op jit(solution)/shard_map/ppermute | solution.py:307
  13.1 14.9 %copy-start.3 = (f32[1,4096]{1,0:T(1,128)S(1)}, f32[1,4096]{1,0:T(1,128)}, u32[]{:S(2)}) copy-start(f32[1,4096]{1,0:T(1,128)} %refs_4_.1) | copy-start | bytes 49156
  15.4 1.9 %collective-permute-start.8 = (bf16[240,256]{1,0:T(8,128)(2,1)S(1)}, bf16[240,256]{1,0:T(8,128)(2,1)S(1)}, u32[]{:S(2)}, u32[]{:S(2)}) collective-permute-start(bf16[240,256]{1,0:T(8,128)(2,1)S(1)} %get-tuple-element.59), channel_id=1, source_target_pairs={{0,1},{1,0},{2,3},{3,2},{4,5},{5,4},{6,7},{7,6},{8,9},{9,8},{10,11... | collective-permute-start | bytes 368648 | tf_op jit(solution)/shard_map/ppermute | solution.py:323
  15.8 12.2 %collective-permute-start.12 = (bf16[352,256]{1,0:T(8,128)(2,1)S(1)}, bf16[352,256]{1,0:T(8,128)(2,1)S(1)}, u32[]{:S(2)}, u32[]{:S(2)}) collective-permute-start(bf16[352,256]{1,0:T(8,128)(2,1)S(1)} %get-tuple-element.63), channel_id=1, source_target_pairs={{0,8},{8,16},{16,24},{24,0},{1,9},{9,17},{17,25},{25,1},{2,10},{10... | collective-permute-start | bytes 540680 | tf_op jit(solution)/shard_map/ppermute | solution.py:360
  17.4 6.9 %collective-permute-start.9 = (bf16[80,256]{1,0:T(8,128)(2,1)S(1)}, bf16[80,256]{1,0:T(8,128)(2,1)S(1)}, u32[]{:S(2)}, u32[]{:S(2)}) collective-permute-start(bf16[80,256]{1,0:T(8,128)(2,1)S(1)} %get-tuple-element.60), channel_id=1, source_target_pairs={{0,12},{1,13},{2,14},{3,15},{4,8},{5,9},{6,10},{7,11},{8,20},{9,21... | collective-permute-start | bytes 122888 | tf_op jit(solution)/shard_map/ppermute | solution.py:362
  19.9 7.8 %collective-permute-start.10 = (bf16[80,256]{1,0:T(8,128)(2,1)S(1)}, bf16[80,256]{1,0:T(8,128)(2,1)S(1)}, u32[]{:S(2)}, u32[]{:S(2)}) collective-permute-start(bf16[80,256]{1,0:T(8,128)(2,1)S(1)} %get-tuple-element.61), channel_id=1, source_target_pairs={{0,14},{1,15},{2,12},{3,13},{4,10},{5,11},{6,8},{7,9},{8,22},{9,23... | collective-permute-start | bytes 122888 | tf_op jit(solution)/shard_map/ppermute | solution.py:362
  21.8 6.2 %collective-permute-start.11 = (bf16[80,256]{1,0:T(8,128)(2,1)S(1)}, bf16[80,256]{1,0:T(8,128)(2,1)S(1)}, u32[]{:S(2)}, u32[]{:S(2)}) collective-permute-start(bf16[80,256]{1,0:T(8,128)(2,1)S(1)} %get-tuple-element.62), channel_id=1, source_target_pairs={{0,10},{1,11},{2,8},{3,9},{4,14},{5,15},{6,12},{7,13},{8,18},{9,19... | collective-permute-start | bytes 122888 | tf_op jit(solution)/shard_map/ppermute | solution.py:362
  28.7 5.4 %collective-permute-start.13 = (bf16[80,256]{1,0:T(8,128)(2,1)S(1)}, bf16[80,256]{1,0:T(8,128)(2,1)S(1)}, u32[]{:S(2)}, u32[]{:S(2)}) collective-permute-start(bf16[80,256]{1,0:T(8,128)(2,1)S(1)} %get-tuple-element.66), channel_id=1, source_target_pairs={{0,4},{1,5},{2,6},{3,7},{4,0},{5,1},{6,2},{7,3},{8,12},{9,13},{10,... | collective-permute-start | bytes 122888 | tf_op jit(solution)/shard_map/ppermute | solution.py:303
  30.0 5.9 %collective-permute-start.14 = (bf16[80,256]{1,0:T(8,128)(2,1)S(1)}, bf16[80,256]{1,0:T(8,128)(2,1)S(1)}, u32[]{:S(2)}, u32[]{:S(2)}) collective-permute-start(bf16[80,256]{1,0:T(8,128)(2,1)S(1)} %get-tuple-element.67), channel_id=1, source_target_pairs={{0,6},{1,7},{2,4},{3,5},{4,2},{5,3},{6,0},{7,1},{8,14},{9,15},{10,... | collective-permute-start | bytes 122888 | tf_op jit(solution)/shard_map/ppermute | solution.py:303
  31.7 4.4 %collective-permute-start.15 = (bf16[80,256]{1,0:T(8,128)(2,1)S(1)}, bf16[80,256]{1,0:T(8,128)(2,1)S(1)}, u32[]{:S(2)}, u32[]{:S(2)}) collective-permute-start(bf16[80,256]{1,0:T(8,128)(2,1)S(1)} %get-tuple-element.68), channel_id=1, source_target_pairs={{0,2},{1,3},{2,0},{3,1},{4,6},{5,7},{6,4},{7,5},{8,10},{9,11},{10,... | collective-permute-start | bytes 122888 | tf_op jit(solution)/shard_map/ppermute | solution.py:303
  32.3 4.1 %collective-permute-start.19 = (bf16[80,256]{1,0:T(8,128)(2,1)S(1)}, bf16[80,256]{1,0:T(8,128)(2,1)S(1)}, u32[]{:S(2)}, u32[]{:S(2)}) collective-permute-start(bf16[80,256]{1,0:T(8,128)(2,1)S(1)} %get-tuple-element.69.refs_3_), channel_id=1, source_target_pairs={{0,1},{1,0},{2,3},{3,2},{4,5},{5,4},{6,7},{7,6},{8,9},{9,8},{10,11... | collective-permute-start | bytes 122888 | tf_op jit(solution)/shard_map/ppermute | solution.py:307
  34.1 2.3 %collective-permute-start.16 = (bf16[80,256]{1,0:T(8,128)(2,1)S(1)}, bf16[80,256]{1,0:T(8,128)(2,1)S(1)}, u32[]{:S(2)}, u32[]{:S(2)}) collective-permute-start(bf16[80,256]{1,0:T(8,128)(2,1)S(1)} %collective-permute-done.13.refs_0_), channel_id=1, source_target_pairs={{0,1},{1,0},{2,3},{3,2},{4,5},{5,4},{6,7},{7,6},{8,9},{9,8},{10,11... | collective-permute-start | bytes 122888 | tf_op jit(solution)/shard_map/ppermute | solution.py:307
  35.9 1.2 %collective-permute-start.17 = (bf16[80,256]{1,0:T(8,128)(2,1)S(1)}, bf16[80,256]{1,0:T(8,128)(2,1)S(1)}, u32[]{:S(2)}, u32[]{:S(2)}) collective-permute-start(bf16[80,256]{1,0:T(8,128)(2,1)S(1)} %collective-permute-done.14.refs_1_), channel_id=1, source_target_pairs={{0,1},{1,0},{2,3},{3,2},{4,5},{5,4},{6,7},{7,6},{8,9},{9,8},{10,11... | collective-permute-start | bytes 122888 | tf_op jit(solution)/shard_map/ppermute | solution.py:307
  36.1 1.2 %collective-permute-start.18 = (bf16[80,256]{1,0:T(8,128)(2,1)S(1)}, bf16[80,256]{1,0:T(8,128)(2,1)S(1)}, u32[]{:S(2)}, u32[]{:S(2)}) collective-permute-start(bf16[80,256]{1,0:T(8,128)(2,1)S(1)} %collective-permute-done.15.refs_2_), channel_id=1, source_target_pairs={{0,1},{1,0},{2,3},{3,2},{4,5},{5,4},{6,7},{7,6},{8,9},{9,8},{10,11... | collective-permute-start | bytes 122888 | tf_op jit(solution)/shard_map/ppermute | solution.py:307
  39.8 1.5 %collective-permute-start.20 = (bf16[320,256]{1,0:T(8,128)(2,1)S(1)}, bf16[320,256]{1,0:T(8,128)(2,1)S(1)}, u32[]{:S(2)}, u32[]{:S(2)}) collective-permute-start(bf16[320,256]{1,0:T(8,128)(2,1)S(1)} %get-tuple-element.71), channel_id=1, source_target_pairs={{0,1},{1,0},{2,3},{3,2},{4,5},{5,4},{6,7},{7,6},{8,9},{9,8},{10,11... | collective-permute-start | bytes 491528 | tf_op jit(solution)/shard_map/ppermute | solution.py:323
  41.3 5.5 %collective-permute-start.21 = (bf16[80,256]{1,0:T(8,128)(2,1)S(1)}, bf16[80,256]{1,0:T(8,128)(2,1)S(1)}, u32[]{:S(2)}, u32[]{:S(2)}) collective-permute-start(bf16[80,256]{1,0:T(8,128)(2,1)S(1)} %get-tuple-element.72), channel_id=1, source_target_pairs={{0,4},{1,5},{2,6},{3,7},{4,0},{5,1},{6,2},{7,3},{8,12},{9,13},{10,... | collective-permute-start | bytes 122888 | tf_op jit(solution)/shard_map/ppermute | solution.py:303
  42.4 5.8 %collective-permute-start.22 = (bf16[80,256]{1,0:T(8,128)(2,1)S(1)}, bf16[80,256]{1,0:T(8,128)(2,1)S(1)}, u32[]{:S(2)}, u32[]{:S(2)}) collective-permute-start(bf16[80,256]{1,0:T(8,128)(2,1)S(1)} %get-tuple-element.73), channel_id=1, source_target_pairs={{0,6},{1,7},{2,4},{3,5},{4,2},{5,3},{6,0},{7,1},{8,14},{9,15},{10,... | collective-permute-start | bytes 122888 | tf_op jit(solution)/shard_map/ppermute | solution.py:303
  43.8 4.4 %collective-permute-start.23 = (bf16[80,256]{1,0:T(8,128)(2,1)S(1)}, bf16[80,256]{1,0:T(8,128)(2,1)S(1)}, u32[]{:S(2)}, u32[]{:S(2)}) collective-permute-start(bf16[80,256]{1,0:T(8,128)(2,1)S(1)} %get-tuple-element.74), channel_id=1, source_target_pairs={{0,2},{1,3},{2,0},{3,1},{4,6},{5,7},{6,4},{7,5},{8,10},{9,11},{10,... | collective-permute-start | bytes 122888 | tf_op jit(solution)/shard_map/ppermute | solution.py:303
